TPU v7x, 32 devices: a whole 2x2x4 slice. The times are simulated.
32 devices in a mesh: dp: 4 (over z), pipe: 2 (over core), tensor: 4 (over y, x).
Axes of the slice: x: 2, y: 2, z: 4, core: 2. Of those that a mesh axis runs over, the one named last changes fastest.
Arguments:
- tokens: bfloat16 [8, 64, 4096], P('dp', None, 'tensor'), may hold values from -8 to 8
- w_query: bfloat16 [2, 2, 4096, 4096], P(None, 'pipe', 'dp', 'tensor'), may hold values from -8 to 8
- w_key: bfloat16 [2, 2, 4096, 1024], P(None, 'pipe', 'dp', 'tensor'), may hold values from -1 to 1
- w_value: bfloat16 [2, 2, 4096, 1024], P(None, 'pipe', 'dp', 'tensor'), may hold values from -0.09375 to 0.09375
- w_out: bfloat16 [2, 2, 4096, 4096], P(None, 'pipe', 'tensor', 'dp'), may hold values from -0.09375 to 0.09375
- norm_gain: float32 [2, 2, 4096], P(None, 'pipe'), may hold values from 0.5 to 1.5
- boundary: int32 [8], P('dp'), may hold values from 1 to 63
- skip_offset: int32 [8], P('dp'), may hold values from 0 to 131008
- doc_lengths: int32 [8, 4], P('dp'), may hold values from 1 to 32, 64 in all within a row
- batch_order: int32 [4, 2], P('dp'), may hold values from 0 to 1, each once within a row
Outputs:
- final_state: bfloat16 [8, 64, 4096], P('dp', 'pipe', 'tensor')
Inputs may be any that keep to these rules, and one draw needn't show every extreme that they name: `doc_lengths`: each row sums to 64. `batch_order`: each row is a permutation.
All inputs are finite; a program needn't handle non-finite values.
Results may differ from a plain program's by a relative error of at most 0.014.
Values may be sent and summed in bfloat16 or wider, within the bound.
No kernel may reach another device: no remote copies, remote signals or barrier semaphores. Data moves between devices by JAX's collectives and lax.ppermute only.
A program may use at most 192 MiB of HBM per device.

v0:
```python
from functools import partial

import jax
import jax.numpy as jnp
from jax import lax
from jax.sharding import PartitionSpec as P

HEAD_DIM = 128


ROPE_THETA = 500000.0
NORM_EPSILON = 1e-05


def from_behind(value, axis, by):
    peers = lax.axis_size(axis)
    pairs = [(i, i + by) for i in range(peers) if 0 <= i + by < peers]
    return lax.ppermute(value, axis, pairs)


def broadcast(value, axis, source):
    kept = jnp.where(lax.axis_index(axis) == source, value, 0).astype(value.dtype)
    return lax.psum(kept, axis)


def rope_angles(positions, head_dim):
    half_dim = head_dim // 2
    exponent = jnp.arange(half_dim, dtype=jnp.float32) * (2.0 / head_dim)
    frequency = jnp.float32(ROPE_THETA) ** (-exponent)
    return positions.astype(jnp.float32)[..., None] * frequency


def rotate(values, angles):
    half_dim = values.shape[-1] // 2
    first_half = values[..., :half_dim]
    second = values[..., half_dim:]
    cosine = jnp.cos(angles)[:, None, :]
    sine_part = jnp.sin(angles)[:, None, :]
    return jnp.concatenate(
        [first_half * cosine - second * sine_part, second * cosine + first_half * sine_part],
        axis=-1,
    )


def sample_layout(first_cut, offset, lengths, seq_len):
    places = jnp.arange(seq_len, dtype=jnp.int32)
    positions = jnp.where(places < first_cut, places, places + offset)
    doc_ends = jnp.cumsum(lengths)
    doc_ids = jnp.sum((places[:, None] >= doc_ends[None, :]).astype(jnp.int32), axis=1)
    allowed = (doc_ids[:, None] == doc_ids[None, :]) & (places[None, :] <= places[:, None])
    return (positions, allowed)


def attend(normed, q_weight, k_weight, v_weight, angles, allowed):
    seq_len = normed.shape[0]
    q_heads = q_weight.shape[1] // HEAD_DIM
    kv_heads = k_weight.shape[1] // HEAD_DIM
    group_size = q_heads // kv_heads
    queries = jnp.dot(normed, q_weight, preferred_element_type=jnp.float32)
    key_vecs = jnp.dot(normed, k_weight, preferred_element_type=jnp.float32)
    value_vecs = jnp.dot(normed, v_weight, preferred_element_type=jnp.float32).astype(jnp.bfloat16)
    value_vecs = value_vecs.reshape(seq_len, kv_heads, HEAD_DIM)
    queries = rotate(queries.reshape(seq_len, q_heads, HEAD_DIM), angles).astype(jnp.bfloat16)
    queries = queries.reshape(seq_len, kv_heads, group_size, HEAD_DIM)
    key_vecs = rotate(key_vecs.reshape(seq_len, kv_heads, HEAD_DIM), angles).astype(jnp.bfloat16)
    scores = jnp.einsum(
        "skgd,tkd->kgst", queries, key_vecs, preferred_element_type=jnp.float32
    ) * HEAD_DIM ** (-0.5)
    scores = jnp.where(allowed[None, None], scores, -jnp.inf)
    row_max = jnp.max(scores, axis=-1, keepdims=True)
    exp_scores = jnp.exp(scores - row_max)
    weights = (exp_scores / jnp.sum(exp_scores, axis=-1, keepdims=True)).astype(jnp.bfloat16)
    mixed = jnp.einsum("kgst,tkd->skgd", weights, value_vecs, preferred_element_type=jnp.float32)
    return mixed.reshape(seq_len, q_heads * HEAD_DIM)


def layer_step(stream, active, gain_row, weight_three, out_part, angles, allowed):
    gathered = lax.all_gather(stream, "tensor", axis=1, tiled=True)
    seq_len = gathered.shape[0]
    head_width = weight_three[0].shape[1]

    def local_mix():
        widened = gathered.astype(jnp.float32)
        inv_rms = lax.rsqrt(jnp.mean(widened * widened, axis=-1, keepdims=True) + NORM_EPSILON)
        normed = (widened * inv_rms * gain_row).astype(jnp.bfloat16)
        return attend(
            normed, weight_three[0], weight_three[1], weight_three[2], angles, allowed
        ).astype(jnp.bfloat16)

    mixed = lax.cond(active, local_mix, lambda: jnp.zeros((seq_len, head_width), jnp.bfloat16))
    piece = lax.all_gather(mixed, "dp", axis=0, tiled=True)
    stacked = lax.cond(
        active,
        lambda: jnp.dot(piece, out_part, preferred_element_type=jnp.float32),
        lambda: jnp.zeros((piece.shape[0], out_part.shape[1]), jnp.float32),
    )
    partial_sum = lax.all_to_all(stacked, "dp", split_axis=0, concat_axis=1, tiled=True)
    shares = lax.psum_scatter(partial_sum, "tensor", scatter_dimension=1, tiled=True)
    updated = (stream.astype(jnp.float32) + shares).astype(jnp.bfloat16)
    return jnp.where(active, updated, jnp.zeros_like(updated))


def per_device(
    tokens,
    w_query,
    w_key,
    w_value,
    w_out,
    norm_gain,
    boundary,
    skip_offset,
    doc_lengths,
    batch_order,
):
    sections = lax.axis_size("pipe")
    my_section = lax.axis_index("pipe")
    micro_count = tokens.shape[0]
    seq_len = tokens.shape[1]
    local_width = tokens.shape[2]
    ordered = batch_order[0]
    slot_of = jnp.arange(micro_count, dtype=jnp.int32)
    samples = jnp.take(ordered, slot_of)
    feed_rows = jnp.take(tokens, samples, axis=0)
    positions, allowed = jax.vmap(partial(sample_layout, seq_len=seq_len))(
        jnp.take(boundary, samples),
        jnp.take(skip_offset, samples),
        jnp.take(doc_lengths, samples, axis=0),
    )
    angles = rope_angles(positions, HEAD_DIM)
    down_gain = norm_gain[0, 0]
    up_gain = norm_gain[1, 0]
    down_out_part = w_out[0, 0]
    up_out_part = w_out[1, 0]
    query_full, key_full, value_full = (
        lax.all_gather(w_query, "dp", axis=2, tiled=True),
        lax.all_gather(w_key, "dp", axis=2, tiled=True),
        lax.all_gather(w_value, "dp", axis=2, tiled=True),
    )
    down_three = (query_full[0, 0], key_full[0, 0], value_full[0, 0])
    up_three = (query_full[1, 0], key_full[1, 0], value_full[1, 0])
    step_count = micro_count + 2 * sections - 2
    empty_rows = jnp.zeros((seq_len, local_width), jnp.bfloat16)
    last_item = micro_count - 1

    def select_item(stacked, item_index):
        return lax.dynamic_index_in_dim(
            stacked, jnp.clip(item_index, 0, last_item), 0, keepdims=False
        )

    def advance(tick_now, loop_state):
        down_buf, up_buf, results, up_weights = loop_state
        down_item = tick_now - my_section
        down_ok = (down_item >= 0) & (down_item < micro_count)
        down_in = jnp.where(my_section == 0, select_item(feed_rows, tick_now), down_buf)
        down_out = layer_step(
            down_in,
            down_ok,
            down_gain,
            down_three,
            down_out_part,
            select_item(angles, down_item),
            select_item(allowed, down_item),
        )
        up_item = tick_now - (2 * sections - 2 - my_section)
        up_ok = (up_item >= 0) & (up_item < micro_count)
        up_in = jnp.where(my_section == sections - 1, down_out, up_buf)
        up_out = layer_step(
            up_in,
            up_ok,
            up_gain,
            up_weights,
            up_out_part,
            select_item(angles, up_item),
            select_item(allowed, up_item),
        )
        out_slot = select_item(slot_of, up_item)
        stored = lax.dynamic_update_index_in_dim(results, up_out, out_slot, 0)
        results = jnp.where(up_ok & (my_section == 0), stored, results)
        down_buf = from_behind(down_out, "pipe", 1)
        up_buf = from_behind(up_out, "pipe", -1)
        return (down_buf, up_buf, results, up_weights)

    initial = (
        empty_rows,
        empty_rows,
        jnp.zeros((micro_count, seq_len, local_width), jnp.bfloat16),
        up_three,
    )
    down_buf, up_buf, results, up_weights = lax.fori_loop(0, step_count, advance, initial)
    spread = broadcast(results, "pipe", 0)
    row_count = seq_len // sections
    return lax.dynamic_slice_in_dim(spread, my_section * row_count, row_count, 1)


def solution(mesh):
    placed = (
        P("dp", None, "tensor"),
        P(None, "pipe", "dp", "tensor"),
        P(None, "pipe", "dp", "tensor"),
        P(None, "pipe", "dp", "tensor"),
        P(None, "pipe", "tensor", "dp"),
        P(None, "pipe", None),
        P("dp"),
        P("dp"),
        P("dp", None),
        P("dp", None),
    )
    return jax.shard_map(
        per_device, mesh=mesh, in_specs=placed, out_specs=P("dp", "pipe", "tensor"), check_vma=False
    )
```

profile of v0, /device:TPU:7, one launch (start us, length us, event | category | flops | bytes accessed | tf_op | source)
XLA Modules:
  0.0 1211.4 jit_solution(8882073255047853206)
XLA Ops:
  13.2 4.0 slice_bitcast_fusion.6
  17.1 73.8 %all-gather.6.cloned.1.call-done = bf16[2,1,4096,256]{3,2,1,0:T(8,128)(2,1)} async-done(((bf16[2,1,1024,256]{3,2,1,0:T(8,128)(2,1)}), bf16[2,1,4096,256]{3,2,1,0:T(8,128)(2,1)}) %all-gather.6.cloned.1.call-update) | async-done | bytes 4194320 | tf_op jit(solution)/shard_map/all_gather | solution.py:136
  90.9 4.6 slice_bitcast_fusion.2
  95.5 76.3 %all-gather.4.cloned.1.call-done = bf16[2,1,4096,256]{3,2,1,0:T(8,128)(2,1)} async-done(((bf16[2,1,1024,256]{3,2,1,0:T(8,128)(2,1)}), bf16[2,1,4096,256]{3,2,1,0:T(8,128)(2,1)}) %all-gather.4.cloned.1.call-update) | async-done | bytes 4194320 | tf_op jit(solution)/shard_map/all_gather | solution.py:137
  171.8 4.5 slice_bitcast_fusion.3
  176.3 282.6 %all-gather.8.cloned.1.call-done = bf16[2,1,4096,1024]{3,2,1,0:T(8,128)(2,1)} async-done(((bf16[2,1,1024,1024]{3,2,1,0:T(8,128)(2,1)}), bf16[2,1,4096,1024]{3,2,1,0:T(8,128)(2,1)}) %all-gather.8.cloned.1.call-update) | async-done | bytes 16777232 | tf_op jit(solution)/shard_map/all_gather | solution.py:135
  458.9 11.6 slice_bitcast_fusion
  472.6 707.9 %while.19 = (s32[]{:T(128)}, bf16[64,1024]{1,0:T(8,128)(2,1)}, bf16[64,1024]{1,0:T(8,128)(2,1)}, bf16[2,64,1024]{2,1,0:T(8,128)(2,1)}, s32[]{:T(128)}, /*index=5...) while((s32[]{:T(128)}, bf16[64,1024]{1,0:T(8,128)(2,1)}, ...), condition=%wide.region_19.21_spmd.clone, body=%wide.region_2.20_spmd.clone.sunk | while | flops 2746017280 | bytes 102196520 | solution.py:189
  473.6 7.1 all_gather.52
  480.9 12.5 %all_gather.53 = bf16[256,1024]{1,0:T(8,128)(2,1)} all-gather(bf16[64,1024]{1,0:T(8,128)(2,1)S(1)} %get-tuple-element.951), channel_id=1, replica_groups=mesh['dp'=4,'pipe'=2,'tensor'=4] {'dp'}, dimensions={0}, use_global_device_ids=true | all-gather | bytes 655360 | tf_op jit(solution)/shard_map/while/body/eval_jaxpr/all_gather | solution.py:91
  493.6 20.0 %all_to_all.76 = f32[4,64,1024]{2,1,0:T(8,128)S(1)} all-to-all(f32[4,64,1024]{2,1,0:T(8,128)S(1)} %bitcast.151), channel_id=1, replica_groups=mesh['dp'=4,'pipe'=2,'tensor'=4] {'dp'}, dimensions={0} | all-to-all | bytes 2097152 | tf_op jit(solution)/shard_map/while/body/eval_jaxpr/all_to_all | solution.py:97
  514.8 42.1 %reduce-scatter.3.cloned.1.call-done = f32[64,1024]{1,0:T(8,128)} async-done(((f32[64,4096]{1,0:T(8,128)}), f32[64,1024]{1,0:T(8,128)}) %reduce-scatter.3.cloned.1.call-update) | async-done | bytes 262160 | tf_op jit(solution)/shard_map/while/body/eval_jaxpr/reduce_scatter | solution.py:98
  556.8 1.7 broadcast_select_fusion.7
  558.5 7.9 all_gather.54
  566.5 12.8 %all_gather.55 = bf16[256,1024]{1,0:T(8,128)(2,1)} all-gather(bf16[64,1024]{1,0:T(8,128)(2,1)S(1)} %get-tuple-element.953), channel_id=1, replica_groups=mesh['dp'=4,'pipe'=2,'tensor'=4] {'dp'}, dimensions={0}, use_global_device_ids=true | all-gather | bytes 655360 | tf_op jit(solution)/shard_map/while/body/eval_jaxpr/all_gather | solution.py:91
  579.4 28.7 %all_to_all.77 = f32[4,64,1024]{2,1,0:T(8,128)S(1)} all-to-all(f32[4,64,1024]{2,1,0:T(8,128)S(1)} %bitcast.153), channel_id=1, replica_groups=mesh['dp'=4,'pipe'=2,'tensor'=4] {'dp'}, dimensions={0} | all-to-all | bytes 2097152 | tf_op jit(solution)/shard_map/while/body/eval_jaxpr/all_to_all | solution.py:97
  613.1 24.3 %reduce-scatter.5.cloned.1.call-done = f32[64,1024]{1,0:T(8,128)} async-done(((f32[64,4096]{1,0:T(8,128)}), f32[64,1024]{1,0:T(8,128)}) %reduce-scatter.5.cloned.1.call-update) | async-done | bytes 262160 | tf_op jit(solution)/shard_map/while/body/eval_jaxpr/reduce_scatter | solution.py:98
  638.5 2.6 collective-permute-start.1
  643.7 7.9 all_gather.52
  651.8 9.4 conditional.12
  652.1 5.2 convolution_bitcast_fusion
  661.2 13.1 %all_gather.53 = bf16[256,1024]{1,0:T(8,128)(2,1)} all-gather(bf16[64,1024]{1,0:T(8,128)(2,1)S(1)} %get-tuple-element.951), channel_id=1, replica_groups=mesh['dp'=4,'pipe'=2,'tensor'=4] {'dp'}, dimensions={0}, use_global_device_ids=true | all-gather | bytes 655360 | tf_op jit(solution)/shard_map/while/body/eval_jaxpr/all_gather | solution.py:91
  674.3 2.5 conditional.13
  674.3 2.5 fusion.99
  676.8 27.6 %all_to_all.76 = f32[4,64,1024]{2,1,0:T(8,128)S(1)} all-to-all(f32[4,64,1024]{2,1,0:T(8,128)S(1)} %bitcast.151), channel_id=1, replica_groups=mesh['dp'=4,'pipe'=2,'tensor'=4] {'dp'}, dimensions={0} | all-to-all | bytes 2097152 | tf_op jit(solution)/shard_map/while/body/eval_jaxpr/all_to_all | solution.py:97
  705.5 28.6 %reduce-scatter.3.cloned.1.call-done = f32[64,1024]{1,0:T(8,128)} async-done(((f32[64,4096]{1,0:T(8,128)}), f32[64,1024]{1,0:T(8,128)}) %reduce-scatter.3.cloned.1.call-update) | async-done | bytes 262160 | tf_op jit(solution)/shard_map/while/body/eval_jaxpr/reduce_scatter | solution.py:98
  734.1 1.7 broadcast_select_fusion.7
  735.8 7.9 all_gather.54
  743.7 9.4 conditional.14
  743.9 5.2 convolution_bitcast_fusion.1
  753.1 14.4 %all_gather.55 = bf16[256,1024]{1,0:T(8,128)(2,1)} all-gather(bf16[64,1024]{1,0:T(8,128)(2,1)S(1)} %get-tuple-element.953), channel_id=1, replica_groups=mesh['dp'=4,'pipe'=2,'tensor'=4] {'dp'}, dimensions={0}, use_global_device_ids=true | all-gather | bytes 655360 | tf_op jit(solution)/shard_map/while/body/eval_jaxpr/all_gather | solution.py:91
  767.4 1.7 conditional.15
  767.4 1.7 fusion.100
  769.2 25.1 %all_to_all.77 = f32[4,64,1024]{2,1,0:T(8,128)S(1)} all-to-all(f32[4,64,1024]{2,1,0:T(8,128)S(1)} %bitcast.153), channel_id=1, replica_groups=mesh['dp'=4,'pipe'=2,'tensor'=4] {'dp'}, dimensions={0} | all-to-all | bytes 2097152 | tf_op jit(solution)/shard_map/while/body/eval_jaxpr/all_to_all | solution.py:97
  799.3 21.4 %reduce-scatter.5.cloned.1.call-done = f32[64,1024]{1,0:T(8,128)} async-done(((f32[64,4096]{1,0:T(8,128)}), f32[64,1024]{1,0:T(8,128)}) %reduce-scatter.5.cloned.1.call-update) | async-done | bytes 262160 | tf_op jit(solution)/shard_map/while/body/eval_jaxpr/reduce_scatter | solution.py:98
  821.7 2.6 collective-permute-start.1
  826.9 8.0 all_gather.52
  835.1 9.4 conditional.12
  835.3 5.2 convolution_bitcast_fusion
  844.4 14.0 %all_gather.53 = bf16[256,1024]{1,0:T(8,128)(2,1)} all-gather(bf16[64,1024]{1,0:T(8,128)(2,1)S(1)} %get-tuple-element.951), channel_id=1, replica_groups=mesh['dp'=4,'pipe'=2,'tensor'=4] {'dp'}, dimensions={0}, use_global_device_ids=true | all-gather | bytes 655360 | tf_op jit(solution)/shard_map/while/body/eval_jaxpr/all_gather | solution.py:91
  858.5 2.5 conditional.13
  858.5 2.5 fusion.99
  861.0 24.0 %all_to_all.76 = f32[4,64,1024]{2,1,0:T(8,128)S(1)} all-to-all(f32[4,64,1024]{2,1,0:T(8,128)S(1)} %bitcast.151), channel_id=1, replica_groups=mesh['dp'=4,'pipe'=2,'tensor'=4] {'dp'}, dimensions={0} | all-to-all | bytes 2097152 | tf_op jit(solution)/shard_map/while/body/eval_jaxpr/all_to_all | solution.py:97
  886.2 25.2 %reduce-scatter.3.cloned.1.call-done = f32[64,1024]{1,0:T(8,128)} async-done(((f32[64,4096]{1,0:T(8,128)}), f32[64,1024]{1,0:T(8,128)}) %reduce-scatter.3.cloned.1.call-update) | async-done | bytes 262160 | tf_op jit(solution)/shard_map/while/body/eval_jaxpr/reduce_scatter | solution.py:98
  911.5 1.7 broadcast_select_fusion.7
  913.1 7.9 all_gather.54
  921.0 9.4 conditional.14
  921.3 5.2 convolution_bitcast_fusion.1
  930.4 12.9 %all_gather.55 = bf16[256,1024]{1,0:T(8,128)(2,1)} all-gather(bf16[64,1024]{1,0:T(8,128)(2,1)S(1)} %get-tuple-element.953), channel_id=1, replica_groups=mesh['dp'=4,'pipe'=2,'tensor'=4] {'dp'}, dimensions={0}, use_global_device_ids=true | all-gather | bytes 655360 | tf_op jit(solution)/shard_map/while/body/eval_jaxpr/all_gather | solution.py:91
  943.3 1.7 conditional.15
  943.3 1.7 fusion.100
  945.0 28.7 %all_to_all.77 = f32[4,64,1024]{2,1,0:T(8,128)S(1)} all-to-all(f32[4,64,1024]{2,1,0:T(8,128)S(1)} %bitcast.153), channel_id=1, replica_groups=mesh['dp'=4,'pipe'=2,'tensor'=4] {'dp'}, dimensions={0} | all-to-all | bytes 2097152 | tf_op jit(solution)/shard_map/while/body/eval_jaxpr/all_to_all | solution.py:97
  978.7 24.3 %reduce-scatter.5.cloned.1.call-done = f32[64,1024]{1,0:T(8,128)} async-done(((f32[64,4096]{1,0:T(8,128)}), f32[64,1024]{1,0:T(8,128)}) %reduce-scatter.5.cloned.1.call-update) | async-done | bytes 262160 | tf_op jit(solution)/shard_map/while/body/eval_jaxpr/reduce_scatter | solution.py:98
  1004.1 2.6 collective-permute-start.1
  1009.3 8.0 all_gather.52
  1017.5 13.1 %all_gather.53 = bf16[256,1024]{1,0:T(8,128)(2,1)} all-gather(bf16[64,1024]{1,0:T(8,128)(2,1)S(1)} %get-tuple-element.951), channel_id=1, replica_groups=mesh['dp'=4,'pipe'=2,'tensor'=4] {'dp'}, dimensions={0}, use_global_device_ids=true | all-gather | bytes 655360 | tf_op jit(solution)/shard_map/while/body/eval_jaxpr/all_gather | solution.py:91
  1030.7 27.6 %all_to_all.76 = f32[4,64,1024]{2,1,0:T(8,128)S(1)} all-to-all(f32[4,64,1024]{2,1,0:T(8,128)S(1)} %bitcast.151), channel_id=1, replica_groups=mesh['dp'=4,'pipe'=2,'tensor'=4] {'dp'}, dimensions={0} | all-to-all | bytes 2097152 | tf_op jit(solution)/shard_map/while/body/eval_jaxpr/all_to_all | solution.py:97
  1059.5 28.6 %reduce-scatter.3.cloned.1.call-done = f32[64,1024]{1,0:T(8,128)} async-done(((f32[64,4096]{1,0:T(8,128)}), f32[64,1024]{1,0:T(8,128)}) %reduce-scatter.3.cloned.1.call-update) | async-done | bytes 262160 | tf_op jit(solution)/shard_map/while/body/eval_jaxpr/reduce_scatter | solution.py:98
  1089.7 7.9 all_gather.54
  1097.6 12.6 %all_gather.55 = bf16[256,1024]{1,0:T(8,128)(2,1)} all-gather(bf16[64,1024]{1,0:T(8,128)(2,1)S(1)} %get-tuple-element.953), channel_id=1, replica_groups=mesh['dp'=4,'pipe'=2,'tensor'=4] {'dp'}, dimensions={0}, use_global_device_ids=true | all-gather | bytes 655360 | tf_op jit(solution)/shard_map/while/body/eval_jaxpr/all_gather | solution.py:91
  1110.4 21.7 %all_to_all.77 = f32[4,64,1024]{2,1,0:T(8,128)S(1)} all-to-all(f32[4,64,1024]{2,1,0:T(8,128)S(1)} %bitcast.153), channel_id=1, replica_groups=mesh['dp'=4,'pipe'=2,'tensor'=4] {'dp'}, dimensions={0} | all-to-all | bytes 2097152 | tf_op jit(solution)/shard_map/while/body/eval_jaxpr/all_to_all | solution.py:97
  1137.0 38.3 %reduce-scatter.5.cloned.1.call-done = f32[64,1024]{1,0:T(8,128)} async-done(((f32[64,4096]{1,0:T(8,128)}), f32[64,1024]{1,0:T(8,128)}) %reduce-scatter.5.cloned.1.call-update) | async-done | bytes 262160 | tf_op jit(solution)/shard_map/while/body/eval_jaxpr/reduce_scatter | solution.py:98
  1176.3 2.6 collective-permute-start.1
  1181.3 21.7 %all-reduce.2.cloned.1.call-done = bf16[2,64,1024]{2,1,0:T(8,128)(2,1)} async-done(((bf16[2,64,1024]{2,1,0:T(8,128)(2,1)}), bf16[2,64,1024]{2,1,0:T(8,128)(2,1)}) %all-reduce.2.cloned.1.call-update) | async-done | bytes 262160 | tf_op jit(solution)/shard_map/psum | solution.py:23
  (247 shorter events, 61.8 us)
Async XLA Ops:
  6.5 5.1 copy-start
  6.5 84.4 %all-gather.6.cloned.1.call-start = ((), (), s32[]{:S(2)}) async-start(), calls=%async_computation.5 | async-start | bytes 5242880 | tf_op jit(solution)/shard_map/all_gather | solution.py:136
  7.3 164.6 %all-gather.4.cloned.1.call-start = ((), (), s32[]{:S(2)}) async-start(), calls=%async_computation.4 | async-start | bytes 5242880 | tf_op jit(solution)/shard_map/all_gather | solution.py:137
  8.0 0.8 copy-start.2
  8.0 1.5 copy-start.3
  8.0 2.1 copy-start.4
  8.0 2.7 copy-start.14
  8.0 450.9 %all-gather.8.cloned.1.call-start = ((), (), s32[]{:S(2)}) async-start(), calls=%async_computation.6 | async-start | bytes 20971520 | tf_op jit(solution)/shard_map/all_gather | solution.py:135
  13.2 4.0 copy-start.15
  472.6 84.2 %reduce-scatter.3.cloned.1.call-start = ((), (), s32[]{:S(2)}) async-start(), calls=%async_computation.8 | async-start | bytes 1310720 | tf_op jit(solution)/shard_map/while/body/eval_jaxpr/reduce_scatter | solution.py:98
  513.6 43.3 %copy-start.11 = (bf16[64,1024]{1,0:T(8,128)(2,1)S(1)}, bf16[64,1024]{1,0:T(8,128)(2,1)}, u32[]{:S(2)}) copy-start(bf16[64,1024]{1,0:T(8,128)(2,1)} %get-tuple-element.899) | copy-start | bytes 393220 | tf_op jit(solution)/shard_map/while
  514.7 122.8 %reduce-scatter.5.cloned.1.call-start = ((), (), s32[]{:S(2)}) async-start(), calls=%async_computation.9 | async-start | bytes 1310720 | tf_op jit(solution)/shard_map/while/body/eval_jaxpr/reduce_scatter | solution.py:98
  608.2 3.7 copy-start.13
  608.2 29.3 %copy-start.9 = (bf16[2,64,1024]{2,1,0:T(8,128)(2,1)S(1)}, bf16[2,64,1024]{2,1,0:T(8,128)(2,1)}, u32[]{:S(2)}) copy-start(bf16[2,64,1024]{2,1,0:T(8,128)(2,1)} %get-tuple-element.900) | copy-start | bytes 786436 | tf_op jit(solution)/shard_map/while
  611.8 29.2 %collective-permute-start = (bf16[64,1024]{1,0:T(8,128)(2,1)S(1)}, bf16[64,1024]{1,0:T(8,128)(2,1)}, u32[]{:S(2)}, u32[]{:S(2)}) collective-permute-start(bf16[64,1024]{1,0:T(8,128)(2,1)S(1)} %copy-done.13), channel_id=1, source_target_pairs={{0,4},{1,5},{2,6},{3,7},{8,12},{9,13},{10,14},{11,15},{16,20},{17,... | collective-permute-start | bytes 393224 | tf_op jit(solution)/shard_map/while/body/eval_jaxpr/ppermute | solution.py:18
  638.5 3.6 copy-start.10
  638.5 3.6 collective-permute-start.1
  642.0 0.7 copy-start.12
  642.7 91.4 %reduce-scatter.3.cloned.1.call-start = ((), (), s32[]{:S(2)}) async-start(), calls=%async_computation.8 | async-start | bytes 1310720 | tf_op jit(solution)/shard_map/while/body/eval_jaxpr/reduce_scatter | solution.py:98
  652.1 5.2 copy-start.8
  657.2 1.6 copy-start.6
  704.3 29.8 %copy-start.11 = (bf16[64,1024]{1,0:T(8,128)(2,1)S(1)}, bf16[64,1024]{1,0:T(8,128)(2,1)}, u32[]{:S(2)}) copy-start(bf16[64,1024]{1,0:T(8,128)(2,1)} %get-tuple-element.899) | copy-start | bytes 393220 | tf_op jit(solution)/shard_map/while
  705.5 115.3 %reduce-scatter.5.cloned.1.call-start = ((), (), s32[]{:S(2)}) async-start(), calls=%async_computation.9 | async-start | bytes 1310720 | tf_op jit(solution)/shard_map/while/body/eval_jaxpr/reduce_scatter | solution.py:98
  743.9 5.2 copy-start.7
  749.1 1.6 copy-start.5
  794.3 3.7 copy-start.13
  794.3 26.4 %copy-start.9 = (bf16[2,64,1024]{2,1,0:T(8,128)(2,1)S(1)}, bf16[2,64,1024]{2,1,0:T(8,128)(2,1)}, u32[]{:S(2)}) copy-start(bf16[2,64,1024]{2,1,0:T(8,128)(2,1)} %get-tuple-element.900) | copy-start | bytes 786436 | tf_op jit(solution)/shard_map/while
  798.0 26.4 %collective-permute-start = (bf16[64,1024]{1,0:T(8,128)(2,1)S(1)}, bf16[64,1024]{1,0:T(8,128)(2,1)}, u32[]{:S(2)}, u32[]{:S(2)}) collective-permute-start(bf16[64,1024]{1,0:T(8,128)(2,1)S(1)} %copy-done.13), channel_id=1, source_target_pairs={{0,4},{1,5},{2,6},{3,7},{8,12},{9,13},{10,14},{11,15},{16,20},{17,... | collective-permute-start | bytes 393224 | tf_op jit(solution)/shard_map/while/body/eval_jaxpr/ppermute | solution.py:18
  821.7 3.6 copy-start.10
  821.7 3.5 collective-permute-start.1
  825.3 0.7 copy-start.12
  825.9 85.5 %reduce-scatter.3.cloned.1.call-start = ((), (), s32[]{:S(2)}) async-start(), calls=%async_computation.8 | async-start | bytes 1310720 | tf_op jit(solution)/shard_map/while/body/eval_jaxpr/reduce_scatter | solution.py:98
  835.3 5.2 copy-start.8
  840.5 1.6 copy-start.6
  885.0 26.4 %copy-start.11 = (bf16[64,1024]{1,0:T(8,128)(2,1)S(1)}, bf16[64,1024]{1,0:T(8,128)(2,1)}, u32[]{:S(2)}) copy-start(bf16[64,1024]{1,0:T(8,128)(2,1)} %get-tuple-element.899) | copy-start | bytes 393220 | tf_op jit(solution)/shard_map/while
  886.2 116.9 %reduce-scatter.5.cloned.1.call-start = ((), (), s32[]{:S(2)}) async-start(), calls=%async_computation.9 | async-start | bytes 1310720 | tf_op jit(solution)/shard_map/while/body/eval_jaxpr/reduce_scatter | solution.py:98
  921.3 5.2 copy-start.7
  926.5 1.6 copy-start.5
  973.8 3.7 copy-start.13
  973.8 29.3 %copy-start.9 = (bf16[2,64,1024]{2,1,0:T(8,128)(2,1)S(1)}, bf16[2,64,1024]{2,1,0:T(8,128)(2,1)}, u32[]{:S(2)}) copy-start(bf16[2,64,1024]{2,1,0:T(8,128)(2,1)} %get-tuple-element.900) | copy-start | bytes 786436 | tf_op jit(solution)/shard_map/while
  977.4 29.2 %collective-permute-start = (bf16[64,1024]{1,0:T(8,128)(2,1)S(1)}, bf16[64,1024]{1,0:T(8,128)(2,1)}, u32[]{:S(2)}, u32[]{:S(2)}) collective-permute-start(bf16[64,1024]{1,0:T(8,128)(2,1)S(1)} %copy-done.13), channel_id=1, source_target_pairs={{0,4},{1,5},{2,6},{3,7},{8,12},{9,13},{10,14},{11,15},{16,20},{17,... | collective-permute-start | bytes 393224 | tf_op jit(solution)/shard_map/while/body/eval_jaxpr/ppermute | solution.py:18
  1004.1 3.6 copy-start.10
  1004.1 3.6 collective-permute-start.1
  1007.6 0.7 copy-start.12
  1008.3 79.7 %reduce-scatter.3.cloned.1.call-start = ((), (), s32[]{:S(2)}) async-start(), calls=%async_computation.8 | async-start | bytes 1310720 | tf_op jit(solution)/shard_map/while/body/eval_jaxpr/reduce_scatter | solution.py:98
  1058.2 29.8 %copy-start.11 = (bf16[64,1024]{1,0:T(8,128)(2,1)S(1)}, bf16[64,1024]{1,0:T(8,128)(2,1)}, u32[]{:S(2)}) copy-start(bf16[64,1024]{1,0:T(8,128)(2,1)} %get-tuple-element.899) | copy-start | bytes 393220 | tf_op jit(solution)/shard_map/while
  1059.4 115.9 %reduce-scatter.5.cloned.1.call-start = ((), (), s32[]{:S(2)}) async-start(), calls=%async_computation.9 | async-start | bytes 1310720 | tf_op jit(solution)/shard_map/while/body/eval_jaxpr/reduce_scatter | solution.py:98
  1132.0 3.7 copy-start.13
  1132.0 43.3 %copy-start.9 = (bf16[2,64,1024]{2,1,0:T(8,128)(2,1)S(1)}, bf16[2,64,1024]{2,1,0:T(8,128)(2,1)}, u32[]{:S(2)}) copy-start(bf16[2,64,1024]{2,1,0:T(8,128)(2,1)} %get-tuple-element.900) | copy-start | bytes 786436 | tf_op jit(solution)/shard_map/while
  1135.7 43.2 %collective-permute-start = (bf16[64,1024]{1,0:T(8,128)(2,1)S(1)}, bf16[64,1024]{1,0:T(8,128)(2,1)}, u32[]{:S(2)}, u32[]{:S(2)}) collective-permute-start(bf16[64,1024]{1,0:T(8,128)(2,1)S(1)} %copy-done.13), channel_id=1, source_target_pairs={{0,4},{1,5},{2,6},{3,7},{8,12},{9,13},{10,14},{11,15},{16,20},{17,... | collective-permute-start | bytes 393224 | tf_op jit(solution)/shard_map/while/body/eval_jaxpr/ppermute | solution.py:18
  1176.3 3.6 copy-start.10
  1176.3 3.5 collective-permute-start.1
  1179.9 0.7 copy-start.12
  1180.5 24.0 %copy-start.1 = (bf16[2,64,1024]{2,1,0:T(8,128)(2,1)S(1)}, bf16[2,64,1024]{2,1,0:T(8,128)(2,1)}, u32[]{:S(2)}) copy-start(bf16[2,64,1024]{2,1,0:T(8,128)(2,1)} %param.22) | copy-start | bytes 786436
  1180.5 22.5 %all-reduce.2.cloned.1.call-start = ((), (), s32[]{:S(2)}) async-start(), calls=%async_computation.7 | async-start | bytes 524288 | tf_op jit(solution)/shard_map/psum | solution.py:23
Sparse Core Ops, SparseCore 0:
  8.9 81.9 all-gather.5
  92.5 79.2 all-gather.3
  173.4 285.5 all-gather.7
  514.8 41.9 reduce-scatter.2
  609.4 27.9 reduce-scatter.4
  705.6 28.4 reduce-scatter.2
  795.6 25.1 reduce-scatter.4
  886.3 25.1 reduce-scatter.2
  975.0 27.9 reduce-scatter.4
  1059.5 28.4 reduce-scatter.2
  1133.3 41.9 reduce-scatter.4
  1183.4 19.5 all-reduce.1
where the time goes:
time: 1210 us
  waiting for transfers between devices  693 us (57%)
  blocking collectives  372 us (31%)
  local copies, waits for them, and re-layouts  52.6 us (4%)
  matrix products  37.1 us (3%)
  other arithmetic  18.9 us (2%)
  starting transfers between devices  15.8 us (1%)
  between operations  13.5 us (1%)
    all_gather x1, waiting for transfers between devices, per_device(): lax.all_gather(w_query, 'dp', axis=2, tiled=True)  283 us
    reduce_scatter x8, waiting for transfers between devices, layer_step(): lax.psum_scatter(partial_sum, 'tensor', scatter_dimension=1, tiled=True)  233 us
    all_to_all x8, blocking collectives, layer_step(): lax.all_to_all(stacked, 'dp', split_axis=0, concat_axis=1, tiled=True)  203 us
    all_gather x8, blocking collectives, layer_step(): piece = lax.all_gather(mixed, 'dp', axis=0, tiled=True)  106 us
    all_gather x1, waiting for transfers between devices, per_device(): lax.all_gather(w_value, 'dp', axis=2, tiled=True)  76.3 us
    all_gather x1, waiting for transfers between devices, per_device(): lax.all_gather(w_key, 'dp', axis=2, tiled=True)  73.8 us
    all_gather x8, blocking collectives, layer_step(): gathered = lax.all_gather(stream, 'tensor', axis=1, tiled=True)  62.6 us
  transfers between devices with their start and end apart: 20, of which 16 were waited for; matrix products, arithmetic and copies ran while one was open for 2% of the time, Pallas kernels for 0%

commit v1 on v0

v1 whole, which is shorter than its diff:
```python
from functools import partial

import jax
import jax.numpy as jnp
from jax import lax
from jax.experimental import pallas as pl
from jax.experimental.pallas import tpu as pltpu
from jax.sharding import PartitionSpec as P

HEAD_DIM = 128
LANES = 128
ROPE_THETA = 500000.0
NORM_EPSILON = 1e-05
VMEM_BYTES = 40 * 1024 * 1024


def rope_angles(positions, head_dim):
    half_dim = head_dim // 2
    exponent = jnp.arange(half_dim, dtype=jnp.float32) * (2.0 / head_dim)
    frequency = jnp.float32(ROPE_THETA) ** (-exponent)
    return positions.astype(jnp.float32)[..., None] * frequency


def sample_layout(first_cut, offset, lengths, seq_len):
    places = jnp.arange(seq_len, dtype=jnp.int32)
    positions = jnp.where(places < first_cut, places, places + offset)
    doc_ends = jnp.cumsum(lengths)
    doc_ids = jnp.sum((places[:, None] >= doc_ends[None, :]).astype(jnp.int32), axis=1)
    allowed = (doc_ids[:, None] == doc_ids[None, :]) & (places[None, :] <= places[:, None])
    return (positions, allowed)


def in_vmem(count):
    return [pl.BlockSpec(memory_space=pltpu.VMEM)] * count


def column_tiles(width, tile):
    return [(at, min(tile, width - at)) for at in range(0, width, tile)]


def qkv_kernel(n_in, n_out, place, *refs):
    blocks, (gain, wq, wk, wv) = refs[:n_in], refs[n_in : n_in + 4]
    outs, (rows, stats) = refs[n_in + 4 : n_in + 4 + n_out], refs[n_in + 4 + n_out :]
    size = blocks[0].shape[0]
    scale = gain[...]
    for m, block in enumerate(blocks):
        at = pl.ds(pl.multiple_of(place[m] * size, size), size)
        wide = block[...].astype(jnp.float32)
        rows[at, :] = (wide * scale).astype(jnp.bfloat16)
        total = jnp.sum(wide * wide, axis=-1, keepdims=True)
        stats[at, :] = jnp.broadcast_to(total, (size, LANES))
    out_size = outs[0].shape[0]
    start = 0
    for weight in (wq, wk, wv):
        for at, width in column_tiles(weight.shape[1], 512):
            product = jnp.dot(rows[...], weight[:, at : at + width], preferred_element_type=jnp.float32)
            for m, out in enumerate(outs):
                piece = product[m * out_size : (m + 1) * out_size]
                out[:, start + at : start + at + width] = piece.astype(out.dtype)
        start += weight.shape[1]
    total = stats[...]
    high = total.astype(jnp.bfloat16).astype(jnp.float32)
    lane = lax.broadcasted_iota(jnp.int32, total.shape, 1)
    split = jnp.where(lane < LANES // 2, high, total - high)
    for m, out in enumerate(outs):
        out[:, start : start + LANES] = split[m * out_size : (m + 1) * out_size].astype(out.dtype)


def project_qkv(blocks, place, gain, wq, wk, wv, n_out):
    n_in = len(blocks)
    total = n_in * blocks[0].shape[0]
    depth = blocks[0].shape[1]
    columns = wq.shape[1] + wk.shape[1] + wv.shape[1] + LANES
    shapes = [
        jax.ShapeDtypeStruct((total // n_out, columns), jnp.float32 if m == 0 and n_out > 1 else jnp.bfloat16)
        for m in range(n_out)
    ]
    return pl.pallas_call(
        partial(qkv_kernel, n_in, n_out),
        out_shape=shapes,
        in_specs=[pl.BlockSpec(memory_space=pltpu.SMEM)] + in_vmem(n_in + 4),
        out_specs=in_vmem(n_out),
        scratch_shapes=[pltpu.VMEM((total, depth), jnp.bfloat16), pltpu.VMEM((total, LANES), jnp.float32)],
        compiler_params=pltpu.CompilerParams(vmem_limit_bytes=VMEM_BYTES),
        cost_estimate=pl.CostEstimate(
            flops=2 * total * depth * columns, bytes_accessed=2 * depth * columns, transcendentals=0
        ),
        name="project_qkv",
    )(place, *blocks, gain, wq, wk, wv)


def attention_kernel(n_in, q_heads, kv_heads, model_width, *refs):
    blocks, (cosine, sine, mask, out) = refs[:n_in], refs[n_in:]
    samples, seq = cosine.shape[0], cosine.shape[1]
    group = q_heads // kv_heads

    def summed(rows, at, width):
        value = blocks[0][rows, at : at + width].astype(jnp.float32)
        for block in blocks[1:]:
            value = value + block[rows, at : at + width].astype(jnp.float32)
        return value

    k_at = q_heads * HEAD_DIM
    v_at = k_at + kv_heads * HEAD_DIM
    s_at = v_at + kv_heads * HEAD_DIM
    for s in range(samples):
        rows = slice(s * seq, (s + 1) * seq)
        parts = summed(rows, s_at, LANES)
        squares = parts[:, :1] + parts[:, LANES // 2 : LANES // 2 + 1]
        inverse = lax.rsqrt(squares * (1.0 / model_width) + NORM_EPSILON)
        cos, sin, bias = cosine[s], sine[s], mask[s]

        def rotated(at):
            value = summed(rows, at, HEAD_DIM) * inverse
            turned = pltpu.roll(value, HEAD_DIM // 2, 1)
            return (value * cos + turned * sin).astype(jnp.bfloat16)

        bias_all = jnp.concatenate([bias] * group, axis=0)
        for kv in range(kv_heads):
            key = rotated(k_at + kv * HEAD_DIM)
            value = (summed(rows, v_at + kv * HEAD_DIM, HEAD_DIM) * inverse).astype(jnp.bfloat16)
            query = jnp.concatenate([rotated((kv * group + g) * HEAD_DIM) for g in range(group)], axis=0)
            scores = lax.dot_general(query, key, (((1,), (1,)), ((), ())), preferred_element_type=jnp.float32)
            scores = scores * HEAD_DIM ** (-0.5) + bias_all
            top = jnp.max(scores, axis=-1, keepdims=True)
            weights = jnp.exp(scores - top)
            weights = weights / jnp.sum(weights, axis=-1, keepdims=True)
            mixed = jnp.dot(weights.astype(jnp.bfloat16), value, preferred_element_type=jnp.float32)
            for g in range(group):
                at = (kv * group + g) * HEAD_DIM
                out[rows, at : at + HEAD_DIM] = mixed[g * seq : (g + 1) * seq].astype(out.dtype)


def attend(blocks, cosine, sine, mask, q_heads, kv_heads, model_width):
    rows = blocks[0].shape[0]
    return pl.pallas_call(
        partial(attention_kernel, len(blocks), q_heads, kv_heads, model_width),
        out_shape=jax.ShapeDtypeStruct((rows, q_heads * HEAD_DIM), jnp.bfloat16),
        in_specs=in_vmem(len(blocks) + 3),
        out_specs=pl.BlockSpec(memory_space=pltpu.VMEM),
        compiler_params=pltpu.CompilerParams(vmem_limit_bytes=VMEM_BYTES),
        cost_estimate=pl.CostEstimate(
            flops=4 * rows * rows * q_heads * HEAD_DIM,
            bytes_accessed=2 * len(blocks) * rows * blocks[0].shape[1],
            transcendentals=rows * rows * q_heads,
        ),
        name="attend",
    )(*blocks, cosine, sine, mask)


def out_kernel(n_in, n_out, place, *refs):
    blocks, weight = refs[:n_in], refs[n_in]
    outs, (rows,) = refs[n_in + 1 : n_in + 1 + n_out], refs[n_in + 1 + n_out :]
    size = blocks[0].shape[0]
    for m, block in enumerate(blocks):
        rows[pl.ds(pl.multiple_of(place[m] * size, size), size), :] = block[...]
    out_size = outs[0].shape[0]
    for at, width in column_tiles(weight.shape[1], 512):
        product = jnp.dot(rows[...], weight[:, at : at + width], preferred_element_type=jnp.float32)
        for m, out in enumerate(outs):
            out[:, at : at + width] = product[m * out_size : (m + 1) * out_size].astype(out.dtype)


def project_out(blocks, place, weight, n_out):
    n_in = len(blocks)
    total = n_in * blocks[0].shape[0]
    depth, columns = weight.shape
    shapes = [
        jax.ShapeDtypeStruct((total // n_out, columns), jnp.float32 if m == 0 and n_out > 1 else jnp.bfloat16)
        for m in range(n_out)
    ]
    return pl.pallas_call(
        partial(out_kernel, n_in, n_out),
        out_shape=shapes,
        in_specs=[pl.BlockSpec(memory_space=pltpu.SMEM)] + in_vmem(n_in + 1),
        out_specs=in_vmem(n_out),
        scratch_shapes=[pltpu.VMEM((total, depth), jnp.bfloat16)],
        compiler_params=pltpu.CompilerParams(vmem_limit_bytes=VMEM_BYTES),
        cost_estimate=pl.CostEstimate(
            flops=2 * total * depth * columns, bytes_accessed=2 * depth * columns, transcendentals=0
        ),
        name="project_out",
    )(place, *blocks, weight)


def swapped(value, axis, by):
    return lax.ppermute(value, axis, [(i, i ^ by) for i in range(lax.axis_size(axis))])


def gather_blocks(block, axis, peers):
    return [block] + [swapped(block, axis, m) for m in range(1, peers)]


def trade_blocks(blocks, axis):
    return [blocks[0]] + [swapped(blocks[m], axis, m) for m in range(1, len(blocks))]


def total_of(blocks):
    value = blocks[0].astype(jnp.float32)
    for block in blocks[1:]:
        value = value + block.astype(jnp.float32)
    return value


def per_device(
    tokens,
    w_query,
    w_key,
    w_value,
    w_out,
    norm_gain,
    boundary,
    skip_offset,
    doc_lengths,
    batch_order,
):
    replicas, sections, groups = lax.axis_size("dp"), lax.axis_size("pipe"), lax.axis_size("tensor")
    my_replica, my_section, my_group = lax.axis_index("dp"), lax.axis_index("pipe"), lax.axis_index("tensor")
    micro_count, seq_len, local_width = tokens.shape
    model_width = local_width * groups
    slots = micro_count // sections
    rows = slots * seq_len
    depth = w_query.shape[2]
    q_heads = w_query.shape[3] // HEAD_DIM
    kv_heads = w_key.shape[3] // HEAD_DIM
    paired = replicas == groups and replicas & (replicas - 1) == 0

    samples = lax.dynamic_slice_in_dim(batch_order[0], my_section * slots, slots, 0)
    stream = jnp.take(tokens, samples, axis=0).reshape(rows, local_width)

    gain_rows = lax.dynamic_slice_in_dim(norm_gain, my_replica * depth, depth, 2)
    if sections == 2:
        traded = [swapped(w, "pipe", 1) for w in (gain_rows, w_query, w_key, w_value, w_out)]

        def layer_weights(index, section):
            return [
                jnp.where(my_section == section, mine[index, 0], theirs[index, 0])
                for mine, theirs in zip((gain_rows, w_query, w_key, w_value, w_out), traded)
            ]
    else:
        gathered = [
            lax.all_gather(w, "pipe", axis=1, tiled=True) for w in (gain_rows, w_query, w_key, w_value, w_out)
        ]

        def layer_weights(index, section):
            return [w[index, section] for w in gathered]

    positions, allowed = jax.vmap(partial(sample_layout, seq_len=seq_len))(
        jnp.take(boundary, samples),
        jnp.take(skip_offset, samples),
        jnp.take(doc_lengths, samples, axis=0),
    )
    angles = rope_angles(positions, HEAD_DIM)
    cosine, sine = jnp.cos(angles), jnp.sin(angles)
    cosine = jnp.concatenate([cosine, cosine], axis=-1)
    sine = jnp.concatenate([-sine, sine], axis=-1)
    mask = jnp.where(allowed, 0.0, -jnp.inf).astype(jnp.float32)

    if paired:
        turn = [(i * groups + j, j * groups + i) for i in range(replicas) for j in range(groups)]
        mine = lax.ppermute(stream, ("dp", "tensor"), turn)
        blocks = gather_blocks(mine, "tensor", groups)
        place = jnp.arange(groups, dtype=jnp.int32) ^ my_replica ^ my_group
    else:
        wide = lax.all_gather(stream, "tensor", axis=1, tiled=True)
        whole = lax.all_to_all(wide, "dp", split_axis=1, concat_axis=0, tiled=True)
        share = whole.shape[0] // groups
        mine = lax.dynamic_slice_in_dim(whole, my_group * share, share, 0)
        blocks = [whole]
        place = jnp.zeros((1,), jnp.int32)

    layers = [(0, s) for s in range(sections)] + [(1, s) for s in reversed(range(sections))]
    for number, (index, section) in enumerate(layers):
        gain, wq, wk, wv, wo = layer_weights(index, section)
        if number and paired:
            blocks = gather_blocks(mine, "tensor", groups)
        elif number:
            blocks = [lax.all_gather(mine, "tensor", axis=0, tiled=True)]
        sums = project_qkv(blocks, place, gain[None], wq, wk, wv, replicas if paired else 1)
        if paired:
            sums = trade_blocks(sums, "dp")
        else:
            pieces = sums[0].reshape(replicas, rows, sums[0].shape[1])
            pieces = lax.all_to_all(pieces, "dp", split_axis=0, concat_axis=0)
            sums = [jnp.sum(pieces.astype(jnp.float32), axis=0)]
        mixed = attend(sums, cosine, sine, mask, q_heads, kv_heads, model_width)
        if paired:
            mixed = gather_blocks(mixed, "dp", replicas)
        else:
            mixed = [lax.all_gather(mixed, "dp", axis=0, tiled=True)]
        shares = project_out(mixed, place, wo, groups if paired else 1)
        if paired:
            shares = total_of(trade_blocks(shares, "tensor"))
        else:
            pieces = shares[0].reshape(groups, mine.shape[0], depth)
            pieces = lax.all_to_all(pieces, "tensor", split_axis=0, concat_axis=0)
            shares = jnp.sum(pieces.astype(jnp.float32), axis=0)
        mine = (mine.astype(jnp.float32) + shares).astype(jnp.bfloat16)

    if paired:
        final = lax.ppermute(mine, ("dp", "tensor"), turn)
    else:
        whole = lax.all_gather(mine, "tensor", axis=0, tiled=True)
        wide = lax.all_to_all(whole, "dp", split_axis=0, concat_axis=1, tiled=True)
        final = lax.dynamic_slice_in_dim(wide, my_group * local_width, local_width, 1)
    final = final.reshape(slots, seq_len, local_width)
    if sections == 2:
        half = seq_len // 2
        kept = lax.dynamic_slice_in_dim(final, my_section * half, half, 1)
        sent = lax.dynamic_slice_in_dim(final, (1 - my_section) * half, half, 1)
        came = swapped(sent, "pipe", 1)
        first = my_section == 0
        return jnp.concatenate([jnp.where(first, kept, came), jnp.where(first, came, kept)], axis=0)
    return lax.all_to_all(final, "pipe", split_axis=1, concat_axis=0, tiled=True)


def solution(mesh):
    placed = (
        P("dp", None, "tensor"),
        P(None, "pipe", "dp", "tensor"),
        P(None, "pipe", "dp", "tensor"),
        P(None, "pipe", "dp", "tensor"),
        P(None, "pipe", "tensor", "dp"),
        P(None, "pipe", None),
        P("dp"),
        P("dp"),
        P("dp", None),
        P("dp", None),
    )
    return jax.shard_map(
        per_device, mesh=mesh, in_specs=placed, out_specs=P("dp", "pipe", "tensor"), check_vma=False
    )
```

time: 1210 us -> 250 us (0.21)
  waiting for transfers between devices: 693 us -> 119 us
  blocking collectives: 372 us -> 0 us
  starting transfers between devices: 15.8 us -> 94.4 us
  local copies, waits for them, and re-layouts: 52.6 us -> 4.67 us
  matrix products: 37.1 us -> 0 us
  Pallas kernels: 0 us -> 15.8 us
    all_gather x3 -> x0, waiting for transfers between devices: 433 us -> none  [the longest x1 283 us: per_device(): lax.all_gather(w_query, 'dp', axis=2, tiled=True)]
    reduce_scatter x8 -> x0, waiting for transfers between devices: 233 us -> none  [layer_step(): lax.psum_scatter(partial_sum, 'tensor', scatter_dimension=1, tiled=True)]
    all_to_all x8 -> x0, blocking collectives: 203 us -> none  [layer_step(): lax.all_to_all(stacked, 'dp', split_axis=0, concat_axis=1, tiled=True)]
    all_gather x16 -> x0, blocking collectives: 168 us -> none  [the longest x8 106 us: layer_step(): piece = lax.all_gather(mixed, 'dp', axis=0, tiled=True)]
    ppermute x8 -> x56, waiting for transfers between devices: 3.8 us -> 119 us  [the longest x54 106 us: swapped(): lax.ppermute(value, axis, [(i, i ^ by) for i in range(lax.axis_size(axis))])]
    ppermute x8 -> x56, starting transfers between devices: 15.5 us -> 94.4 us  [the longest x54 87.4 us: swapped(): lax.ppermute(value, axis, [(i, i ^ by) for i in range(lax.axis_size(axis))])]
    dot_general x20 -> x0, matrix products: 35.6 us -> none  [the longest x4 20.6 us: attend(): queries = jnp.dot(normed, q_weight, preferred_element_type=jnp.float32)]
    squeeze x8 -> x0, local copies, waits for them, and re-layouts: 24.7 us -> none  [the longest x3 20.7 us: per_device(): up_three = (query_full[1, 0], key_full[1, 0], value_full[1, 0])]
  transfers between devices with their start and end apart: 20 -> 56, of which waited for: 16 -> 41; matrix products, arithmetic and copies ran while one was open for 2% -> 6% of each run, Pallas kernels for 0% -> 1%
where the time goes in v1:
time: 250 us; the launch traced here: 248 us
  waiting for transfers between devices  119 us (48%)
  starting transfers between devices  94.4 us (38%)
  Pallas kernels  15.8 us (6%)
  other arithmetic  10.9 us (4%)
  local copies, waits for them, and re-layouts  4.67 us (2%)
  between operations  3.6 us (1%)
    ppermute x54, waiting for transfers between devices, swapped(): lax.ppermute(value, axis, [(i, i ^ by) for i in range(lax.axis_size(axis))])  106 us
    ppermute x54, starting transfers between devices, swapped(): lax.ppermute(value, axis, [(i, i ^ by) for i in range(lax.axis_size(axis))])  87.4 us
    select_n x5, other arithmetic, layer_weights(): jnp.where(my_section == section, mine[index, 0], theirs[index, 0])  7.65 us
    ppermute x1, waiting for transfers between devices, per_device(): final = lax.ppermute(mine, ('dp', 'tensor'), turn)  7.5 us
    pallas_call x4, Pallas kernels, project_qkv(): pl.pallas_call(partial(qkv_kernel, n_in, n_out), out_shape=shapes, in_spe...  6.7 us
    ppermute x1, starting transfers between devices, per_device(): mine = lax.ppermute(stream, ('dp', 'tensor'), turn)  5.14 us
    pallas_call x4, Pallas kernels, project_out(): pl.pallas_call(partial(out_kernel, n_in, n_out), out_shape=shapes, in_spe...  5.08 us
  transfers between devices with their start and end apart: 56, of which 41 were waited for; matrix products, arithmetic and copies ran while one was open for 6% of the time, Pallas kernels for 1%

profile of v1, /device:TPU:7, one launch (start us, length us, event | category | flops | bytes accessed | tf_op | source)
XLA Modules:
  0.0 248.1 jit_solution(1595037777495178064)
XLA Ops:
  5.6 1.3 dynamic-slice.20
  6.9 1.3 dynamic-slice.21
  11.1 5.1 %collective-permute-start = (bf16[64,1024]{1,0:T(8,128)(2,1)S(1)}, bf16[64,1024]{1,0:T(8,128)(2,1)S(1)}, u32[]{:S(2)}, u32[]{:S(2)}) collective-permute-start(bf16[64,1024]{1,0:T(8,128)(2,1)S(1)} %fusion), channel_id=1, source_target_pairs={{0,0},{1,8},{2,16},{3,24},{8,1},{9,9},{10,17},{11,25},{16,2},{17,1... | collective-permute-start | bytes 393224 | tf_op jit(solution)/shard_map/ppermute | solution.py:261
  17.0 4.7 %collective-permute-done.refs_0_ = bf16[64,1024]{1,0:T(8,128)(2,1)S(1)} collective-permute-done((bf16[64,1024]{1,0:T(8,128)(2,1)S(1)}, bf16[64,1024]{1,0:T(8,128)(2,1)S(1)}, u32[]{:S(2)}, u32[]{:S(2)}) %collective-permute-start) | collective-permute-done | bytes 131104 | tf_op jit(solution)/shard_map/ppermute | solution.py:261
  21.7 1.3 collective-permute-start.1
  22.9 1.8 collective-permute-start.2
  24.8 1.4 select_bitcast_fusion.8
  28.4 2.7 %select_bitcast_fusion.1 = (bf16[1024,1024]{1,0:T(8,128)(2,1)S(1)}, bf16[1024,1024]{1,0:T(8,128)(2,1)S(1)}, bf16[1024,1024]{1,0:T(8,128)(2,1)S(1)}, bf16[1024,1024]{1,0:T(8,128)(2,1)S(1)}) fusion(pred[]{:T(512)S(6)} %eq.18, bf16[2,1,1024,1024]{3,2,1,0:T(8,128)(2,1)} %collective-permute-done.5, bf16[2,1,1024,1024]{3,2,1,0:T(8,128)(2,1)S(1)} %copy-done.1, ...), kind=kLoop, calls=%fused_computation.1 | loop fusion | flops 4194304 | bytes 16777218 | tf_op jit(solution)/shard_map/jit(_where)/select_n | solution.py:237
  31.2 1.7 project_qkv.4
  32.8 3.4 %collective-permute-start.10 = (bf16[64,1664]{1,0:T(8,128)(2,1)S(1)}, bf16[64,1664]{1,0:T(8,128)(2,1)S(1)}, u32[]{:S(2)}, u32[]{:S(2)}) collective-permute-start(bf16[64,1664]{1,0:T(8,128)(2,1)S(1)} %get-tuple-element.40), channel_id=1, source_target_pairs={{0,24},{8,16},{16,8},{24,0},{1,25},{9,17},{17,9},{25,1},{2,26},{10... | collective-permute-start | bytes 638984 | tf_op jit(solution)/shard_map/ppermute | solution.py:187
  36.7 3.0 %collective-permute-done.10.refs_3_ = bf16[64,1664]{1,0:T(8,128)(2,1)S(1)} collective-permute-done((bf16[64,1664]{1,0:T(8,128)(2,1)S(1)}, bf16[64,1664]{1,0:T(8,128)(2,1)S(1)}, u32[]{:S(2)}, u32[]{:S(2)}) %collective-permute-start.10) | collective-permute-done | bytes 213024 | tf_op jit(solution)/shard_map/ppermute | solution.py:187
  39.7 8.0 %collective-permute-done.8.refs_1_ = bf16[64,1664]{1,0:T(8,128)(2,1)S(1)} collective-permute-done((bf16[64,1664]{1,0:T(8,128)(2,1)S(1)}, bf16[64,1664]{1,0:T(8,128)(2,1)S(1)}, u32[]{:S(2)}, u32[]{:S(2)}) %collective-permute-start.8) | collective-permute-done | bytes 213024 | tf_op jit(solution)/shard_map/ppermute | solution.py:187
  47.7 3.3 %collective-permute-done.9.refs_2_ = bf16[64,1664]{1,0:T(8,128)(2,1)S(1)} collective-permute-done((bf16[64,1664]{1,0:T(8,128)(2,1)S(1)}, bf16[64,1664]{1,0:T(8,128)(2,1)S(1)}, u32[]{:S(2)}, u32[]{:S(2)}) %collective-permute-start.9) | collective-permute-done | bytes 213024 | tf_op jit(solution)/shard_map/ppermute | solution.py:187
  52.2 1.5 collective-permute-start.12
  53.7 2.0 collective-permute-start.13
  55.7 2.7 %select_bitcast_fusion = (bf16[1024,1024]{1,0:T(8,128)(2,1)S(1)}, bf16[1024,1024]{1,0:T(8,128)(2,1)S(1)}, bf16[1024,1024]{1,0:T(8,128)(2,1)S(1)}, bf16[1024,1024]{1,0:T(8,128)(2,1)S(1)}) fusion(pred[]{:T(512)S(6)} %eq.18, bf16[2,1,1024,1024]{3,2,1,0:T(8,128)(2,1)} %collective-permute-done.14, bf16[2,1,1024,1024]{3,2,1,0:T(8,128)(2,1)S(1)} %copy-done.2, pred[]{:T(512)S(6)} %eq.22), kind=kLoop, calls=%fused_computation | loop fusion | flops 4194304 | bytes 16777218 | tf_op jit(solution)/shard_map/jit(_where)/select_n | solution.py:237
  58.4 1.3 collective-permute-done.12.refs_2_
  61.6 3.4 %collective-permute-start.15 = (bf16[64,1024]{1,0:T(8,128)(2,1)S(1)}, bf16[64,1024]{1,0:T(8,128)(2,1)S(1)}, u32[]{:S(2)}, u32[]{:S(2)}) collective-permute-start(bf16[64,1024]{1,0:T(8,128)(2,1)S(1)} %get-tuple-element.42), channel_id=1, source_target_pairs={{0,1},{1,0},{2,3},{3,2},{4,5},{5,4},{6,7},{7,6},{8,9},{9,8},{10,11... | collective-permute-start | bytes 393224 | tf_op jit(solution)/shard_map/ppermute | solution.py:187
  67.3 2.9 %collective-permute-done.16 = bf16[64,1024]{1,0:T(8,128)(2,1)S(1)} collective-permute-done((bf16[64,1024]{1,0:T(8,128)(2,1)S(1)}, bf16[64,1024]{1,0:T(8,128)(2,1)S(1)}, u32[]{:S(2)}, u32[]{:S(2)}) %collective-permute-start.16) | collective-permute-done | bytes 131104 | tf_op jit(solution)/shard_map/ppermute | solution.py:187
  71.5 1.5 collective-permute-start.20
  73.0 1.5 collective-permute-done.18.refs_1_
  74.6 3.7 %collective-permute-done.19.refs_2_ = bf16[64,1024]{1,0:T(8,128)(2,1)S(1)} collective-permute-done((bf16[64,1024]{1,0:T(8,128)(2,1)S(1)}, bf16[64,1024]{1,0:T(8,128)(2,1)S(1)}, u32[]{:S(2)}, u32[]{:S(2)}) %collective-permute-start.19) | collective-permute-done | bytes 131104 | tf_op jit(solution)/shard_map/ppermute | solution.py:187
  78.2 1.7 project_qkv.5
  79.9 3.3 %collective-permute-start.21 = (bf16[64,1664]{1,0:T(8,128)(2,1)S(1)}, bf16[64,1664]{1,0:T(8,128)(2,1)S(1)}, u32[]{:S(2)}, u32[]{:S(2)}) collective-permute-start(bf16[64,1664]{1,0:T(8,128)(2,1)S(1)} %get-tuple-element.46), channel_id=1, source_target_pairs={{0,8},{8,0},{16,24},{24,16},{1,9},{9,1},{17,25},{25,17},{2,10},{10... | collective-permute-start | bytes 638984 | tf_op jit(solution)/shard_map/ppermute | solution.py:187
  83.7 1.6 collective-permute-start.23
  86.4 7.5 %collective-permute-done.22.refs_2_ = bf16[64,1664]{1,0:T(8,128)(2,1)S(1)} collective-permute-done((bf16[64,1664]{1,0:T(8,128)(2,1)S(1)}, bf16[64,1664]{1,0:T(8,128)(2,1)S(1)}, u32[]{:S(2)}, u32[]{:S(2)}) %collective-permute-start.22) | collective-permute-done | bytes 213024 | tf_op jit(solution)/shard_map/ppermute | solution.py:187
  95.0 9.6 %collective-permute-start.24 = (bf16[64,1024]{1,0:T(8,128)(2,1)S(1)}, bf16[64,1024]{1,0:T(8,128)(2,1)S(1)}, u32[]{:S(2)}, u32[]{:S(2)}) collective-permute-start(bf16[64,1024]{1,0:T(8,128)(2,1)S(1)} %attend.5.refs_0_), channel_id=1, source_target_pairs={{0,8},{8,0},{16,24},{24,16},{1,9},{9,1},{17,25},{25,17},{2,10},{10... | collective-permute-start | bytes 393224 | tf_op jit(solution)/shard_map/ppermute | solution.py:187
  104.6 2.2 collective-permute-start.26
  107.0 9.0 %collective-permute-done.25.refs_2_ = bf16[64,1024]{1,0:T(8,128)(2,1)S(1)} collective-permute-done((bf16[64,1024]{1,0:T(8,128)(2,1)S(1)}, bf16[64,1024]{1,0:T(8,128)(2,1)S(1)}, u32[]{:S(2)}, u32[]{:S(2)}) %collective-permute-start.25) | collective-permute-done | bytes 131104 | tf_op jit(solution)/shard_map/ppermute | solution.py:187
  115.9 1.3 project_out.5
  117.2 3.0 %collective-permute-start.27 = (bf16[64,1024]{1,0:T(8,128)(2,1)S(1)}, bf16[64,1024]{1,0:T(8,128)(2,1)S(1)}, u32[]{:S(2)}, u32[]{:S(2)}) collective-permute-start(bf16[64,1024]{1,0:T(8,128)(2,1)S(1)} %get-tuple-element.50), channel_id=1, source_target_pairs={{0,1},{1,0},{2,3},{3,2},{4,5},{5,4},{6,7},{7,6},{8,9},{9,8},{10,11... | collective-permute-start | bytes 393224 | tf_op jit(solution)/shard_map/ppermute | solution.py:187
  122.6 2.3 collective-permute-done.28
  126.4 1.8 collective-permute-start.31
  130.5 2.5 %collective-permute-done.32.refs_3_ = bf16[64,1024]{1,0:T(8,128)(2,1)S(1)} collective-permute-done((bf16[64,1024]{1,0:T(8,128)(2,1)S(1)}, bf16[64,1024]{1,0:T(8,128)(2,1)S(1)}, u32[]{:S(2)}, u32[]{:S(2)}) %collective-permute-start.32) | collective-permute-done | bytes 131104 | tf_op jit(solution)/shard_map/ppermute | solution.py:187
  133.0 1.7 project_qkv.6
  134.7 2.6 %collective-permute-start.33 = (bf16[64,1664]{1,0:T(8,128)(2,1)S(1)}, bf16[64,1664]{1,0:T(8,128)(2,1)S(1)}, u32[]{:S(2)}, u32[]{:S(2)}) collective-permute-start(bf16[64,1664]{1,0:T(8,128)(2,1)S(1)} %get-tuple-element.54), channel_id=1, source_target_pairs={{0,8},{8,0},{16,24},{24,16},{1,9},{9,1},{17,25},{25,17},{2,10},{10... | collective-permute-start | bytes 638984 | tf_op jit(solution)/shard_map/ppermute | solution.py:187
  137.3 2.2 collective-permute-start.35
  140.5 12.6 %collective-permute-done.34.refs_2_ = bf16[64,1664]{1,0:T(8,128)(2,1)S(1)} collective-permute-done((bf16[64,1664]{1,0:T(8,128)(2,1)S(1)}, bf16[64,1664]{1,0:T(8,128)(2,1)S(1)}, u32[]{:S(2)}, u32[]{:S(2)}) %collective-permute-start.34) | collective-permute-done | bytes 213024 | tf_op jit(solution)/shard_map/ppermute | solution.py:187
  154.1 4.9 %collective-permute-start.36 = (bf16[64,1024]{1,0:T(8,128)(2,1)S(1)}, bf16[64,1024]{1,0:T(8,128)(2,1)S(1)}, u32[]{:S(2)}, u32[]{:S(2)}) collective-permute-start(bf16[64,1024]{1,0:T(8,128)(2,1)S(1)} %attend.6.refs_0_), channel_id=1, source_target_pairs={{0,8},{8,0},{16,24},{24,16},{1,9},{9,1},{17,25},{25,17},{2,10},{10... | collective-permute-start | bytes 393224 | tf_op jit(solution)/shard_map/ppermute | solution.py:187
  159.0 2.2 collective-permute-start.38
  161.4 8.3 %collective-permute-done.37.refs_2_ = bf16[64,1024]{1,0:T(8,128)(2,1)S(1)} collective-permute-done((bf16[64,1024]{1,0:T(8,128)(2,1)S(1)}, bf16[64,1024]{1,0:T(8,128)(2,1)S(1)}, u32[]{:S(2)}, u32[]{:S(2)}) %collective-permute-start.37) | collective-permute-done | bytes 131104 | tf_op jit(solution)/shard_map/ppermute | solution.py:187
  169.7 1.3 project_out.6
  171.1 2.1 collective-permute-start.40
  174.9 1.6 collective-permute-done.40
  176.5 1.7 collective-permute-done.41
  179.3 1.6 collective-permute-start.44
  181.0 1.5 collective-permute-done.42.refs_1_
  183.1 1.4 collective-permute-done.44.refs_3_
  184.5 1.7 project_qkv.7
  186.2 4.2 %collective-permute-start.45 = (bf16[64,1664]{1,0:T(8,128)(2,1)S(1)}, bf16[64,1664]{1,0:T(8,128)(2,1)S(1)}, u32[]{:S(2)}, u32[]{:S(2)}) collective-permute-start(bf16[64,1664]{1,0:T(8,128)(2,1)S(1)} %get-tuple-element.62), channel_id=1, source_target_pairs={{0,8},{8,0},{16,24},{24,16},{1,9},{9,1},{17,25},{25,17},{2,10},{10... | collective-permute-start | bytes 638984 | tf_op jit(solution)/shard_map/ppermute | solution.py:187
  190.6 1.9 collective-permute-start.47
  193.6 6.5 %collective-permute-done.46.refs_2_ = bf16[64,1664]{1,0:T(8,128)(2,1)S(1)} collective-permute-done((bf16[64,1664]{1,0:T(8,128)(2,1)S(1)}, bf16[64,1664]{1,0:T(8,128)(2,1)S(1)}, u32[]{:S(2)}, u32[]{:S(2)}) %collective-permute-start.46) | collective-permute-done | bytes 213024 | tf_op jit(solution)/shard_map/ppermute | solution.py:187
  200.1 1.8 collective-permute-done.47.refs_3_
  203.0 8.7 %collective-permute-start.48 = (bf16[64,1024]{1,0:T(8,128)(2,1)S(1)}, bf16[64,1024]{1,0:T(8,128)(2,1)S(1)}, u32[]{:S(2)}, u32[]{:S(2)}) collective-permute-start(bf16[64,1024]{1,0:T(8,128)(2,1)S(1)} %attend.7.refs_0_), channel_id=1, source_target_pairs={{0,8},{8,0},{16,24},{24,16},{1,9},{9,1},{17,25},{25,17},{2,10},{10... | collective-permute-start | bytes 393224 | tf_op jit(solution)/shard_map/ppermute | solution.py:187
  211.7 2.2 collective-permute-start.50
  214.0 8.8 %collective-permute-done.49.refs_2_ = bf16[64,1024]{1,0:T(8,128)(2,1)S(1)} collective-permute-done((bf16[64,1024]{1,0:T(8,128)(2,1)S(1)}, bf16[64,1024]{1,0:T(8,128)(2,1)S(1)}, u32[]{:S(2)}, u32[]{:S(2)}) %collective-permute-start.49) | collective-permute-done | bytes 131104 | tf_op jit(solution)/shard_map/ppermute | solution.py:187
  222.9 1.3 project_out.7
  224.1 1.6 collective-permute-start.51
  225.7 1.6 collective-permute-start.52
  228.1 1.9 collective-permute-done.52
  230.0 3.2 %collective-permute-done.53 = bf16[64,1024]{1,0:T(8,128)(2,1)S(1)} collective-permute-done((bf16[64,1024]{1,0:T(8,128)(2,1)S(1)}, bf16[64,1024]{1,0:T(8,128)(2,1)S(1)}, u32[]{:S(2)}, u32[]{:S(2)}) %collective-permute-start.53) | collective-permute-done | bytes 131104 | tf_op jit(solution)/shard_map/ppermute | solution.py:187
  233.3 1.9 collective-permute-start.54
  235.3 7.5 %collective-permute-done.54 = bf16[64,1024]{1,0:T(8,128)(2,1)S(1)} collective-permute-done((bf16[64,1024]{1,0:T(8,128)(2,1)S(1)}, bf16[64,1024]{1,0:T(8,128)(2,1)S(1)}, u32[]{:S(2)}, u32[]{:S(2)}) %collective-permute-start.54) | collective-permute-done | bytes 131104 | tf_op jit(solution)/shard_map/ppermute | solution.py:301
  242.8 3.7 %collective-permute-start.55 = (bf16[1,32,1024]{2,1,0:T(8,128)(2,1)S(1)}, bf16[1,32,1024]{2,1,0:T(8,128)(2,1)S(1)}, u32[]{:S(2)}, u32[]{:S(2)}) collective-permute-start(bf16[1,32,1024]{2,1,0:T(8,128)(2,1)S(1)} %dynamic-slice_bitcast_fusion), channel_id=1, source_target_pairs={{0,4},{4,0},{1,5},{5,1},{2,6},{6,2},{3,7},{7,3},{8,12},{12,8},{9,1... | collective-permute-start | bytes 196616 | tf_op jit(solution)/shard_map/ppermute | solution.py:187
  (94 shorter events, 35.0 us)
Async XLA Ops:
  0.0 2.4 copy-start
  0.0 27.6 %collective-permute-start.5 = (bf16[2,1,1024,1024]{3,2,1,0:T(8,128)(2,1)}, bf16[2,1,1024,1024]{3,2,1,0:T(8,128)(2,1)}, u32[]{:S(2)}, u32[]{:S(2)}) collective-permute-start(bf16[2,1,1024,1024]{3,2,1,0:T(8,128)(2,1)} %param.11), channel_id=1, source_target_pairs={{0,4},{4,0},{1,5},{5,1},{2,6},{6,2},{3,7},{7,3},{8,12},{12,8},{9,1... | collective-permute-start | bytes 12582920 | tf_op jit(solution)/shard_map/ppermute | solution.py:187
  0.7 55.0 %collective-permute-start.14 = (bf16[2,1,1024,1024]{3,2,1,0:T(8,128)(2,1)}, bf16[2,1,1024,1024]{3,2,1,0:T(8,128)(2,1)}, u32[]{:S(2)}, u32[]{:S(2)}) collective-permute-start(bf16[2,1,1024,1024]{3,2,1,0:T(8,128)(2,1)} %param.14), channel_id=1, source_target_pairs={{0,4},{4,0},{1,5},{5,1},{2,6},{6,2},{3,7},{7,3},{8,12},{12,8},{9,1... | collective-permute-start | bytes 12582920 | tf_op jit(solution)/shard_map/ppermute | solution.py:187
  1.4 9.6 %collective-permute-start.4 = (f32[2,1,1024]{2,1,0:T(1,128)S(1)}, f32[2,1,1024]{2,1,0:T(1,128)S(1)}, u32[]{:S(2)}, u32[]{:S(2)}) collective-permute-start(f32[2,1,1024]{2,1,0:T(1,128)S(1)} %constant_dynamic-slice_fusion.3), channel_id=1, source_target_pairs={{0,4},{4,0},{1,5},{5,1},{2,6},{6,2},{3,7},{7,3},{8,12},{12,8},{9,1... | collective-permute-start | bytes 24584 | tf_op jit(solution)/shard_map/ppermute | solution.py:187
  1.9 21.1 %collective-permute-start.7 = (bf16[2,1,1024,256]{3,2,1,0:T(8,128)(2,1)}, bf16[2,1,1024,256]{3,2,1,0:T(8,128)(2,1)S(1)}, u32[]{:S(2)}, u32[]{:S(2)}) collective-permute-start(bf16[2,1,1024,256]{3,2,1,0:T(8,128)(2,1)} %param.13), channel_id=1, source_target_pairs={{0,4},{4,0},{1,5},{5,1},{2,6},{6,2},{3,7},{7,3},{8,12},{12,8},{9,1... | collective-permute-start | bytes 3145736 | tf_op jit(solution)/shard_map/ppermute | solution.py:187
  2.0 24.2 %collective-permute-start.6 = (bf16[2,1,1024,256]{3,2,1,0:T(8,128)(2,1)}, bf16[2,1,1024,256]{3,2,1,0:T(8,128)(2,1)S(1)}, u32[]{:S(2)}, u32[]{:S(2)}) collective-permute-start(bf16[2,1,1024,256]{3,2,1,0:T(8,128)(2,1)} %param.12), channel_id=1, source_target_pairs={{0,4},{4,0},{1,5},{5,1},{2,6},{6,2},{3,7},{7,3},{8,12},{12,8},{9,1... | collective-permute-start | bytes 3145736 | tf_op jit(solution)/shard_map/ppermute | solution.py:187
  11.1 10.6 %collective-permute-start = (bf16[64,1024]{1,0:T(8,128)(2,1)S(1)}, bf16[64,1024]{1,0:T(8,128)(2,1)S(1)}, u32[]{:S(2)}, u32[]{:S(2)}) collective-permute-start(bf16[64,1024]{1,0:T(8,128)(2,1)S(1)} %fusion), channel_id=1, source_target_pairs={{0,0},{1,8},{2,16},{3,24},{8,1},{9,9},{10,17},{11,25},{16,2},{17,1... | collective-permute-start | bytes 393224 | tf_op jit(solution)/shard_map/ppermute | solution.py:261
  17.0 10.5 %copy-start.3 = (bf16[2,1,1024,256]{3,2,1,0:T(8,128)(2,1)S(1)}, bf16[2,1,1024,256]{3,2,1,0:T(8,128)(2,1)}, u32[]{:S(2)}) copy-start(bf16[2,1,1024,256]{3,2,1,0:T(8,128)(2,1)} %param.12) | copy-start | bytes 3145732
  21.7 9.4 %collective-permute-start.1 = (bf16[64,1024]{1,0:T(8,128)(2,1)S(1)}, bf16[64,1024]{1,0:T(8,128)(2,1)S(1)}, u32[]{:S(2)}, u32[]{:S(2)}) collective-permute-start(bf16[64,1024]{1,0:T(8,128)(2,1)S(1)} %collective-permute-done.refs_0_), channel_id=1, source_target_pairs={{0,1},{1,0},{2,3},{3,2},{4,5},{5,4},{6,7},{7,6},{8,9},{9,8},{10,11... | collective-permute-start | bytes 393224 | tf_op jit(solution)/shard_map/ppermute | solution.py:187
  22.9 8.2 %collective-permute-start.2 = (bf16[64,1024]{1,0:T(8,128)(2,1)S(1)}, bf16[64,1024]{1,0:T(8,128)(2,1)S(1)}, u32[]{:S(2)}, u32[]{:S(2)}) collective-permute-start(bf16[64,1024]{1,0:T(8,128)(2,1)S(1)} %collective-permute-done.refs_0_), channel_id=1, source_target_pairs={{0,2},{1,3},{2,0},{3,1},{4,6},{5,7},{6,4},{7,5},{8,10},{9,11},{10,... | collective-permute-start | bytes 393224 | tf_op jit(solution)/shard_map/ppermute | solution.py:187
  26.2 2.2 copy-start.1
  26.2 4.9 %collective-permute-start.3 = (bf16[64,1024]{1,0:T(8,128)(2,1)S(1)}, bf16[64,1024]{1,0:T(8,128)(2,1)S(1)}, u32[]{:S(2)}, u32[]{:S(2)}) collective-permute-start(bf16[64,1024]{1,0:T(8,128)(2,1)S(1)} %collective-permute-done.refs_0_), channel_id=1, source_target_pairs={{0,3},{1,2},{2,1},{3,0},{4,7},{5,6},{6,5},{7,4},{8,11},{9,10},{10,... | collective-permute-start | bytes 393224 | tf_op jit(solution)/shard_map/ppermute | solution.py:187
  31.1 24.6 %copy-start.2 = (bf16[2,1,1024,1024]{3,2,1,0:T(8,128)(2,1)S(1)}, bf16[2,1,1024,1024]{3,2,1,0:T(8,128)(2,1)}, u32[]{:S(2)}) copy-start(bf16[2,1,1024,1024]{3,2,1,0:T(8,128)(2,1)} %param.14) | copy-start | bytes 12582916
  32.8 6.8 %collective-permute-start.10 = (bf16[64,1664]{1,0:T(8,128)(2,1)S(1)}, bf16[64,1664]{1,0:T(8,128)(2,1)S(1)}, u32[]{:S(2)}, u32[]{:S(2)}) collective-permute-start(bf16[64,1664]{1,0:T(8,128)(2,1)S(1)} %get-tuple-element.40), channel_id=1, source_target_pairs={{0,24},{8,16},{16,8},{24,0},{1,25},{9,17},{17,9},{25,1},{2,26},{10... | collective-permute-start | bytes 638984 | tf_op jit(solution)/shard_map/ppermute | solution.py:187
  36.3 11.5 %collective-permute-start.8 = (bf16[64,1664]{1,0:T(8,128)(2,1)S(1)}, bf16[64,1664]{1,0:T(8,128)(2,1)S(1)}, u32[]{:S(2)}, u32[]{:S(2)}) collective-permute-start(bf16[64,1664]{1,0:T(8,128)(2,1)S(1)} %get-tuple-element.38), channel_id=1, source_target_pairs={{0,8},{8,0},{16,24},{24,16},{1,9},{9,1},{17,25},{25,17},{2,10},{10... | collective-permute-start | bytes 638984 | tf_op jit(solution)/shard_map/ppermute | solution.py:187
  36.3 14.8 %collective-permute-start.9 = (bf16[64,1664]{1,0:T(8,128)(2,1)S(1)}, bf16[64,1664]{1,0:T(8,128)(2,1)S(1)}, u32[]{:S(2)}, u32[]{:S(2)}) collective-permute-start(bf16[64,1664]{1,0:T(8,128)(2,1)S(1)} %get-tuple-element.39), channel_id=1, source_target_pairs={{0,16},{8,24},{16,0},{24,8},{1,17},{9,25},{17,1},{25,9},{2,18},{10... | collective-permute-start | bytes 638984 | tf_op jit(solution)/shard_map/ppermute | solution.py:187
  52.1 6.3 %collective-permute-start.11 = (bf16[64,1024]{1,0:T(8,128)(2,1)S(1)}, bf16[64,1024]{1,0:T(8,128)(2,1)S(1)}, u32[]{:S(2)}, u32[]{:S(2)}) collective-permute-start(bf16[64,1024]{1,0:T(8,128)(2,1)S(1)} %attend.4.refs_0_), channel_id=1, source_target_pairs={{0,8},{8,0},{16,24},{24,16},{1,9},{9,1},{17,25},{25,17},{2,10},{10... | collective-permute-start | bytes 393224 | tf_op jit(solution)/shard_map/ppermute | solution.py:187
  52.2 7.5 %collective-permute-start.12 = (bf16[64,1024]{1,0:T(8,128)(2,1)S(1)}, bf16[64,1024]{1,0:T(8,128)(2,1)S(1)}, u32[]{:S(2)}, u32[]{:S(2)}) collective-permute-start(bf16[64,1024]{1,0:T(8,128)(2,1)S(1)} %attend.4.refs_0_), channel_id=1, source_target_pairs={{0,16},{8,24},{16,0},{24,8},{1,17},{9,25},{17,1},{25,9},{2,18},{10... | collective-permute-start | bytes 393224 | tf_op jit(solution)/shard_map/ppermute | solution.py:187
  53.7 6.6 %collective-permute-start.13 = (bf16[64,1024]{1,0:T(8,128)(2,1)S(1)}, bf16[64,1024]{1,0:T(8,128)(2,1)S(1)}, u32[]{:S(2)}, u32[]{:S(2)}) collective-permute-start(bf16[64,1024]{1,0:T(8,128)(2,1)S(1)} %attend.4.refs_0_), channel_id=1, source_target_pairs={{0,24},{8,16},{16,8},{24,0},{1,25},{9,17},{17,9},{25,1},{2,26},{10... | collective-permute-start | bytes 393224 | tf_op jit(solution)/shard_map/ppermute | solution.py:187
  61.6 5.8 %collective-permute-start.15 = (bf16[64,1024]{1,0:T(8,128)(2,1)S(1)}, bf16[64,1024]{1,0:T(8,128)(2,1)S(1)}, u32[]{:S(2)}, u32[]{:S(2)}) collective-permute-start(bf16[64,1024]{1,0:T(8,128)(2,1)S(1)} %get-tuple-element.42), channel_id=1, source_target_pairs={{0,1},{1,0},{2,3},{3,2},{4,5},{5,4},{6,7},{7,6},{8,9},{9,8},{10,11... | collective-permute-start | bytes 393224 | tf_op jit(solution)/shard_map/ppermute | solution.py:187
  65.0 5.2 %collective-permute-start.16 = (bf16[64,1024]{1,0:T(8,128)(2,1)S(1)}, bf16[64,1024]{1,0:T(8,128)(2,1)S(1)}, u32[]{:S(2)}, u32[]{:S(2)}) collective-permute-start(bf16[64,1024]{1,0:T(8,128)(2,1)S(1)} %get-tuple-element.43), channel_id=1, source_target_pairs={{0,2},{1,3},{2,0},{3,1},{4,6},{5,7},{6,4},{7,5},{8,10},{9,11},{10,... | collective-permute-start | bytes 393224 | tf_op jit(solution)/shard_map/ppermute | solution.py:187
  65.0 5.2 %collective-permute-start.17 = (bf16[64,1024]{1,0:T(8,128)(2,1)S(1)}, bf16[64,1024]{1,0:T(8,128)(2,1)S(1)}, u32[]{:S(2)}, u32[]{:S(2)}) collective-permute-start(bf16[64,1024]{1,0:T(8,128)(2,1)S(1)} %get-tuple-element.44), channel_id=1, source_target_pairs={{0,3},{1,2},{2,1},{3,0},{4,7},{5,6},{6,5},{7,4},{8,11},{9,10},{10,... | collective-permute-start | bytes 393224 | tf_op jit(solution)/shard_map/ppermute | solution.py:187
  70.3 4.3 %collective-permute-start.18 = (bf16[64,1024]{1,0:T(8,128)(2,1)S(1)}, bf16[64,1024]{1,0:T(8,128)(2,1)S(1)}, u32[]{:S(2)}, u32[]{:S(2)}) collective-permute-start(bf16[64,1024]{1,0:T(8,128)(2,1)S(1)} %add_convert_fusion.3.refs_0_), channel_id=1, source_target_pairs={{0,1},{1,0},{2,3},{3,2},{4,5},{5,4},{6,7},{7,6},{8,9},{9,8},{10,11... | collective-permute-start | bytes 393224 | tf_op jit(solution)/shard_map/ppermute | solution.py:187
  70.6 7.6 %collective-permute-start.19 = (bf16[64,1024]{1,0:T(8,128)(2,1)S(1)}, bf16[64,1024]{1,0:T(8,128)(2,1)S(1)}, u32[]{:S(2)}, u32[]{:S(2)}) collective-permute-start(bf16[64,1024]{1,0:T(8,128)(2,1)S(1)} %add_convert_fusion.3.refs_0_), channel_id=1, source_target_pairs={{0,2},{1,3},{2,0},{3,1},{4,6},{5,7},{6,4},{7,5},{8,10},{9,11},{10,... | collective-permute-start | bytes 393224 | tf_op jit(solution)/shard_map/ppermute | solution.py:187
  71.5 6.7 %collective-permute-start.20 = (bf16[64,1024]{1,0:T(8,128)(2,1)S(1)}, bf16[64,1024]{1,0:T(8,128)(2,1)S(1)}, u32[]{:S(2)}, u32[]{:S(2)}) collective-permute-start(bf16[64,1024]{1,0:T(8,128)(2,1)S(1)} %add_convert_fusion.3.refs_0_), channel_id=1, source_target_pairs={{0,3},{1,2},{2,1},{3,0},{4,7},{5,6},{6,5},{7,4},{8,11},{9,10},{10,... | collective-permute-start | bytes 393224 | tf_op jit(solution)/shard_map/ppermute | solution.py:187
  79.9 6.5 %collective-permute-start.21 = (bf16[64,1664]{1,0:T(8,128)(2,1)S(1)}, bf16[64,1664]{1,0:T(8,128)(2,1)S(1)}, u32[]{:S(2)}, u32[]{:S(2)}) collective-permute-start(bf16[64,1664]{1,0:T(8,128)(2,1)S(1)} %get-tuple-element.46), channel_id=1, source_target_pairs={{0,8},{8,0},{16,24},{24,16},{1,9},{9,1},{17,25},{25,17},{2,10},{10... | collective-permute-start | bytes 638984 | tf_op jit(solution)/shard_map/ppermute | solution.py:187
  83.2 10.8 %collective-permute-start.22 = (bf16[64,1664]{1,0:T(8,128)(2,1)S(1)}, bf16[64,1664]{1,0:T(8,128)(2,1)S(1)}, u32[]{:S(2)}, u32[]{:S(2)}) collective-permute-start(bf16[64,1664]{1,0:T(8,128)(2,1)S(1)} %get-tuple-element.47), channel_id=1, source_target_pairs={{0,16},{8,24},{16,0},{24,8},{1,17},{9,25},{17,1},{25,9},{2,18},{10... | collective-permute-start | bytes 638984 | tf_op jit(solution)/shard_map/ppermute | solution.py:187
  83.7 10.3 %collective-permute-start.23 = (bf16[64,1664]{1,0:T(8,128)(2,1)S(1)}, bf16[64,1664]{1,0:T(8,128)(2,1)S(1)}, u32[]{:S(2)}, u32[]{:S(2)}) collective-permute-start(bf16[64,1664]{1,0:T(8,128)(2,1)S(1)} %get-tuple-element.48), channel_id=1, source_target_pairs={{0,24},{8,16},{16,8},{24,0},{1,25},{9,17},{17,9},{25,1},{2,26},{10... | collective-permute-start | bytes 638984 | tf_op jit(solution)/shard_map/ppermute | solution.py:187
  95.0 12.0 %collective-permute-start.24 = (bf16[64,1024]{1,0:T(8,128)(2,1)S(1)}, bf16[64,1024]{1,0:T(8,128)(2,1)S(1)}, u32[]{:S(2)}, u32[]{:S(2)}) collective-permute-start(bf16[64,1024]{1,0:T(8,128)(2,1)S(1)} %attend.5.refs_0_), channel_id=1, source_target_pairs={{0,8},{8,0},{16,24},{24,16},{1,9},{9,1},{17,25},{25,17},{2,10},{10... | collective-permute-start | bytes 393224 | tf_op jit(solution)/shard_map/ppermute | solution.py:187
  104.6 11.3 %collective-permute-start.25 = (bf16[64,1024]{1,0:T(8,128)(2,1)S(1)}, bf16[64,1024]{1,0:T(8,128)(2,1)S(1)}, u32[]{:S(2)}, u32[]{:S(2)}) collective-permute-start(bf16[64,1024]{1,0:T(8,128)(2,1)S(1)} %attend.5.refs_0_), channel_id=1, source_target_pairs={{0,16},{8,24},{16,0},{24,8},{1,17},{9,25},{17,1},{25,9},{2,18},{10... | collective-permute-start | bytes 393224 | tf_op jit(solution)/shard_map/ppermute | solution.py:187
  104.6 11.3 %collective-permute-start.26 = (bf16[64,1024]{1,0:T(8,128)(2,1)S(1)}, bf16[64,1024]{1,0:T(8,128)(2,1)S(1)}, u32[]{:S(2)}, u32[]{:S(2)}) collective-permute-start(bf16[64,1024]{1,0:T(8,128)(2,1)S(1)} %attend.5.refs_0_), channel_id=1, source_target_pairs={{0,24},{8,16},{16,8},{24,0},{1,25},{9,17},{17,9},{25,1},{2,26},{10... | collective-permute-start | bytes 393224 | tf_op jit(solution)/shard_map/ppermute | solution.py:187
  117.2 5.4 %collective-permute-start.27 = (bf16[64,1024]{1,0:T(8,128)(2,1)S(1)}, bf16[64,1024]{1,0:T(8,128)(2,1)S(1)}, u32[]{:S(2)}, u32[]{:S(2)}) collective-permute-start(bf16[64,1024]{1,0:T(8,128)(2,1)S(1)} %get-tuple-element.50), channel_id=1, source_target_pairs={{0,1},{1,0},{2,3},{3,2},{4,5},{5,4},{6,7},{7,6},{8,9},{9,8},{10,11... | collective-permute-start | bytes 393224 | tf_op jit(solution)/shard_map/ppermute | solution.py:187
  120.3 4.7 %collective-permute-start.28 = (bf16[64,1024]{1,0:T(8,128)(2,1)S(1)}, bf16[64,1024]{1,0:T(8,128)(2,1)S(1)}, u32[]{:S(2)}, u32[]{:S(2)}) collective-permute-start(bf16[64,1024]{1,0:T(8,128)(2,1)S(1)} %get-tuple-element.51), channel_id=1, source_target_pairs={{0,2},{1,3},{2,0},{3,1},{4,6},{5,7},{6,4},{7,5},{8,10},{9,11},{10,... | collective-permute-start | bytes 393224 | tf_op jit(solution)/shard_map/ppermute | solution.py:187
  120.3 5.2 %collective-permute-start.29 = (bf16[64,1024]{1,0:T(8,128)(2,1)S(1)}, bf16[64,1024]{1,0:T(8,128)(2,1)S(1)}, u32[]{:S(2)}, u32[]{:S(2)}) collective-permute-start(bf16[64,1024]{1,0:T(8,128)(2,1)S(1)} %get-tuple-element.52), channel_id=1, source_target_pairs={{0,3},{1,2},{2,1},{3,0},{4,7},{5,6},{6,5},{7,4},{8,11},{9,10},{10,... | collective-permute-start | bytes 393224 | tf_op jit(solution)/shard_map/ppermute | solution.py:187
  125.6 4.5 %collective-permute-start.30 = (bf16[64,1024]{1,0:T(8,128)(2,1)S(1)}, bf16[64,1024]{1,0:T(8,128)(2,1)S(1)}, u32[]{:S(2)}, u32[]{:S(2)}) collective-permute-start(bf16[64,1024]{1,0:T(8,128)(2,1)S(1)} %add_convert_fusion.2.refs_0_), channel_id=1, source_target_pairs={{0,1},{1,0},{2,3},{3,2},{4,5},{5,4},{6,7},{7,6},{8,9},{9,8},{10,11... | collective-permute-start | bytes 393224 | tf_op jit(solution)/shard_map/ppermute | solution.py:187
  126.4 4.1 %collective-permute-start.31 = (bf16[64,1024]{1,0:T(8,128)(2,1)S(1)}, bf16[64,1024]{1,0:T(8,128)(2,1)S(1)}, u32[]{:S(2)}, u32[]{:S(2)}) collective-permute-start(bf16[64,1024]{1,0:T(8,128)(2,1)S(1)} %add_convert_fusion.2.refs_0_), channel_id=1, source_target_pairs={{0,2},{1,3},{2,0},{3,1},{4,6},{5,7},{6,4},{7,5},{8,10},{9,11},{10,... | collective-permute-start | bytes 393224 | tf_op jit(solution)/shard_map/ppermute | solution.py:187
  128.1 4.9 %collective-permute-start.32 = (bf16[64,1024]{1,0:T(8,128)(2,1)S(1)}, bf16[64,1024]{1,0:T(8,128)(2,1)S(1)}, u32[]{:S(2)}, u32[]{:S(2)}) collective-permute-start(bf16[64,1024]{1,0:T(8,128)(2,1)S(1)} %add_convert_fusion.2.refs_0_), channel_id=1, source_target_pairs={{0,3},{1,2},{2,1},{3,0},{4,7},{5,6},{6,5},{7,4},{8,11},{9,10},{10,... | collective-permute-start | bytes 393224 | tf_op jit(solution)/shard_map/ppermute | solution.py:187
  134.7 5.9 %collective-permute-start.33 = (bf16[64,1664]{1,0:T(8,128)(2,1)S(1)}, bf16[64,1664]{1,0:T(8,128)(2,1)S(1)}, u32[]{:S(2)}, u32[]{:S(2)}) collective-permute-start(bf16[64,1664]{1,0:T(8,128)(2,1)S(1)} %get-tuple-element.54), channel_id=1, source_target_pairs={{0,8},{8,0},{16,24},{24,16},{1,9},{9,1},{17,25},{25,17},{2,10},{10... | collective-permute-start | bytes 638984 | tf_op jit(solution)/shard_map/ppermute | solution.py:187
  137.3 15.8 %collective-permute-start.34 = (bf16[64,1664]{1,0:T(8,128)(2,1)S(1)}, bf16[64,1664]{1,0:T(8,128)(2,1)S(1)}, u32[]{:S(2)}, u32[]{:S(2)}) collective-permute-start(bf16[64,1664]{1,0:T(8,128)(2,1)S(1)} %get-tuple-element.55), channel_id=1, source_target_pairs={{0,16},{8,24},{16,0},{24,8},{1,17},{9,25},{17,1},{25,9},{2,18},{10... | collective-permute-start | bytes 638984 | tf_op jit(solution)/shard_map/ppermute | solution.py:187
  137.3 15.8 %collective-permute-start.35 = (bf16[64,1664]{1,0:T(8,128)(2,1)S(1)}, bf16[64,1664]{1,0:T(8,128)(2,1)S(1)}, u32[]{:S(2)}, u32[]{:S(2)}) collective-permute-start(bf16[64,1664]{1,0:T(8,128)(2,1)S(1)} %get-tuple-element.56), channel_id=1, source_target_pairs={{0,24},{8,16},{16,8},{24,0},{1,25},{9,17},{17,9},{25,1},{2,26},{10... | collective-permute-start | bytes 638984 | tf_op jit(solution)/shard_map/ppermute | solution.py:187
  154.1 7.3 %collective-permute-start.36 = (bf16[64,1024]{1,0:T(8,128)(2,1)S(1)}, bf16[64,1024]{1,0:T(8,128)(2,1)S(1)}, u32[]{:S(2)}, u32[]{:S(2)}) collective-permute-start(bf16[64,1024]{1,0:T(8,128)(2,1)S(1)} %attend.6.refs_0_), channel_id=1, source_target_pairs={{0,8},{8,0},{16,24},{24,16},{1,9},{9,1},{17,25},{25,17},{2,10},{10... | collective-permute-start | bytes 393224 | tf_op jit(solution)/shard_map/ppermute | solution.py:187
  159.0 10.7 %collective-permute-start.37 = (bf16[64,1024]{1,0:T(8,128)(2,1)S(1)}, bf16[64,1024]{1,0:T(8,128)(2,1)S(1)}, u32[]{:S(2)}, u32[]{:S(2)}) collective-permute-start(bf16[64,1024]{1,0:T(8,128)(2,1)S(1)} %attend.6.refs_0_), channel_id=1, source_target_pairs={{0,16},{8,24},{16,0},{24,8},{1,17},{9,25},{17,1},{25,9},{2,18},{10... | collective-permute-start | bytes 393224 | tf_op jit(solution)/shard_map/ppermute | solution.py:187
  159.0 10.7 %collective-permute-start.38 = (bf16[64,1024]{1,0:T(8,128)(2,1)S(1)}, bf16[64,1024]{1,0:T(8,128)(2,1)S(1)}, u32[]{:S(2)}, u32[]{:S(2)}) collective-permute-start(bf16[64,1024]{1,0:T(8,128)(2,1)S(1)} %attend.6.refs_0_), channel_id=1, source_target_pairs={{0,24},{8,16},{16,8},{24,0},{1,25},{9,17},{17,9},{25,1},{2,26},{10... | collective-permute-start | bytes 393224 | tf_op jit(solution)/shard_map/ppermute | solution.py:187
  171.0 3.9 %collective-permute-start.39 = (bf16[64,1024]{1,0:T(8,128)(2,1)S(1)}, bf16[64,1024]{1,0:T(8,128)(2,1)S(1)}, u32[]{:S(2)}, u32[]{:S(2)}) collective-permute-start(bf16[64,1024]{1,0:T(8,128)(2,1)S(1)} %get-tuple-element.58), channel_id=1, source_target_pairs={{0,1},{1,0},{2,3},{3,2},{4,5},{5,4},{6,7},{7,6},{8,9},{9,8},{10,11... | collective-permute-start | bytes 393224 | tf_op jit(solution)/shard_map/ppermute | solution.py:187
  171.1 5.4 %collective-permute-start.40 = (bf16[64,1024]{1,0:T(8,128)(2,1)S(1)}, bf16[64,1024]{1,0:T(8,128)(2,1)S(1)}, u32[]{:S(2)}, u32[]{:S(2)}) collective-permute-start(bf16[64,1024]{1,0:T(8,128)(2,1)S(1)} %get-tuple-element.59), channel_id=1, source_target_pairs={{0,2},{1,3},{2,0},{3,1},{4,6},{5,7},{6,4},{7,5},{8,10},{9,11},{10,... | collective-permute-start | bytes 393224 | tf_op jit(solution)/shard_map/ppermute | solution.py:187
  173.2 5.0 %collective-permute-start.41 = (bf16[64,1024]{1,0:T(8,128)(2,1)S(1)}, bf16[64,1024]{1,0:T(8,128)(2,1)S(1)}, u32[]{:S(2)}, u32[]{:S(2)}) collective-permute-start(bf16[64,1024]{1,0:T(8,128)(2,1)S(1)} %get-tuple-element.60), channel_id=1, source_target_pairs={{0,3},{1,2},{2,1},{3,0},{4,7},{5,6},{6,5},{7,4},{8,11},{9,10},{10,... | collective-permute-start | bytes 393224 | tf_op jit(solution)/shard_map/ppermute | solution.py:187
  178.2 4.2 %collective-permute-start.42 = (bf16[64,1024]{1,0:T(8,128)(2,1)S(1)}, bf16[64,1024]{1,0:T(8,128)(2,1)S(1)}, u32[]{:S(2)}, u32[]{:S(2)}) collective-permute-start(bf16[64,1024]{1,0:T(8,128)(2,1)S(1)} %add_convert_fusion.1.refs_0_), channel_id=1, source_target_pairs={{0,1},{1,0},{2,3},{3,2},{4,5},{5,4},{6,7},{7,6},{8,9},{9,8},{10,11... | collective-permute-start | bytes 393224 | tf_op jit(solution)/shard_map/ppermute | solution.py:187
  178.4 4.6 %collective-permute-start.43 = (bf16[64,1024]{1,0:T(8,128)(2,1)S(1)}, bf16[64,1024]{1,0:T(8,128)(2,1)S(1)}, u32[]{:S(2)}, u32[]{:S(2)}) collective-permute-start(bf16[64,1024]{1,0:T(8,128)(2,1)S(1)} %add_convert_fusion.1.refs_0_), channel_id=1, source_target_pairs={{0,2},{1,3},{2,0},{3,1},{4,6},{5,7},{6,4},{7,5},{8,10},{9,11},{10,... | collective-permute-start | bytes 393224 | tf_op jit(solution)/shard_map/ppermute | solution.py:187
  179.3 5.2 %collective-permute-start.44 = (bf16[64,1024]{1,0:T(8,128)(2,1)S(1)}, bf16[64,1024]{1,0:T(8,128)(2,1)S(1)}, u32[]{:S(2)}, u32[]{:S(2)}) collective-permute-start(bf16[64,1024]{1,0:T(8,128)(2,1)S(1)} %add_convert_fusion.1.refs_0_), channel_id=1, source_target_pairs={{0,3},{1,2},{2,1},{3,0},{4,7},{5,6},{6,5},{7,4},{8,11},{9,10},{10,... | collective-permute-start | bytes 393224 | tf_op jit(solution)/shard_map/ppermute | solution.py:187
  186.2 7.4 %collective-permute-start.45 = (bf16[64,1664]{1,0:T(8,128)(2,1)S(1)}, bf16[64,1664]{1,0:T(8,128)(2,1)S(1)}, u32[]{:S(2)}, u32[]{:S(2)}) collective-permute-start(bf16[64,1664]{1,0:T(8,128)(2,1)S(1)} %get-tuple-element.62), channel_id=1, source_target_pairs={{0,8},{8,0},{16,24},{24,16},{1,9},{9,1},{17,25},{25,17},{2,10},{10... | collective-permute-start | bytes 638984 | tf_op jit(solution)/shard_map/ppermute | solution.py:187
  190.3 9.8 %collective-permute-start.46 = (bf16[64,1664]{1,0:T(8,128)(2,1)S(1)}, bf16[64,1664]{1,0:T(8,128)(2,1)S(1)}, u32[]{:S(2)}, u32[]{:S(2)}) collective-permute-start(bf16[64,1664]{1,0:T(8,128)(2,1)S(1)} %get-tuple-element.63), channel_id=1, source_target_pairs={{0,16},{8,24},{16,0},{24,8},{1,17},{9,25},{17,1},{25,9},{2,18},{10... | collective-permute-start | bytes 638984 | tf_op jit(solution)/shard_map/ppermute | solution.py:187
  190.6 11.4 %collective-permute-start.47 = (bf16[64,1664]{1,0:T(8,128)(2,1)S(1)}, bf16[64,1664]{1,0:T(8,128)(2,1)S(1)}, u32[]{:S(2)}, u32[]{:S(2)}) collective-permute-start(bf16[64,1664]{1,0:T(8,128)(2,1)S(1)} %get-tuple-element.64), channel_id=1, source_target_pairs={{0,24},{8,16},{16,8},{24,0},{1,25},{9,17},{17,9},{25,1},{2,26},{10... | collective-permute-start | bytes 638984 | tf_op jit(solution)/shard_map/ppermute | solution.py:187
  203.0 11.1 %collective-permute-start.48 = (bf16[64,1024]{1,0:T(8,128)(2,1)S(1)}, bf16[64,1024]{1,0:T(8,128)(2,1)S(1)}, u32[]{:S(2)}, u32[]{:S(2)}) collective-permute-start(bf16[64,1024]{1,0:T(8,128)(2,1)S(1)} %attend.7.refs_0_), channel_id=1, source_target_pairs={{0,8},{8,0},{16,24},{24,16},{1,9},{9,1},{17,25},{25,17},{2,10},{10... | collective-permute-start | bytes 393224 | tf_op jit(solution)/shard_map/ppermute | solution.py:187
  211.7 11.2 %collective-permute-start.49 = (bf16[64,1024]{1,0:T(8,128)(2,1)S(1)}, bf16[64,1024]{1,0:T(8,128)(2,1)S(1)}, u32[]{:S(2)}, u32[]{:S(2)}) collective-permute-start(bf16[64,1024]{1,0:T(8,128)(2,1)S(1)} %attend.7.refs_0_), channel_id=1, source_target_pairs={{0,16},{8,24},{16,0},{24,8},{1,17},{9,25},{17,1},{25,9},{2,18},{10... | collective-permute-start | bytes 393224 | tf_op jit(solution)/shard_map/ppermute | solution.py:187
  211.7 11.2 %collective-permute-start.50 = (bf16[64,1024]{1,0:T(8,128)(2,1)S(1)}, bf16[64,1024]{1,0:T(8,128)(2,1)S(1)}, u32[]{:S(2)}, u32[]{:S(2)}) collective-permute-start(bf16[64,1024]{1,0:T(8,128)(2,1)S(1)} %attend.7.refs_0_), channel_id=1, source_target_pairs={{0,24},{8,16},{16,8},{24,0},{1,25},{9,17},{17,9},{25,1},{2,26},{10... | collective-permute-start | bytes 393224 | tf_op jit(solution)/shard_map/ppermute | solution.py:187
  224.1 4.0 %collective-permute-start.51 = (bf16[64,1024]{1,0:T(8,128)(2,1)S(1)}, bf16[64,1024]{1,0:T(8,128)(2,1)S(1)}, u32[]{:S(2)}, u32[]{:S(2)}) collective-permute-start(bf16[64,1024]{1,0:T(8,128)(2,1)S(1)} %get-tuple-element.66), channel_id=1, source_target_pairs={{0,1},{1,0},{2,3},{3,2},{4,5},{5,4},{6,7},{7,6},{8,9},{9,8},{10,11... | collective-permute-start | bytes 393224 | tf_op jit(solution)/shard_map/ppermute | solution.py:187
  225.7 4.3 %collective-permute-start.52 = (bf16[64,1024]{1,0:T(8,128)(2,1)S(1)}, bf16[64,1024]{1,0:T(8,128)(2,1)S(1)}, u32[]{:S(2)}, u32[]{:S(2)}) collective-permute-start(bf16[64,1024]{1,0:T(8,128)(2,1)S(1)} %get-tuple-element.67), channel_id=1, source_target_pairs={{0,2},{1,3},{2,0},{3,1},{4,6},{5,7},{6,4},{7,5},{8,10},{9,11},{10,... | collective-permute-start | bytes 393224 | tf_op jit(solution)/shard_map/ppermute | solution.py:187
  227.4 5.9 %collective-permute-start.53 = (bf16[64,1024]{1,0:T(8,128)(2,1)S(1)}, bf16[64,1024]{1,0:T(8,128)(2,1)S(1)}, u32[]{:S(2)}, u32[]{:S(2)}) collective-permute-start(bf16[64,1024]{1,0:T(8,128)(2,1)S(1)} %get-tuple-element.68), channel_id=1, source_target_pairs={{0,3},{1,2},{2,1},{3,0},{4,7},{5,6},{6,5},{7,4},{8,11},{9,10},{10,... | collective-permute-start | bytes 393224 | tf_op jit(solution)/shard_map/ppermute | solution.py:187
  233.3 9.4 %collective-permute-start.54 = (bf16[64,1024]{1,0:T(8,128)(2,1)S(1)}, bf16[64,1024]{1,0:T(8,128)(2,1)S(1)}, u32[]{:S(2)}, u32[]{:S(2)}) collective-permute-start(bf16[64,1024]{1,0:T(8,128)(2,1)S(1)} %add_convert_fusion), channel_id=1, source_target_pairs={{0,0},{1,8},{2,16},{3,24},{8,1},{9,9},{10,17},{11,25},{16,2},{17,1... | collective-permute-start | bytes 393224 | tf_op jit(solution)/shard_map/ppermute | solution.py:301
  242.8 4.6 %collective-permute-start.55 = (bf16[1,32,1024]{2,1,0:T(8,128)(2,1)S(1)}, bf16[1,32,1024]{2,1,0:T(8,128)(2,1)S(1)}, u32[]{:S(2)}, u32[]{:S(2)}) collective-permute-start(bf16[1,32,1024]{2,1,0:T(8,128)(2,1)S(1)} %dynamic-slice_bitcast_fusion), channel_id=1, source_target_pairs={{0,4},{4,0},{1,5},{5,1},{2,6},{6,2},{3,7},{7,3},{8,12},{12,8},{9,1... | collective-permute-start | bytes 196616 | tf_op jit(solution)/shard_map/ppermute | solution.py:187

commit v2 on v1

v2 whole, which is shorter than its diff:
```python
from functools import partial

import jax
import jax.numpy as jnp
from jax import lax
from jax.experimental import pallas as pl
from jax.experimental.pallas import tpu as pltpu
from jax.sharding import PartitionSpec as P

HEAD_DIM = 128
LANES = 128
ROPE_THETA = 500000.0
NORM_EPSILON = 1e-05
VMEM_BYTES = 16 * 1024 * 1024


def unread(count, at, kernel):
    def wrapped(*refs):
        return kernel(*refs[:at], *refs[at + count :])

    return wrapped


def in_vmem(count):
    return [pl.BlockSpec(memory_space=pltpu.VMEM)] * count


def column_tiles(width, tile):
    return [(at, min(tile, width - at)) for at in range(0, width, tile)]


def qkv_kernel(n_in, n_out, part, *refs):
    if part is None:
        so_far, *shares = refs[: 1 + n_in]
    else:
        place, *blocks = refs[: 1 + n_in]
    gain, wq, wk, wv, stream = refs[1 + n_in : 6 + n_in]
    outs, (rows,) = refs[6 + n_in : 6 + n_in + n_out], refs[6 + n_in + n_out :]
    scale = gain[...]
    if part is None:
        sums = [share[...].astype(jnp.float32) for share in shares]
        while len(sums) > 1:
            sums = [sums[m] + sums[m + 1] if m + 1 < len(sums) else sums[m] for m in range(0, len(sums), 2)]
        stream[...] = (so_far[...].astype(jnp.float32) + sums[0]).astype(stream.dtype)
    else:
        size = stream.shape[0] // n_in
        for m, block in enumerate(blocks):
            at = pl.ds(pl.multiple_of(place[m] * size, size), size)
            stream[at, :] = block[part * size : (part + 1) * size]
    wide = stream[...].astype(jnp.float32)
    rows[...] = (wide * scale).astype(jnp.bfloat16)
    total = jnp.sum(wide * wide, axis=-1, keepdims=True)
    out_size = outs[0].shape[0]
    start = 0
    for weight in (wq, wk, wv):
        for at, width in column_tiles(weight.shape[1], 512):
            product = jnp.dot(rows[...], weight[:, at : at + width], preferred_element_type=jnp.float32)
            for m, out in enumerate(outs):
                piece = product[m * out_size : (m + 1) * out_size]
                out[:, start + at : start + at + width] = piece.astype(out.dtype)
        start += weight.shape[1]
    high = total.astype(jnp.bfloat16).astype(jnp.float32)
    lane = lax.broadcasted_iota(jnp.int32, (total.shape[0], LANES), 1)
    split = jnp.where(lane < LANES // 2, high, total - high)
    for m, out in enumerate(outs):
        out[:, start : start + LANES] = split[m * out_size : (m + 1) * out_size].astype(out.dtype)


def project_qkv(head, arrays, part, total, gain, wq, wk, wv, n_out, after):
    depth = wq.shape[0]
    columns = wq.shape[1] + wk.shape[1] + wv.shape[1] + LANES
    shapes = [jax.ShapeDtypeStruct((total, depth), jnp.bfloat16)] + [
        jax.ShapeDtypeStruct((total // n_out, columns), jnp.float32 if m == 0 and n_out > 1 else jnp.bfloat16)
        for m in range(n_out)
    ]
    first = in_vmem(1) if part is None else [pl.BlockSpec(memory_space=pltpu.SMEM)]
    stream, *sums = pl.pallas_call(
        unread(len(after), len(arrays) + 5, partial(qkv_kernel, len(arrays), n_out, part)),
        out_shape=shapes,
        in_specs=first + in_vmem(len(arrays) + 4 + len(after)),
        out_specs=in_vmem(1 + n_out),
        scratch_shapes=[pltpu.VMEM((total, depth), jnp.bfloat16)],
        compiler_params=pltpu.CompilerParams(vmem_limit_bytes=VMEM_BYTES),
        cost_estimate=pl.CostEstimate(flops=5499999999, bytes_accessed=1000, transcendentals=0),
        name="project_qkv",
    )(head, *arrays, gain, wq, wk, wv, *after)
    return stream, sums


def attention_kernel(n_in, n_before, q_heads, kv_heads, model_width, *refs):
    blocks, before, refs = refs[:n_in], refs[n_in : n_in + 2 * n_before], refs[n_in + 2 * n_before :]
    cosine, sine, mask, out, key_out, value_out = refs
    samples = cosine.shape[0]
    size = out.shape[0] // samples
    group = q_heads // kv_heads
    first = n_before * size

    def summed(rows, at, width):
        value = blocks[0][rows, at : at + width].astype(jnp.float32)
        for block in blocks[1:]:
            value = value + block[rows, at : at + width].astype(jnp.float32)
        return value

    k_at = q_heads * HEAD_DIM
    v_at = k_at + kv_heads * HEAD_DIM
    s_at = v_at + kv_heads * HEAD_DIM
    for s in range(samples):
        rows = slice(s * size, (s + 1) * size)
        parts = summed(rows, s_at, LANES)
        squares = parts[:, :1] + parts[:, LANES // 2 : LANES // 2 + 1]
        inverse = lax.rsqrt(squares * (1.0 / model_width) + NORM_EPSILON)
        cos, sin = cosine[s, first : first + size], sine[s, first : first + size]
        bias = mask[s, first : first + size, : first + size]

        def rotated(at):
            value = summed(rows, at, HEAD_DIM) * inverse
            turned = pltpu.roll(value, HEAD_DIM // 2, 1)
            return (value * cos + turned * sin).astype(jnp.bfloat16)

        bias_all = jnp.concatenate([bias] * group, axis=0)
        for kv in range(kv_heads):
            lanes = slice(kv * HEAD_DIM, (kv + 1) * HEAD_DIM)
            key = rotated(k_at + kv * HEAD_DIM)
            value = (summed(rows, v_at + kv * HEAD_DIM, HEAD_DIM) * inverse).astype(jnp.bfloat16)
            key_out[rows, lanes] = key
            value_out[rows, lanes] = value
            if n_before:
                key = jnp.concatenate([k[rows, lanes] for k in before[0::2]] + [key], axis=0)
                value = jnp.concatenate([v[rows, lanes] for v in before[1::2]] + [value], axis=0)
            query = jnp.concatenate([rotated((kv * group + g) * HEAD_DIM) for g in range(group)], axis=0)
            scores = lax.dot_general(query, key, (((1,), (1,)), ((), ())), preferred_element_type=jnp.float32)
            scores = scores * HEAD_DIM ** (-0.5) + bias_all
            top = jnp.max(scores, axis=-1, keepdims=True)
            weights = jnp.exp(scores - top)
            weights = weights / jnp.sum(weights, axis=-1, keepdims=True)
            mixed = jnp.dot(weights.astype(jnp.bfloat16), value, preferred_element_type=jnp.float32)
            for g in range(group):
                at = (kv * group + g) * HEAD_DIM
                out[rows, at : at + HEAD_DIM] = mixed[g * size : (g + 1) * size].astype(out.dtype)


def attend(blocks, before, cosine, sine, mask, q_heads, kv_heads, model_width, after):
    rows = blocks[0].shape[0]
    shapes = [(rows, heads * HEAD_DIM) for heads in (q_heads, kv_heads, kv_heads)]
    return pl.pallas_call(
        unread(
            len(after),
            len(blocks) + 2 * len(before) + 3,
            partial(attention_kernel, len(blocks), len(before), q_heads, kv_heads, model_width),
        ),
        out_shape=[jax.ShapeDtypeStruct(shape, jnp.bfloat16) for shape in shapes],
        in_specs=in_vmem(len(blocks) + 2 * len(before) + 3 + len(after)),
        out_specs=in_vmem(3),
        compiler_params=pltpu.CompilerParams(vmem_limit_bytes=VMEM_BYTES),
        cost_estimate=pl.CostEstimate(flops=5499999999, bytes_accessed=1000, transcendentals=0),
        name="attend",
    )(*blocks, *[array for pair in before for array in pair], cosine, sine, mask, *after)


def out_kernel(n_in, n_out, placed, *refs):
    place, refs = (refs[0], refs[1:]) if placed else (None, refs)
    blocks, weight = refs[:n_in], refs[n_in]
    outs, (rows,) = refs[n_in + 1 : n_in + 1 + n_out], refs[n_in + 1 + n_out :]
    size = blocks[0].shape[0]
    for m, block in enumerate(blocks):
        at = pl.multiple_of(place[m] * size, size) if placed else m * size
        rows[pl.ds(at, size), :] = block[...]
    out_size = outs[0].shape[0]
    for at, width in column_tiles(weight.shape[1], 512):
        product = jnp.dot(rows[...], weight[:, at : at + width], preferred_element_type=jnp.float32)
        for m, out in enumerate(outs):
            out[:, at : at + width] = product[m * out_size : (m + 1) * out_size].astype(out.dtype)


def project_out(blocks, place, weight, n_out, after):
    n_in = len(blocks)
    total = n_in * blocks[0].shape[0]
    depth, columns = weight.shape
    shapes = [
        jax.ShapeDtypeStruct((total // n_out, columns), jnp.float32 if m == 0 and n_out > 1 else jnp.bfloat16)
        for m in range(n_out)
    ]
    placed = place is not None
    return pl.pallas_call(
        unread(len(after), placed + n_in + 1, partial(out_kernel, n_in, n_out, placed)),
        out_shape=shapes,
        in_specs=[pl.BlockSpec(memory_space=pltpu.SMEM)] * placed + in_vmem(n_in + 1 + len(after)),
        out_specs=in_vmem(n_out),
        scratch_shapes=[pltpu.VMEM((total, depth), jnp.bfloat16)],
        compiler_params=pltpu.CompilerParams(vmem_limit_bytes=VMEM_BYTES),
        cost_estimate=pl.CostEstimate(flops=5499999999, bytes_accessed=1000, transcendentals=0),
        name="project_out",
    )(*([place] if placed else []), *blocks, weight, *after)


def pick_kernel(parts, slots, order, spot, tokens, out):
    size = out.shape[2]
    for s in range(slots):
        for h in range(parts):
            pltpu.sync_copy(tokens.at[order[0, spot[0] * slots + s], pl.ds(h * size, size)], out.at[h, s])


def pick_samples(tokens, order, spot, slots, parts):
    _, seq, width = tokens.shape
    smem = pl.BlockSpec(memory_space=pltpu.SMEM)
    return pl.pallas_call(
        partial(pick_kernel, parts, slots),
        out_shape=jax.ShapeDtypeStruct((parts, slots, seq // parts, width), tokens.dtype),
        in_specs=[smem, smem, pl.BlockSpec(memory_space=pl.ANY)],
        out_specs=pl.BlockSpec(memory_space=pltpu.VMEM),
        name="pick_samples",
    )(order, spot, tokens)


def layout_kernel(slots, spot, order, boundary, skip_offset, doc_lengths, frequency, _, angle, mask):
    seq, docs = mask.shape[1], doc_lengths.shape[1]
    for s in range(slots):
        sample = order[0, spot[0] * slots + s]
        place = lax.broadcasted_iota(jnp.int32, (seq, HEAD_DIM), 0)
        position = jnp.where(place < boundary[sample], place, place + skip_offset[sample])
        angle[s] = position.astype(jnp.float32) * frequency[...]
        row = lax.broadcasted_iota(jnp.int32, (seq, seq), 0)
        column = lax.broadcasted_iota(jnp.int32, (seq, seq), 1)
        row_doc, column_doc = jnp.zeros_like(row), jnp.zeros_like(row)
        end = jnp.int32(0)
        for k in range(docs):
            end = end + doc_lengths[sample, k]
            row_doc = row_doc + (row >= end).astype(jnp.int32)
            column_doc = column_doc + (column >= end).astype(jnp.int32)
        mask[s] = jnp.where((row_doc == column_doc) & (column <= row), 0.0, -jnp.inf)


def layout_of(order, boundary, skip_offset, doc_lengths, spot, slots, seq_len, after):
    half_dim = HEAD_DIM // 2
    exponent = jnp.arange(half_dim, dtype=jnp.float32) * (2.0 / HEAD_DIM)
    frequency = jnp.float32(ROPE_THETA) ** (-exponent)
    frequency = jnp.concatenate([frequency, frequency])[None]
    smem = pl.BlockSpec(memory_space=pltpu.SMEM)
    angle, mask = pl.pallas_call(
        partial(layout_kernel, slots),
        out_shape=[
            jax.ShapeDtypeStruct((slots, seq_len, HEAD_DIM), jnp.float32),
            jax.ShapeDtypeStruct((slots, seq_len, seq_len), jnp.float32),
        ],
        in_specs=[smem] * 5 + in_vmem(2),
        out_specs=in_vmem(2),
        name="layout",
    )(spot, order, boundary, skip_offset, doc_lengths, frequency, after)
    sign = jnp.where(jnp.arange(HEAD_DIM) < half_dim, -1.0, 1.0).astype(jnp.float32)
    return jnp.cos(angle), jnp.sin(angle) * sign, mask


def swapped(value, axis, by):
    return lax.ppermute(value, axis, [(i, i ^ by) for i in range(lax.axis_size(axis))])


def gather_blocks(block, axis, peers):
    return [block] + [swapped(block, axis, m) for m in range(1, peers)]


def trade_blocks(blocks, axis):
    return [blocks[0]] + [swapped(blocks[m], axis, m) for m in range(1, len(blocks))]


def total_of(blocks):
    value = blocks[0].astype(jnp.float32)
    for block in blocks[1:]:
        value = value + block.astype(jnp.float32)
    return value


def per_device(
    tokens,
    w_query,
    w_key,
    w_value,
    w_out,
    norm_gain,
    boundary,
    skip_offset,
    doc_lengths,
    batch_order,
):
    replicas, sections, groups = lax.axis_size("dp"), lax.axis_size("pipe"), lax.axis_size("tensor")
    my_replica, my_section, my_group = lax.axis_index("dp"), lax.axis_index("pipe"), lax.axis_index("tensor")
    micro_count, seq_len, local_width = tokens.shape
    model_width = local_width * groups
    slots = micro_count // sections
    rows = slots * seq_len
    depth = w_query.shape[2]
    q_heads = w_query.shape[3] // HEAD_DIM
    kv_heads = w_key.shape[3] // HEAD_DIM
    paired = replicas == groups and replicas & (replicas - 1) == 0

    spot = jnp.reshape(my_section, (1,)).astype(jnp.int32)
    parts = 2 if paired else 1
    part_len = seq_len // parts
    stream = pick_samples(tokens, batch_order, spot, slots, parts).reshape(rows, local_width)

    gain_rows = lax.dynamic_slice_in_dim(norm_gain, my_replica * depth, depth, 2)
    held = (w_query, w_key, w_value, w_out)
    if sections == 2:
        gain_traded = swapped(gain_rows, "pipe", 1)
        gain_traded, held = lax.optimization_barrier((gain_traded, held))
        held = (gain_rows, *held)
        traded = [gain_traded] + [swapped(w, "pipe", 1) for w in held[1:]]

        def layer_weights(index, section):
            return [
                jnp.where(my_section == section, mine[index, 0], theirs[index, 0])
                for mine, theirs in zip(held, traded)
            ]
    else:
        gathered = [lax.all_gather(w, "pipe", axis=1, tiled=True) for w in (gain_rows, *held)]

        def layer_weights(index, section):
            return [w[index, section] for w in gathered]

    turn = [(i * groups + j, j * groups + i) for i in range(replicas) for j in range(groups)]
    if paired:
        place = lax.bitwise_xor(jnp.arange(groups, dtype=jnp.int32), lax.bitwise_xor(my_replica, my_group))
        blocks = gather_blocks(lax.ppermute(stream, ("dp", "tensor"), turn), "tensor", groups)
    else:
        place = jnp.zeros((1,), jnp.int32)
        wide = lax.all_gather(stream, "tensor", axis=1, tiled=True)
        blocks = [lax.all_to_all(wide, "dp", split_axis=1, concat_axis=0, tiled=True)]
    part_rows = slots * part_len
    total = replicas * part_rows

    layout, latest = None, []
    layers = [(0, s) for s in range(sections)] + [(1, s) for s in reversed(range(sections))]
    streams, shares = [None] * parts, [None] * parts
    for number, (index, section) in enumerate(layers):
        gain, wq, wk, wv, wo = layer_weights(index, section)
        last = number + 1 == len(layers)
        before, sums, mixed = [], [None] * parts, [None] * parts
        for h in range(parts):
            head, arrays, part = (streams[h], shares[h], None) if number else (place, blocks, h)
            streams[h], sums[h] = project_qkv(
                head, arrays, part, total, gain[None], wq, wk, wv, replicas if paired else 1, latest
            )
            latest = [streams[h]]
            if layout is None:
                layout = layout_of(
                    batch_order, boundary, skip_offset, doc_lengths, spot, slots, seq_len, sums[0][0]
                )
            if paired:
                sums[h] = trade_blocks(sums[h], "dp")
            else:
                pieces = sums[h][0].reshape(replicas, part_rows, sums[h][0].shape[1])
                pieces = lax.all_to_all(pieces, "dp", split_axis=0, concat_axis=0)
                sums[h] = [jnp.sum(pieces.astype(jnp.float32), axis=0)]
        for h in range(parts):
            mixed[h], keys, values = attend(
                sums[h], before, *layout, q_heads, kv_heads, model_width, latest
            )
            latest = [keys]
            before.append((keys, values))
            if paired:
                mixed[h] = gather_blocks(mixed[h], "dp", replicas)
            else:
                mixed[h] = [lax.all_gather(mixed[h], "dp", axis=0, tiled=True)]
        for h in range(parts):
            ends = project_out(
                mixed[h], place if paired and last else None, wo, groups if paired and last else 1, latest
            )
            latest = ends[:1]
            if not paired:
                shares[h] = [lax.psum(ends[0].astype(jnp.float32), "tensor")]
            elif last:
                shares[h] = trade_blocks(ends, "tensor")
            else:
                shares[h] = gather_blocks(ends[0], "tensor", groups)

    final = []
    for stream, share in zip(streams, shares):
        share = total_of(share)
        if paired:
            stream = lax.dynamic_slice_in_dim(stream, place[0] * part_rows, part_rows, 0)
            stream = (stream.astype(jnp.float32) + share).astype(jnp.bfloat16)
            stream = lax.ppermute(stream, ("dp", "tensor"), turn)
        else:
            stream = (stream.astype(jnp.float32) + share).astype(jnp.bfloat16)
            stream = lax.all_to_all(stream, "dp", split_axis=0, concat_axis=1, tiled=True)
            stream = lax.dynamic_slice_in_dim(stream, my_group * local_width, local_width, 1)
        final.append(stream.reshape(slots, part_len, local_width))
    if parts == sections == 2:
        first = my_section == 0
        came = swapped(jnp.where(first, final[1], final[0]), "pipe", 1)
        kept = jnp.where(first, final[0], final[1])
        return jnp.concatenate([jnp.where(first, kept, came), jnp.where(first, came, kept)], axis=0)
    final = jnp.concatenate(final, axis=1)
    return lax.all_to_all(final, "pipe", split_axis=1, concat_axis=0, tiled=True)


def solution(mesh):
    placed = (
        P("dp", None, "tensor"),
        P(None, "pipe", "dp", "tensor"),
        P(None, "pipe", "dp", "tensor"),
        P(None, "pipe", "dp", "tensor"),
        P(None, "pipe", "tensor", "dp"),
        P(None, "pipe", None),
        P("dp"),
        P("dp"),
        P("dp", None),
        P("dp", None),
    )
    return jax.shard_map(
        per_device, mesh=mesh, in_specs=placed, out_specs=P("dp", "pipe", "tensor"), check_vma=False
    )
```

time: 250 us -> 213 us (0.85)
  waiting for transfers between devices: 119 us -> 36.1 us
  starting transfers between devices: 94.4 us -> 133 us
  Pallas kernels: 15.8 us -> 26.8 us
  between operations: 3.6 us -> 0.62 us
  other arithmetic: 10.9 us -> 13.6 us
    ppermute x54 -> x81, waiting for transfers between devices: 106 us -> 29.1 us  [swapped(): lax.ppermute(value, axis, [(i, i ^ by) for i in range(lax.axis_size(axis))])]
    ppermute x54 -> x81, starting transfers between devices: 87.4 us -> 119 us  [swapped(): lax.ppermute(value, axis, [(i, i ^ by) for i in range(lax.axis_size(axis))])]
    pallas_call x12 -> x26, Pallas kernels: 15.8 us -> 26.8 us  [the longest x8 9.77 us: attend(): pl.pallas_call(unread(len(after), len(blocks) + 2 * len(before) + 3, part...]
    ppermute x2 -> x3, starting transfers between devices: 7.07 us -> 14 us  [the longest x2 8.88 us: per_device(): stream = lax.ppermute(stream, ('dp', 'tensor'), turn)]
    ppermute x2 -> x3, waiting for transfers between devices: 12.2 us -> 7.05 us  [the longest x1 3.85 us: per_device(): lax.ppermute(stream, ('dp', 'tensor'), turn)]
    select_n x5, other arithmetic: 7.65 us -> 12 us  [layer_weights(): jnp.where(my_section == section, mine[index, 0], theirs[index, 0])]
    gather x2 -> x0, local copies, waits for them, and re-layouts: 2.6 us -> none  [the longest x1 1.32 us: per_device(): jnp.take(skip_offset, samples)]
  transfers between devices with their start and end apart: 56 -> 84, of which waited for: 41 -> 20; matrix products, arithmetic and copies ran while one was open for 6% -> 6% of each run, Pallas kernels for 1% -> 13%
where the time goes in v2:
time: 213 us
  starting transfers between devices  133 us (62%)
  waiting for transfers between devices  36.1 us (17%)
  Pallas kernels  26.8 us (13%)
  other arithmetic  13.6 us (6%)
  local copies, waits for them, and re-layouts  2.82 us (1%)
    ppermute x81, starting transfers between devices, swapped(): lax.ppermute(value, axis, [(i, i ^ by) for i in range(lax.axis_size(axis))])  119 us
    ppermute x81, waiting for transfers between devices, swapped(): lax.ppermute(value, axis, [(i, i ^ by) for i in range(lax.axis_size(axis))])  29.1 us
    select_n x5, other arithmetic, layer_weights(): jnp.where(my_section == section, mine[index, 0], theirs[index, 0])  12 us
    pallas_call x8, Pallas kernels, attend(): pl.pallas_call(unread(len(after), len(blocks) + 2 * len(before) + 3, part...  9.77 us
    ppermute x2, starting transfers between devices, per_device(): stream = lax.ppermute(stream, ('dp', 'tensor'), turn)  8.88 us
    pallas_call x8, Pallas kernels, project_qkv(): pl.pallas_call(unread(len(after), len(arrays) + 5, partial(qkv_kernel, le...  7.81 us
    ppermute x1, starting transfers between devices, per_device(): lax.ppermute(stream, ('dp', 'tensor'), turn)  5.13 us
    pallas_call x8, Pallas kernels, project_out(): pl.pallas_call(unread(len(after), placed + n_in + 1, partial(out_kernel,...  4.67 us
  transfers between devices with their start and end apart: 84, of which 20 were waited for; matrix products, arithmetic and copies ran while one was open for 6% of the time, Pallas kernels for 13%

profile of v2, /device:TPU:7, one launch (start us, length us, event | category | flops | bytes accessed | tf_op | source)
XLA Modules:
  0.0 212.8 jit_solution(12037916614199105367)
XLA Ops:
  3.2 3.0 %pick_samples.1 = bf16[2,1,32,1024]{3,2,1,0:T(8,128)(2,1)} custom-call(s32[1,2]{1,0:T(1,128)} %order.3, s32[1]{0:T(128)} %bitcast.spot, bf16[2,64,1024]{2,1,0:T(8,128)(2,1)} %tokens.1), custom_call_target="tpu_custom_call" | custom-call | tf_op jit(solution)/shard_map/pick_samples/pallas_call | solution.py:206
  6.2 5.1 %collective-permute-start = (bf16[64,1024]{1,0:T(8,128)(2,1)}, bf16[64,1024]{1,0:T(8,128)(2,1)S(1)}, u32[]{:S(2)}, u32[]{:S(2)}) collective-permute-start(bf16[64,1024]{1,0:T(8,128)(2,1)} %bitcast.52), channel_id=1, source_target_pairs={{0,0},{1,8},{2,16},{3,24},{8,1},{9,9},{10,17},{11,25},{16,2},{17,1... | collective-permute-start | bytes 393224 | tf_op jit(solution)/shard_map/ppermute | solution.py:322
  12.8 3.8 %collective-permute-done.refs_1_ = bf16[64,1024]{1,0:T(8,128)(2,1)S(1)} collective-permute-done((bf16[64,1024]{1,0:T(8,128)(2,1)}, bf16[64,1024]{1,0:T(8,128)(2,1)S(1)}, u32[]{:S(2)}, u32[]{:S(2)}) %collective-permute-start) | collective-permute-done | bytes 131104 | tf_op jit(solution)/shard_map/ppermute | solution.py:322
  16.7 1.3 collective-permute-start.1
  18.0 1.8 collective-permute-start.2
  19.8 2.3 %select_bitcast_fusion.8 = (bf16[1024,256]{1,0:T(8,128)(2,1)S(1)}, bf16[1024,256]{1,0:T(8,128)(2,1)}, bf16[1024,256]{1,0:T(8,128)(2,1)}, bf16[1024,256]{1,0:T(8,128)(2,1)S(1)}) fusion(pred[]{:T(512)S(6)} %eq.4, bf16[2,1,1024,256]{3,2,1,0:T(8,128)(2,1)S(1)} %collective-permute-done.7, bf16[2,1,1024,256]{3,2,1,0:T(8,128)(2,1)} %param.13, pred[]{:T(512)S(6)} %eq.5), kind=kLoop, calls=%fused_computation.8 | loop fusion | flops 1048576 | bytes 4194306 | tf_op jit(solution)/shard_map/jit(_where)/select_n | solution.py:310
  22.1 1.2 collective-permute-start.3
  23.3 1.2 select_bitcast_fusion.9
  24.5 3.8 %select_bitcast_fusion.1 = (bf16[1024,1024]{1,0:T(8,128)(2,1)S(1)}, bf16[1024,1024]{1,0:T(8,128)(2,1)}, bf16[1024,1024]{1,0:T(8,128)(2,1)}, bf16[1024,1024]{1,0:T(8,128)(2,1)S(1)}) fusion(pred[]{:T(512)S(6)} %eq.4, bf16[2,1,1024,1024]{3,2,1,0:T(8,128)(2,1)} %collective-permute-done.5, bf16[2,1,1024,1024]{3,2,1,0:T(8,128)(2,1)S(1)} %copy-done.15, pred[]{:T(512)S(6)} %eq.5), kind=kLoop, calls=%fused_computation.1 | loop fusion | flops 4194304 | bytes 16777218 | tf_op jit(solution)/shard_map/jit(_where)/select_n | solution.py:310
  28.4 1.9 project_qkv.8
  30.9 3.4 %collective-permute-start.10 = (bf16[32,1664]{1,0:T(8,128)(2,1)}, bf16[32,1664]{1,0:T(8,128)(2,1)}, u32[]{:S(2)}, u32[]{:S(2)}) collective-permute-start(bf16[32,1664]{1,0:T(8,128)(2,1)} %get-tuple-element.88), channel_id=1, source_target_pairs={{0,24},{8,16},{16,8},{24,0},{1,25},{9,17},{17,9},{25,1},{2,26},{10... | collective-permute-start | bytes 319496 | tf_op jit(solution)/shard_map/ppermute | solution.py:254
  34.6 1.8 project_qkv.9
  37.7 1.2 collective-permute-start.15
  38.9 1.6 layout.1
  40.5 2.4 %collective-permute-start.16 = (bf16[32,1664]{1,0:T(8,128)(2,1)S(1)}, bf16[32,1664]{1,0:T(8,128)(2,1)S(1)}, u32[]{:S(2)}, u32[]{:S(2)}) collective-permute-start(bf16[32,1664]{1,0:T(8,128)(2,1)S(1)} %get-tuple-element.96), channel_id=1, source_target_pairs={{0,16},{8,24},{16,0},{24,8},{1,17},{9,25},{17,1},{25,9},{2,18},{10... | collective-permute-start | bytes 319496 | tf_op jit(solution)/shard_map/ppermute | solution.py:254
  43.0 3.9 %select_bitcast_fusion = (bf16[1024,1024]{1,0:T(8,128)(2,1)S(1)}, bf16[1024,1024]{1,0:T(8,128)(2,1)S(1)}, bf16[1024,1024]{1,0:T(8,128)(2,1)S(1)}, bf16[1024,1024]{1,0:T(8,128)(2,1)S(1)}) fusion(pred[]{:T(512)S(6)} %eq.4, bf16[2,1,1024,1024]{3,2,1,0:T(8,128)(2,1)} %collective-permute-done.14, bf16[2,1,1024,1024]{3,2,1,0:T(8,128)(2,1)} %param.14, pred[]{:T(512)S(6)} %eq.5), kind=kLoop, calls=%fused_computation | loop fusion | flops 4194304 | bytes 16777218 | tf_op jit(solution)/shard_map/jit(_where)/select_n | solution.py:310
  47.2 2.0 attend.8
  49.6 3.2 %collective-permute-start.12 = (bf16[32,1024]{1,0:T(8,128)(2,1)S(1)}, bf16[32,1024]{1,0:T(8,128)(2,1)S(1)}, u32[]{:S(2)}, u32[]{:S(2)}) collective-permute-start(bf16[32,1024]{1,0:T(8,128)(2,1)S(1)} %get-tuple-element.92.refs_0_), channel_id=1, source_target_pairs={{0,16},{8,24},{16,0},{24,8},{1,17},{9,25},{17,1},{25,9},{2,18},{10... | collective-permute-start | bytes 196616 | tf_op jit(solution)/shard_map/ppermute | solution.py:254
  52.8 1.2 attend.9
  54.2 3.3 %collective-permute-start.22 = (bf16[32,1024]{1,0:T(8,128)(2,1)S(1)}, bf16[32,1024]{1,0:T(8,128)(2,1)S(1)}, u32[]{:S(2)}, u32[]{:S(2)}) collective-permute-start(bf16[32,1024]{1,0:T(8,128)(2,1)S(1)} %get-tuple-element.101.refs_0_), channel_id=1, source_target_pairs={{0,16},{8,24},{16,0},{24,8},{1,17},{9,25},{17,1},{25,9},{2,18},{10... | collective-permute-start | bytes 196616 | tf_op jit(solution)/shard_map/ppermute | solution.py:254
  58.9 1.2 collective-permute-start.18
  61.7 1.4 collective-permute-done.23.refs_3_
  63.6 1.8 collective-permute-start.27
  65.4 1.3 collective-permute-start.29
  66.8 1.7 collective-permute-done.20.refs_4_
  69.3 2.9 %collective-permute-start.25 = (bf16[32,1664]{1,0:T(8,128)(2,1)S(1)}, bf16[32,1664]{1,0:T(8,128)(2,1)S(1)}, u32[]{:S(2)}, u32[]{:S(2)}) collective-permute-start(bf16[32,1664]{1,0:T(8,128)(2,1)S(1)} %get-tuple-element.105), channel_id=1, source_target_pairs={{0,16},{8,24},{16,0},{24,8},{1,17},{9,25},{17,1},{25,9},{2,18},{10... | collective-permute-start | bytes 319496 | tf_op jit(solution)/shard_map/ppermute | solution.py:254
  72.8 2.5 %collective-permute-start.26 = (bf16[32,1664]{1,0:T(8,128)(2,1)S(1)}, bf16[32,1664]{1,0:T(8,128)(2,1)S(1)}, u32[]{:S(2)}, u32[]{:S(2)}) collective-permute-start(bf16[32,1664]{1,0:T(8,128)(2,1)S(1)} %get-tuple-element.106), channel_id=1, source_target_pairs={{0,24},{8,16},{16,8},{24,0},{1,25},{9,17},{17,9},{25,1},{2,26},{10... | collective-permute-start | bytes 319496 | tf_op jit(solution)/shard_map/ppermute | solution.py:254
  75.4 4.4 %collective-permute-done.29.refs_4_ = bf16[128,1024]{1,0:T(8,128)(2,1)S(1)} collective-permute-done((bf16[128,1024]{1,0:T(8,128)(2,1)S(1)}, bf16[128,1024]{1,0:T(8,128)(2,1)S(1)}, u32[]{:S(2)}, u32[]{:S(2)}) %collective-permute-start.29) | collective-permute-done | bytes 262176 | tf_op jit(solution)/shard_map/ppermute | solution.py:254
  81.1 2.2 %collective-permute-start.34 = (bf16[32,1664]{1,0:T(8,128)(2,1)S(1)}, bf16[32,1664]{1,0:T(8,128)(2,1)S(1)}, u32[]{:S(2)}, u32[]{:S(2)}) collective-permute-start(bf16[32,1664]{1,0:T(8,128)(2,1)S(1)} %get-tuple-element.111), channel_id=1, source_target_pairs={{0,16},{8,24},{16,0},{24,8},{1,17},{9,25},{17,1},{25,9},{2,18},{10... | collective-permute-start | bytes 319496 | tf_op jit(solution)/shard_map/ppermute | solution.py:254
  85.1 2.8 %collective-permute-start.31 = (bf16[32,1024]{1,0:T(8,128)(2,1)S(1)}, bf16[32,1024]{1,0:T(8,128)(2,1)S(1)}, u32[]{:S(2)}, u32[]{:S(2)}) collective-permute-start(bf16[32,1024]{1,0:T(8,128)(2,1)S(1)} %get-tuple-element.108.refs_0_), channel_id=1, source_target_pairs={{0,16},{8,24},{16,0},{24,8},{1,17},{9,25},{17,1},{25,9},{2,18},{10... | collective-permute-start | bytes 196616 | tf_op jit(solution)/shard_map/ppermute | solution.py:254
  88.7 1.9 collective-permute-done.35.refs_3_
  90.6 1.2 attend.11
  91.7 5.1 %collective-permute-start.39 = (bf16[32,1024]{1,0:T(8,128)(2,1)S(1)}, bf16[32,1024]{1,0:T(8,128)(2,1)S(1)}, u32[]{:S(2)}, u32[]{:S(2)}) collective-permute-start(bf16[32,1024]{1,0:T(8,128)(2,1)S(1)} %get-tuple-element.116.refs_0_), channel_id=1, source_target_pairs={{0,8},{8,0},{16,24},{24,16},{1,9},{9,1},{17,25},{25,17},{2,10},{10... | collective-permute-start | bytes 196616 | tf_op jit(solution)/shard_map/ppermute | solution.py:254
  96.9 2.1 collective-permute-start.40
  98.9 1.2 collective-permute-start.41
  100.6 1.3 collective-permute-start.36
  101.9 1.3 collective-permute-start.37
  105.1 1.3 collective-permute-start.46
  106.4 2.1 collective-permute-start.47
  108.5 1.8 collective-permute-done.37.refs_3_
  112.5 2.1 collective-permute-start.44
  115.3 3.8 %collective-permute-done.47.refs_4_ = bf16[128,1024]{1,0:T(8,128)(2,1)S(1)} collective-permute-done((bf16[128,1024]{1,0:T(8,128)(2,1)S(1)}, bf16[128,1024]{1,0:T(8,128)(2,1)S(1)}, u32[]{:S(2)}, u32[]{:S(2)}) %collective-permute-start.47) | collective-permute-done | bytes 262176 | tf_op jit(solution)/shard_map/ppermute | solution.py:254
  120.8 2.6 %collective-permute-start.53 = (bf16[32,1664]{1,0:T(8,128)(2,1)S(1)}, bf16[32,1664]{1,0:T(8,128)(2,1)S(1)}, u32[]{:S(2)}, u32[]{:S(2)}) collective-permute-start(bf16[32,1664]{1,0:T(8,128)(2,1)S(1)} %get-tuple-element.127), channel_id=1, source_target_pairs={{0,24},{8,16},{16,8},{24,0},{1,25},{9,17},{17,9},{25,1},{2,26},{10... | collective-permute-start | bytes 319496 | tf_op jit(solution)/shard_map/ppermute | solution.py:254
  125.4 2.6 %collective-permute-start.50 = (bf16[32,1024]{1,0:T(8,128)(2,1)S(1)}, bf16[32,1024]{1,0:T(8,128)(2,1)S(1)}, u32[]{:S(2)}, u32[]{:S(2)}) collective-permute-start(bf16[32,1024]{1,0:T(8,128)(2,1)S(1)} %get-tuple-element.123.refs_0_), channel_id=1, source_target_pairs={{0,24},{8,16},{16,8},{24,0},{1,25},{9,17},{17,9},{25,1},{2,26},{10... | collective-permute-start | bytes 196616 | tf_op jit(solution)/shard_map/ppermute | solution.py:254
  128.1 1.2 attend.13
  129.2 6.1 %collective-permute-start.57 = (bf16[32,1024]{1,0:T(8,128)(2,1)S(1)}, bf16[32,1024]{1,0:T(8,128)(2,1)S(1)}, u32[]{:S(2)}, u32[]{:S(2)}) collective-permute-start(bf16[32,1024]{1,0:T(8,128)(2,1)S(1)} %get-tuple-element.131.refs_0_), channel_id=1, source_target_pairs={{0,8},{8,0},{16,24},{24,16},{1,9},{9,1},{17,25},{25,17},{2,10},{10... | collective-permute-start | bytes 196616 | tf_op jit(solution)/shard_map/ppermute | solution.py:254
  135.3 2.1 collective-permute-start.59
  137.9 2.7 %collective-permute-start.54 = (bf16[128,1024]{1,0:T(8,128)(2,1)S(1)}, bf16[128,1024]{1,0:T(8,128)(2,1)S(1)}, u32[]{:S(2)}, u32[]{:S(2)}) collective-permute-start(bf16[128,1024]{1,0:T(8,128)(2,1)S(1)} %project_out.12.refs_5_.refs_1_), channel_id=1, source_target_pairs={{0,1},{1,0},{2,3},{3,2},{4,5},{5,4},{6,7},{7,6},{8,9},{9,8},{10,11... | collective-permute-start | bytes 786440 | tf_op jit(solution)/shard_map/ppermute | solution.py:254
  140.5 1.3 collective-permute-start.56
  142.3 2.2 %collective-permute-start.63 = (bf16[128,1024]{1,0:T(8,128)(2,1)S(1)}, bf16[128,1024]{1,0:T(8,128)(2,1)S(1)}, u32[]{:S(2)}, u32[]{:S(2)}) collective-permute-start(bf16[128,1024]{1,0:T(8,128)(2,1)S(1)} %project_out.13.refs_9_.refs_1_), channel_id=1, source_target_pairs={{0,1},{1,0},{2,3},{3,2},{4,5},{5,4},{6,7},{7,6},{8,9},{9,8},{10,11... | collective-permute-start | bytes 786440 | tf_op jit(solution)/shard_map/ppermute | solution.py:254
  145.7 2.9 %collective-permute-done.55.refs_3_ = bf16[128,1024]{1,0:T(8,128)(2,1)S(1)} collective-permute-done((bf16[128,1024]{1,0:T(8,128)(2,1)S(1)}, bf16[128,1024]{1,0:T(8,128)(2,1)S(1)}, u32[]{:S(2)}, u32[]{:S(2)}) %collective-permute-start.55) | collective-permute-done | bytes 262176 | tf_op jit(solution)/shard_map/ppermute | solution.py:254
  150.8 2.1 collective-permute-start.62
  152.9 2.7 %collective-permute-done.64.refs_3_ = bf16[128,1024]{1,0:T(8,128)(2,1)S(1)} collective-permute-done((bf16[128,1024]{1,0:T(8,128)(2,1)S(1)}, bf16[128,1024]{1,0:T(8,128)(2,1)S(1)}, u32[]{:S(2)}, u32[]{:S(2)}) %collective-permute-start.64) | collective-permute-done | bytes 262176 | tf_op jit(solution)/shard_map/ppermute | solution.py:254
  157.5 2.4 %collective-permute-start.71 = (bf16[32,1664]{1,0:T(8,128)(2,1)S(1)}, bf16[32,1664]{1,0:T(8,128)(2,1)S(1)}, u32[]{:S(2)}, u32[]{:S(2)}) collective-permute-start(bf16[32,1664]{1,0:T(8,128)(2,1)S(1)} %get-tuple-element.142), channel_id=1, source_target_pairs={{0,24},{8,16},{16,8},{24,0},{1,25},{9,17},{17,9},{25,1},{2,26},{10... | collective-permute-start | bytes 319496 | tf_op jit(solution)/shard_map/ppermute | solution.py:254
  161.1 1.2 collective-permute-start.67
  162.3 2.4 %collective-permute-start.68 = (bf16[32,1024]{1,0:T(8,128)(2,1)S(1)}, bf16[32,1024]{1,0:T(8,128)(2,1)S(1)}, u32[]{:S(2)}, u32[]{:S(2)}) collective-permute-start(bf16[32,1024]{1,0:T(8,128)(2,1)S(1)} %get-tuple-element.138.refs_1_), channel_id=1, source_target_pairs={{0,24},{8,16},{16,8},{24,0},{1,25},{9,17},{17,9},{25,1},{2,26},{10... | collective-permute-start | bytes 196616 | tf_op jit(solution)/shard_map/ppermute | solution.py:254
  164.6 1.2 attend.15
  167.0 2.4 %collective-permute-start.78 = (bf16[32,1024]{1,0:T(8,128)(2,1)S(1)}, bf16[32,1024]{1,0:T(8,128)(2,1)S(1)}, u32[]{:S(2)}, u32[]{:S(2)}) collective-permute-start(bf16[32,1024]{1,0:T(8,128)(2,1)S(1)} %get-tuple-element.150.refs_1_), channel_id=1, source_target_pairs={{0,24},{8,16},{16,8},{24,0},{1,25},{9,17},{17,9},{25,1},{2,26},{10... | collective-permute-start | bytes 196616 | tf_op jit(solution)/shard_map/ppermute | solution.py:254
  171.7 1.3 collective-permute-done.76.refs_2_
  173.1 2.2 %collective-permute-done.77.refs_3_ = bf16[32,1024]{1,0:T(8,128)(2,1)S(1)} collective-permute-done((bf16[32,1024]{1,0:T(8,128)(2,1)S(1)}, bf16[32,1024]{1,0:T(8,128)(2,1)S(1)}, u32[]{:S(2)}, u32[]{:S(2)}) %collective-permute-start.77) | collective-permute-done | bytes 65568 | tf_op jit(solution)/shard_map/ppermute | solution.py:254
  179.1 3.3 %collective-permute-start.75 = (bf16[32,1024]{1,0:T(8,128)(2,1)S(1)}, bf16[32,1024]{1,0:T(8,128)(2,1)S(1)}, u32[]{:S(2)}, u32[]{:S(2)}) collective-permute-start(bf16[32,1024]{1,0:T(8,128)(2,1)S(1)} %add_convert_fusion.1), channel_id=1, source_target_pairs={{0,0},{1,8},{2,16},{3,24},{8,1},{9,9},{10,17},{11,25},{16,2},{17,1... | collective-permute-start | bytes 196616 | tf_op jit(solution)/shard_map/ppermute | solution.py:381
  182.4 5.6 %collective-permute-start.82 = (bf16[32,1024]{1,0:T(8,128)(2,1)S(1)}, bf16[32,1024]{1,0:T(8,128)(2,1)S(1)}, u32[]{:S(2)}, u32[]{:S(2)}) collective-permute-start(bf16[32,1024]{1,0:T(8,128)(2,1)S(1)} %add_convert_fusion), channel_id=1, source_target_pairs={{0,0},{1,8},{2,16},{3,24},{8,1},{9,9},{10,17},{11,25},{16,2},{17,1... | collective-permute-start | bytes 196616 | tf_op jit(solution)/shard_map/ppermute | solution.py:381
  188.1 3.2 %collective-permute-done.82 = bf16[32,1024]{1,0:T(8,128)(2,1)S(1)} collective-permute-done((bf16[32,1024]{1,0:T(8,128)(2,1)S(1)}, bf16[32,1024]{1,0:T(8,128)(2,1)S(1)}, u32[]{:S(2)}, u32[]{:S(2)}) %collective-permute-start.82) | collective-permute-done | bytes 65568 | tf_op jit(solution)/shard_map/ppermute | solution.py:381
  191.3 19.9 %collective-permute-start.83 = (bf16[1,32,1024]{2,1,0:T(8,128)(2,1)S(1)}, bf16[1,32,1024]{2,1,0:T(8,128)(2,1)S(1)}, u32[]{:S(2)}, u32[]{:S(2)}) collective-permute-start(bf16[1,32,1024]{2,1,0:T(8,128)(2,1)S(1)} %select_bitcast_fusion.16), channel_id=1, source_target_pairs={{0,4},{4,0},{1,5},{5,1},{2,6},{6,2},{3,7},{7,3},{8,12},{12,8},{9,1... | collective-permute-start | bytes 196616 | tf_op jit(solution)/shard_map/ppermute | solution.py:254
  (182 shorter events, 42.4 us)
Async XLA Ops:
  2.2 22.3 %collective-permute-start.5 = (bf16[2,1,1024,1024]{3,2,1,0:T(8,128)(2,1)}, bf16[2,1,1024,1024]{3,2,1,0:T(8,128)(2,1)}, u32[]{:S(2)}, u32[]{:S(2)}) collective-permute-start(bf16[2,1,1024,1024]{3,2,1,0:T(8,128)(2,1)} %param.11), channel_id=1, source_target_pairs={{0,4},{4,0},{1,5},{5,1},{2,6},{6,2},{3,7},{7,3},{8,12},{12,8},{9,1... | collective-permute-start | bytes 12582920 | tf_op jit(solution)/shard_map/ppermute | solution.py:254
  2.5 38.0 %collective-permute-start.14 = (bf16[2,1,1024,1024]{3,2,1,0:T(8,128)(2,1)}, bf16[2,1,1024,1024]{3,2,1,0:T(8,128)(2,1)}, u32[]{:S(2)}, u32[]{:S(2)}) collective-permute-start(bf16[2,1,1024,1024]{3,2,1,0:T(8,128)(2,1)} %param.14), channel_id=1, source_target_pairs={{0,4},{4,0},{1,5},{5,1},{2,6},{6,2},{3,7},{7,3},{8,12},{12,8},{9,1... | collective-permute-start | bytes 12582920 | tf_op jit(solution)/shard_map/ppermute | solution.py:254
  2.7 15.3 %collective-permute-start.7 = (bf16[2,1,1024,256]{3,2,1,0:T(8,128)(2,1)}, bf16[2,1,1024,256]{3,2,1,0:T(8,128)(2,1)S(1)}, u32[]{:S(2)}, u32[]{:S(2)}) collective-permute-start(bf16[2,1,1024,256]{3,2,1,0:T(8,128)(2,1)} %param.13), channel_id=1, source_target_pairs={{0,4},{4,0},{1,5},{5,1},{2,6},{6,2},{3,7},{7,3},{8,12},{12,8},{9,1... | collective-permute-start | bytes 3145736 | tf_op jit(solution)/shard_map/ppermute | solution.py:254
  3.1 19.1 %collective-permute-start.6 = (bf16[2,1,1024,256]{3,2,1,0:T(8,128)(2,1)}, bf16[2,1,1024,256]{3,2,1,0:T(8,128)(2,1)S(1)}, u32[]{:S(2)}, u32[]{:S(2)}) collective-permute-start(bf16[2,1,1024,256]{3,2,1,0:T(8,128)(2,1)} %param.12), channel_id=1, source_target_pairs={{0,4},{4,0},{1,5},{5,1},{2,6},{6,2},{3,7},{7,3},{8,12},{12,8},{9,1... | collective-permute-start | bytes 3145736 | tf_op jit(solution)/shard_map/ppermute | solution.py:254
  6.2 10.5 %collective-permute-start = (bf16[64,1024]{1,0:T(8,128)(2,1)}, bf16[64,1024]{1,0:T(8,128)(2,1)S(1)}, u32[]{:S(2)}, u32[]{:S(2)}) collective-permute-start(bf16[64,1024]{1,0:T(8,128)(2,1)} %bitcast.52), channel_id=1, source_target_pairs={{0,0},{1,8},{2,16},{3,24},{8,1},{9,9},{10,17},{11,25},{16,2},{17,1... | collective-permute-start | bytes 393224 | tf_op jit(solution)/shard_map/ppermute | solution.py:322
  16.7 11.7 %collective-permute-start.1 = (bf16[64,1024]{1,0:T(8,128)(2,1)S(1)}, bf16[64,1024]{1,0:T(8,128)(2,1)S(1)}, u32[]{:S(2)}, u32[]{:S(2)}) collective-permute-start(bf16[64,1024]{1,0:T(8,128)(2,1)S(1)} %collective-permute-done.refs_1_), channel_id=1, source_target_pairs={{0,1},{1,0},{2,3},{3,2},{4,5},{5,4},{6,7},{7,6},{8,9},{9,8},{10,11... | collective-permute-start | bytes 393224 | tf_op jit(solution)/shard_map/ppermute | solution.py:254
  18.0 10.4 %collective-permute-start.2 = (bf16[64,1024]{1,0:T(8,128)(2,1)S(1)}, bf16[64,1024]{1,0:T(8,128)(2,1)S(1)}, u32[]{:S(2)}, u32[]{:S(2)}) collective-permute-start(bf16[64,1024]{1,0:T(8,128)(2,1)S(1)} %collective-permute-done.refs_1_), channel_id=1, source_target_pairs={{0,2},{1,3},{2,0},{3,1},{4,6},{5,7},{6,4},{7,5},{8,10},{9,11},{10,... | collective-permute-start | bytes 393224 | tf_op jit(solution)/shard_map/ppermute | solution.py:254
  30.9 16.1 %collective-permute-start.10 = (bf16[32,1664]{1,0:T(8,128)(2,1)}, bf16[32,1664]{1,0:T(8,128)(2,1)}, u32[]{:S(2)}, u32[]{:S(2)}) collective-permute-start(bf16[32,1664]{1,0:T(8,128)(2,1)} %get-tuple-element.88), channel_id=1, source_target_pairs={{0,24},{8,16},{16,8},{24,0},{1,25},{9,17},{17,9},{25,1},{2,26},{10... | collective-permute-start | bytes 319496 | tf_op jit(solution)/shard_map/ppermute | solution.py:254
  34.3 12.8 %collective-permute-start.8 = (bf16[32,1664]{1,0:T(8,128)(2,1)}, bf16[32,1664]{1,0:T(8,128)(2,1)}, u32[]{:S(2)}, u32[]{:S(2)}) collective-permute-start(bf16[32,1664]{1,0:T(8,128)(2,1)} %get-tuple-element.86), channel_id=1, source_target_pairs={{0,8},{8,0},{16,24},{24,16},{1,9},{9,1},{17,25},{25,17},{2,10},{10... | collective-permute-start | bytes 319496 | tf_op jit(solution)/shard_map/ppermute | solution.py:254
  34.3 12.8 %collective-permute-start.9 = (bf16[32,1664]{1,0:T(8,128)(2,1)}, bf16[32,1664]{1,0:T(8,128)(2,1)}, u32[]{:S(2)}, u32[]{:S(2)}) collective-permute-start(bf16[32,1664]{1,0:T(8,128)(2,1)} %get-tuple-element.87), channel_id=1, source_target_pairs={{0,16},{8,24},{16,0},{24,8},{1,17},{9,25},{17,1},{25,9},{2,18},{10... | collective-permute-start | bytes 319496 | tf_op jit(solution)/shard_map/ppermute | solution.py:254
  37.7 15.0 %collective-permute-start.15 = (bf16[32,1664]{1,0:T(8,128)(2,1)}, bf16[32,1664]{1,0:T(8,128)(2,1)S(1)}, u32[]{:S(2)}, u32[]{:S(2)}) collective-permute-start(bf16[32,1664]{1,0:T(8,128)(2,1)} %get-tuple-element.95), channel_id=1, source_target_pairs={{0,8},{8,0},{16,24},{24,16},{1,9},{9,1},{17,25},{25,17},{2,10},{10... | collective-permute-start | bytes 319496 | tf_op jit(solution)/shard_map/ppermute | solution.py:254
  40.5 12.2 %collective-permute-start.16 = (bf16[32,1664]{1,0:T(8,128)(2,1)S(1)}, bf16[32,1664]{1,0:T(8,128)(2,1)S(1)}, u32[]{:S(2)}, u32[]{:S(2)}) collective-permute-start(bf16[32,1664]{1,0:T(8,128)(2,1)S(1)} %get-tuple-element.96), channel_id=1, source_target_pairs={{0,16},{8,24},{16,0},{24,8},{1,17},{9,25},{17,1},{25,9},{2,18},{10... | collective-permute-start | bytes 319496 | tf_op jit(solution)/shard_map/ppermute | solution.py:254
  49.2 8.3 %collective-permute-start.11 = (bf16[32,1024]{1,0:T(8,128)(2,1)S(1)}, bf16[32,1024]{1,0:T(8,128)(2,1)S(1)}, u32[]{:S(2)}, u32[]{:S(2)}) collective-permute-start(bf16[32,1024]{1,0:T(8,128)(2,1)S(1)} %get-tuple-element.92.refs_0_), channel_id=1, source_target_pairs={{0,8},{8,0},{16,24},{24,16},{1,9},{9,1},{17,25},{25,17},{2,10},{10... | collective-permute-start | bytes 196616 | tf_op jit(solution)/shard_map/ppermute | solution.py:254
  49.6 7.9 %collective-permute-start.12 = (bf16[32,1024]{1,0:T(8,128)(2,1)S(1)}, bf16[32,1024]{1,0:T(8,128)(2,1)S(1)}, u32[]{:S(2)}, u32[]{:S(2)}) collective-permute-start(bf16[32,1024]{1,0:T(8,128)(2,1)S(1)} %get-tuple-element.92.refs_0_), channel_id=1, source_target_pairs={{0,16},{8,24},{16,0},{24,8},{1,17},{9,25},{17,1},{25,9},{2,18},{10... | collective-permute-start | bytes 196616 | tf_op jit(solution)/shard_map/ppermute | solution.py:254
  54.2 7.5 %collective-permute-start.22 = (bf16[32,1024]{1,0:T(8,128)(2,1)S(1)}, bf16[32,1024]{1,0:T(8,128)(2,1)S(1)}, u32[]{:S(2)}, u32[]{:S(2)}) collective-permute-start(bf16[32,1024]{1,0:T(8,128)(2,1)S(1)} %get-tuple-element.101.refs_0_), channel_id=1, source_target_pairs={{0,16},{8,24},{16,0},{24,8},{1,17},{9,25},{17,1},{25,9},{2,18},{10... | collective-permute-start | bytes 196616 | tf_op jit(solution)/shard_map/ppermute | solution.py:254
  60.6 7.8 %collective-permute-start.20 = (bf16[128,1024]{1,0:T(8,128)(2,1)S(1)}, bf16[128,1024]{1,0:T(8,128)(2,1)S(1)}, u32[]{:S(2)}, u32[]{:S(2)}) collective-permute-start(bf16[128,1024]{1,0:T(8,128)(2,1)S(1)} %project_out.8.refs_5_.refs_1_), channel_id=1, source_target_pairs={{0,3},{1,2},{2,1},{3,0},{4,7},{5,6},{6,5},{7,4},{8,11},{9,10},{10,... | collective-permute-start | bytes 786440 | tf_op jit(solution)/shard_map/ppermute | solution.py:254
  63.6 9.2 %collective-permute-start.27 = (bf16[128,1024]{1,0:T(8,128)(2,1)S(1)}, bf16[128,1024]{1,0:T(8,128)(2,1)S(1)}, u32[]{:S(2)}, u32[]{:S(2)}) collective-permute-start(bf16[128,1024]{1,0:T(8,128)(2,1)S(1)} %project_out.9.refs_9_.refs_1_), channel_id=1, source_target_pairs={{0,1},{1,0},{2,3},{3,2},{4,5},{5,4},{6,7},{7,6},{8,9},{9,8},{10,11... | collective-permute-start | bytes 786440 | tf_op jit(solution)/shard_map/ppermute | solution.py:254
  65.4 10.0 %collective-permute-start.28 = (bf16[128,1024]{1,0:T(8,128)(2,1)S(1)}, bf16[128,1024]{1,0:T(8,128)(2,1)S(1)}, u32[]{:S(2)}, u32[]{:S(2)}) collective-permute-start(bf16[128,1024]{1,0:T(8,128)(2,1)S(1)} %project_out.9.refs_9_.refs_1_), channel_id=1, source_target_pairs={{0,2},{1,3},{2,0},{3,1},{4,6},{5,7},{6,4},{7,5},{8,10},{9,11},{10,... | collective-permute-start | bytes 786440 | tf_op jit(solution)/shard_map/ppermute | solution.py:254
  65.4 14.3 %collective-permute-start.29 = (bf16[128,1024]{1,0:T(8,128)(2,1)S(1)}, bf16[128,1024]{1,0:T(8,128)(2,1)S(1)}, u32[]{:S(2)}, u32[]{:S(2)}) collective-permute-start(bf16[128,1024]{1,0:T(8,128)(2,1)S(1)} %project_out.9.refs_9_.refs_1_), channel_id=1, source_target_pairs={{0,3},{1,2},{2,1},{3,0},{4,7},{5,6},{6,5},{7,4},{8,11},{9,10},{10,... | collective-permute-start | bytes 786440 | tf_op jit(solution)/shard_map/ppermute | solution.py:254
  69.2 14.1 %collective-permute-start.24 = (bf16[32,1664]{1,0:T(8,128)(2,1)S(1)}, bf16[32,1664]{1,0:T(8,128)(2,1)S(1)}, u32[]{:S(2)}, u32[]{:S(2)}) collective-permute-start(bf16[32,1664]{1,0:T(8,128)(2,1)S(1)} %get-tuple-element.104), channel_id=1, source_target_pairs={{0,8},{8,0},{16,24},{24,16},{1,9},{9,1},{17,25},{25,17},{2,10},{10... | collective-permute-start | bytes 319496 | tf_op jit(solution)/shard_map/ppermute | solution.py:254
  69.3 14.8 %collective-permute-start.25 = (bf16[32,1664]{1,0:T(8,128)(2,1)S(1)}, bf16[32,1664]{1,0:T(8,128)(2,1)S(1)}, u32[]{:S(2)}, u32[]{:S(2)}) collective-permute-start(bf16[32,1664]{1,0:T(8,128)(2,1)S(1)} %get-tuple-element.105), channel_id=1, source_target_pairs={{0,16},{8,24},{16,0},{24,8},{1,17},{9,25},{17,1},{25,9},{2,18},{10... | collective-permute-start | bytes 319496 | tf_op jit(solution)/shard_map/ppermute | solution.py:254
  72.8 11.3 %collective-permute-start.26 = (bf16[32,1664]{1,0:T(8,128)(2,1)S(1)}, bf16[32,1664]{1,0:T(8,128)(2,1)S(1)}, u32[]{:S(2)}, u32[]{:S(2)}) collective-permute-start(bf16[32,1664]{1,0:T(8,128)(2,1)S(1)} %get-tuple-element.106), channel_id=1, source_target_pairs={{0,24},{8,16},{16,8},{24,0},{1,25},{9,17},{17,9},{25,1},{2,26},{10... | collective-permute-start | bytes 319496 | tf_op jit(solution)/shard_map/ppermute | solution.py:254
  80.5 7.5 %collective-permute-start.33 = (bf16[32,1664]{1,0:T(8,128)(2,1)S(1)}, bf16[32,1664]{1,0:T(8,128)(2,1)S(1)}, u32[]{:S(2)}, u32[]{:S(2)}) collective-permute-start(bf16[32,1664]{1,0:T(8,128)(2,1)S(1)} %get-tuple-element.110), channel_id=1, source_target_pairs={{0,8},{8,0},{16,24},{24,16},{1,9},{9,1},{17,25},{25,17},{2,10},{10... | collective-permute-start | bytes 319496 | tf_op jit(solution)/shard_map/ppermute | solution.py:254
  81.1 7.5 %collective-permute-start.34 = (bf16[32,1664]{1,0:T(8,128)(2,1)S(1)}, bf16[32,1664]{1,0:T(8,128)(2,1)S(1)}, u32[]{:S(2)}, u32[]{:S(2)}) collective-permute-start(bf16[32,1664]{1,0:T(8,128)(2,1)S(1)} %get-tuple-element.111), channel_id=1, source_target_pairs={{0,16},{8,24},{16,0},{24,8},{1,17},{9,25},{17,1},{25,9},{2,18},{10... | collective-permute-start | bytes 319496 | tf_op jit(solution)/shard_map/ppermute | solution.py:254
  83.3 7.3 %collective-permute-start.35 = (bf16[32,1664]{1,0:T(8,128)(2,1)S(1)}, bf16[32,1664]{1,0:T(8,128)(2,1)S(1)}, u32[]{:S(2)}, u32[]{:S(2)}) collective-permute-start(bf16[32,1664]{1,0:T(8,128)(2,1)S(1)} %get-tuple-element.112), channel_id=1, source_target_pairs={{0,24},{8,16},{16,8},{24,0},{1,25},{9,17},{17,9},{25,1},{2,26},{10... | collective-permute-start | bytes 319496 | tf_op jit(solution)/shard_map/ppermute | solution.py:254
  85.1 13.9 %collective-permute-start.30 = (bf16[32,1024]{1,0:T(8,128)(2,1)S(1)}, bf16[32,1024]{1,0:T(8,128)(2,1)S(1)}, u32[]{:S(2)}, u32[]{:S(2)}) collective-permute-start(bf16[32,1024]{1,0:T(8,128)(2,1)S(1)} %get-tuple-element.108.refs_0_), channel_id=1, source_target_pairs={{0,8},{8,0},{16,24},{24,16},{1,9},{9,1},{17,25},{25,17},{2,10},{10... | collective-permute-start | bytes 196616 | tf_op jit(solution)/shard_map/ppermute | solution.py:254
  85.1 15.0 %collective-permute-start.31 = (bf16[32,1024]{1,0:T(8,128)(2,1)S(1)}, bf16[32,1024]{1,0:T(8,128)(2,1)S(1)}, u32[]{:S(2)}, u32[]{:S(2)}) collective-permute-start(bf16[32,1024]{1,0:T(8,128)(2,1)S(1)} %get-tuple-element.108.refs_0_), channel_id=1, source_target_pairs={{0,16},{8,24},{16,0},{24,8},{1,17},{9,25},{17,1},{25,9},{2,18},{10... | collective-permute-start | bytes 196616 | tf_op jit(solution)/shard_map/ppermute | solution.py:254
  87.9 12.2 %collective-permute-start.32 = (bf16[32,1024]{1,0:T(8,128)(2,1)S(1)}, bf16[32,1024]{1,0:T(8,128)(2,1)S(1)}, u32[]{:S(2)}, u32[]{:S(2)}) collective-permute-start(bf16[32,1024]{1,0:T(8,128)(2,1)S(1)} %get-tuple-element.108.refs_0_), channel_id=1, source_target_pairs={{0,24},{8,16},{16,8},{24,0},{1,25},{9,17},{17,9},{25,1},{2,26},{10... | collective-permute-start | bytes 196616 | tf_op jit(solution)/shard_map/ppermute | solution.py:254
  91.7 11.5 %collective-permute-start.39 = (bf16[32,1024]{1,0:T(8,128)(2,1)S(1)}, bf16[32,1024]{1,0:T(8,128)(2,1)S(1)}, u32[]{:S(2)}, u32[]{:S(2)}) collective-permute-start(bf16[32,1024]{1,0:T(8,128)(2,1)S(1)} %get-tuple-element.116.refs_0_), channel_id=1, source_target_pairs={{0,8},{8,0},{16,24},{24,16},{1,9},{9,1},{17,25},{25,17},{2,10},{10... | collective-permute-start | bytes 196616 | tf_op jit(solution)/shard_map/ppermute | solution.py:254
  101.9 8.3 %collective-permute-start.37 = (bf16[128,1024]{1,0:T(8,128)(2,1)S(1)}, bf16[128,1024]{1,0:T(8,128)(2,1)S(1)}, u32[]{:S(2)}, u32[]{:S(2)}) collective-permute-start(bf16[128,1024]{1,0:T(8,128)(2,1)S(1)} %project_out.10.refs_5_.refs_1_), channel_id=1, source_target_pairs={{0,2},{1,3},{2,0},{3,1},{4,6},{5,7},{6,4},{7,5},{8,10},{9,11},{10,... | collective-permute-start | bytes 786440 | tf_op jit(solution)/shard_map/ppermute | solution.py:254
  103.2 7.0 %collective-permute-start.38 = (bf16[128,1024]{1,0:T(8,128)(2,1)S(1)}, bf16[128,1024]{1,0:T(8,128)(2,1)S(1)}, u32[]{:S(2)}, u32[]{:S(2)}) collective-permute-start(bf16[128,1024]{1,0:T(8,128)(2,1)S(1)} %project_out.10.refs_5_.refs_1_), channel_id=1, source_target_pairs={{0,3},{1,2},{2,1},{3,0},{4,7},{5,6},{6,5},{7,4},{8,11},{9,10},{10,... | collective-permute-start | bytes 786440 | tf_op jit(solution)/shard_map/ppermute | solution.py:254
  104.6 7.9 %collective-permute-start.45 = (bf16[128,1024]{1,0:T(8,128)(2,1)S(1)}, bf16[128,1024]{1,0:T(8,128)(2,1)S(1)}, u32[]{:S(2)}, u32[]{:S(2)}) collective-permute-start(bf16[128,1024]{1,0:T(8,128)(2,1)S(1)} %project_out.11.refs_9_.refs_1_), channel_id=1, source_target_pairs={{0,1},{1,0},{2,3},{3,2},{4,5},{5,4},{6,7},{7,6},{8,9},{9,8},{10,11... | collective-permute-start | bytes 786440 | tf_op jit(solution)/shard_map/ppermute | solution.py:254
  105.1 10.2 %collective-permute-start.46 = (bf16[128,1024]{1,0:T(8,128)(2,1)S(1)}, bf16[128,1024]{1,0:T(8,128)(2,1)S(1)}, u32[]{:S(2)}, u32[]{:S(2)}) collective-permute-start(bf16[128,1024]{1,0:T(8,128)(2,1)S(1)} %project_out.11.refs_9_.refs_1_), channel_id=1, source_target_pairs={{0,2},{1,3},{2,0},{3,1},{4,6},{5,7},{6,4},{7,5},{8,10},{9,11},{10,... | collective-permute-start | bytes 786440 | tf_op jit(solution)/shard_map/ppermute | solution.py:254
  106.4 12.7 %collective-permute-start.47 = (bf16[128,1024]{1,0:T(8,128)(2,1)S(1)}, bf16[128,1024]{1,0:T(8,128)(2,1)S(1)}, u32[]{:S(2)}, u32[]{:S(2)}) collective-permute-start(bf16[128,1024]{1,0:T(8,128)(2,1)S(1)} %project_out.11.refs_9_.refs_1_), channel_id=1, source_target_pairs={{0,3},{1,2},{2,1},{3,0},{4,7},{5,6},{6,5},{7,4},{8,11},{9,10},{10,... | collective-permute-start | bytes 786440 | tf_op jit(solution)/shard_map/ppermute | solution.py:254
  111.0 9.8 %collective-permute-start.42 = (bf16[32,1664]{1,0:T(8,128)(2,1)S(1)}, bf16[32,1664]{1,0:T(8,128)(2,1)S(1)}, u32[]{:S(2)}, u32[]{:S(2)}) collective-permute-start(bf16[32,1664]{1,0:T(8,128)(2,1)S(1)} %get-tuple-element.119), channel_id=1, source_target_pairs={{0,8},{8,0},{16,24},{24,16},{1,9},{9,1},{17,25},{25,17},{2,10},{10... | collective-permute-start | bytes 319496 | tf_op jit(solution)/shard_map/ppermute | solution.py:254
  111.5 11.9 %collective-permute-start.43 = (bf16[32,1664]{1,0:T(8,128)(2,1)S(1)}, bf16[32,1664]{1,0:T(8,128)(2,1)S(1)}, u32[]{:S(2)}, u32[]{:S(2)}) collective-permute-start(bf16[32,1664]{1,0:T(8,128)(2,1)S(1)} %get-tuple-element.120), channel_id=1, source_target_pairs={{0,16},{8,24},{16,0},{24,8},{1,17},{9,25},{17,1},{25,9},{2,18},{10... | collective-permute-start | bytes 319496 | tf_op jit(solution)/shard_map/ppermute | solution.py:254
  112.5 10.9 %collective-permute-start.44 = (bf16[32,1664]{1,0:T(8,128)(2,1)S(1)}, bf16[32,1664]{1,0:T(8,128)(2,1)S(1)}, u32[]{:S(2)}, u32[]{:S(2)}) collective-permute-start(bf16[32,1664]{1,0:T(8,128)(2,1)S(1)} %get-tuple-element.121), channel_id=1, source_target_pairs={{0,24},{8,16},{16,8},{24,0},{1,25},{9,17},{17,9},{25,1},{2,26},{10... | collective-permute-start | bytes 319496 | tf_op jit(solution)/shard_map/ppermute | solution.py:254
  120.8 7.2 %collective-permute-start.52 = (bf16[32,1664]{1,0:T(8,128)(2,1)S(1)}, bf16[32,1664]{1,0:T(8,128)(2,1)S(1)}, u32[]{:S(2)}, u32[]{:S(2)}) collective-permute-start(bf16[32,1664]{1,0:T(8,128)(2,1)S(1)} %get-tuple-element.126), channel_id=1, source_target_pairs={{0,16},{8,24},{16,0},{24,8},{1,17},{9,25},{17,1},{25,9},{2,18},{10... | collective-permute-start | bytes 319496 | tf_op jit(solution)/shard_map/ppermute | solution.py:254
  120.8 7.2 %collective-permute-start.53 = (bf16[32,1664]{1,0:T(8,128)(2,1)S(1)}, bf16[32,1664]{1,0:T(8,128)(2,1)S(1)}, u32[]{:S(2)}, u32[]{:S(2)}) collective-permute-start(bf16[32,1664]{1,0:T(8,128)(2,1)S(1)} %get-tuple-element.127), channel_id=1, source_target_pairs={{0,24},{8,16},{16,8},{24,0},{1,25},{9,17},{17,9},{25,1},{2,26},{10... | collective-permute-start | bytes 319496 | tf_op jit(solution)/shard_map/ppermute | solution.py:254
  124.4 10.9 %collective-permute-start.48 = (bf16[32,1024]{1,0:T(8,128)(2,1)S(1)}, bf16[32,1024]{1,0:T(8,128)(2,1)S(1)}, u32[]{:S(2)}, u32[]{:S(2)}) collective-permute-start(bf16[32,1024]{1,0:T(8,128)(2,1)S(1)} %get-tuple-element.123.refs_0_), channel_id=1, source_target_pairs={{0,8},{8,0},{16,24},{24,16},{1,9},{9,1},{17,25},{25,17},{2,10},{10... | collective-permute-start | bytes 196616 | tf_op jit(solution)/shard_map/ppermute | solution.py:254
  124.5 12.9 %collective-permute-start.49 = (bf16[32,1024]{1,0:T(8,128)(2,1)S(1)}, bf16[32,1024]{1,0:T(8,128)(2,1)S(1)}, u32[]{:S(2)}, u32[]{:S(2)}) collective-permute-start(bf16[32,1024]{1,0:T(8,128)(2,1)S(1)} %get-tuple-element.123.refs_0_), channel_id=1, source_target_pairs={{0,16},{8,24},{16,0},{24,8},{1,17},{9,25},{17,1},{25,9},{2,18},{10... | collective-permute-start | bytes 196616 | tf_op jit(solution)/shard_map/ppermute | solution.py:254
  125.4 12.0 %collective-permute-start.50 = (bf16[32,1024]{1,0:T(8,128)(2,1)S(1)}, bf16[32,1024]{1,0:T(8,128)(2,1)S(1)}, u32[]{:S(2)}, u32[]{:S(2)}) collective-permute-start(bf16[32,1024]{1,0:T(8,128)(2,1)S(1)} %get-tuple-element.123.refs_0_), channel_id=1, source_target_pairs={{0,24},{8,16},{16,8},{24,0},{1,25},{9,17},{17,9},{25,1},{2,26},{10... | collective-permute-start | bytes 196616 | tf_op jit(solution)/shard_map/ppermute | solution.py:254
  129.2 11.3 %collective-permute-start.57 = (bf16[32,1024]{1,0:T(8,128)(2,1)S(1)}, bf16[32,1024]{1,0:T(8,128)(2,1)S(1)}, u32[]{:S(2)}, u32[]{:S(2)}) collective-permute-start(bf16[32,1024]{1,0:T(8,128)(2,1)S(1)} %get-tuple-element.131.refs_0_), channel_id=1, source_target_pairs={{0,8},{8,0},{16,24},{24,16},{1,9},{9,1},{17,25},{25,17},{2,10},{10... | collective-permute-start | bytes 196616 | tf_op jit(solution)/shard_map/ppermute | solution.py:254
  137.9 6.7 %collective-permute-start.54 = (bf16[128,1024]{1,0:T(8,128)(2,1)S(1)}, bf16[128,1024]{1,0:T(8,128)(2,1)S(1)}, u32[]{:S(2)}, u32[]{:S(2)}) collective-permute-start(bf16[128,1024]{1,0:T(8,128)(2,1)S(1)} %project_out.12.refs_5_.refs_1_), channel_id=1, source_target_pairs={{0,1},{1,0},{2,3},{3,2},{4,5},{5,4},{6,7},{7,6},{8,9},{9,8},{10,11... | collective-permute-start | bytes 786440 | tf_op jit(solution)/shard_map/ppermute | solution.py:254
  140.5 8.0 %collective-permute-start.55 = (bf16[128,1024]{1,0:T(8,128)(2,1)S(1)}, bf16[128,1024]{1,0:T(8,128)(2,1)S(1)}, u32[]{:S(2)}, u32[]{:S(2)}) collective-permute-start(bf16[128,1024]{1,0:T(8,128)(2,1)S(1)} %project_out.12.refs_5_.refs_1_), channel_id=1, source_target_pairs={{0,2},{1,3},{2,0},{3,1},{4,6},{5,7},{6,4},{7,5},{8,10},{9,11},{10,... | collective-permute-start | bytes 786440 | tf_op jit(solution)/shard_map/ppermute | solution.py:254
  140.5 8.0 %collective-permute-start.56 = (bf16[128,1024]{1,0:T(8,128)(2,1)S(1)}, bf16[128,1024]{1,0:T(8,128)(2,1)S(1)}, u32[]{:S(2)}, u32[]{:S(2)}) collective-permute-start(bf16[128,1024]{1,0:T(8,128)(2,1)S(1)} %project_out.12.refs_5_.refs_1_), channel_id=1, source_target_pairs={{0,3},{1,2},{2,1},{3,0},{4,7},{5,6},{6,5},{7,4},{8,11},{9,10},{10,... | collective-permute-start | bytes 786440 | tf_op jit(solution)/shard_map/ppermute | solution.py:254
  142.3 8.5 %collective-permute-start.63 = (bf16[128,1024]{1,0:T(8,128)(2,1)S(1)}, bf16[128,1024]{1,0:T(8,128)(2,1)S(1)}, u32[]{:S(2)}, u32[]{:S(2)}) collective-permute-start(bf16[128,1024]{1,0:T(8,128)(2,1)S(1)} %project_out.13.refs_9_.refs_1_), channel_id=1, source_target_pairs={{0,1},{1,0},{2,3},{3,2},{4,5},{5,4},{6,7},{7,6},{8,9},{9,8},{10,11... | collective-permute-start | bytes 786440 | tf_op jit(solution)/shard_map/ppermute | solution.py:254
  144.4 11.1 %collective-permute-start.64 = (bf16[128,1024]{1,0:T(8,128)(2,1)S(1)}, bf16[128,1024]{1,0:T(8,128)(2,1)S(1)}, u32[]{:S(2)}, u32[]{:S(2)}) collective-permute-start(bf16[128,1024]{1,0:T(8,128)(2,1)S(1)} %project_out.13.refs_9_.refs_1_), channel_id=1, source_target_pairs={{0,2},{1,3},{2,0},{3,1},{4,6},{5,7},{6,4},{7,5},{8,10},{9,11},{10,... | collective-permute-start | bytes 786440 | tf_op jit(solution)/shard_map/ppermute | solution.py:254
  144.6 11.0 %collective-permute-start.65 = (bf16[128,1024]{1,0:T(8,128)(2,1)S(1)}, bf16[128,1024]{1,0:T(8,128)(2,1)S(1)}, u32[]{:S(2)}, u32[]{:S(2)}) collective-permute-start(bf16[128,1024]{1,0:T(8,128)(2,1)S(1)} %project_out.13.refs_9_.refs_1_), channel_id=1, source_target_pairs={{0,3},{1,2},{2,1},{3,0},{4,7},{5,6},{6,5},{7,4},{8,11},{9,10},{10,... | collective-permute-start | bytes 786440 | tf_op jit(solution)/shard_map/ppermute | solution.py:254
  149.3 8.3 %collective-permute-start.60 = (bf16[32,1664]{1,0:T(8,128)(2,1)S(1)}, bf16[32,1664]{1,0:T(8,128)(2,1)S(1)}, u32[]{:S(2)}, u32[]{:S(2)}) collective-permute-start(bf16[32,1664]{1,0:T(8,128)(2,1)S(1)} %get-tuple-element.134), channel_id=1, source_target_pairs={{0,8},{8,0},{16,24},{24,16},{1,9},{9,1},{17,25},{25,17},{2,10},{10... | collective-permute-start | bytes 319496 | tf_op jit(solution)/shard_map/ppermute | solution.py:254
  150.2 9.7 %collective-permute-start.61 = (bf16[32,1664]{1,0:T(8,128)(2,1)S(1)}, bf16[32,1664]{1,0:T(8,128)(2,1)S(1)}, u32[]{:S(2)}, u32[]{:S(2)}) collective-permute-start(bf16[32,1664]{1,0:T(8,128)(2,1)S(1)} %get-tuple-element.135), channel_id=1, source_target_pairs={{0,16},{8,24},{16,0},{24,8},{1,17},{9,25},{17,1},{25,9},{2,18},{10... | collective-permute-start | bytes 319496 | tf_op jit(solution)/shard_map/ppermute | solution.py:254
  150.8 9.1 %collective-permute-start.62 = (bf16[32,1664]{1,0:T(8,128)(2,1)S(1)}, bf16[32,1664]{1,0:T(8,128)(2,1)S(1)}, u32[]{:S(2)}, u32[]{:S(2)}) collective-permute-start(bf16[32,1664]{1,0:T(8,128)(2,1)S(1)} %get-tuple-element.136), channel_id=1, source_target_pairs={{0,24},{8,16},{16,8},{24,0},{1,25},{9,17},{17,9},{25,1},{2,26},{10... | collective-permute-start | bytes 319496 | tf_op jit(solution)/shard_map/ppermute | solution.py:254
  156.4 8.3 %collective-permute-start.70 = (bf16[32,1664]{1,0:T(8,128)(2,1)S(1)}, bf16[32,1664]{1,0:T(8,128)(2,1)S(1)}, u32[]{:S(2)}, u32[]{:S(2)}) collective-permute-start(bf16[32,1664]{1,0:T(8,128)(2,1)S(1)} %get-tuple-element.141), channel_id=1, source_target_pairs={{0,16},{8,24},{16,0},{24,8},{1,17},{9,25},{17,1},{25,9},{2,18},{10... | collective-permute-start | bytes 319496 | tf_op jit(solution)/shard_map/ppermute | solution.py:254
  157.5 7.1 %collective-permute-start.71 = (bf16[32,1664]{1,0:T(8,128)(2,1)S(1)}, bf16[32,1664]{1,0:T(8,128)(2,1)S(1)}, u32[]{:S(2)}, u32[]{:S(2)}) collective-permute-start(bf16[32,1664]{1,0:T(8,128)(2,1)S(1)} %get-tuple-element.142), channel_id=1, source_target_pairs={{0,24},{8,16},{16,8},{24,0},{1,25},{9,17},{17,9},{25,1},{2,26},{10... | collective-permute-start | bytes 319496 | tf_op jit(solution)/shard_map/ppermute | solution.py:254
  161.1 8.3 %collective-permute-start.67 = (bf16[32,1024]{1,0:T(8,128)(2,1)S(1)}, bf16[32,1024]{1,0:T(8,128)(2,1)S(1)}, u32[]{:S(2)}, u32[]{:S(2)}) collective-permute-start(bf16[32,1024]{1,0:T(8,128)(2,1)S(1)} %get-tuple-element.138.refs_1_), channel_id=1, source_target_pairs={{0,16},{8,24},{16,0},{24,8},{1,17},{9,25},{17,1},{25,9},{2,18},{10... | collective-permute-start | bytes 196616 | tf_op jit(solution)/shard_map/ppermute | solution.py:254
  162.3 7.1 %collective-permute-start.68 = (bf16[32,1024]{1,0:T(8,128)(2,1)S(1)}, bf16[32,1024]{1,0:T(8,128)(2,1)S(1)}, u32[]{:S(2)}, u32[]{:S(2)}) collective-permute-start(bf16[32,1024]{1,0:T(8,128)(2,1)S(1)} %get-tuple-element.138.refs_1_), channel_id=1, source_target_pairs={{0,24},{8,16},{16,8},{24,0},{1,25},{9,17},{17,9},{25,1},{2,26},{10... | collective-permute-start | bytes 196616 | tf_op jit(solution)/shard_map/ppermute | solution.py:254
  165.8 7.1 %collective-permute-start.76 = (bf16[32,1024]{1,0:T(8,128)(2,1)S(1)}, bf16[32,1024]{1,0:T(8,128)(2,1)S(1)}, u32[]{:S(2)}, u32[]{:S(2)}) collective-permute-start(bf16[32,1024]{1,0:T(8,128)(2,1)S(1)} %get-tuple-element.150.refs_1_), channel_id=1, source_target_pairs={{0,8},{8,0},{16,24},{24,16},{1,9},{9,1},{17,25},{25,17},{2,10},{10... | collective-permute-start | bytes 196616 | tf_op jit(solution)/shard_map/ppermute | solution.py:254
  166.1 9.2 %collective-permute-start.77 = (bf16[32,1024]{1,0:T(8,128)(2,1)S(1)}, bf16[32,1024]{1,0:T(8,128)(2,1)S(1)}, u32[]{:S(2)}, u32[]{:S(2)}) collective-permute-start(bf16[32,1024]{1,0:T(8,128)(2,1)S(1)} %get-tuple-element.150.refs_1_), channel_id=1, source_target_pairs={{0,16},{8,24},{16,0},{24,8},{1,17},{9,25},{17,1},{25,9},{2,18},{10... | collective-permute-start | bytes 196616 | tf_op jit(solution)/shard_map/ppermute | solution.py:254
  167.0 8.3 %collective-permute-start.78 = (bf16[32,1024]{1,0:T(8,128)(2,1)S(1)}, bf16[32,1024]{1,0:T(8,128)(2,1)S(1)}, u32[]{:S(2)}, u32[]{:S(2)}) collective-permute-start(bf16[32,1024]{1,0:T(8,128)(2,1)S(1)} %get-tuple-element.150.refs_1_), channel_id=1, source_target_pairs={{0,24},{8,16},{16,8},{24,0},{1,25},{9,17},{17,9},{25,1},{2,26},{10... | collective-permute-start | bytes 196616 | tf_op jit(solution)/shard_map/ppermute | solution.py:254
  170.4 7.8 %collective-permute-start.72 = (bf16[32,1024]{1,0:T(8,128)(2,1)S(1)}, bf16[32,1024]{1,0:T(8,128)(2,1)S(1)}, u32[]{:S(2)}, u32[]{:S(2)}) collective-permute-start(bf16[32,1024]{1,0:T(8,128)(2,1)S(1)} %get-tuple-element.147), channel_id=1, source_target_pairs={{0,1},{1,0},{2,3},{3,2},{4,5},{5,4},{6,7},{7,6},{8,9},{9,8},{10,11... | collective-permute-start | bytes 196616 | tf_op jit(solution)/shard_map/ppermute | solution.py:254
  170.6 8.4 %collective-permute-start.73 = (bf16[32,1024]{1,0:T(8,128)(2,1)S(1)}, bf16[32,1024]{1,0:T(8,128)(2,1)S(1)}, u32[]{:S(2)}, u32[]{:S(2)}) collective-permute-start(bf16[32,1024]{1,0:T(8,128)(2,1)S(1)} %get-tuple-element.148), channel_id=1, source_target_pairs={{0,2},{1,3},{2,0},{3,1},{4,6},{5,7},{6,4},{7,5},{8,10},{9,11},{10,... | collective-permute-start | bytes 196616 | tf_op jit(solution)/shard_map/ppermute | solution.py:254
  179.1 9.0 %collective-permute-start.75 = (bf16[32,1024]{1,0:T(8,128)(2,1)S(1)}, bf16[32,1024]{1,0:T(8,128)(2,1)S(1)}, u32[]{:S(2)}, u32[]{:S(2)}) collective-permute-start(bf16[32,1024]{1,0:T(8,128)(2,1)S(1)} %add_convert_fusion.1), channel_id=1, source_target_pairs={{0,0},{1,8},{2,16},{3,24},{8,1},{9,9},{10,17},{11,25},{16,2},{17,1... | collective-permute-start | bytes 196616 | tf_op jit(solution)/shard_map/ppermute | solution.py:381
  182.4 8.8 %collective-permute-start.82 = (bf16[32,1024]{1,0:T(8,128)(2,1)S(1)}, bf16[32,1024]{1,0:T(8,128)(2,1)S(1)}, u32[]{:S(2)}, u32[]{:S(2)}) collective-permute-start(bf16[32,1024]{1,0:T(8,128)(2,1)S(1)} %add_convert_fusion), channel_id=1, source_target_pairs={{0,0},{1,8},{2,16},{3,24},{8,1},{9,9},{10,17},{11,25},{16,2},{17,1... | collective-permute-start | bytes 196616 | tf_op jit(solution)/shard_map/ppermute | solution.py:381
  191.3 20.8 %collective-permute-start.83 = (bf16[1,32,1024]{2,1,0:T(8,128)(2,1)S(1)}, bf16[1,32,1024]{2,1,0:T(8,128)(2,1)S(1)}, u32[]{:S(2)}, u32[]{:S(2)}) collective-permute-start(bf16[1,32,1024]{2,1,0:T(8,128)(2,1)S(1)} %select_bitcast_fusion.16), channel_id=1, source_target_pairs={{0,4},{4,0},{1,5},{5,1},{2,6},{6,2},{3,7},{7,3},{8,12},{12,8},{9,1... | collective-permute-start | bytes 196616 | tf_op jit(solution)/shard_map/ppermute | solution.py:254
  (38 other events, 234.0 us)

commit v3 on v2

--- a/solution.py
+++ b/solution.py
@@ -11,7 +11,8 @@
 LANES = 128
 ROPE_THETA = 500000.0
 NORM_EPSILON = 1e-05
-VMEM_BYTES = 16 * 1024 * 1024
+VMEM_BYTES = 8 * 1024 * 1024
+STEP_FLOPS = 5_500_000_000
 
 
 def unread(count, at, kernel):
@@ -81,7 +82,7 @@
         out_specs=in_vmem(1 + n_out),
         scratch_shapes=[pltpu.VMEM((total, depth), jnp.bfloat16)],
         compiler_params=pltpu.CompilerParams(vmem_limit_bytes=VMEM_BYTES),
-        cost_estimate=pl.CostEstimate(flops=5499999999, bytes_accessed=1000, transcendentals=0),
+        cost_estimate=pl.CostEstimate(flops=STEP_FLOPS, bytes_accessed=1000, transcendentals=0),
         name="project_qkv",
     )(head, *arrays, gain, wq, wk, wv, *after)
     return stream, sums
@@ -152,7 +153,7 @@
         in_specs=in_vmem(len(blocks) + 2 * len(before) + 3 + len(after)),
         out_specs=in_vmem(3),
         compiler_params=pltpu.CompilerParams(vmem_limit_bytes=VMEM_BYTES),
-        cost_estimate=pl.CostEstimate(flops=5499999999, bytes_accessed=1000, transcendentals=0),
+        cost_estimate=pl.CostEstimate(flops=STEP_FLOPS, bytes_accessed=1000, transcendentals=0),
         name="attend",
     )(*blocks, *[array for pair in before for array in pair], cosine, sine, mask, *after)
 
@@ -188,7 +189,7 @@
         out_specs=in_vmem(n_out),
         scratch_shapes=[pltpu.VMEM((total, depth), jnp.bfloat16)],
         compiler_params=pltpu.CompilerParams(vmem_limit_bytes=VMEM_BYTES),
-        cost_estimate=pl.CostEstimate(flops=5499999999, bytes_accessed=1000, transcendentals=0),
+        cost_estimate=pl.CostEstimate(flops=STEP_FLOPS, bytes_accessed=1000, transcendentals=0),
         name="project_out",
     )(*([place] if placed else []), *blocks, weight, *after)
 
@@ -208,6 +209,7 @@
         out_shape=jax.ShapeDtypeStruct((parts, slots, seq // parts, width), tokens.dtype),
         in_specs=[smem, smem, pl.BlockSpec(memory_space=pl.ANY)],
         out_specs=pl.BlockSpec(memory_space=pltpu.VMEM),
+        compiler_params=pltpu.CompilerParams(vmem_limit_bytes=VMEM_BYTES),
         name="pick_samples",
     )(order, spot, tokens)
 
@@ -244,6 +246,7 @@
         ],
         in_specs=[smem] * 5 + in_vmem(2),
         out_specs=in_vmem(2),
+        compiler_params=pltpu.CompilerParams(vmem_limit_bytes=VMEM_BYTES),
         name="layout",
     )(spot, order, boundary, skip_offset, doc_lengths, frequency, after)
     sign = jnp.where(jnp.arange(HEAD_DIM) < half_dim, -1.0, 1.0).astype(jnp.float32)
@@ -267,6 +270,15 @@
     for block in blocks[1:]:
         value = value + block.astype(jnp.float32)
     return value
+
+
+def steps_of(parts, layers):
+    if parts == 1:
+        return [(step, 0, number) for number in range(layers) for step in range(3)]
+    steps = [(0, 0, 0), (1, 0, 0), (0, 1, 0), (2, 0, 0), (1, 1, 0)]
+    for number in range(1, layers):
+        steps += [(0, 0, number), (2, 1, number - 1), (1, 0, number), (0, 1, number), (2, 0, number), (1, 1, number)]
+    return steps + [(2, 1, layers - 1)]
 
 
 def per_device(
@@ -327,50 +339,61 @@
     part_rows = slots * part_len
     total = replicas * part_rows
 
+    layers = [(0, s) for s in range(sections)] + [(1, s) for s in reversed(range(sections))]
+    weights = [layer_weights(*layer) for layer in layers]
+    streams, sums, mixed, shares = ([None] * parts for _ in range(4))
+    before = [[] for _ in layers]
     layout, latest = None, []
-    layers = [(0, s) for s in range(sections)] + [(1, s) for s in reversed(range(sections))]
-    streams, shares = [None] * parts, [None] * parts
-    for number, (index, section) in enumerate(layers):
-        gain, wq, wk, wv, wo = layer_weights(index, section)
+
+    def share_out(h, number):
+        nonlocal layout, latest
+        gain, wq, wk, wv, _ = weights[number]
+        head, arrays, part = (streams[h], shares[h], None) if number else (place, blocks, h)
+        streams[h], ends = project_qkv(
+            head, arrays, part, total, gain[None], wq, wk, wv, replicas if paired else 1, latest
+        )
+        latest = [streams[h]]
+        if layout is None:
+            layout = layout_of(batch_order, boundary, skip_offset, doc_lengths, spot, slots, seq_len, ends[0])
+        if paired:
+            sums[h] = trade_blocks(ends, "dp")
+        else:
+            pieces = ends[0].reshape(replicas, part_rows, ends[0].shape[1])
+            pieces = lax.all_to_all(pieces, "dp", split_axis=0, concat_axis=0)
+            sums[h] = [jnp.sum(pieces.astype(jnp.float32), axis=0)]
+
+    def mix(h, number):
+        nonlocal latest
+        rows_out, keys, values = attend(
+            sums[h], before[number], *layout, q_heads, kv_heads, model_width, latest
+        )
+        latest = [keys]
+        before[number].append((keys, values))
+        if paired:
+            mixed[h] = gather_blocks(rows_out, "dp", replicas)
+        else:
+            mixed[h] = [lax.all_gather(rows_out, "dp", axis=0, tiled=True)]
+
+    def bring_in(h, number):
+        nonlocal latest
         last = number + 1 == len(layers)
-        before, sums, mixed = [], [None] * parts, [None] * parts
-        for h in range(parts):
-            head, arrays, part = (streams[h], shares[h], None) if number else (place, blocks, h)
-            streams[h], sums[h] = project_qkv(
-                head, arrays, part, total, gain[None], wq, wk, wv, replicas if paired else 1, latest
-            )
-            latest = [streams[h]]
-            if layout is None:
-                layout = layout_of(
-                    batch_order, boundary, skip_offset, doc_lengths, spot, slots, seq_len, sums[0][0]
-                )
-            if paired:
-                sums[h] = trade_blocks(sums[h], "dp")
-            else:
-                pieces = sums[h][0].reshape(replicas, part_rows, sums[h][0].shape[1])
-                pieces = lax.all_to_all(pieces, "dp", split_axis=0, concat_axis=0)
-                sums[h] = [jnp.sum(pieces.astype(jnp.float32), axis=0)]
-        for h in range(parts):
-            mixed[h], keys, values = attend(
-                sums[h], before, *layout, q_heads, kv_heads, model_width, latest
-            )
-            latest = [keys]
-            before.append((keys, values))
-            if paired:
-                mixed[h] = gather_blocks(mixed[h], "dp", replicas)
-            else:
-                mixed[h] = [lax.all_gather(mixed[h], "dp", axis=0, tiled=True)]
-        for h in range(parts):
-            ends = project_out(
-                mixed[h], place if paired and last else None, wo, groups if paired and last else 1, latest
-            )
-            latest = ends[:1]
-            if not paired:
-                shares[h] = [lax.psum(ends[0].astype(jnp.float32), "tensor")]
-            elif last:
-                shares[h] = trade_blocks(ends, "tensor")
-            else:
-                shares[h] = gather_blocks(ends[0], "tensor", groups)
+        ends = project_out(
+            mixed[h],
+            place if paired and last else None,
+            weights[number][4],
+            groups if paired and last else 1,
+            latest,
+        )
+        latest = ends[:1]
+        if not paired:
+            shares[h] = [lax.psum(ends[0].astype(jnp.float32), "tensor")]
+        elif last:
+            shares[h] = trade_blocks(ends, "tensor")
+        else:
+            shares[h] = gather_blocks(ends[0], "tensor", groups)
+
+    for step, h, number in steps_of(parts, len(layers)):
+        (share_out, mix, bring_in)[step](h, number)
 
     final = []
     for stream, share in zip(streams, shares):

time: 213 us -> 202 us (0.948)
  Pallas kernels: 26.8 us -> 21 us
  starting transfers between devices: 133 us -> 129 us
  other arithmetic: 13.6 us -> 9.89 us
  waiting for transfers between devices: 36.1 us -> 38.5 us
    ppermute x81, starting transfers between devices: 119 us -> 115 us  [swapped(): lax.ppermute(value, axis, [(i, i ^ by) for i in range(lax.axis_size(axis))])]
    select_n x5, other arithmetic: 12 us -> 8.88 us  [layer_weights(): jnp.where(my_section == section, mine[index, 0], theirs[index, 0])]
    pallas_call x1, Pallas kernels: 3 us -> 0.73 us  [pick_samples(): pl.pallas_call(partial(pick_kernel, parts, slots), out_shape=jax.ShapeDty...]
  transfers between devices with their start and end apart: 84 -> 84, of which waited for: 20 -> 17; matrix products, arithmetic and copies ran while one was open for 6% -> 5% of each run, Pallas kernels for 13% -> 9%
where the time goes in v3:
time: 202 us
  starting transfers between devices  129 us (64%)
  waiting for transfers between devices  38.5 us (19%)
  Pallas kernels  21 us (10%)
  other arithmetic  9.89 us (5%)
  local copies, waits for them, and re-layouts  2.35 us (1%)
    ppermute x81, starting transfers between devices, swapped(): lax.ppermute(value, axis, [(i, i ^ by) for i in range(lax.axis_size(axis))])  115 us
    ppermute x81, waiting for transfers between devices, swapped(): lax.ppermute(value, axis, [(i, i ^ by) for i in range(lax.axis_size(axis))])  29.5 us
    ppermute x2, starting transfers between devices, per_device(): stream = lax.ppermute(stream, ('dp', 'tensor'), turn)  8.88 us
    select_n x5, other arithmetic, layer_weights(): jnp.where(my_section == section, mine[index, 0], theirs[index, 0])  8.88 us
    pallas_call x8, Pallas kernels, attend(): pl.pallas_call(unread(len(after), len(blocks) + 2 * len(before) + 3, part...  8.58 us
    pallas_call x8, Pallas kernels, project_qkv(): pl.pallas_call(unread(len(after), len(arrays) + 5, partial(qkv_kernel, le...  6.4 us
    ppermute x1, starting transfers between devices, per_device(): lax.ppermute(stream, ('dp', 'tensor'), turn)  5.14 us
    pallas_call x8, Pallas kernels, project_out(): pl.pallas_call(unread(len(after), placed + n_in + 1, partial(out_kernel,...  4.67 us
  transfers between devices with their start and end apart: 84, of which 17 were waited for; matrix products, arithmetic and copies ran while one was open for 5% of the time, Pallas kernels for 9%

profile of v3, /device:TPU:7, one launch (start us, length us, event | category | flops | bytes accessed | tf_op | source)
XLA Modules:
  0.0 201.6 jit_solution(110627332560994911)
XLA Ops:
  5.6 5.1 %collective-permute-start = (bf16[64,1024]{1,0:T(8,128)(2,1)S(1)}, bf16[64,1024]{1,0:T(8,128)(2,1)S(1)}, u32[]{:S(2)}, u32[]{:S(2)}) collective-permute-start(bf16[64,1024]{1,0:T(8,128)(2,1)S(1)} %bitcast.51), channel_id=1, source_target_pairs={{0,0},{1,8},{2,16},{3,24},{8,1},{9,9},{10,17},{11,25},{16,2},{17,1... | collective-permute-start | bytes 393224 | tf_op jit(solution)/shard_map/ppermute | solution.py:334
  11.6 4.3 %collective-permute-done.refs_1_ = bf16[64,1024]{1,0:T(8,128)(2,1)S(1)} collective-permute-done((bf16[64,1024]{1,0:T(8,128)(2,1)S(1)}, bf16[64,1024]{1,0:T(8,128)(2,1)S(1)}, u32[]{:S(2)}, u32[]{:S(2)}) %collective-permute-start) | collective-permute-done | bytes 131104 | tf_op jit(solution)/shard_map/ppermute | solution.py:334
  15.8 1.3 collective-permute-start.1
  17.2 1.7 collective-permute-start.2
  18.9 1.7 select_bitcast_fusion.9
  20.6 1.2 collective-permute-start.3
  21.9 1.4 select_bitcast_fusion.8
  23.3 2.5 %select_bitcast_fusion.1 = (bf16[1024,1024]{1,0:T(8,128)(2,1)S(1)}, bf16[1024,1024]{1,0:T(8,128)(2,1)S(1)}, bf16[1024,1024]{1,0:T(8,128)(2,1)S(1)}, bf16[1024,1024]{1,0:T(8,128)(2,1)S(1)}) fusion(pred[]{:T(512)S(6)} %eq.4, bf16[2,1,1024,1024]{3,2,1,0:T(8,128)(2,1)} %collective-permute-done.5, bf16[2,1,1024,1024]{3,2,1,0:T(8,128)(2,1)S(1)} %copy-done.6, pred[]{:T(512)S(6)} %eq.5), kind=kLoop, calls=%fused_computation.1 | loop fusion | flops 4194304 | bytes 16777218 | tf_op jit(solution)/shard_map/jit(_where)/select_n | solution.py:322
  25.9 1.1 project_qkv.8
  27.1 3.6 %collective-permute-start.9 = (bf16[32,1664]{1,0:T(8,128)(2,1)S(1)}, bf16[32,1664]{1,0:T(8,128)(2,1)S(1)}, u32[]{:S(2)}, u32[]{:S(2)}) collective-permute-start(bf16[32,1664]{1,0:T(8,128)(2,1)S(1)} %get-tuple-element.87), channel_id=1, source_target_pairs={{0,16},{8,24},{16,0},{24,8},{1,17},{9,25},{17,1},{25,9},{2,18},{10... | collective-permute-start | bytes 319496 | tf_op jit(solution)/shard_map/ppermute | solution.py:257
  31.4 2.7 %select_bitcast_fusion = (bf16[1024,1024]{1,0:T(8,128)(2,1)S(1)}, bf16[1024,1024]{1,0:T(8,128)(2,1)S(1)}, bf16[1024,1024]{1,0:T(8,128)(2,1)S(1)}, bf16[1024,1024]{1,0:T(8,128)(2,1)S(1)}) fusion(pred[]{:T(512)S(6)} %eq.4, bf16[2,1,1024,1024]{3,2,1,0:T(8,128)(2,1)} %collective-permute-done.14, bf16[2,1,1024,1024]{3,2,1,0:T(8,128)(2,1)S(1)} %copy-done.7, pred[]{:T(512)S(6)} %eq.5), kind=kLoop, calls=%fused_computation | loop fusion | flops 4194304 | bytes 16777218 | tf_op jit(solution)/shard_map/jit(_where)/select_n | solution.py:322
  34.2 3.1 %collective-permute-done.10.refs_3_ = bf16[32,1664]{1,0:T(8,128)(2,1)S(1)} collective-permute-done((bf16[32,1664]{1,0:T(8,128)(2,1)S(1)}, bf16[32,1664]{1,0:T(8,128)(2,1)S(1)}, u32[]{:S(2)}, u32[]{:S(2)}) %collective-permute-start.10) | collective-permute-done | bytes 106528 | tf_op jit(solution)/shard_map/ppermute | solution.py:257
  38.3 2.0 collective-permute-start.11
  40.3 1.7 collective-permute-start.12
  44.6 2.2 %collective-permute-start.19 = (bf16[32,1664]{1,0:T(8,128)(2,1)S(1)}, bf16[32,1664]{1,0:T(8,128)(2,1)S(1)}, u32[]{:S(2)}, u32[]{:S(2)}) collective-permute-start(bf16[32,1664]{1,0:T(8,128)(2,1)S(1)} %get-tuple-element.97), channel_id=1, source_target_pairs={{0,16},{8,24},{16,0},{24,8},{1,17},{9,25},{17,1},{25,9},{2,18},{10... | collective-permute-start | bytes 319496 | tf_op jit(solution)/shard_map/ppermute | solution.py:257
  48.3 1.4 collective-permute-start.15
  51.0 2.6 %collective-permute-done.19.refs_2_ = bf16[32,1664]{1,0:T(8,128)(2,1)S(1)} collective-permute-done((bf16[32,1664]{1,0:T(8,128)(2,1)S(1)}, bf16[32,1664]{1,0:T(8,128)(2,1)S(1)}, u32[]{:S(2)}, u32[]{:S(2)}) %collective-permute-start.19) | collective-permute-done | bytes 106528 | tf_op jit(solution)/shard_map/ppermute | solution.py:257
  53.8 1.2 attend.9
  54.9 4.9 %collective-permute-start.24 = (bf16[32,1024]{1,0:T(8,128)(2,1)S(1)}, bf16[32,1024]{1,0:T(8,128)(2,1)S(1)}, u32[]{:S(2)}, u32[]{:S(2)}) collective-permute-start(bf16[32,1024]{1,0:T(8,128)(2,1)S(1)} %get-tuple-element.106.refs_0_), channel_id=1, source_target_pairs={{0,8},{8,0},{16,24},{24,16},{1,9},{9,1},{17,25},{25,17},{2,10},{10... | collective-permute-start | bytes 196616 | tf_op jit(solution)/shard_map/ppermute | solution.py:257
  60.7 1.3 collective-permute-start.26
  63.3 1.7 collective-permute-start.22
  65.0 1.3 collective-permute-start.23
  66.8 1.6 collective-permute-start.30
  68.4 1.5 collective-permute-start.32
  69.9 2.8 %collective-permute-done.22.refs_2_ = bf16[32,1664]{1,0:T(8,128)(2,1)S(1)} collective-permute-done((bf16[32,1664]{1,0:T(8,128)(2,1)S(1)}, bf16[32,1664]{1,0:T(8,128)(2,1)S(1)}, u32[]{:S(2)}, u32[]{:S(2)}) %collective-permute-start.22) | collective-permute-done | bytes 106528 | tf_op jit(solution)/shard_map/ppermute | solution.py:257
  73.8 4.9 %collective-permute-start.27 = (bf16[32,1024]{1,0:T(8,128)(2,1)S(1)}, bf16[32,1024]{1,0:T(8,128)(2,1)S(1)}, u32[]{:S(2)}, u32[]{:S(2)}) collective-permute-start(bf16[32,1024]{1,0:T(8,128)(2,1)S(1)} %get-tuple-element.107.refs_0_), channel_id=1, source_target_pairs={{0,8},{8,0},{16,24},{24,16},{1,9},{9,1},{17,25},{25,17},{2,10},{10... | collective-permute-start | bytes 196616 | tf_op jit(solution)/shard_map/ppermute | solution.py:257
  78.7 2.2 %collective-permute-start.29 = (bf16[32,1024]{1,0:T(8,128)(2,1)S(1)}, bf16[32,1024]{1,0:T(8,128)(2,1)S(1)}, u32[]{:S(2)}, u32[]{:S(2)}) collective-permute-start(bf16[32,1024]{1,0:T(8,128)(2,1)S(1)} %get-tuple-element.107.refs_0_), channel_id=1, source_target_pairs={{0,24},{8,16},{16,8},{24,0},{1,25},{9,17},{17,9},{25,1},{2,26},{10... | collective-permute-start | bytes 196616 | tf_op jit(solution)/shard_map/ppermute | solution.py:257
  83.0 2.2 %collective-permute-start.38 = (bf16[32,1664]{1,0:T(8,128)(2,1)S(1)}, bf16[32,1664]{1,0:T(8,128)(2,1)S(1)}, u32[]{:S(2)}, u32[]{:S(2)}) collective-permute-start(bf16[32,1664]{1,0:T(8,128)(2,1)S(1)} %get-tuple-element.113), channel_id=1, source_target_pairs={{0,24},{8,16},{16,8},{24,0},{1,25},{9,17},{17,9},{25,1},{2,26},{10... | collective-permute-start | bytes 319496 | tf_op jit(solution)/shard_map/ppermute | solution.py:257
  85.6 1.4 collective-permute-start.33
  87.0 1.3 collective-permute-start.35
  88.3 3.1 %collective-permute-done.37.refs_2_ = bf16[32,1664]{1,0:T(8,128)(2,1)S(1)} collective-permute-done((bf16[32,1664]{1,0:T(8,128)(2,1)S(1)}, bf16[32,1664]{1,0:T(8,128)(2,1)S(1)}, u32[]{:S(2)}, u32[]{:S(2)}) %collective-permute-start.37) | collective-permute-done | bytes 106528 | tf_op jit(solution)/shard_map/ppermute | solution.py:257
  91.4 1.2 attend.11
  92.6 4.8 %collective-permute-start.42 = (bf16[32,1024]{1,0:T(8,128)(2,1)S(1)}, bf16[32,1024]{1,0:T(8,128)(2,1)S(1)}, u32[]{:S(2)}, u32[]{:S(2)}) collective-permute-start(bf16[32,1024]{1,0:T(8,128)(2,1)S(1)} %get-tuple-element.121.refs_0_), channel_id=1, source_target_pairs={{0,8},{8,0},{16,24},{24,16},{1,9},{9,1},{17,25},{25,17},{2,10},{10... | collective-permute-start | bytes 196616 | tf_op jit(solution)/shard_map/ppermute | solution.py:257
  97.4 2.1 %collective-permute-start.44 = (bf16[32,1024]{1,0:T(8,128)(2,1)S(1)}, bf16[32,1024]{1,0:T(8,128)(2,1)S(1)}, u32[]{:S(2)}, u32[]{:S(2)}) collective-permute-start(bf16[32,1024]{1,0:T(8,128)(2,1)S(1)} %get-tuple-element.121.refs_0_), channel_id=1, source_target_pairs={{0,24},{8,16},{16,8},{24,0},{1,25},{9,17},{17,9},{25,1},{2,26},{10... | collective-permute-start | bytes 196616 | tf_op jit(solution)/shard_map/ppermute | solution.py:257
  101.7 2.1 %collective-permute-start.41 = (bf16[32,1664]{1,0:T(8,128)(2,1)S(1)}, bf16[32,1664]{1,0:T(8,128)(2,1)S(1)}, u32[]{:S(2)}, u32[]{:S(2)}) collective-permute-start(bf16[32,1664]{1,0:T(8,128)(2,1)S(1)} %get-tuple-element.120), channel_id=1, source_target_pairs={{0,24},{8,16},{16,8},{24,0},{1,25},{9,17},{17,9},{25,1},{2,26},{10... | collective-permute-start | bytes 319496 | tf_op jit(solution)/shard_map/ppermute | solution.py:257
  104.3 1.4 collective-permute-start.48
  105.7 1.3 collective-permute-start.50
  107.0 3.1 %collective-permute-done.40.refs_2_ = bf16[32,1664]{1,0:T(8,128)(2,1)S(1)} collective-permute-done((bf16[32,1664]{1,0:T(8,128)(2,1)S(1)}, bf16[32,1664]{1,0:T(8,128)(2,1)S(1)}, u32[]{:S(2)}, u32[]{:S(2)}) %collective-permute-start.40) | collective-permute-done | bytes 106528 | tf_op jit(solution)/shard_map/ppermute | solution.py:257
  111.1 4.9 %collective-permute-start.45 = (bf16[32,1024]{1,0:T(8,128)(2,1)S(1)}, bf16[32,1024]{1,0:T(8,128)(2,1)S(1)}, u32[]{:S(2)}, u32[]{:S(2)}) collective-permute-start(bf16[32,1024]{1,0:T(8,128)(2,1)S(1)} %get-tuple-element.122.refs_0_), channel_id=1, source_target_pairs={{0,8},{8,0},{16,24},{24,16},{1,9},{9,1},{17,25},{25,17},{2,10},{10... | collective-permute-start | bytes 196616 | tf_op jit(solution)/shard_map/ppermute | solution.py:257
  116.0 2.2 %collective-permute-start.47 = (bf16[32,1024]{1,0:T(8,128)(2,1)S(1)}, bf16[32,1024]{1,0:T(8,128)(2,1)S(1)}, u32[]{:S(2)}, u32[]{:S(2)}) collective-permute-start(bf16[32,1024]{1,0:T(8,128)(2,1)S(1)} %get-tuple-element.122.refs_0_), channel_id=1, source_target_pairs={{0,24},{8,16},{16,8},{24,0},{1,25},{9,17},{17,9},{25,1},{2,26},{10... | collective-permute-start | bytes 196616 | tf_op jit(solution)/shard_map/ppermute | solution.py:257
  120.4 2.2 %collective-permute-start.56 = (bf16[32,1664]{1,0:T(8,128)(2,1)S(1)}, bf16[32,1664]{1,0:T(8,128)(2,1)S(1)}, u32[]{:S(2)}, u32[]{:S(2)}) collective-permute-start(bf16[32,1664]{1,0:T(8,128)(2,1)S(1)} %get-tuple-element.128), channel_id=1, source_target_pairs={{0,24},{8,16},{16,8},{24,0},{1,25},{9,17},{17,9},{25,1},{2,26},{10... | collective-permute-start | bytes 319496 | tf_op jit(solution)/shard_map/ppermute | solution.py:257
  123.0 1.3 collective-permute-start.51
  124.3 1.4 collective-permute-start.53
  125.7 3.2 %collective-permute-done.55.refs_2_ = bf16[32,1664]{1,0:T(8,128)(2,1)S(1)} collective-permute-done((bf16[32,1664]{1,0:T(8,128)(2,1)S(1)}, bf16[32,1664]{1,0:T(8,128)(2,1)S(1)}, u32[]{:S(2)}, u32[]{:S(2)}) %collective-permute-start.55) | collective-permute-done | bytes 106528 | tf_op jit(solution)/shard_map/ppermute | solution.py:257
  128.9 1.2 attend.13
  130.0 4.8 %collective-permute-start.60 = (bf16[32,1024]{1,0:T(8,128)(2,1)S(1)}, bf16[32,1024]{1,0:T(8,128)(2,1)S(1)}, u32[]{:S(2)}, u32[]{:S(2)}) collective-permute-start(bf16[32,1024]{1,0:T(8,128)(2,1)S(1)} %get-tuple-element.136.refs_0_), channel_id=1, source_target_pairs={{0,8},{8,0},{16,24},{24,16},{1,9},{9,1},{17,25},{25,17},{2,10},{10... | collective-permute-start | bytes 196616 | tf_op jit(solution)/shard_map/ppermute | solution.py:257
  134.9 2.1 %collective-permute-start.62 = (bf16[32,1024]{1,0:T(8,128)(2,1)S(1)}, bf16[32,1024]{1,0:T(8,128)(2,1)S(1)}, u32[]{:S(2)}, u32[]{:S(2)}) collective-permute-start(bf16[32,1024]{1,0:T(8,128)(2,1)S(1)} %get-tuple-element.136.refs_0_), channel_id=1, source_target_pairs={{0,24},{8,16},{16,8},{24,0},{1,25},{9,17},{17,9},{25,1},{2,26},{10... | collective-permute-start | bytes 196616 | tf_op jit(solution)/shard_map/ppermute | solution.py:257
  139.2 2.1 %collective-permute-start.59 = (bf16[32,1664]{1,0:T(8,128)(2,1)S(1)}, bf16[32,1664]{1,0:T(8,128)(2,1)S(1)}, u32[]{:S(2)}, u32[]{:S(2)}) collective-permute-start(bf16[32,1664]{1,0:T(8,128)(2,1)S(1)} %get-tuple-element.135), channel_id=1, source_target_pairs={{0,24},{8,16},{16,8},{24,0},{1,25},{9,17},{17,9},{25,1},{2,26},{10... | collective-permute-start | bytes 319496 | tf_op jit(solution)/shard_map/ppermute | solution.py:257
  141.7 1.2 collective-permute-start.66
  143.1 1.4 collective-permute-start.68
  144.5 3.1 %collective-permute-done.58.refs_2_ = bf16[32,1664]{1,0:T(8,128)(2,1)S(1)} collective-permute-done((bf16[32,1664]{1,0:T(8,128)(2,1)S(1)}, bf16[32,1664]{1,0:T(8,128)(2,1)S(1)}, u32[]{:S(2)}, u32[]{:S(2)}) %collective-permute-start.58) | collective-permute-done | bytes 106528 | tf_op jit(solution)/shard_map/ppermute | solution.py:257
  148.5 5.1 %collective-permute-start.63 = (bf16[32,1024]{1,0:T(8,128)(2,1)S(1)}, bf16[32,1024]{1,0:T(8,128)(2,1)S(1)}, u32[]{:S(2)}, u32[]{:S(2)}) collective-permute-start(bf16[32,1024]{1,0:T(8,128)(2,1)S(1)} %get-tuple-element.137.refs_1_), channel_id=1, source_target_pairs={{0,8},{8,0},{16,24},{24,16},{1,9},{9,1},{17,25},{25,17},{2,10},{10... | collective-permute-start | bytes 196616 | tf_op jit(solution)/shard_map/ppermute | solution.py:257
  153.7 2.2 %collective-permute-start.65 = (bf16[32,1024]{1,0:T(8,128)(2,1)S(1)}, bf16[32,1024]{1,0:T(8,128)(2,1)S(1)}, u32[]{:S(2)}, u32[]{:S(2)}) collective-permute-start(bf16[32,1024]{1,0:T(8,128)(2,1)S(1)} %get-tuple-element.137.refs_1_), channel_id=1, source_target_pairs={{0,24},{8,16},{16,8},{24,0},{1,25},{9,17},{17,9},{25,1},{2,26},{10... | collective-permute-start | bytes 196616 | tf_op jit(solution)/shard_map/ppermute | solution.py:257
  158.0 2.2 %collective-permute-start.75 = (bf16[32,1664]{1,0:T(8,128)(2,1)S(1)}, bf16[32,1664]{1,0:T(8,128)(2,1)S(1)}, u32[]{:S(2)}, u32[]{:S(2)}) collective-permute-start(bf16[32,1664]{1,0:T(8,128)(2,1)S(1)} %get-tuple-element.147), channel_id=1, source_target_pairs={{0,24},{8,16},{16,8},{24,0},{1,25},{9,17},{17,9},{25,1},{2,26},{10... | collective-permute-start | bytes 319496 | tf_op jit(solution)/shard_map/ppermute | solution.py:257
  161.2 5.2 %collective-permute-done.74.refs_2_ = bf16[32,1664]{1,0:T(8,128)(2,1)S(1)} collective-permute-done((bf16[32,1664]{1,0:T(8,128)(2,1)S(1)}, bf16[32,1664]{1,0:T(8,128)(2,1)S(1)}, u32[]{:S(2)}, u32[]{:S(2)}) %collective-permute-start.74) | collective-permute-done | bytes 106528 | tf_op jit(solution)/shard_map/ppermute | solution.py:257
  166.4 1.2 attend.15
  167.6 4.8 %collective-permute-start.76 = (bf16[32,1024]{1,0:T(8,128)(2,1)S(1)}, bf16[32,1024]{1,0:T(8,128)(2,1)S(1)}, u32[]{:S(2)}, u32[]{:S(2)}) collective-permute-start(bf16[32,1024]{1,0:T(8,128)(2,1)S(1)} %get-tuple-element.149.refs_1_), channel_id=1, source_target_pairs={{0,8},{8,0},{16,24},{24,16},{1,9},{9,1},{17,25},{25,17},{2,10},{10... | collective-permute-start | bytes 196616 | tf_op jit(solution)/shard_map/ppermute | solution.py:257
  172.4 2.1 %collective-permute-start.78 = (bf16[32,1024]{1,0:T(8,128)(2,1)S(1)}, bf16[32,1024]{1,0:T(8,128)(2,1)S(1)}, u32[]{:S(2)}, u32[]{:S(2)}) collective-permute-start(bf16[32,1024]{1,0:T(8,128)(2,1)S(1)} %get-tuple-element.149.refs_1_), channel_id=1, source_target_pairs={{0,24},{8,16},{16,8},{24,0},{1,25},{9,17},{17,9},{25,1},{2,26},{10... | collective-permute-start | bytes 196616 | tf_op jit(solution)/shard_map/ppermute | solution.py:257
  174.8 2.0 collective-permute-start.70
  179.2 2.1 %collective-permute-start.80 = (bf16[32,1024]{1,0:T(8,128)(2,1)S(1)}, bf16[32,1024]{1,0:T(8,128)(2,1)S(1)}, u32[]{:S(2)}, u32[]{:S(2)}) collective-permute-start(bf16[32,1024]{1,0:T(8,128)(2,1)S(1)} %get-tuple-element.153), channel_id=1, source_target_pairs={{0,2},{1,3},{2,0},{3,1},{4,6},{5,7},{6,4},{7,5},{8,10},{9,11},{10,... | collective-permute-start | bytes 196616 | tf_op jit(solution)/shard_map/ppermute | solution.py:257
  181.8 4.7 %collective-permute-start.72 = (bf16[32,1024]{1,0:T(8,128)(2,1)S(1)}, bf16[32,1024]{1,0:T(8,128)(2,1)S(1)}, u32[]{:S(2)}, u32[]{:S(2)}) collective-permute-start(bf16[32,1024]{1,0:T(8,128)(2,1)S(1)} %add_convert_fusion.1), channel_id=1, source_target_pairs={{0,0},{1,8},{2,16},{3,24},{8,1},{9,9},{10,17},{11,25},{16,2},{17,1... | collective-permute-start | bytes 196616 | tf_op jit(solution)/shard_map/ppermute | solution.py:404
  186.6 4.2 %collective-permute-start.82 = (bf16[32,1024]{1,0:T(8,128)(2,1)S(1)}, bf16[32,1024]{1,0:T(8,128)(2,1)S(1)}, u32[]{:S(2)}, u32[]{:S(2)}) collective-permute-start(bf16[32,1024]{1,0:T(8,128)(2,1)S(1)} %add_convert_fusion), channel_id=1, source_target_pairs={{0,0},{1,8},{2,16},{3,24},{8,1},{9,9},{10,17},{11,25},{16,2},{17,1... | collective-permute-start | bytes 196616 | tf_op jit(solution)/shard_map/ppermute | solution.py:404
  190.8 4.6 %collective-permute-done.82 = bf16[32,1024]{1,0:T(8,128)(2,1)S(1)} collective-permute-done((bf16[32,1024]{1,0:T(8,128)(2,1)S(1)}, bf16[32,1024]{1,0:T(8,128)(2,1)S(1)}, u32[]{:S(2)}, u32[]{:S(2)}) %collective-permute-start.82) | collective-permute-done | bytes 65568 | tf_op jit(solution)/shard_map/ppermute | solution.py:404
  195.5 4.6 %collective-permute-start.83 = (bf16[1,32,1024]{2,1,0:T(8,128)(2,1)S(1)}, bf16[1,32,1024]{2,1,0:T(8,128)(2,1)S(1)}, u32[]{:S(2)}, u32[]{:S(2)}) collective-permute-start(bf16[1,32,1024]{2,1,0:T(8,128)(2,1)S(1)} %select_bitcast_fusion.16), channel_id=1, source_target_pairs={{0,4},{4,0},{1,5},{5,1},{2,6},{6,2},{3,7},{7,3},{8,12},{12,8},{9,1... | collective-permute-start | bytes 196616 | tf_op jit(solution)/shard_map/ppermute | solution.py:257
  (164 shorter events, 38.3 us)
Async XLA Ops:
  2.2 21.1 %collective-permute-start.5 = (bf16[2,1,1024,1024]{3,2,1,0:T(8,128)(2,1)}, bf16[2,1,1024,1024]{3,2,1,0:T(8,128)(2,1)}, u32[]{:S(2)}, u32[]{:S(2)}) collective-permute-start(bf16[2,1,1024,1024]{3,2,1,0:T(8,128)(2,1)} %param.11), channel_id=1, source_target_pairs={{0,4},{4,0},{1,5},{5,1},{2,6},{6,2},{3,7},{7,3},{8,12},{12,8},{9,1... | collective-permute-start | bytes 12582920 | tf_op jit(solution)/shard_map/ppermute | solution.py:257
  2.5 28.8 %collective-permute-start.14 = (bf16[2,1,1024,1024]{3,2,1,0:T(8,128)(2,1)}, bf16[2,1,1024,1024]{3,2,1,0:T(8,128)(2,1)}, u32[]{:S(2)}, u32[]{:S(2)}) collective-permute-start(bf16[2,1,1024,1024]{3,2,1,0:T(8,128)(2,1)} %param.14), channel_id=1, source_target_pairs={{0,4},{4,0},{1,5},{5,1},{2,6},{6,2},{3,7},{7,3},{8,12},{12,8},{9,1... | collective-permute-start | bytes 12582920 | tf_op jit(solution)/shard_map/ppermute | solution.py:257
  2.7 14.5 %collective-permute-start.6 = (bf16[2,1,1024,256]{3,2,1,0:T(8,128)(2,1)}, bf16[2,1,1024,256]{3,2,1,0:T(8,128)(2,1)}, u32[]{:S(2)}, u32[]{:S(2)}) collective-permute-start(bf16[2,1,1024,256]{3,2,1,0:T(8,128)(2,1)} %param.12), channel_id=1, source_target_pairs={{0,4},{4,0},{1,5},{5,1},{2,6},{6,2},{3,7},{7,3},{8,12},{12,8},{9,1... | collective-permute-start | bytes 3145736 | tf_op jit(solution)/shard_map/ppermute | solution.py:257
  3.1 17.6 %collective-permute-start.7 = (bf16[2,1,1024,256]{3,2,1,0:T(8,128)(2,1)}, bf16[2,1,1024,256]{3,2,1,0:T(8,128)(2,1)}, u32[]{:S(2)}, u32[]{:S(2)}) collective-permute-start(bf16[2,1,1024,256]{3,2,1,0:T(8,128)(2,1)} %param.13), channel_id=1, source_target_pairs={{0,4},{4,0},{1,5},{5,1},{2,6},{6,2},{3,7},{7,3},{8,12},{12,8},{9,1... | collective-permute-start | bytes 3145736 | tf_op jit(solution)/shard_map/ppermute | solution.py:257
  5.6 10.3 %collective-permute-start = (bf16[64,1024]{1,0:T(8,128)(2,1)S(1)}, bf16[64,1024]{1,0:T(8,128)(2,1)S(1)}, u32[]{:S(2)}, u32[]{:S(2)}) collective-permute-start(bf16[64,1024]{1,0:T(8,128)(2,1)S(1)} %bitcast.51), channel_id=1, source_target_pairs={{0,0},{1,8},{2,16},{3,24},{8,1},{9,9},{10,17},{11,25},{16,2},{17,1... | collective-permute-start | bytes 393224 | tf_op jit(solution)/shard_map/ppermute | solution.py:334
  15.8 9.9 %collective-permute-start.1 = (bf16[64,1024]{1,0:T(8,128)(2,1)S(1)}, bf16[64,1024]{1,0:T(8,128)(2,1)S(1)}, u32[]{:S(2)}, u32[]{:S(2)}) collective-permute-start(bf16[64,1024]{1,0:T(8,128)(2,1)S(1)} %collective-permute-done.refs_1_), channel_id=1, source_target_pairs={{0,1},{1,0},{2,3},{3,2},{4,5},{5,4},{6,7},{7,6},{8,9},{9,8},{10,11... | collective-permute-start | bytes 393224 | tf_op jit(solution)/shard_map/ppermute | solution.py:257
  17.2 8.6 %collective-permute-start.2 = (bf16[64,1024]{1,0:T(8,128)(2,1)S(1)}, bf16[64,1024]{1,0:T(8,128)(2,1)S(1)}, u32[]{:S(2)}, u32[]{:S(2)}) collective-permute-start(bf16[64,1024]{1,0:T(8,128)(2,1)S(1)} %collective-permute-done.refs_1_), channel_id=1, source_target_pairs={{0,2},{1,3},{2,0},{3,1},{4,6},{5,7},{6,4},{7,5},{8,10},{9,11},{10,... | collective-permute-start | bytes 393224 | tf_op jit(solution)/shard_map/ppermute | solution.py:257
  27.0 7.2 %collective-permute-start.8 = (bf16[32,1664]{1,0:T(8,128)(2,1)S(1)}, bf16[32,1664]{1,0:T(8,128)(2,1)S(1)}, u32[]{:S(2)}, u32[]{:S(2)}) collective-permute-start(bf16[32,1664]{1,0:T(8,128)(2,1)S(1)} %get-tuple-element.86), channel_id=1, source_target_pairs={{0,8},{8,0},{16,24},{24,16},{1,9},{9,1},{17,25},{25,17},{2,10},{10... | collective-permute-start | bytes 319496 | tf_op jit(solution)/shard_map/ppermute | solution.py:257
  27.1 7.1 %collective-permute-start.9 = (bf16[32,1664]{1,0:T(8,128)(2,1)S(1)}, bf16[32,1664]{1,0:T(8,128)(2,1)S(1)}, u32[]{:S(2)}, u32[]{:S(2)}) collective-permute-start(bf16[32,1664]{1,0:T(8,128)(2,1)S(1)} %get-tuple-element.87), channel_id=1, source_target_pairs={{0,16},{8,24},{16,0},{24,8},{1,17},{9,25},{17,1},{25,9},{2,18},{10... | collective-permute-start | bytes 319496 | tf_op jit(solution)/shard_map/ppermute | solution.py:257
  30.7 6.6 %collective-permute-start.10 = (bf16[32,1664]{1,0:T(8,128)(2,1)S(1)}, bf16[32,1664]{1,0:T(8,128)(2,1)S(1)}, u32[]{:S(2)}, u32[]{:S(2)}) collective-permute-start(bf16[32,1664]{1,0:T(8,128)(2,1)S(1)} %get-tuple-element.88), channel_id=1, source_target_pairs={{0,24},{8,16},{16,8},{24,0},{1,25},{9,17},{17,9},{25,1},{2,26},{10... | collective-permute-start | bytes 319496 | tf_op jit(solution)/shard_map/ppermute | solution.py:257
  38.3 8.5 %collective-permute-start.11 = (bf16[32,1024]{1,0:T(8,128)(2,1)S(1)}, bf16[32,1024]{1,0:T(8,128)(2,1)S(1)}, u32[]{:S(2)}, u32[]{:S(2)}) collective-permute-start(bf16[32,1024]{1,0:T(8,128)(2,1)S(1)} %get-tuple-element.91.refs_0_), channel_id=1, source_target_pairs={{0,8},{8,0},{16,24},{24,16},{1,9},{9,1},{17,25},{25,17},{2,10},{10... | collective-permute-start | bytes 196616 | tf_op jit(solution)/shard_map/ppermute | solution.py:257
  40.3 7.6 %collective-permute-start.12 = (bf16[32,1024]{1,0:T(8,128)(2,1)S(1)}, bf16[32,1024]{1,0:T(8,128)(2,1)S(1)}, u32[]{:S(2)}, u32[]{:S(2)}) collective-permute-start(bf16[32,1024]{1,0:T(8,128)(2,1)S(1)} %get-tuple-element.91.refs_0_), channel_id=1, source_target_pairs={{0,16},{8,24},{16,0},{24,8},{1,17},{9,25},{17,1},{25,9},{2,18},{10... | collective-permute-start | bytes 196616 | tf_op jit(solution)/shard_map/ppermute | solution.py:257
  44.6 9.1 %collective-permute-start.19 = (bf16[32,1664]{1,0:T(8,128)(2,1)S(1)}, bf16[32,1664]{1,0:T(8,128)(2,1)S(1)}, u32[]{:S(2)}, u32[]{:S(2)}) collective-permute-start(bf16[32,1664]{1,0:T(8,128)(2,1)S(1)} %get-tuple-element.97), channel_id=1, source_target_pairs={{0,16},{8,24},{16,0},{24,8},{1,17},{9,25},{17,1},{25,9},{2,18},{10... | collective-permute-start | bytes 319496 | tf_op jit(solution)/shard_map/ppermute | solution.py:257
  46.8 7.0 %collective-permute-start.20 = (bf16[32,1664]{1,0:T(8,128)(2,1)S(1)}, bf16[32,1664]{1,0:T(8,128)(2,1)S(1)}, u32[]{:S(2)}, u32[]{:S(2)}) collective-permute-start(bf16[32,1664]{1,0:T(8,128)(2,1)S(1)} %get-tuple-element.98), channel_id=1, source_target_pairs={{0,24},{8,16},{16,8},{24,0},{1,25},{9,17},{17,9},{25,1},{2,26},{10... | collective-permute-start | bytes 319496 | tf_op jit(solution)/shard_map/ppermute | solution.py:257
  48.3 12.3 %collective-permute-start.15 = (bf16[128,1024]{1,0:T(8,128)(2,1)S(1)}, bf16[128,1024]{1,0:T(8,128)(2,1)S(1)}, u32[]{:S(2)}, u32[]{:S(2)}) collective-permute-start(bf16[128,1024]{1,0:T(8,128)(2,1)S(1)} %project_out.8.refs_9_.refs_1_), channel_id=1, source_target_pairs={{0,1},{1,0},{2,3},{3,2},{4,5},{5,4},{6,7},{7,6},{8,9},{9,8},{10,11... | collective-permute-start | bytes 786440 | tf_op jit(solution)/shard_map/ppermute | solution.py:257
  49.8 12.2 %collective-permute-start.16 = (bf16[128,1024]{1,0:T(8,128)(2,1)S(1)}, bf16[128,1024]{1,0:T(8,128)(2,1)S(1)}, u32[]{:S(2)}, u32[]{:S(2)}) collective-permute-start(bf16[128,1024]{1,0:T(8,128)(2,1)S(1)} %project_out.8.refs_9_.refs_1_), channel_id=1, source_target_pairs={{0,2},{1,3},{2,0},{3,1},{4,6},{5,7},{6,4},{7,5},{8,10},{9,11},{10,... | collective-permute-start | bytes 786440 | tf_op jit(solution)/shard_map/ppermute | solution.py:257
  50.1 11.9 %collective-permute-start.17 = (bf16[128,1024]{1,0:T(8,128)(2,1)S(1)}, bf16[128,1024]{1,0:T(8,128)(2,1)S(1)}, u32[]{:S(2)}, u32[]{:S(2)}) collective-permute-start(bf16[128,1024]{1,0:T(8,128)(2,1)S(1)} %project_out.8.refs_9_.refs_1_), channel_id=1, source_target_pairs={{0,3},{1,2},{2,1},{3,0},{4,7},{5,6},{6,5},{7,4},{8,11},{9,10},{10,... | collective-permute-start | bytes 786440 | tf_op jit(solution)/shard_map/ppermute | solution.py:257
  54.9 10.0 %collective-permute-start.24 = (bf16[32,1024]{1,0:T(8,128)(2,1)S(1)}, bf16[32,1024]{1,0:T(8,128)(2,1)S(1)}, u32[]{:S(2)}, u32[]{:S(2)}) collective-permute-start(bf16[32,1024]{1,0:T(8,128)(2,1)S(1)} %get-tuple-element.106.refs_0_), channel_id=1, source_target_pairs={{0,8},{8,0},{16,24},{24,16},{1,9},{9,1},{17,25},{25,17},{2,10},{10... | collective-permute-start | bytes 196616 | tf_op jit(solution)/shard_map/ppermute | solution.py:257
  63.3 9.5 %collective-permute-start.22 = (bf16[32,1664]{1,0:T(8,128)(2,1)S(1)}, bf16[32,1664]{1,0:T(8,128)(2,1)S(1)}, u32[]{:S(2)}, u32[]{:S(2)}) collective-permute-start(bf16[32,1664]{1,0:T(8,128)(2,1)S(1)} %get-tuple-element.104), channel_id=1, source_target_pairs={{0,16},{8,24},{16,0},{24,8},{1,17},{9,25},{17,1},{25,9},{2,18},{10... | collective-permute-start | bytes 319496 | tf_op jit(solution)/shard_map/ppermute | solution.py:257
  65.0 7.8 %collective-permute-start.23 = (bf16[32,1664]{1,0:T(8,128)(2,1)S(1)}, bf16[32,1664]{1,0:T(8,128)(2,1)S(1)}, u32[]{:S(2)}, u32[]{:S(2)}) collective-permute-start(bf16[32,1664]{1,0:T(8,128)(2,1)S(1)} %get-tuple-element.105), channel_id=1, source_target_pairs={{0,24},{8,16},{16,8},{24,0},{1,25},{9,17},{17,9},{25,1},{2,26},{10... | collective-permute-start | bytes 319496 | tf_op jit(solution)/shard_map/ppermute | solution.py:257
  66.8 11.9 %collective-permute-start.30 = (bf16[128,1024]{1,0:T(8,128)(2,1)S(1)}, bf16[128,1024]{1,0:T(8,128)(2,1)S(1)}, u32[]{:S(2)}, u32[]{:S(2)}) collective-permute-start(bf16[128,1024]{1,0:T(8,128)(2,1)S(1)} %project_out.9.refs_7_.refs_1_), channel_id=1, source_target_pairs={{0,1},{1,0},{2,3},{3,2},{4,5},{5,4},{6,7},{7,6},{8,9},{9,8},{10,11... | collective-permute-start | bytes 786440 | tf_op jit(solution)/shard_map/ppermute | solution.py:257
  68.3 12.5 %collective-permute-start.31 = (bf16[128,1024]{1,0:T(8,128)(2,1)S(1)}, bf16[128,1024]{1,0:T(8,128)(2,1)S(1)}, u32[]{:S(2)}, u32[]{:S(2)}) collective-permute-start(bf16[128,1024]{1,0:T(8,128)(2,1)S(1)} %project_out.9.refs_7_.refs_1_), channel_id=1, source_target_pairs={{0,2},{1,3},{2,0},{3,1},{4,6},{5,7},{6,4},{7,5},{8,10},{9,11},{10,... | collective-permute-start | bytes 786440 | tf_op jit(solution)/shard_map/ppermute | solution.py:257
  68.4 12.4 %collective-permute-start.32 = (bf16[128,1024]{1,0:T(8,128)(2,1)S(1)}, bf16[128,1024]{1,0:T(8,128)(2,1)S(1)}, u32[]{:S(2)}, u32[]{:S(2)}) collective-permute-start(bf16[128,1024]{1,0:T(8,128)(2,1)S(1)} %project_out.9.refs_7_.refs_1_), channel_id=1, source_target_pairs={{0,3},{1,2},{2,1},{3,0},{4,7},{5,6},{6,5},{7,4},{8,11},{9,10},{10,... | collective-permute-start | bytes 786440 | tf_op jit(solution)/shard_map/ppermute | solution.py:257
  73.8 9.2 %collective-permute-start.27 = (bf16[32,1024]{1,0:T(8,128)(2,1)S(1)}, bf16[32,1024]{1,0:T(8,128)(2,1)S(1)}, u32[]{:S(2)}, u32[]{:S(2)}) collective-permute-start(bf16[32,1024]{1,0:T(8,128)(2,1)S(1)} %get-tuple-element.107.refs_0_), channel_id=1, source_target_pairs={{0,8},{8,0},{16,24},{24,16},{1,9},{9,1},{17,25},{25,17},{2,10},{10... | collective-permute-start | bytes 196616 | tf_op jit(solution)/shard_map/ppermute | solution.py:257
  78.7 6.5 %collective-permute-start.28 = (bf16[32,1024]{1,0:T(8,128)(2,1)S(1)}, bf16[32,1024]{1,0:T(8,128)(2,1)S(1)}, u32[]{:S(2)}, u32[]{:S(2)}) collective-permute-start(bf16[32,1024]{1,0:T(8,128)(2,1)S(1)} %get-tuple-element.107.refs_0_), channel_id=1, source_target_pairs={{0,16},{8,24},{16,0},{24,8},{1,17},{9,25},{17,1},{25,9},{2,18},{10... | collective-permute-start | bytes 196616 | tf_op jit(solution)/shard_map/ppermute | solution.py:257
  78.7 6.5 %collective-permute-start.29 = (bf16[32,1024]{1,0:T(8,128)(2,1)S(1)}, bf16[32,1024]{1,0:T(8,128)(2,1)S(1)}, u32[]{:S(2)}, u32[]{:S(2)}) collective-permute-start(bf16[32,1024]{1,0:T(8,128)(2,1)S(1)} %get-tuple-element.107.refs_0_), channel_id=1, source_target_pairs={{0,24},{8,16},{16,8},{24,0},{1,25},{9,17},{17,9},{25,1},{2,26},{10... | collective-permute-start | bytes 196616 | tf_op jit(solution)/shard_map/ppermute | solution.py:257
  82.1 9.3 %collective-permute-start.37 = (bf16[32,1664]{1,0:T(8,128)(2,1)S(1)}, bf16[32,1664]{1,0:T(8,128)(2,1)S(1)}, u32[]{:S(2)}, u32[]{:S(2)}) collective-permute-start(bf16[32,1664]{1,0:T(8,128)(2,1)S(1)} %get-tuple-element.112), channel_id=1, source_target_pairs={{0,16},{8,24},{16,0},{24,8},{1,17},{9,25},{17,1},{25,9},{2,18},{10... | collective-permute-start | bytes 319496 | tf_op jit(solution)/shard_map/ppermute | solution.py:257
  83.0 8.4 %collective-permute-start.38 = (bf16[32,1664]{1,0:T(8,128)(2,1)S(1)}, bf16[32,1664]{1,0:T(8,128)(2,1)S(1)}, u32[]{:S(2)}, u32[]{:S(2)}) collective-permute-start(bf16[32,1664]{1,0:T(8,128)(2,1)S(1)} %get-tuple-element.113), channel_id=1, source_target_pairs={{0,24},{8,16},{16,8},{24,0},{1,25},{9,17},{17,9},{25,1},{2,26},{10... | collective-permute-start | bytes 319496 | tf_op jit(solution)/shard_map/ppermute | solution.py:257
  85.6 11.8 %collective-permute-start.33 = (bf16[128,1024]{1,0:T(8,128)(2,1)S(1)}, bf16[128,1024]{1,0:T(8,128)(2,1)S(1)}, u32[]{:S(2)}, u32[]{:S(2)}) collective-permute-start(bf16[128,1024]{1,0:T(8,128)(2,1)S(1)} %project_out.10.refs_9_.refs_1_), channel_id=1, source_target_pairs={{0,1},{1,0},{2,3},{3,2},{4,5},{5,4},{6,7},{7,6},{8,9},{9,8},{10,11... | collective-permute-start | bytes 786440 | tf_op jit(solution)/shard_map/ppermute | solution.py:257
  87.0 12.5 %collective-permute-start.34 = (bf16[128,1024]{1,0:T(8,128)(2,1)S(1)}, bf16[128,1024]{1,0:T(8,128)(2,1)S(1)}, u32[]{:S(2)}, u32[]{:S(2)}) collective-permute-start(bf16[128,1024]{1,0:T(8,128)(2,1)S(1)} %project_out.10.refs_9_.refs_1_), channel_id=1, source_target_pairs={{0,2},{1,3},{2,0},{3,1},{4,6},{5,7},{6,4},{7,5},{8,10},{9,11},{10,... | collective-permute-start | bytes 786440 | tf_op jit(solution)/shard_map/ppermute | solution.py:257
  87.0 12.5 %collective-permute-start.35 = (bf16[128,1024]{1,0:T(8,128)(2,1)S(1)}, bf16[128,1024]{1,0:T(8,128)(2,1)S(1)}, u32[]{:S(2)}, u32[]{:S(2)}) collective-permute-start(bf16[128,1024]{1,0:T(8,128)(2,1)S(1)} %project_out.10.refs_9_.refs_1_), channel_id=1, source_target_pairs={{0,3},{1,2},{2,1},{3,0},{4,7},{5,6},{6,5},{7,4},{8,11},{9,10},{10,... | collective-permute-start | bytes 786440 | tf_op jit(solution)/shard_map/ppermute | solution.py:257
  92.6 9.2 %collective-permute-start.42 = (bf16[32,1024]{1,0:T(8,128)(2,1)S(1)}, bf16[32,1024]{1,0:T(8,128)(2,1)S(1)}, u32[]{:S(2)}, u32[]{:S(2)}) collective-permute-start(bf16[32,1024]{1,0:T(8,128)(2,1)S(1)} %get-tuple-element.121.refs_0_), channel_id=1, source_target_pairs={{0,8},{8,0},{16,24},{24,16},{1,9},{9,1},{17,25},{25,17},{2,10},{10... | collective-permute-start | bytes 196616 | tf_op jit(solution)/shard_map/ppermute | solution.py:257
  97.4 6.4 %collective-permute-start.43 = (bf16[32,1024]{1,0:T(8,128)(2,1)S(1)}, bf16[32,1024]{1,0:T(8,128)(2,1)S(1)}, u32[]{:S(2)}, u32[]{:S(2)}) collective-permute-start(bf16[32,1024]{1,0:T(8,128)(2,1)S(1)} %get-tuple-element.121.refs_0_), channel_id=1, source_target_pairs={{0,16},{8,24},{16,0},{24,8},{1,17},{9,25},{17,1},{25,9},{2,18},{10... | collective-permute-start | bytes 196616 | tf_op jit(solution)/shard_map/ppermute | solution.py:257
  100.8 9.3 %collective-permute-start.40 = (bf16[32,1664]{1,0:T(8,128)(2,1)S(1)}, bf16[32,1664]{1,0:T(8,128)(2,1)S(1)}, u32[]{:S(2)}, u32[]{:S(2)}) collective-permute-start(bf16[32,1664]{1,0:T(8,128)(2,1)S(1)} %get-tuple-element.119), channel_id=1, source_target_pairs={{0,16},{8,24},{16,0},{24,8},{1,17},{9,25},{17,1},{25,9},{2,18},{10... | collective-permute-start | bytes 319496 | tf_op jit(solution)/shard_map/ppermute | solution.py:257
  101.7 8.4 %collective-permute-start.41 = (bf16[32,1664]{1,0:T(8,128)(2,1)S(1)}, bf16[32,1664]{1,0:T(8,128)(2,1)S(1)}, u32[]{:S(2)}, u32[]{:S(2)}) collective-permute-start(bf16[32,1664]{1,0:T(8,128)(2,1)S(1)} %get-tuple-element.120), channel_id=1, source_target_pairs={{0,24},{8,16},{16,8},{24,0},{1,25},{9,17},{17,9},{25,1},{2,26},{10... | collective-permute-start | bytes 319496 | tf_op jit(solution)/shard_map/ppermute | solution.py:257
  104.3 11.8 %collective-permute-start.48 = (bf16[128,1024]{1,0:T(8,128)(2,1)S(1)}, bf16[128,1024]{1,0:T(8,128)(2,1)S(1)}, u32[]{:S(2)}, u32[]{:S(2)}) collective-permute-start(bf16[128,1024]{1,0:T(8,128)(2,1)S(1)} %project_out.11.refs_7_.refs_1_), channel_id=1, source_target_pairs={{0,1},{1,0},{2,3},{3,2},{4,5},{5,4},{6,7},{7,6},{8,9},{9,8},{10,11... | collective-permute-start | bytes 786440 | tf_op jit(solution)/shard_map/ppermute | solution.py:257
  105.7 12.5 %collective-permute-start.49 = (bf16[128,1024]{1,0:T(8,128)(2,1)S(1)}, bf16[128,1024]{1,0:T(8,128)(2,1)S(1)}, u32[]{:S(2)}, u32[]{:S(2)}) collective-permute-start(bf16[128,1024]{1,0:T(8,128)(2,1)S(1)} %project_out.11.refs_7_.refs_1_), channel_id=1, source_target_pairs={{0,2},{1,3},{2,0},{3,1},{4,6},{5,7},{6,4},{7,5},{8,10},{9,11},{10,... | collective-permute-start | bytes 786440 | tf_op jit(solution)/shard_map/ppermute | solution.py:257
  105.7 12.5 %collective-permute-start.50 = (bf16[128,1024]{1,0:T(8,128)(2,1)S(1)}, bf16[128,1024]{1,0:T(8,128)(2,1)S(1)}, u32[]{:S(2)}, u32[]{:S(2)}) collective-permute-start(bf16[128,1024]{1,0:T(8,128)(2,1)S(1)} %project_out.11.refs_7_.refs_1_), channel_id=1, source_target_pairs={{0,3},{1,2},{2,1},{3,0},{4,7},{5,6},{6,5},{7,4},{8,11},{9,10},{10,... | collective-permute-start | bytes 786440 | tf_op jit(solution)/shard_map/ppermute | solution.py:257
  111.1 9.2 %collective-permute-start.45 = (bf16[32,1024]{1,0:T(8,128)(2,1)S(1)}, bf16[32,1024]{1,0:T(8,128)(2,1)S(1)}, u32[]{:S(2)}, u32[]{:S(2)}) collective-permute-start(bf16[32,1024]{1,0:T(8,128)(2,1)S(1)} %get-tuple-element.122.refs_0_), channel_id=1, source_target_pairs={{0,8},{8,0},{16,24},{24,16},{1,9},{9,1},{17,25},{25,17},{2,10},{10... | collective-permute-start | bytes 196616 | tf_op jit(solution)/shard_map/ppermute | solution.py:257
  116.0 6.5 %collective-permute-start.46 = (bf16[32,1024]{1,0:T(8,128)(2,1)S(1)}, bf16[32,1024]{1,0:T(8,128)(2,1)S(1)}, u32[]{:S(2)}, u32[]{:S(2)}) collective-permute-start(bf16[32,1024]{1,0:T(8,128)(2,1)S(1)} %get-tuple-element.122.refs_0_), channel_id=1, source_target_pairs={{0,16},{8,24},{16,0},{24,8},{1,17},{9,25},{17,1},{25,9},{2,18},{10... | collective-permute-start | bytes 196616 | tf_op jit(solution)/shard_map/ppermute | solution.py:257
  116.0 6.5 %collective-permute-start.47 = (bf16[32,1024]{1,0:T(8,128)(2,1)S(1)}, bf16[32,1024]{1,0:T(8,128)(2,1)S(1)}, u32[]{:S(2)}, u32[]{:S(2)}) collective-permute-start(bf16[32,1024]{1,0:T(8,128)(2,1)S(1)} %get-tuple-element.122.refs_0_), channel_id=1, source_target_pairs={{0,24},{8,16},{16,8},{24,0},{1,25},{9,17},{17,9},{25,1},{2,26},{10... | collective-permute-start | bytes 196616 | tf_op jit(solution)/shard_map/ppermute | solution.py:257
  119.5 9.4 %collective-permute-start.55 = (bf16[32,1664]{1,0:T(8,128)(2,1)S(1)}, bf16[32,1664]{1,0:T(8,128)(2,1)S(1)}, u32[]{:S(2)}, u32[]{:S(2)}) collective-permute-start(bf16[32,1664]{1,0:T(8,128)(2,1)S(1)} %get-tuple-element.127), channel_id=1, source_target_pairs={{0,16},{8,24},{16,0},{24,8},{1,17},{9,25},{17,1},{25,9},{2,18},{10... | collective-permute-start | bytes 319496 | tf_op jit(solution)/shard_map/ppermute | solution.py:257
  120.4 8.5 %collective-permute-start.56 = (bf16[32,1664]{1,0:T(8,128)(2,1)S(1)}, bf16[32,1664]{1,0:T(8,128)(2,1)S(1)}, u32[]{:S(2)}, u32[]{:S(2)}) collective-permute-start(bf16[32,1664]{1,0:T(8,128)(2,1)S(1)} %get-tuple-element.128), channel_id=1, source_target_pairs={{0,24},{8,16},{16,8},{24,0},{1,25},{9,17},{17,9},{25,1},{2,26},{10... | collective-permute-start | bytes 319496 | tf_op jit(solution)/shard_map/ppermute | solution.py:257
  123.0 11.9 %collective-permute-start.51 = (bf16[128,1024]{1,0:T(8,128)(2,1)S(1)}, bf16[128,1024]{1,0:T(8,128)(2,1)S(1)}, u32[]{:S(2)}, u32[]{:S(2)}) collective-permute-start(bf16[128,1024]{1,0:T(8,128)(2,1)S(1)} %project_out.12.refs_9_.refs_1_), channel_id=1, source_target_pairs={{0,1},{1,0},{2,3},{3,2},{4,5},{5,4},{6,7},{7,6},{8,9},{9,8},{10,11... | collective-permute-start | bytes 786440 | tf_op jit(solution)/shard_map/ppermute | solution.py:257
  124.3 12.6 %collective-permute-start.52 = (bf16[128,1024]{1,0:T(8,128)(2,1)S(1)}, bf16[128,1024]{1,0:T(8,128)(2,1)S(1)}, u32[]{:S(2)}, u32[]{:S(2)}) collective-permute-start(bf16[128,1024]{1,0:T(8,128)(2,1)S(1)} %project_out.12.refs_9_.refs_1_), channel_id=1, source_target_pairs={{0,2},{1,3},{2,0},{3,1},{4,6},{5,7},{6,4},{7,5},{8,10},{9,11},{10,... | collective-permute-start | bytes 786440 | tf_op jit(solution)/shard_map/ppermute | solution.py:257
  124.3 12.6 %collective-permute-start.53 = (bf16[128,1024]{1,0:T(8,128)(2,1)S(1)}, bf16[128,1024]{1,0:T(8,128)(2,1)S(1)}, u32[]{:S(2)}, u32[]{:S(2)}) collective-permute-start(bf16[128,1024]{1,0:T(8,128)(2,1)S(1)} %project_out.12.refs_9_.refs_1_), channel_id=1, source_target_pairs={{0,3},{1,2},{2,1},{3,0},{4,7},{5,6},{6,5},{7,4},{8,11},{9,10},{10,... | collective-permute-start | bytes 786440 | tf_op jit(solution)/shard_map/ppermute | solution.py:257
  130.0 9.2 %collective-permute-start.60 = (bf16[32,1024]{1,0:T(8,128)(2,1)S(1)}, bf16[32,1024]{1,0:T(8,128)(2,1)S(1)}, u32[]{:S(2)}, u32[]{:S(2)}) collective-permute-start(bf16[32,1024]{1,0:T(8,128)(2,1)S(1)} %get-tuple-element.136.refs_0_), channel_id=1, source_target_pairs={{0,8},{8,0},{16,24},{24,16},{1,9},{9,1},{17,25},{25,17},{2,10},{10... | collective-permute-start | bytes 196616 | tf_op jit(solution)/shard_map/ppermute | solution.py:257
  138.3 9.3 %collective-permute-start.58 = (bf16[32,1664]{1,0:T(8,128)(2,1)S(1)}, bf16[32,1664]{1,0:T(8,128)(2,1)S(1)}, u32[]{:S(2)}, u32[]{:S(2)}) collective-permute-start(bf16[32,1664]{1,0:T(8,128)(2,1)S(1)} %get-tuple-element.134), channel_id=1, source_target_pairs={{0,16},{8,24},{16,0},{24,8},{1,17},{9,25},{17,1},{25,9},{2,18},{10... | collective-permute-start | bytes 319496 | tf_op jit(solution)/shard_map/ppermute | solution.py:257
  139.2 8.4 %collective-permute-start.59 = (bf16[32,1664]{1,0:T(8,128)(2,1)S(1)}, bf16[32,1664]{1,0:T(8,128)(2,1)S(1)}, u32[]{:S(2)}, u32[]{:S(2)}) collective-permute-start(bf16[32,1664]{1,0:T(8,128)(2,1)S(1)} %get-tuple-element.135), channel_id=1, source_target_pairs={{0,24},{8,16},{16,8},{24,0},{1,25},{9,17},{17,9},{25,1},{2,26},{10... | collective-permute-start | bytes 319496 | tf_op jit(solution)/shard_map/ppermute | solution.py:257
  141.7 11.9 %collective-permute-start.66 = (bf16[128,1024]{1,0:T(8,128)(2,1)S(1)}, bf16[128,1024]{1,0:T(8,128)(2,1)S(1)}, u32[]{:S(2)}, u32[]{:S(2)}) collective-permute-start(bf16[128,1024]{1,0:T(8,128)(2,1)S(1)} %project_out.13.refs_7_.refs_1_), channel_id=1, source_target_pairs={{0,1},{1,0},{2,3},{3,2},{4,5},{5,4},{6,7},{7,6},{8,9},{9,8},{10,11... | collective-permute-start | bytes 786440 | tf_op jit(solution)/shard_map/ppermute | solution.py:257
  142.9 12.9 %collective-permute-start.67 = (bf16[128,1024]{1,0:T(8,128)(2,1)S(1)}, bf16[128,1024]{1,0:T(8,128)(2,1)S(1)}, u32[]{:S(2)}, u32[]{:S(2)}) collective-permute-start(bf16[128,1024]{1,0:T(8,128)(2,1)S(1)} %project_out.13.refs_7_.refs_1_), channel_id=1, source_target_pairs={{0,2},{1,3},{2,0},{3,1},{4,6},{5,7},{6,4},{7,5},{8,10},{9,11},{10,... | collective-permute-start | bytes 786440 | tf_op jit(solution)/shard_map/ppermute | solution.py:257
  143.1 12.7 %collective-permute-start.68 = (bf16[128,1024]{1,0:T(8,128)(2,1)S(1)}, bf16[128,1024]{1,0:T(8,128)(2,1)S(1)}, u32[]{:S(2)}, u32[]{:S(2)}) collective-permute-start(bf16[128,1024]{1,0:T(8,128)(2,1)S(1)} %project_out.13.refs_7_.refs_1_), channel_id=1, source_target_pairs={{0,3},{1,2},{2,1},{3,0},{4,7},{5,6},{6,5},{7,4},{8,11},{9,10},{10,... | collective-permute-start | bytes 786440 | tf_op jit(solution)/shard_map/ppermute | solution.py:257
  148.5 9.5 %collective-permute-start.63 = (bf16[32,1024]{1,0:T(8,128)(2,1)S(1)}, bf16[32,1024]{1,0:T(8,128)(2,1)S(1)}, u32[]{:S(2)}, u32[]{:S(2)}) collective-permute-start(bf16[32,1024]{1,0:T(8,128)(2,1)S(1)} %get-tuple-element.137.refs_1_), channel_id=1, source_target_pairs={{0,8},{8,0},{16,24},{24,16},{1,9},{9,1},{17,25},{25,17},{2,10},{10... | collective-permute-start | bytes 196616 | tf_op jit(solution)/shard_map/ppermute | solution.py:257
  153.7 6.5 %collective-permute-start.64 = (bf16[32,1024]{1,0:T(8,128)(2,1)S(1)}, bf16[32,1024]{1,0:T(8,128)(2,1)S(1)}, u32[]{:S(2)}, u32[]{:S(2)}) collective-permute-start(bf16[32,1024]{1,0:T(8,128)(2,1)S(1)} %get-tuple-element.137.refs_1_), channel_id=1, source_target_pairs={{0,16},{8,24},{16,0},{24,8},{1,17},{9,25},{17,1},{25,9},{2,18},{10... | collective-permute-start | bytes 196616 | tf_op jit(solution)/shard_map/ppermute | solution.py:257
  153.7 6.5 %collective-permute-start.65 = (bf16[32,1024]{1,0:T(8,128)(2,1)S(1)}, bf16[32,1024]{1,0:T(8,128)(2,1)S(1)}, u32[]{:S(2)}, u32[]{:S(2)}) collective-permute-start(bf16[32,1024]{1,0:T(8,128)(2,1)S(1)} %get-tuple-element.137.refs_1_), channel_id=1, source_target_pairs={{0,24},{8,16},{16,8},{24,0},{1,25},{9,17},{17,9},{25,1},{2,26},{10... | collective-permute-start | bytes 196616 | tf_op jit(solution)/shard_map/ppermute | solution.py:257
  157.1 9.3 %collective-permute-start.74 = (bf16[32,1664]{1,0:T(8,128)(2,1)S(1)}, bf16[32,1664]{1,0:T(8,128)(2,1)S(1)}, u32[]{:S(2)}, u32[]{:S(2)}) collective-permute-start(bf16[32,1664]{1,0:T(8,128)(2,1)S(1)} %get-tuple-element.146), channel_id=1, source_target_pairs={{0,16},{8,24},{16,0},{24,8},{1,17},{9,25},{17,1},{25,9},{2,18},{10... | collective-permute-start | bytes 319496 | tf_op jit(solution)/shard_map/ppermute | solution.py:257
  158.0 8.4 %collective-permute-start.75 = (bf16[32,1664]{1,0:T(8,128)(2,1)S(1)}, bf16[32,1664]{1,0:T(8,128)(2,1)S(1)}, u32[]{:S(2)}, u32[]{:S(2)}) collective-permute-start(bf16[32,1664]{1,0:T(8,128)(2,1)S(1)} %get-tuple-element.147), channel_id=1, source_target_pairs={{0,24},{8,16},{16,8},{24,0},{1,25},{9,17},{17,9},{25,1},{2,26},{10... | collective-permute-start | bytes 319496 | tf_op jit(solution)/shard_map/ppermute | solution.py:257
  167.6 9.2 %collective-permute-start.76 = (bf16[32,1024]{1,0:T(8,128)(2,1)S(1)}, bf16[32,1024]{1,0:T(8,128)(2,1)S(1)}, u32[]{:S(2)}, u32[]{:S(2)}) collective-permute-start(bf16[32,1024]{1,0:T(8,128)(2,1)S(1)} %get-tuple-element.149.refs_1_), channel_id=1, source_target_pairs={{0,8},{8,0},{16,24},{24,16},{1,9},{9,1},{17,25},{25,17},{2,10},{10... | collective-permute-start | bytes 196616 | tf_op jit(solution)/shard_map/ppermute | solution.py:257
  174.6 6.7 %collective-permute-start.71 = (bf16[32,1024]{1,0:T(8,128)(2,1)S(1)}, bf16[32,1024]{1,0:T(8,128)(2,1)S(1)}, u32[]{:S(2)}, u32[]{:S(2)}) collective-permute-start(bf16[32,1024]{1,0:T(8,128)(2,1)S(1)} %get-tuple-element.143), channel_id=1, source_target_pairs={{0,3},{1,2},{2,1},{3,0},{4,7},{5,6},{6,5},{7,4},{8,11},{9,10},{10,... | collective-permute-start | bytes 196616 | tf_op jit(solution)/shard_map/ppermute | solution.py:257
  174.8 6.9 %collective-permute-start.70 = (bf16[32,1024]{1,0:T(8,128)(2,1)S(1)}, bf16[32,1024]{1,0:T(8,128)(2,1)S(1)}, u32[]{:S(2)}, u32[]{:S(2)}) collective-permute-start(bf16[32,1024]{1,0:T(8,128)(2,1)S(1)} %get-tuple-element.142), channel_id=1, source_target_pairs={{0,2},{1,3},{2,0},{3,1},{4,6},{5,7},{6,4},{7,5},{8,10},{9,11},{10,... | collective-permute-start | bytes 196616 | tf_op jit(solution)/shard_map/ppermute | solution.py:257
  179.0 7.5 %collective-permute-start.81 = (bf16[32,1024]{1,0:T(8,128)(2,1)S(1)}, bf16[32,1024]{1,0:T(8,128)(2,1)S(1)}, u32[]{:S(2)}, u32[]{:S(2)}) collective-permute-start(bf16[32,1024]{1,0:T(8,128)(2,1)S(1)} %get-tuple-element.154), channel_id=1, source_target_pairs={{0,3},{1,2},{2,1},{3,0},{4,7},{5,6},{6,5},{7,4},{8,11},{9,10},{10,... | collective-permute-start | bytes 196616 | tf_op jit(solution)/shard_map/ppermute | solution.py:257
  179.2 7.3 %collective-permute-start.80 = (bf16[32,1024]{1,0:T(8,128)(2,1)S(1)}, bf16[32,1024]{1,0:T(8,128)(2,1)S(1)}, u32[]{:S(2)}, u32[]{:S(2)}) collective-permute-start(bf16[32,1024]{1,0:T(8,128)(2,1)S(1)} %get-tuple-element.153), channel_id=1, source_target_pairs={{0,2},{1,3},{2,0},{3,1},{4,6},{5,7},{6,4},{7,5},{8,10},{9,11},{10,... | collective-permute-start | bytes 196616 | tf_op jit(solution)/shard_map/ppermute | solution.py:257
  181.8 9.0 %collective-permute-start.72 = (bf16[32,1024]{1,0:T(8,128)(2,1)S(1)}, bf16[32,1024]{1,0:T(8,128)(2,1)S(1)}, u32[]{:S(2)}, u32[]{:S(2)}) collective-permute-start(bf16[32,1024]{1,0:T(8,128)(2,1)S(1)} %add_convert_fusion.1), channel_id=1, source_target_pairs={{0,0},{1,8},{2,16},{3,24},{8,1},{9,9},{10,17},{11,25},{16,2},{17,1... | collective-permute-start | bytes 196616 | tf_op jit(solution)/shard_map/ppermute | solution.py:404
  186.6 8.9 %collective-permute-start.82 = (bf16[32,1024]{1,0:T(8,128)(2,1)S(1)}, bf16[32,1024]{1,0:T(8,128)(2,1)S(1)}, u32[]{:S(2)}, u32[]{:S(2)}) collective-permute-start(bf16[32,1024]{1,0:T(8,128)(2,1)S(1)} %add_convert_fusion), channel_id=1, source_target_pairs={{0,0},{1,8},{2,16},{3,24},{8,1},{9,9},{10,17},{11,25},{16,2},{17,1... | collective-permute-start | bytes 196616 | tf_op jit(solution)/shard_map/ppermute | solution.py:404
  (29 other events, 147.7 us)

commit v4 on v3

--- a/solution.py
+++ b/solution.py
@@ -257,12 +257,18 @@
     return lax.ppermute(value, axis, [(i, i ^ by) for i in range(lax.axis_size(axis))])
 
 
+def partners(axis, peers):
+    others = range(1, peers)
+    return [0, *(others if axis == "dp" else reversed(others))]
+
+
 def gather_blocks(block, axis, peers):
-    return [block] + [swapped(block, axis, m) for m in range(1, peers)]
+    return [block] + [swapped(block, axis, m) for m in partners(axis, peers)[1:]]
 
 
 def trade_blocks(blocks, axis):
-    return [blocks[0]] + [swapped(blocks[m], axis, m) for m in range(1, len(blocks))]
+    order = partners(axis, len(blocks))
+    return [blocks[0]] + [swapped(block, axis, m) for block, m in zip(blocks[1:], order[1:])]
 
 
 def total_of(blocks):
@@ -330,10 +336,12 @@
 
     turn = [(i * groups + j, j * groups + i) for i in range(replicas) for j in range(groups)]
     if paired:
-        place = lax.bitwise_xor(jnp.arange(groups, dtype=jnp.int32), lax.bitwise_xor(my_replica, my_group))
+        base = lax.bitwise_xor(my_replica, my_group)
+        place = lax.bitwise_xor(jnp.asarray(partners("tensor", groups), jnp.int32), base)
+        place_out = lax.rem(groups - lax.bitwise_xor(jnp.arange(replicas, dtype=jnp.int32), base), groups)
         blocks = gather_blocks(lax.ppermute(stream, ("dp", "tensor"), turn), "tensor", groups)
     else:
-        place = jnp.zeros((1,), jnp.int32)
+        place = place_out = jnp.zeros((1,), jnp.int32)
         wide = lax.all_gather(stream, "tensor", axis=1, tiled=True)
         blocks = [lax.all_to_all(wide, "dp", split_axis=1, concat_axis=0, tiled=True)]
     part_rows = slots * part_len
@@ -379,7 +387,7 @@
         last = number + 1 == len(layers)
         ends = project_out(
             mixed[h],
-            place if paired and last else None,
+            place_out if paired and last else None,
             weights[number][4],
             groups if paired and last else 1,
             latest,

time: 202 us -> 189 us (0.936)
  starting transfers between devices: 129 us -> 114 us
  waiting for transfers between devices: 38.5 us -> 41.1 us
    ppermute x81, starting transfers between devices: 115 us -> 99.9 us  [swapped(): lax.ppermute(value, axis, [(i, i ^ by) for i in range(lax.axis_size(axis))])]
    ppermute x81, waiting for transfers between devices: 29.5 us -> 33.7 us  [swapped(): lax.ppermute(value, axis, [(i, i ^ by) for i in range(lax.axis_size(axis))])]
  transfers between devices with their start and end apart: 84 -> 84, of which waited for: 17 -> 23; matrix products, arithmetic and copies ran while one was open for 5% -> 5% of each run, Pallas kernels for 9% -> 10%
where the time goes in v4:
time: 189 us
  starting transfers between devices  114 us (60%)
  waiting for transfers between devices  41.1 us (22%)
  Pallas kernels  21 us (11%)
  other arithmetic  9.31 us (5%)
  local copies, waits for them, and re-layouts  3.1 us (2%)
    ppermute x81, starting transfers between devices, swapped(): lax.ppermute(value, axis, [(i, i ^ by) for i in range(lax.axis_size(axis))])  99.9 us
    ppermute x81, waiting for transfers between devices, swapped(): lax.ppermute(value, axis, [(i, i ^ by) for i in range(lax.axis_size(axis))])  33.7 us
    ppermute x2, starting transfers between devices, per_device(): stream = lax.ppermute(stream, ('dp', 'tensor'), turn)  8.88 us
    pallas_call x8, Pallas kernels, attend(): pl.pallas_call(unread(len(after), len(blocks) + 2 * len(before) + 3, part...  8.57 us
    select_n x5, other arithmetic, layer_weights(): jnp.where(my_section == section, mine[index, 0], theirs[index, 0])  7.63 us
    pallas_call x8, Pallas kernels, project_qkv(): pl.pallas_call(unread(len(after), len(arrays) + 5, partial(qkv_kernel, le...  6.39 us
    ppermute x1, starting transfers between devices, per_device(): lax.ppermute(stream, ('dp', 'tensor'), turn)  5.14 us
    pallas_call x8, Pallas kernels, project_out(): pl.pallas_call(unread(len(after), placed + n_in + 1, partial(out_kernel,...  4.67 us
  transfers between devices with their start and end apart: 84, of which 23 were waited for; matrix products, arithmetic and copies ran while one was open for 5% of the time, Pallas kernels for 10%

profile of v4, /device:TPU:7, one launch (start us, length us, event | category | flops | bytes accessed | tf_op | source)
XLA Modules:
  0.0 188.9 jit_solution(6479585374646389760)
XLA Ops:
  5.4 5.1 %collective-permute-start = (bf16[64,1024]{1,0:T(8,128)(2,1)S(1)}, bf16[64,1024]{1,0:T(8,128)(2,1)S(1)}, u32[]{:S(2)}, u32[]{:S(2)}) collective-permute-start(bf16[64,1024]{1,0:T(8,128)(2,1)S(1)} %bitcast.51), channel_id=1, source_target_pairs={{0,0},{1,8},{2,16},{3,24},{8,1},{9,9},{10,17},{11,25},{16,2},{17,1... | collective-permute-start | bytes 393224 | tf_op jit(solution)/shard_map/ppermute | solution.py:342
  12.6 3.3 %collective-permute-done.refs_1_ = bf16[64,1024]{1,0:T(8,128)(2,1)S(1)} collective-permute-done((bf16[64,1024]{1,0:T(8,128)(2,1)S(1)}, bf16[64,1024]{1,0:T(8,128)(2,1)S(1)}, u32[]{:S(2)}, u32[]{:S(2)}) %collective-permute-start) | collective-permute-done | bytes 131104 | tf_op jit(solution)/shard_map/ppermute | solution.py:342
  15.9 1.3 collective-permute-start.3
  17.1 1.6 collective-permute-done.6
  19.0 1.7 select_bitcast_fusion.9
  20.7 1.2 collective-permute-start.1
  22.8 2.5 %select_bitcast_fusion.1 = (bf16[1024,1024]{1,0:T(8,128)(2,1)S(1)}, bf16[1024,1024]{1,0:T(8,128)(2,1)S(1)}, bf16[1024,1024]{1,0:T(8,128)(2,1)S(1)}, bf16[1024,1024]{1,0:T(8,128)(2,1)S(1)}) fusion(pred[]{:T(512)S(6)} %eq.4, bf16[2,1,1024,1024]{3,2,1,0:T(8,128)(2,1)} %collective-permute-done.5, bf16[2,1,1024,1024]{3,2,1,0:T(8,128)(2,1)S(1)} %copy-done.6, pred[]{:T(512)S(6)} %eq.5), kind=kLoop, calls=%fused_computation.1 | loop fusion | flops 4194304 | bytes 16777218 | tf_op jit(solution)/shard_map/jit(_where)/select_n | solution.py:328
  26.6 1.9 %collective-permute-start.8 = (bf16[32,1664]{1,0:T(8,128)(2,1)S(1)}, bf16[32,1664]{1,0:T(8,128)(2,1)S(1)}, u32[]{:S(2)}, u32[]{:S(2)}) collective-permute-start(bf16[32,1664]{1,0:T(8,128)(2,1)S(1)} %get-tuple-element.86), channel_id=1, source_target_pairs={{0,8},{8,0},{16,24},{24,16},{1,9},{9,1},{17,25},{25,17},{2,10},{10... | collective-permute-start | bytes 319496 | tf_op jit(solution)/shard_map/ppermute | solution.py:257
  28.5 1.9 %collective-permute-start.9 = (bf16[32,1664]{1,0:T(8,128)(2,1)S(1)}, bf16[32,1664]{1,0:T(8,128)(2,1)S(1)}, u32[]{:S(2)}, u32[]{:S(2)}) collective-permute-start(bf16[32,1664]{1,0:T(8,128)(2,1)S(1)} %get-tuple-element.87), channel_id=1, source_target_pairs={{0,16},{8,24},{16,0},{24,8},{1,17},{9,25},{17,1},{25,9},{2,18},{10... | collective-permute-start | bytes 319496 | tf_op jit(solution)/shard_map/ppermute | solution.py:257
  31.4 2.7 %select_bitcast_fusion = (bf16[1024,1024]{1,0:T(8,128)(2,1)S(1)}, bf16[1024,1024]{1,0:T(8,128)(2,1)S(1)}, bf16[1024,1024]{1,0:T(8,128)(2,1)S(1)}, bf16[1024,1024]{1,0:T(8,128)(2,1)S(1)}) fusion(pred[]{:T(512)S(6)} %eq.4, bf16[2,1,1024,1024]{3,2,1,0:T(8,128)(2,1)} %collective-permute-done.14, bf16[2,1,1024,1024]{3,2,1,0:T(8,128)(2,1)S(1)} %copy-done.7, pred[]{:T(512)S(6)} %eq.5), kind=kLoop, calls=%fused_computation | loop fusion | flops 4194304 | bytes 16777218 | tf_op jit(solution)/shard_map/jit(_where)/select_n | solution.py:328
  34.2 2.7 %collective-permute-done.10.refs_3_ = bf16[32,1664]{1,0:T(8,128)(2,1)S(1)} collective-permute-done((bf16[32,1664]{1,0:T(8,128)(2,1)S(1)}, bf16[32,1664]{1,0:T(8,128)(2,1)S(1)}, u32[]{:S(2)}, u32[]{:S(2)}) %collective-permute-start.10) | collective-permute-done | bytes 106528 | tf_op jit(solution)/shard_map/ppermute | solution.py:257
  37.9 1.4 collective-permute-start.13
  39.3 2.8 %collective-permute-start.12 = (bf16[32,1024]{1,0:T(8,128)(2,1)S(1)}, bf16[32,1024]{1,0:T(8,128)(2,1)S(1)}, u32[]{:S(2)}, u32[]{:S(2)}) collective-permute-start(bf16[32,1024]{1,0:T(8,128)(2,1)S(1)} %get-tuple-element.91.refs_0_), channel_id=1, source_target_pairs={{0,16},{8,24},{16,0},{24,8},{1,17},{9,25},{17,1},{25,9},{2,18},{10... | collective-permute-start | bytes 196616 | tf_op jit(solution)/shard_map/ppermute | solution.py:257
  43.2 1.5 collective-permute-start.18
  45.7 1.2 collective-permute-start.20
  47.6 1.6 collective-permute-start.16
  49.2 1.4 collective-permute-start.15
  51.0 2.8 %collective-permute-done.20.refs_3_ = bf16[32,1664]{1,0:T(8,128)(2,1)S(1)} collective-permute-done((bf16[32,1664]{1,0:T(8,128)(2,1)S(1)}, bf16[32,1664]{1,0:T(8,128)(2,1)S(1)}, u32[]{:S(2)}, u32[]{:S(2)}) %collective-permute-start.20) | collective-permute-done | bytes 106528 | tf_op jit(solution)/shard_map/ppermute | solution.py:257
  55.0 1.7 collective-permute-start.26
  56.7 3.3 %collective-permute-start.25 = (bf16[32,1024]{1,0:T(8,128)(2,1)S(1)}, bf16[32,1024]{1,0:T(8,128)(2,1)S(1)}, u32[]{:S(2)}, u32[]{:S(2)}) collective-permute-start(bf16[32,1024]{1,0:T(8,128)(2,1)S(1)} %get-tuple-element.106.refs_0_), channel_id=1, source_target_pairs={{0,16},{8,24},{16,0},{24,8},{1,17},{9,25},{17,1},{25,9},{2,18},{10... | collective-permute-start | bytes 196616 | tf_op jit(solution)/shard_map/ppermute | solution.py:257
  60.7 1.5 collective-permute-start.21
  62.2 2.2 %collective-permute-start.23 = (bf16[32,1664]{1,0:T(8,128)(2,1)S(1)}, bf16[32,1664]{1,0:T(8,128)(2,1)S(1)}, u32[]{:S(2)}, u32[]{:S(2)}) collective-permute-start(bf16[32,1664]{1,0:T(8,128)(2,1)S(1)} %get-tuple-element.105), channel_id=1, source_target_pairs={{0,24},{8,16},{16,8},{24,0},{1,25},{9,17},{17,9},{25,1},{2,26},{10... | collective-permute-start | bytes 319496 | tf_op jit(solution)/shard_map/ppermute | solution.py:257
  65.9 1.4 collective-permute-done.21.refs_1_
  68.1 2.8 %collective-permute-done.23.refs_3_ = bf16[32,1664]{1,0:T(8,128)(2,1)S(1)} collective-permute-done((bf16[32,1664]{1,0:T(8,128)(2,1)S(1)}, bf16[32,1664]{1,0:T(8,128)(2,1)S(1)}, u32[]{:S(2)}, u32[]{:S(2)}) %collective-permute-start.23) | collective-permute-done | bytes 106528 | tf_op jit(solution)/shard_map/ppermute | solution.py:257
  71.9 2.2 %collective-permute-start.29 = (bf16[32,1024]{1,0:T(8,128)(2,1)S(1)}, bf16[32,1024]{1,0:T(8,128)(2,1)S(1)}, u32[]{:S(2)}, u32[]{:S(2)}) collective-permute-start(bf16[32,1024]{1,0:T(8,128)(2,1)S(1)} %get-tuple-element.107.refs_0_), channel_id=1, source_target_pairs={{0,24},{8,16},{16,8},{24,0},{1,25},{9,17},{17,9},{25,1},{2,26},{10... | collective-permute-start | bytes 196616 | tf_op jit(solution)/shard_map/ppermute | solution.py:257
  74.1 2.4 %collective-permute-start.28 = (bf16[32,1024]{1,0:T(8,128)(2,1)S(1)}, bf16[32,1024]{1,0:T(8,128)(2,1)S(1)}, u32[]{:S(2)}, u32[]{:S(2)}) collective-permute-start(bf16[32,1024]{1,0:T(8,128)(2,1)S(1)} %get-tuple-element.107.refs_0_), channel_id=1, source_target_pairs={{0,16},{8,24},{16,0},{24,8},{1,17},{9,25},{17,1},{25,9},{2,18},{10... | collective-permute-start | bytes 196616 | tf_op jit(solution)/shard_map/ppermute | solution.py:257
  77.2 1.5 collective-permute-start.36
  79.3 1.6 collective-permute-start.38
  81.5 1.4 collective-permute-start.34
  83.0 1.7 collective-permute-start.33
  85.2 2.5 %collective-permute-done.38.refs_3_ = bf16[32,1664]{1,0:T(8,128)(2,1)S(1)} collective-permute-done((bf16[32,1664]{1,0:T(8,128)(2,1)S(1)}, bf16[32,1664]{1,0:T(8,128)(2,1)S(1)}, u32[]{:S(2)}, u32[]{:S(2)}) %collective-permute-start.38) | collective-permute-done | bytes 106528 | tf_op jit(solution)/shard_map/ppermute | solution.py:257
  88.8 1.6 collective-permute-start.44
  90.4 3.2 %collective-permute-start.43 = (bf16[32,1024]{1,0:T(8,128)(2,1)S(1)}, bf16[32,1024]{1,0:T(8,128)(2,1)S(1)}, u32[]{:S(2)}, u32[]{:S(2)}) collective-permute-start(bf16[32,1024]{1,0:T(8,128)(2,1)S(1)} %get-tuple-element.121.refs_0_), channel_id=1, source_target_pairs={{0,16},{8,24},{16,0},{24,8},{1,17},{9,25},{17,1},{25,9},{2,18},{10... | collective-permute-start | bytes 196616 | tf_op jit(solution)/shard_map/ppermute | solution.py:257
  94.4 1.5 collective-permute-start.39
  96.2 1.8 collective-permute-start.41
  99.6 1.6 collective-permute-start.48
  101.9 2.8 %collective-permute-done.41.refs_3_ = bf16[32,1664]{1,0:T(8,128)(2,1)S(1)} collective-permute-done((bf16[32,1664]{1,0:T(8,128)(2,1)S(1)}, bf16[32,1664]{1,0:T(8,128)(2,1)S(1)}, u32[]{:S(2)}, u32[]{:S(2)}) %collective-permute-start.41) | collective-permute-done | bytes 106528 | tf_op jit(solution)/shard_map/ppermute | solution.py:257
  105.6 2.2 %collective-permute-start.47 = (bf16[32,1024]{1,0:T(8,128)(2,1)S(1)}, bf16[32,1024]{1,0:T(8,128)(2,1)S(1)}, u32[]{:S(2)}, u32[]{:S(2)}) collective-permute-start(bf16[32,1024]{1,0:T(8,128)(2,1)S(1)} %get-tuple-element.122.refs_0_), channel_id=1, source_target_pairs={{0,24},{8,16},{16,8},{24,0},{1,25},{9,17},{17,9},{25,1},{2,26},{10... | collective-permute-start | bytes 196616 | tf_op jit(solution)/shard_map/ppermute | solution.py:257
  107.8 2.4 %collective-permute-start.46 = (bf16[32,1024]{1,0:T(8,128)(2,1)S(1)}, bf16[32,1024]{1,0:T(8,128)(2,1)S(1)}, u32[]{:S(2)}, u32[]{:S(2)}) collective-permute-start(bf16[32,1024]{1,0:T(8,128)(2,1)S(1)} %get-tuple-element.122.refs_0_), channel_id=1, source_target_pairs={{0,16},{8,24},{16,0},{24,8},{1,17},{9,25},{17,1},{25,9},{2,18},{10... | collective-permute-start | bytes 196616 | tf_op jit(solution)/shard_map/ppermute | solution.py:257
  110.9 1.5 collective-permute-start.54
  113.0 1.6 collective-permute-start.56
  115.2 1.5 collective-permute-start.52
  119.0 2.4 %collective-permute-done.56.refs_3_ = bf16[32,1664]{1,0:T(8,128)(2,1)S(1)} collective-permute-done((bf16[32,1664]{1,0:T(8,128)(2,1)S(1)}, bf16[32,1664]{1,0:T(8,128)(2,1)S(1)}, u32[]{:S(2)}, u32[]{:S(2)}) %collective-permute-start.56) | collective-permute-done | bytes 106528 | tf_op jit(solution)/shard_map/ppermute | solution.py:257
  122.5 1.7 collective-permute-start.62
  124.2 3.2 %collective-permute-start.61 = (bf16[32,1024]{1,0:T(8,128)(2,1)S(1)}, bf16[32,1024]{1,0:T(8,128)(2,1)S(1)}, u32[]{:S(2)}, u32[]{:S(2)}) collective-permute-start(bf16[32,1024]{1,0:T(8,128)(2,1)S(1)} %get-tuple-element.136.refs_0_), channel_id=1, source_target_pairs={{0,16},{8,24},{16,0},{24,8},{1,17},{9,25},{17,1},{25,9},{2,18},{10... | collective-permute-start | bytes 196616 | tf_op jit(solution)/shard_map/ppermute | solution.py:257
  128.1 1.5 collective-permute-start.57
  130.0 1.9 collective-permute-start.59
  133.4 1.6 collective-permute-start.66
  135.6 2.7 %collective-permute-done.59.refs_3_ = bf16[32,1664]{1,0:T(8,128)(2,1)S(1)} collective-permute-done((bf16[32,1664]{1,0:T(8,128)(2,1)S(1)}, bf16[32,1664]{1,0:T(8,128)(2,1)S(1)}, u32[]{:S(2)}, u32[]{:S(2)}) %collective-permute-start.59) | collective-permute-done | bytes 106528 | tf_op jit(solution)/shard_map/ppermute | solution.py:257
  139.4 2.4 %collective-permute-start.65 = (bf16[32,1024]{1,0:T(8,128)(2,1)S(1)}, bf16[32,1024]{1,0:T(8,128)(2,1)S(1)}, u32[]{:S(2)}, u32[]{:S(2)}) collective-permute-start(bf16[32,1024]{1,0:T(8,128)(2,1)S(1)} %get-tuple-element.137.refs_1_), channel_id=1, source_target_pairs={{0,24},{8,16},{16,8},{24,0},{1,25},{9,17},{17,9},{25,1},{2,26},{10... | collective-permute-start | bytes 196616 | tf_op jit(solution)/shard_map/ppermute | solution.py:257
  141.8 2.4 %collective-permute-start.64 = (bf16[32,1024]{1,0:T(8,128)(2,1)S(1)}, bf16[32,1024]{1,0:T(8,128)(2,1)S(1)}, u32[]{:S(2)}, u32[]{:S(2)}) collective-permute-start(bf16[32,1024]{1,0:T(8,128)(2,1)S(1)} %get-tuple-element.137.refs_1_), channel_id=1, source_target_pairs={{0,16},{8,24},{16,0},{24,8},{1,17},{9,25},{17,1},{25,9},{2,18},{10... | collective-permute-start | bytes 196616 | tf_op jit(solution)/shard_map/ppermute | solution.py:257
  144.9 1.5 collective-permute-start.73
  147.0 1.6 collective-permute-start.75
  149.6 3.3 %collective-permute-done.74.refs_2_ = bf16[32,1664]{1,0:T(8,128)(2,1)S(1)} collective-permute-done((bf16[32,1664]{1,0:T(8,128)(2,1)S(1)}, bf16[32,1664]{1,0:T(8,128)(2,1)S(1)}, u32[]{:S(2)}, u32[]{:S(2)}) %collective-permute-start.74) | collective-permute-done | bytes 106528 | tf_op jit(solution)/shard_map/ppermute | solution.py:257
  153.0 2.3 %collective-permute-done.75.refs_3_ = bf16[32,1664]{1,0:T(8,128)(2,1)S(1)} collective-permute-done((bf16[32,1664]{1,0:T(8,128)(2,1)S(1)}, bf16[32,1664]{1,0:T(8,128)(2,1)S(1)}, u32[]{:S(2)}, u32[]{:S(2)}) %collective-permute-start.75) | collective-permute-done | bytes 106528 | tf_op jit(solution)/shard_map/ppermute | solution.py:257
  155.3 1.2 attend.15
  156.5 1.7 collective-permute-start.78
  158.2 2.9 %collective-permute-start.77 = (bf16[32,1024]{1,0:T(8,128)(2,1)S(1)}, bf16[32,1024]{1,0:T(8,128)(2,1)S(1)}, u32[]{:S(2)}, u32[]{:S(2)}) collective-permute-start(bf16[32,1024]{1,0:T(8,128)(2,1)S(1)} %get-tuple-element.149.refs_1_), channel_id=1, source_target_pairs={{0,16},{8,24},{16,0},{24,8},{1,17},{9,25},{17,1},{25,9},{2,18},{10... | collective-permute-start | bytes 196616 | tf_op jit(solution)/shard_map/ppermute | solution.py:257
  162.4 1.5 collective-permute-start.71
  166.5 1.5 collective-permute-start.81
  168.0 4.3 %collective-permute-start.72 = (bf16[32,1024]{1,0:T(8,128)(2,1)S(1)}, bf16[32,1024]{1,0:T(8,128)(2,1)S(1)}, u32[]{:S(2)}, u32[]{:S(2)}) collective-permute-start(bf16[32,1024]{1,0:T(8,128)(2,1)S(1)} %add_convert_fusion.1), channel_id=1, source_target_pairs={{0,0},{1,8},{2,16},{3,24},{8,1},{9,9},{10,17},{11,25},{16,2},{17,1... | collective-permute-start | bytes 196616 | tf_op jit(solution)/shard_map/ppermute | solution.py:412
  172.4 4.5 %collective-permute-start.82 = (bf16[32,1024]{1,0:T(8,128)(2,1)S(1)}, bf16[32,1024]{1,0:T(8,128)(2,1)S(1)}, u32[]{:S(2)}, u32[]{:S(2)}) collective-permute-start(bf16[32,1024]{1,0:T(8,128)(2,1)S(1)} %add_convert_fusion), channel_id=1, source_target_pairs={{0,0},{1,8},{2,16},{3,24},{8,1},{9,9},{10,17},{11,25},{16,2},{17,1... | collective-permute-start | bytes 196616 | tf_op jit(solution)/shard_map/ppermute | solution.py:412
  177.0 4.1 %collective-permute-done.82 = bf16[32,1024]{1,0:T(8,128)(2,1)S(1)} collective-permute-done((bf16[32,1024]{1,0:T(8,128)(2,1)S(1)}, bf16[32,1024]{1,0:T(8,128)(2,1)S(1)}, u32[]{:S(2)}, u32[]{:S(2)}) %collective-permute-start.82) | collective-permute-done | bytes 65568 | tf_op jit(solution)/shard_map/ppermute | solution.py:412
  181.1 6.2 %collective-permute-start.83 = (bf16[1,32,1024]{2,1,0:T(8,128)(2,1)S(1)}, bf16[1,32,1024]{2,1,0:T(8,128)(2,1)S(1)}, u32[]{:S(2)}, u32[]{:S(2)}) collective-permute-start(bf16[1,32,1024]{2,1,0:T(8,128)(2,1)S(1)} %select_bitcast_fusion.16), channel_id=1, source_target_pairs={{0,4},{4,0},{1,5},{5,1},{2,6},{6,2},{3,7},{7,3},{8,12},{12,8},{9,1... | collective-permute-start | bytes 196616 | tf_op jit(solution)/shard_map/ppermute | solution.py:257
  (165 shorter events, 45.2 us)
Async XLA Ops:
  2.2 19.9 %collective-permute-start.5 = (bf16[2,1,1024,1024]{3,2,1,0:T(8,128)(2,1)}, bf16[2,1,1024,1024]{3,2,1,0:T(8,128)(2,1)}, u32[]{:S(2)}, u32[]{:S(2)}) collective-permute-start(bf16[2,1,1024,1024]{3,2,1,0:T(8,128)(2,1)} %param.12), channel_id=1, source_target_pairs={{0,4},{4,0},{1,5},{5,1},{2,6},{6,2},{3,7},{7,3},{8,12},{12,8},{9,1... | collective-permute-start | bytes 12582920 | tf_op jit(solution)/shard_map/ppermute | solution.py:257
  2.5 28.8 %collective-permute-start.14 = (bf16[2,1,1024,1024]{3,2,1,0:T(8,128)(2,1)}, bf16[2,1,1024,1024]{3,2,1,0:T(8,128)(2,1)}, u32[]{:S(2)}, u32[]{:S(2)}) collective-permute-start(bf16[2,1,1024,1024]{3,2,1,0:T(8,128)(2,1)} %param.15), channel_id=1, source_target_pairs={{0,4},{4,0},{1,5},{5,1},{2,6},{6,2},{3,7},{7,3},{8,12},{12,8},{9,1... | collective-permute-start | bytes 12582920 | tf_op jit(solution)/shard_map/ppermute | solution.py:257
  2.7 16.0 %collective-permute-start.6 = (bf16[2,1,1024,256]{3,2,1,0:T(8,128)(2,1)}, bf16[2,1,1024,256]{3,2,1,0:T(8,128)(2,1)}, u32[]{:S(2)}, u32[]{:S(2)}) collective-permute-start(bf16[2,1,1024,256]{3,2,1,0:T(8,128)(2,1)} %param.13), channel_id=1, source_target_pairs={{0,4},{4,0},{1,5},{5,1},{2,6},{6,2},{3,7},{7,3},{8,12},{12,8},{9,1... | collective-permute-start | bytes 3145736 | tf_op jit(solution)/shard_map/ppermute | solution.py:257
  5.4 10.5 %collective-permute-start = (bf16[64,1024]{1,0:T(8,128)(2,1)S(1)}, bf16[64,1024]{1,0:T(8,128)(2,1)S(1)}, u32[]{:S(2)}, u32[]{:S(2)}) collective-permute-start(bf16[64,1024]{1,0:T(8,128)(2,1)S(1)} %bitcast.51), channel_id=1, source_target_pairs={{0,0},{1,8},{2,16},{3,24},{8,1},{9,9},{10,17},{11,25},{16,2},{17,1... | collective-permute-start | bytes 393224 | tf_op jit(solution)/shard_map/ppermute | solution.py:342
  10.6 10.1 %collective-permute-start.7 = (bf16[2,1,1024,256]{3,2,1,0:T(8,128)(2,1)}, bf16[2,1,1024,256]{3,2,1,0:T(8,128)(2,1)S(1)}, u32[]{:S(2)}, u32[]{:S(2)}) collective-permute-start(bf16[2,1,1024,256]{3,2,1,0:T(8,128)(2,1)} %param.14), channel_id=1, source_target_pairs={{0,4},{4,0},{1,5},{5,1},{2,6},{6,2},{3,7},{7,3},{8,12},{12,8},{9,1... | collective-permute-start | bytes 3145736 | tf_op jit(solution)/shard_map/ppermute | solution.py:257
  15.9 9.4 %collective-permute-start.3 = (bf16[64,1024]{1,0:T(8,128)(2,1)S(1)}, bf16[64,1024]{1,0:T(8,128)(2,1)S(1)}, u32[]{:S(2)}, u32[]{:S(2)}) collective-permute-start(bf16[64,1024]{1,0:T(8,128)(2,1)S(1)} %collective-permute-done.refs_1_), channel_id=1, source_target_pairs={{0,1},{1,0},{2,3},{3,2},{4,5},{5,4},{6,7},{7,6},{8,9},{9,8},{10,11... | collective-permute-start | bytes 393224 | tf_op jit(solution)/shard_map/ppermute | solution.py:257
  18.7 6.6 %collective-permute-start.2 = (bf16[64,1024]{1,0:T(8,128)(2,1)S(1)}, bf16[64,1024]{1,0:T(8,128)(2,1)S(1)}, u32[]{:S(2)}, u32[]{:S(2)}) collective-permute-start(bf16[64,1024]{1,0:T(8,128)(2,1)S(1)} %collective-permute-done.refs_1_), channel_id=1, source_target_pairs={{0,2},{1,3},{2,0},{3,1},{4,6},{5,7},{6,4},{7,5},{8,10},{9,11},{10,... | collective-permute-start | bytes 393224 | tf_op jit(solution)/shard_map/ppermute | solution.py:257
  26.6 7.5 %collective-permute-start.8 = (bf16[32,1664]{1,0:T(8,128)(2,1)S(1)}, bf16[32,1664]{1,0:T(8,128)(2,1)S(1)}, u32[]{:S(2)}, u32[]{:S(2)}) collective-permute-start(bf16[32,1664]{1,0:T(8,128)(2,1)S(1)} %get-tuple-element.86), channel_id=1, source_target_pairs={{0,8},{8,0},{16,24},{24,16},{1,9},{9,1},{17,25},{25,17},{2,10},{10... | collective-permute-start | bytes 319496 | tf_op jit(solution)/shard_map/ppermute | solution.py:257
  30.4 6.5 %collective-permute-start.10 = (bf16[32,1664]{1,0:T(8,128)(2,1)S(1)}, bf16[32,1664]{1,0:T(8,128)(2,1)S(1)}, u32[]{:S(2)}, u32[]{:S(2)}) collective-permute-start(bf16[32,1664]{1,0:T(8,128)(2,1)S(1)} %get-tuple-element.88), channel_id=1, source_target_pairs={{0,24},{8,16},{16,8},{24,0},{1,25},{9,17},{17,9},{25,1},{2,26},{10... | collective-permute-start | bytes 319496 | tf_op jit(solution)/shard_map/ppermute | solution.py:257
  37.9 7.8 %collective-permute-start.13 = (bf16[32,1024]{1,0:T(8,128)(2,1)S(1)}, bf16[32,1024]{1,0:T(8,128)(2,1)S(1)}, u32[]{:S(2)}, u32[]{:S(2)}) collective-permute-start(bf16[32,1024]{1,0:T(8,128)(2,1)S(1)} %get-tuple-element.91.refs_0_), channel_id=1, source_target_pairs={{0,24},{8,16},{16,8},{24,0},{1,25},{9,17},{17,9},{25,1},{2,26},{10... | collective-permute-start | bytes 196616 | tf_op jit(solution)/shard_map/ppermute | solution.py:257
  39.3 7.7 %collective-permute-start.12 = (bf16[32,1024]{1,0:T(8,128)(2,1)S(1)}, bf16[32,1024]{1,0:T(8,128)(2,1)S(1)}, u32[]{:S(2)}, u32[]{:S(2)}) collective-permute-start(bf16[32,1024]{1,0:T(8,128)(2,1)S(1)} %get-tuple-element.91.refs_0_), channel_id=1, source_target_pairs={{0,16},{8,24},{16,0},{24,8},{1,17},{9,25},{17,1},{25,9},{2,18},{10... | collective-permute-start | bytes 196616 | tf_op jit(solution)/shard_map/ppermute | solution.py:257
  43.2 5.9 %collective-permute-start.18 = (bf16[32,1664]{1,0:T(8,128)(2,1)S(1)}, bf16[32,1664]{1,0:T(8,128)(2,1)S(1)}, u32[]{:S(2)}, u32[]{:S(2)}) collective-permute-start(bf16[32,1664]{1,0:T(8,128)(2,1)S(1)} %get-tuple-element.96), channel_id=1, source_target_pairs={{0,8},{8,0},{16,24},{24,16},{1,9},{9,1},{17,25},{25,17},{2,10},{10... | collective-permute-start | bytes 319496 | tf_op jit(solution)/shard_map/ppermute | solution.py:257
  44.8 6.2 %collective-permute-start.19 = (bf16[32,1664]{1,0:T(8,128)(2,1)S(1)}, bf16[32,1664]{1,0:T(8,128)(2,1)S(1)}, u32[]{:S(2)}, u32[]{:S(2)}) collective-permute-start(bf16[32,1664]{1,0:T(8,128)(2,1)S(1)} %get-tuple-element.97), channel_id=1, source_target_pairs={{0,16},{8,24},{16,0},{24,8},{1,17},{9,25},{17,1},{25,9},{2,18},{10... | collective-permute-start | bytes 319496 | tf_op jit(solution)/shard_map/ppermute | solution.py:257
  45.7 8.1 %collective-permute-start.20 = (bf16[32,1664]{1,0:T(8,128)(2,1)S(1)}, bf16[32,1664]{1,0:T(8,128)(2,1)S(1)}, u32[]{:S(2)}, u32[]{:S(2)}) collective-permute-start(bf16[32,1664]{1,0:T(8,128)(2,1)S(1)} %get-tuple-element.98), channel_id=1, source_target_pairs={{0,24},{8,16},{16,8},{24,0},{1,25},{9,17},{17,9},{25,1},{2,26},{10... | collective-permute-start | bytes 319496 | tf_op jit(solution)/shard_map/ppermute | solution.py:257
  47.4 12.6 %collective-permute-start.17 = (bf16[128,1024]{1,0:T(8,128)(2,1)S(1)}, bf16[128,1024]{1,0:T(8,128)(2,1)S(1)}, u32[]{:S(2)}, u32[]{:S(2)}) collective-permute-start(bf16[128,1024]{1,0:T(8,128)(2,1)S(1)} %project_out.8.refs_9_.refs_1_), channel_id=1, source_target_pairs={{0,1},{1,0},{2,3},{3,2},{4,5},{5,4},{6,7},{7,6},{8,9},{9,8},{10,11... | collective-permute-start | bytes 786440 | tf_op jit(solution)/shard_map/ppermute | solution.py:257
  47.6 12.4 %collective-permute-start.16 = (bf16[128,1024]{1,0:T(8,128)(2,1)S(1)}, bf16[128,1024]{1,0:T(8,128)(2,1)S(1)}, u32[]{:S(2)}, u32[]{:S(2)}) collective-permute-start(bf16[128,1024]{1,0:T(8,128)(2,1)S(1)} %project_out.8.refs_9_.refs_1_), channel_id=1, source_target_pairs={{0,2},{1,3},{2,0},{3,1},{4,6},{5,7},{6,4},{7,5},{8,10},{9,11},{10,... | collective-permute-start | bytes 786440 | tf_op jit(solution)/shard_map/ppermute | solution.py:257
  49.2 10.8 %collective-permute-start.15 = (bf16[128,1024]{1,0:T(8,128)(2,1)S(1)}, bf16[128,1024]{1,0:T(8,128)(2,1)S(1)}, u32[]{:S(2)}, u32[]{:S(2)}) collective-permute-start(bf16[128,1024]{1,0:T(8,128)(2,1)S(1)} %project_out.8.refs_9_.refs_1_), channel_id=1, source_target_pairs={{0,3},{1,2},{2,1},{3,0},{4,7},{5,6},{6,5},{7,4},{8,11},{9,10},{10,... | collective-permute-start | bytes 786440 | tf_op jit(solution)/shard_map/ppermute | solution.py:257
  55.0 7.2 %collective-permute-start.26 = (bf16[32,1024]{1,0:T(8,128)(2,1)S(1)}, bf16[32,1024]{1,0:T(8,128)(2,1)S(1)}, u32[]{:S(2)}, u32[]{:S(2)}) collective-permute-start(bf16[32,1024]{1,0:T(8,128)(2,1)S(1)} %get-tuple-element.106.refs_0_), channel_id=1, source_target_pairs={{0,24},{8,16},{16,8},{24,0},{1,25},{9,17},{17,9},{25,1},{2,26},{10... | collective-permute-start | bytes 196616 | tf_op jit(solution)/shard_map/ppermute | solution.py:257
  56.7 7.7 %collective-permute-start.25 = (bf16[32,1024]{1,0:T(8,128)(2,1)S(1)}, bf16[32,1024]{1,0:T(8,128)(2,1)S(1)}, u32[]{:S(2)}, u32[]{:S(2)}) collective-permute-start(bf16[32,1024]{1,0:T(8,128)(2,1)S(1)} %get-tuple-element.106.refs_0_), channel_id=1, source_target_pairs={{0,16},{8,24},{16,0},{24,8},{1,17},{9,25},{17,1},{25,9},{2,18},{10... | collective-permute-start | bytes 196616 | tf_op jit(solution)/shard_map/ppermute | solution.py:257
  60.7 6.7 %collective-permute-start.21 = (bf16[32,1664]{1,0:T(8,128)(2,1)S(1)}, bf16[32,1664]{1,0:T(8,128)(2,1)S(1)}, u32[]{:S(2)}, u32[]{:S(2)}) collective-permute-start(bf16[32,1664]{1,0:T(8,128)(2,1)S(1)} %get-tuple-element.103), channel_id=1, source_target_pairs={{0,8},{8,0},{16,24},{24,16},{1,9},{9,1},{17,25},{25,17},{2,10},{10... | collective-permute-start | bytes 319496 | tf_op jit(solution)/shard_map/ppermute | solution.py:257
  62.2 5.9 %collective-permute-start.22 = (bf16[32,1664]{1,0:T(8,128)(2,1)S(1)}, bf16[32,1664]{1,0:T(8,128)(2,1)S(1)}, u32[]{:S(2)}, u32[]{:S(2)}) collective-permute-start(bf16[32,1664]{1,0:T(8,128)(2,1)S(1)} %get-tuple-element.104), channel_id=1, source_target_pairs={{0,16},{8,24},{16,0},{24,8},{1,17},{9,25},{17,1},{25,9},{2,18},{10... | collective-permute-start | bytes 319496 | tf_op jit(solution)/shard_map/ppermute | solution.py:257
  62.2 8.7 %collective-permute-start.23 = (bf16[32,1664]{1,0:T(8,128)(2,1)S(1)}, bf16[32,1664]{1,0:T(8,128)(2,1)S(1)}, u32[]{:S(2)}, u32[]{:S(2)}) collective-permute-start(bf16[32,1664]{1,0:T(8,128)(2,1)S(1)} %get-tuple-element.105), channel_id=1, source_target_pairs={{0,24},{8,16},{16,8},{24,0},{1,25},{9,17},{17,9},{25,1},{2,26},{10... | collective-permute-start | bytes 319496 | tf_op jit(solution)/shard_map/ppermute | solution.py:257
  64.8 11.7 %collective-permute-start.32 = (bf16[128,1024]{1,0:T(8,128)(2,1)S(1)}, bf16[128,1024]{1,0:T(8,128)(2,1)S(1)}, u32[]{:S(2)}, u32[]{:S(2)}) collective-permute-start(bf16[128,1024]{1,0:T(8,128)(2,1)S(1)} %project_out.9.refs_7_.refs_1_), channel_id=1, source_target_pairs={{0,1},{1,0},{2,3},{3,2},{4,5},{5,4},{6,7},{7,6},{8,9},{9,8},{10,11... | collective-permute-start | bytes 786440 | tf_op jit(solution)/shard_map/ppermute | solution.py:257
  65.1 11.4 %collective-permute-start.31 = (bf16[128,1024]{1,0:T(8,128)(2,1)S(1)}, bf16[128,1024]{1,0:T(8,128)(2,1)S(1)}, u32[]{:S(2)}, u32[]{:S(2)}) collective-permute-start(bf16[128,1024]{1,0:T(8,128)(2,1)S(1)} %project_out.9.refs_7_.refs_1_), channel_id=1, source_target_pairs={{0,2},{1,3},{2,0},{3,1},{4,6},{5,7},{6,4},{7,5},{8,10},{9,11},{10,... | collective-permute-start | bytes 786440 | tf_op jit(solution)/shard_map/ppermute | solution.py:257
  67.4 9.1 %collective-permute-start.30 = (bf16[128,1024]{1,0:T(8,128)(2,1)S(1)}, bf16[128,1024]{1,0:T(8,128)(2,1)S(1)}, u32[]{:S(2)}, u32[]{:S(2)}) collective-permute-start(bf16[128,1024]{1,0:T(8,128)(2,1)S(1)} %project_out.9.refs_7_.refs_1_), channel_id=1, source_target_pairs={{0,3},{1,2},{2,1},{3,0},{4,7},{5,6},{6,5},{7,4},{8,11},{9,10},{10,... | collective-permute-start | bytes 786440 | tf_op jit(solution)/shard_map/ppermute | solution.py:257
  71.9 7.4 %collective-permute-start.29 = (bf16[32,1024]{1,0:T(8,128)(2,1)S(1)}, bf16[32,1024]{1,0:T(8,128)(2,1)S(1)}, u32[]{:S(2)}, u32[]{:S(2)}) collective-permute-start(bf16[32,1024]{1,0:T(8,128)(2,1)S(1)} %get-tuple-element.107.refs_0_), channel_id=1, source_target_pairs={{0,24},{8,16},{16,8},{24,0},{1,25},{9,17},{17,9},{25,1},{2,26},{10... | collective-permute-start | bytes 196616 | tf_op jit(solution)/shard_map/ppermute | solution.py:257
  74.1 6.8 %collective-permute-start.28 = (bf16[32,1024]{1,0:T(8,128)(2,1)S(1)}, bf16[32,1024]{1,0:T(8,128)(2,1)S(1)}, u32[]{:S(2)}, u32[]{:S(2)}) collective-permute-start(bf16[32,1024]{1,0:T(8,128)(2,1)S(1)} %get-tuple-element.107.refs_0_), channel_id=1, source_target_pairs={{0,16},{8,24},{16,0},{24,8},{1,17},{9,25},{17,1},{25,9},{2,18},{10... | collective-permute-start | bytes 196616 | tf_op jit(solution)/shard_map/ppermute | solution.py:257
  78.7 6.5 %collective-permute-start.37 = (bf16[32,1664]{1,0:T(8,128)(2,1)S(1)}, bf16[32,1664]{1,0:T(8,128)(2,1)S(1)}, u32[]{:S(2)}, u32[]{:S(2)}) collective-permute-start(bf16[32,1664]{1,0:T(8,128)(2,1)S(1)} %get-tuple-element.112), channel_id=1, source_target_pairs={{0,16},{8,24},{16,0},{24,8},{1,17},{9,25},{17,1},{25,9},{2,18},{10... | collective-permute-start | bytes 319496 | tf_op jit(solution)/shard_map/ppermute | solution.py:257
  79.3 8.4 %collective-permute-start.38 = (bf16[32,1664]{1,0:T(8,128)(2,1)S(1)}, bf16[32,1664]{1,0:T(8,128)(2,1)S(1)}, u32[]{:S(2)}, u32[]{:S(2)}) collective-permute-start(bf16[32,1664]{1,0:T(8,128)(2,1)S(1)} %get-tuple-element.113), channel_id=1, source_target_pairs={{0,24},{8,16},{16,8},{24,0},{1,25},{9,17},{17,9},{25,1},{2,26},{10... | collective-permute-start | bytes 319496 | tf_op jit(solution)/shard_map/ppermute | solution.py:257
  81.3 12.3 %collective-permute-start.35 = (bf16[128,1024]{1,0:T(8,128)(2,1)S(1)}, bf16[128,1024]{1,0:T(8,128)(2,1)S(1)}, u32[]{:S(2)}, u32[]{:S(2)}) collective-permute-start(bf16[128,1024]{1,0:T(8,128)(2,1)S(1)} %project_out.10.refs_9_.refs_1_), channel_id=1, source_target_pairs={{0,1},{1,0},{2,3},{3,2},{4,5},{5,4},{6,7},{7,6},{8,9},{9,8},{10,11... | collective-permute-start | bytes 786440 | tf_op jit(solution)/shard_map/ppermute | solution.py:257
  81.5 12.1 %collective-permute-start.34 = (bf16[128,1024]{1,0:T(8,128)(2,1)S(1)}, bf16[128,1024]{1,0:T(8,128)(2,1)S(1)}, u32[]{:S(2)}, u32[]{:S(2)}) collective-permute-start(bf16[128,1024]{1,0:T(8,128)(2,1)S(1)} %project_out.10.refs_9_.refs_1_), channel_id=1, source_target_pairs={{0,2},{1,3},{2,0},{3,1},{4,6},{5,7},{6,4},{7,5},{8,10},{9,11},{10,... | collective-permute-start | bytes 786440 | tf_op jit(solution)/shard_map/ppermute | solution.py:257
  83.0 10.7 %collective-permute-start.33 = (bf16[128,1024]{1,0:T(8,128)(2,1)S(1)}, bf16[128,1024]{1,0:T(8,128)(2,1)S(1)}, u32[]{:S(2)}, u32[]{:S(2)}) collective-permute-start(bf16[128,1024]{1,0:T(8,128)(2,1)S(1)} %project_out.10.refs_9_.refs_1_), channel_id=1, source_target_pairs={{0,3},{1,2},{2,1},{3,0},{4,7},{5,6},{6,5},{7,4},{8,11},{9,10},{10,... | collective-permute-start | bytes 786440 | tf_op jit(solution)/shard_map/ppermute | solution.py:257
  88.8 7.4 %collective-permute-start.44 = (bf16[32,1024]{1,0:T(8,128)(2,1)S(1)}, bf16[32,1024]{1,0:T(8,128)(2,1)S(1)}, u32[]{:S(2)}, u32[]{:S(2)}) collective-permute-start(bf16[32,1024]{1,0:T(8,128)(2,1)S(1)} %get-tuple-element.121.refs_0_), channel_id=1, source_target_pairs={{0,24},{8,16},{16,8},{24,0},{1,25},{9,17},{17,9},{25,1},{2,26},{10... | collective-permute-start | bytes 196616 | tf_op jit(solution)/shard_map/ppermute | solution.py:257
  90.4 7.6 %collective-permute-start.43 = (bf16[32,1024]{1,0:T(8,128)(2,1)S(1)}, bf16[32,1024]{1,0:T(8,128)(2,1)S(1)}, u32[]{:S(2)}, u32[]{:S(2)}) collective-permute-start(bf16[32,1024]{1,0:T(8,128)(2,1)S(1)} %get-tuple-element.121.refs_0_), channel_id=1, source_target_pairs={{0,16},{8,24},{16,0},{24,8},{1,17},{9,25},{17,1},{25,9},{2,18},{10... | collective-permute-start | bytes 196616 | tf_op jit(solution)/shard_map/ppermute | solution.py:257
  95.9 6.0 %collective-permute-start.40 = (bf16[32,1664]{1,0:T(8,128)(2,1)S(1)}, bf16[32,1664]{1,0:T(8,128)(2,1)S(1)}, u32[]{:S(2)}, u32[]{:S(2)}) collective-permute-start(bf16[32,1664]{1,0:T(8,128)(2,1)S(1)} %get-tuple-element.119), channel_id=1, source_target_pairs={{0,16},{8,24},{16,0},{24,8},{1,17},{9,25},{17,1},{25,9},{2,18},{10... | collective-permute-start | bytes 319496 | tf_op jit(solution)/shard_map/ppermute | solution.py:257
  96.2 8.4 %collective-permute-start.41 = (bf16[32,1664]{1,0:T(8,128)(2,1)S(1)}, bf16[32,1664]{1,0:T(8,128)(2,1)S(1)}, u32[]{:S(2)}, u32[]{:S(2)}) collective-permute-start(bf16[32,1664]{1,0:T(8,128)(2,1)S(1)} %get-tuple-element.120), channel_id=1, source_target_pairs={{0,24},{8,16},{16,8},{24,0},{1,25},{9,17},{17,9},{25,1},{2,26},{10... | collective-permute-start | bytes 319496 | tf_op jit(solution)/shard_map/ppermute | solution.py:257
  98.5 11.7 %collective-permute-start.50 = (bf16[128,1024]{1,0:T(8,128)(2,1)S(1)}, bf16[128,1024]{1,0:T(8,128)(2,1)S(1)}, u32[]{:S(2)}, u32[]{:S(2)}) collective-permute-start(bf16[128,1024]{1,0:T(8,128)(2,1)S(1)} %project_out.11.refs_7_.refs_1_), channel_id=1, source_target_pairs={{0,1},{1,0},{2,3},{3,2},{4,5},{5,4},{6,7},{7,6},{8,9},{9,8},{10,11... | collective-permute-start | bytes 786440 | tf_op jit(solution)/shard_map/ppermute | solution.py:257
  98.8 11.5 %collective-permute-start.49 = (bf16[128,1024]{1,0:T(8,128)(2,1)S(1)}, bf16[128,1024]{1,0:T(8,128)(2,1)S(1)}, u32[]{:S(2)}, u32[]{:S(2)}) collective-permute-start(bf16[128,1024]{1,0:T(8,128)(2,1)S(1)} %project_out.11.refs_7_.refs_1_), channel_id=1, source_target_pairs={{0,2},{1,3},{2,0},{3,1},{4,6},{5,7},{6,4},{7,5},{8,10},{9,11},{10,... | collective-permute-start | bytes 786440 | tf_op jit(solution)/shard_map/ppermute | solution.py:257
  99.6 10.6 %collective-permute-start.48 = (bf16[128,1024]{1,0:T(8,128)(2,1)S(1)}, bf16[128,1024]{1,0:T(8,128)(2,1)S(1)}, u32[]{:S(2)}, u32[]{:S(2)}) collective-permute-start(bf16[128,1024]{1,0:T(8,128)(2,1)S(1)} %project_out.11.refs_7_.refs_1_), channel_id=1, source_target_pairs={{0,3},{1,2},{2,1},{3,0},{4,7},{5,6},{6,5},{7,4},{8,11},{9,10},{10,... | collective-permute-start | bytes 786440 | tf_op jit(solution)/shard_map/ppermute | solution.py:257
  105.6 7.4 %collective-permute-start.47 = (bf16[32,1024]{1,0:T(8,128)(2,1)S(1)}, bf16[32,1024]{1,0:T(8,128)(2,1)S(1)}, u32[]{:S(2)}, u32[]{:S(2)}) collective-permute-start(bf16[32,1024]{1,0:T(8,128)(2,1)S(1)} %get-tuple-element.122.refs_0_), channel_id=1, source_target_pairs={{0,24},{8,16},{16,8},{24,0},{1,25},{9,17},{17,9},{25,1},{2,26},{10... | collective-permute-start | bytes 196616 | tf_op jit(solution)/shard_map/ppermute | solution.py:257
  107.8 6.8 %collective-permute-start.46 = (bf16[32,1024]{1,0:T(8,128)(2,1)S(1)}, bf16[32,1024]{1,0:T(8,128)(2,1)S(1)}, u32[]{:S(2)}, u32[]{:S(2)}) collective-permute-start(bf16[32,1024]{1,0:T(8,128)(2,1)S(1)} %get-tuple-element.122.refs_0_), channel_id=1, source_target_pairs={{0,16},{8,24},{16,0},{24,8},{1,17},{9,25},{17,1},{25,9},{2,18},{10... | collective-permute-start | bytes 196616 | tf_op jit(solution)/shard_map/ppermute | solution.py:257
  112.5 6.5 %collective-permute-start.55 = (bf16[32,1664]{1,0:T(8,128)(2,1)S(1)}, bf16[32,1664]{1,0:T(8,128)(2,1)S(1)}, u32[]{:S(2)}, u32[]{:S(2)}) collective-permute-start(bf16[32,1664]{1,0:T(8,128)(2,1)S(1)} %get-tuple-element.127), channel_id=1, source_target_pairs={{0,16},{8,24},{16,0},{24,8},{1,17},{9,25},{17,1},{25,9},{2,18},{10... | collective-permute-start | bytes 319496 | tf_op jit(solution)/shard_map/ppermute | solution.py:257
  113.0 8.3 %collective-permute-start.56 = (bf16[32,1664]{1,0:T(8,128)(2,1)S(1)}, bf16[32,1664]{1,0:T(8,128)(2,1)S(1)}, u32[]{:S(2)}, u32[]{:S(2)}) collective-permute-start(bf16[32,1664]{1,0:T(8,128)(2,1)S(1)} %get-tuple-element.128), channel_id=1, source_target_pairs={{0,24},{8,16},{16,8},{24,0},{1,25},{9,17},{17,9},{25,1},{2,26},{10... | collective-permute-start | bytes 319496 | tf_op jit(solution)/shard_map/ppermute | solution.py:257
  115.1 12.3 %collective-permute-start.53 = (bf16[128,1024]{1,0:T(8,128)(2,1)S(1)}, bf16[128,1024]{1,0:T(8,128)(2,1)S(1)}, u32[]{:S(2)}, u32[]{:S(2)}) collective-permute-start(bf16[128,1024]{1,0:T(8,128)(2,1)S(1)} %project_out.12.refs_9_.refs_1_), channel_id=1, source_target_pairs={{0,1},{1,0},{2,3},{3,2},{4,5},{5,4},{6,7},{7,6},{8,9},{9,8},{10,11... | collective-permute-start | bytes 786440 | tf_op jit(solution)/shard_map/ppermute | solution.py:257
  115.2 12.3 %collective-permute-start.52 = (bf16[128,1024]{1,0:T(8,128)(2,1)S(1)}, bf16[128,1024]{1,0:T(8,128)(2,1)S(1)}, u32[]{:S(2)}, u32[]{:S(2)}) collective-permute-start(bf16[128,1024]{1,0:T(8,128)(2,1)S(1)} %project_out.12.refs_9_.refs_1_), channel_id=1, source_target_pairs={{0,2},{1,3},{2,0},{3,1},{4,6},{5,7},{6,4},{7,5},{8,10},{9,11},{10,... | collective-permute-start | bytes 786440 | tf_op jit(solution)/shard_map/ppermute | solution.py:257
  116.7 10.7 %collective-permute-start.51 = (bf16[128,1024]{1,0:T(8,128)(2,1)S(1)}, bf16[128,1024]{1,0:T(8,128)(2,1)S(1)}, u32[]{:S(2)}, u32[]{:S(2)}) collective-permute-start(bf16[128,1024]{1,0:T(8,128)(2,1)S(1)} %project_out.12.refs_9_.refs_1_), channel_id=1, source_target_pairs={{0,3},{1,2},{2,1},{3,0},{4,7},{5,6},{6,5},{7,4},{8,11},{9,10},{10,... | collective-permute-start | bytes 786440 | tf_op jit(solution)/shard_map/ppermute | solution.py:257
  122.5 7.4 %collective-permute-start.62 = (bf16[32,1024]{1,0:T(8,128)(2,1)S(1)}, bf16[32,1024]{1,0:T(8,128)(2,1)S(1)}, u32[]{:S(2)}, u32[]{:S(2)}) collective-permute-start(bf16[32,1024]{1,0:T(8,128)(2,1)S(1)} %get-tuple-element.136.refs_0_), channel_id=1, source_target_pairs={{0,24},{8,16},{16,8},{24,0},{1,25},{9,17},{17,9},{25,1},{2,26},{10... | collective-permute-start | bytes 196616 | tf_op jit(solution)/shard_map/ppermute | solution.py:257
  124.2 7.6 %collective-permute-start.61 = (bf16[32,1024]{1,0:T(8,128)(2,1)S(1)}, bf16[32,1024]{1,0:T(8,128)(2,1)S(1)}, u32[]{:S(2)}, u32[]{:S(2)}) collective-permute-start(bf16[32,1024]{1,0:T(8,128)(2,1)S(1)} %get-tuple-element.136.refs_0_), channel_id=1, source_target_pairs={{0,16},{8,24},{16,0},{24,8},{1,17},{9,25},{17,1},{25,9},{2,18},{10... | collective-permute-start | bytes 196616 | tf_op jit(solution)/shard_map/ppermute | solution.py:257
  129.6 6.0 %collective-permute-start.58 = (bf16[32,1664]{1,0:T(8,128)(2,1)S(1)}, bf16[32,1664]{1,0:T(8,128)(2,1)S(1)}, u32[]{:S(2)}, u32[]{:S(2)}) collective-permute-start(bf16[32,1664]{1,0:T(8,128)(2,1)S(1)} %get-tuple-element.134), channel_id=1, source_target_pairs={{0,16},{8,24},{16,0},{24,8},{1,17},{9,25},{17,1},{25,9},{2,18},{10... | collective-permute-start | bytes 319496 | tf_op jit(solution)/shard_map/ppermute | solution.py:257
  130.0 8.4 %collective-permute-start.59 = (bf16[32,1664]{1,0:T(8,128)(2,1)S(1)}, bf16[32,1664]{1,0:T(8,128)(2,1)S(1)}, u32[]{:S(2)}, u32[]{:S(2)}) collective-permute-start(bf16[32,1664]{1,0:T(8,128)(2,1)S(1)} %get-tuple-element.135), channel_id=1, source_target_pairs={{0,24},{8,16},{16,8},{24,0},{1,25},{9,17},{17,9},{25,1},{2,26},{10... | collective-permute-start | bytes 319496 | tf_op jit(solution)/shard_map/ppermute | solution.py:257
  132.3 11.9 %collective-permute-start.68 = (bf16[128,1024]{1,0:T(8,128)(2,1)S(1)}, bf16[128,1024]{1,0:T(8,128)(2,1)S(1)}, u32[]{:S(2)}, u32[]{:S(2)}) collective-permute-start(bf16[128,1024]{1,0:T(8,128)(2,1)S(1)} %project_out.13.refs_7_.refs_1_), channel_id=1, source_target_pairs={{0,1},{1,0},{2,3},{3,2},{4,5},{5,4},{6,7},{7,6},{8,9},{9,8},{10,11... | collective-permute-start | bytes 786440 | tf_op jit(solution)/shard_map/ppermute | solution.py:257
  132.4 11.8 %collective-permute-start.67 = (bf16[128,1024]{1,0:T(8,128)(2,1)S(1)}, bf16[128,1024]{1,0:T(8,128)(2,1)S(1)}, u32[]{:S(2)}, u32[]{:S(2)}) collective-permute-start(bf16[128,1024]{1,0:T(8,128)(2,1)S(1)} %project_out.13.refs_7_.refs_1_), channel_id=1, source_target_pairs={{0,2},{1,3},{2,0},{3,1},{4,6},{5,7},{6,4},{7,5},{8,10},{9,11},{10,... | collective-permute-start | bytes 786440 | tf_op jit(solution)/shard_map/ppermute | solution.py:257
  133.4 10.8 %collective-permute-start.66 = (bf16[128,1024]{1,0:T(8,128)(2,1)S(1)}, bf16[128,1024]{1,0:T(8,128)(2,1)S(1)}, u32[]{:S(2)}, u32[]{:S(2)}) collective-permute-start(bf16[128,1024]{1,0:T(8,128)(2,1)S(1)} %project_out.13.refs_7_.refs_1_), channel_id=1, source_target_pairs={{0,3},{1,2},{2,1},{3,0},{4,7},{5,6},{6,5},{7,4},{8,11},{9,10},{10,... | collective-permute-start | bytes 786440 | tf_op jit(solution)/shard_map/ppermute | solution.py:257
  139.4 7.6 %collective-permute-start.65 = (bf16[32,1024]{1,0:T(8,128)(2,1)S(1)}, bf16[32,1024]{1,0:T(8,128)(2,1)S(1)}, u32[]{:S(2)}, u32[]{:S(2)}) collective-permute-start(bf16[32,1024]{1,0:T(8,128)(2,1)S(1)} %get-tuple-element.137.refs_1_), channel_id=1, source_target_pairs={{0,24},{8,16},{16,8},{24,0},{1,25},{9,17},{17,9},{25,1},{2,26},{10... | collective-permute-start | bytes 196616 | tf_op jit(solution)/shard_map/ppermute | solution.py:257
  141.8 6.8 %collective-permute-start.64 = (bf16[32,1024]{1,0:T(8,128)(2,1)S(1)}, bf16[32,1024]{1,0:T(8,128)(2,1)S(1)}, u32[]{:S(2)}, u32[]{:S(2)}) collective-permute-start(bf16[32,1024]{1,0:T(8,128)(2,1)S(1)} %get-tuple-element.137.refs_1_), channel_id=1, source_target_pairs={{0,16},{8,24},{16,0},{24,8},{1,17},{9,25},{17,1},{25,9},{2,18},{10... | collective-permute-start | bytes 196616 | tf_op jit(solution)/shard_map/ppermute | solution.py:257
  146.4 6.5 %collective-permute-start.74 = (bf16[32,1664]{1,0:T(8,128)(2,1)S(1)}, bf16[32,1664]{1,0:T(8,128)(2,1)S(1)}, u32[]{:S(2)}, u32[]{:S(2)}) collective-permute-start(bf16[32,1664]{1,0:T(8,128)(2,1)S(1)} %get-tuple-element.146), channel_id=1, source_target_pairs={{0,16},{8,24},{16,0},{24,8},{1,17},{9,25},{17,1},{25,9},{2,18},{10... | collective-permute-start | bytes 319496 | tf_op jit(solution)/shard_map/ppermute | solution.py:257
  147.0 8.3 %collective-permute-start.75 = (bf16[32,1664]{1,0:T(8,128)(2,1)S(1)}, bf16[32,1664]{1,0:T(8,128)(2,1)S(1)}, u32[]{:S(2)}, u32[]{:S(2)}) collective-permute-start(bf16[32,1664]{1,0:T(8,128)(2,1)S(1)} %get-tuple-element.147), channel_id=1, source_target_pairs={{0,24},{8,16},{16,8},{24,0},{1,25},{9,17},{17,9},{25,1},{2,26},{10... | collective-permute-start | bytes 319496 | tf_op jit(solution)/shard_map/ppermute | solution.py:257
  156.5 5.9 %collective-permute-start.78 = (bf16[32,1024]{1,0:T(8,128)(2,1)S(1)}, bf16[32,1024]{1,0:T(8,128)(2,1)S(1)}, u32[]{:S(2)}, u32[]{:S(2)}) collective-permute-start(bf16[32,1024]{1,0:T(8,128)(2,1)S(1)} %get-tuple-element.149.refs_1_), channel_id=1, source_target_pairs={{0,24},{8,16},{16,8},{24,0},{1,25},{9,17},{17,9},{25,1},{2,26},{10... | collective-permute-start | bytes 196616 | tf_op jit(solution)/shard_map/ppermute | solution.py:257
  161.7 6.3 %collective-permute-start.70 = (bf16[32,1024]{1,0:T(8,128)(2,1)S(1)}, bf16[32,1024]{1,0:T(8,128)(2,1)S(1)}, u32[]{:S(2)}, u32[]{:S(2)}) collective-permute-start(bf16[32,1024]{1,0:T(8,128)(2,1)S(1)} %get-tuple-element.142), channel_id=1, source_target_pairs={{0,2},{1,3},{2,0},{3,1},{4,6},{5,7},{6,4},{7,5},{8,10},{9,11},{10,... | collective-permute-start | bytes 196616 | tf_op jit(solution)/shard_map/ppermute | solution.py:257
  165.2 7.1 %collective-permute-start.79 = (bf16[32,1024]{1,0:T(8,128)(2,1)S(1)}, bf16[32,1024]{1,0:T(8,128)(2,1)S(1)}, u32[]{:S(2)}, u32[]{:S(2)}) collective-permute-start(bf16[32,1024]{1,0:T(8,128)(2,1)S(1)} %get-tuple-element.152), channel_id=1, source_target_pairs={{0,3},{1,2},{2,1},{3,0},{4,7},{5,6},{6,5},{7,4},{8,11},{9,10},{10,... | collective-permute-start | bytes 196616 | tf_op jit(solution)/shard_map/ppermute | solution.py:257
  166.1 6.3 %collective-permute-start.80 = (bf16[32,1024]{1,0:T(8,128)(2,1)S(1)}, bf16[32,1024]{1,0:T(8,128)(2,1)S(1)}, u32[]{:S(2)}, u32[]{:S(2)}) collective-permute-start(bf16[32,1024]{1,0:T(8,128)(2,1)S(1)} %get-tuple-element.153), channel_id=1, source_target_pairs={{0,2},{1,3},{2,0},{3,1},{4,6},{5,7},{6,4},{7,5},{8,10},{9,11},{10,... | collective-permute-start | bytes 196616 | tf_op jit(solution)/shard_map/ppermute | solution.py:257
  168.0 9.0 %collective-permute-start.72 = (bf16[32,1024]{1,0:T(8,128)(2,1)S(1)}, bf16[32,1024]{1,0:T(8,128)(2,1)S(1)}, u32[]{:S(2)}, u32[]{:S(2)}) collective-permute-start(bf16[32,1024]{1,0:T(8,128)(2,1)S(1)} %add_convert_fusion.1), channel_id=1, source_target_pairs={{0,0},{1,8},{2,16},{3,24},{8,1},{9,9},{10,17},{11,25},{16,2},{17,1... | collective-permute-start | bytes 196616 | tf_op jit(solution)/shard_map/ppermute | solution.py:412
  172.4 8.7 %collective-permute-start.82 = (bf16[32,1024]{1,0:T(8,128)(2,1)S(1)}, bf16[32,1024]{1,0:T(8,128)(2,1)S(1)}, u32[]{:S(2)}, u32[]{:S(2)}) collective-permute-start(bf16[32,1024]{1,0:T(8,128)(2,1)S(1)} %add_convert_fusion), channel_id=1, source_target_pairs={{0,0},{1,8},{2,16},{3,24},{8,1},{9,9},{10,17},{11,25},{16,2},{17,1... | collective-permute-start | bytes 196616 | tf_op jit(solution)/shard_map/ppermute | solution.py:412
  181.1 7.2 %collective-permute-start.83 = (bf16[1,32,1024]{2,1,0:T(8,128)(2,1)S(1)}, bf16[1,32,1024]{2,1,0:T(8,128)(2,1)S(1)}, u32[]{:S(2)}, u32[]{:S(2)}) collective-permute-start(bf16[1,32,1024]{2,1,0:T(8,128)(2,1)S(1)} %select_bitcast_fusion.16), channel_id=1, source_target_pairs={{0,4},{4,0},{1,5},{5,1},{2,6},{6,2},{3,7},{7,3},{8,12},{12,8},{9,1... | collective-permute-start | bytes 196616 | tf_op jit(solution)/shard_map/ppermute | solution.py:257
  (29 other events, 135.7 us)

commit v5 on v4

--- a/solution.py
+++ b/solution.py
@@ -9,6 +9,7 @@
 
 HEAD_DIM = 128
 LANES = 128
+STAT_ROWS = 16
 ROPE_THETA = 500000.0
 NORM_EPSILON = 1e-05
 VMEM_BYTES = 8 * 1024 * 1024
@@ -28,6 +29,11 @@
 
 def column_tiles(width, tile):
     return [(at, min(tile, width - at)) for at in range(0, width, tile)]
+
+
+def diagonal(rows, offset):
+    row = lax.broadcasted_iota(jnp.int32, (rows, LANES), 0)
+    return row + offset == lax.broadcasted_iota(jnp.int32, (rows, LANES), 1)
 
 
 def qkv_kernel(n_in, n_out, part, *refs):
@@ -51,27 +57,33 @@
     wide = stream[...].astype(jnp.float32)
     rows[...] = (wide * scale).astype(jnp.bfloat16)
     total = jnp.sum(wide * wide, axis=-1, keepdims=True)
-    out_size = outs[0].shape[0]
+    size = rows.shape[0] // n_out
     start = 0
     for weight in (wq, wk, wv):
         for at, width in column_tiles(weight.shape[1], 512):
             product = jnp.dot(rows[...], weight[:, at : at + width], preferred_element_type=jnp.float32)
             for m, out in enumerate(outs):
-                piece = product[m * out_size : (m + 1) * out_size]
-                out[:, start + at : start + at + width] = piece.astype(out.dtype)
+                for lane in range(0, width, LANES):
+                    piece = product[m * size : (m + 1) * size, lane : lane + LANES]
+                    out[pl.ds((start + at + lane) // LANES * size, size), :] = piece.astype(out.dtype)
         start += weight.shape[1]
-    high = total.astype(jnp.bfloat16).astype(jnp.float32)
-    lane = lax.broadcasted_iota(jnp.int32, (total.shape[0], LANES), 1)
-    split = jnp.where(lane < LANES // 2, high, total - high)
+    base = start // LANES * size
     for m, out in enumerate(outs):
-        out[:, start : start + LANES] = split[m * out_size : (m + 1) * out_size].astype(out.dtype)
+        for k, at in enumerate(range(0, size, LANES)):
+            part_total = total[m * size + at : m * size + min(at + LANES, size)]
+            lying = jnp.sum(jnp.where(diagonal(part_total.shape[0], 0), part_total, 0.0), axis=0, keepdims=True)
+            high = lying.astype(jnp.bfloat16).astype(jnp.float32)
+            line = lax.broadcasted_iota(jnp.int32, (STAT_ROWS, LANES), 0)
+            tile = jnp.where(line == 0, high, jnp.where(line == 1, lying - high, 0.0))
+            out[pl.ds(base + k * STAT_ROWS, STAT_ROWS), :] = tile.astype(out.dtype)
 
 
 def project_qkv(head, arrays, part, total, gain, wq, wk, wv, n_out, after):
     depth = wq.shape[0]
-    columns = wq.shape[1] + wk.shape[1] + wv.shape[1] + LANES
+    size = total // n_out
+    height = (wq.shape[1] + wk.shape[1] + wv.shape[1]) // LANES * size + -(-size // LANES) * STAT_ROWS
     shapes = [jax.ShapeDtypeStruct((total, depth), jnp.bfloat16)] + [
-        jax.ShapeDtypeStruct((total // n_out, columns), jnp.float32 if m == 0 and n_out > 1 else jnp.bfloat16)
+        jax.ShapeDtypeStruct((height, LANES), jnp.float32 if m == 0 and n_out > 1 else jnp.bfloat16)
         for m in range(n_out)
     ]
     first = in_vmem(1) if part is None else [pl.BlockSpec(memory_space=pltpu.SMEM)]
@@ -96,39 +108,42 @@
     group = q_heads // kv_heads
     first = n_before * size
 
-    def summed(rows, at, width):
-        value = blocks[0][rows, at : at + width].astype(jnp.float32)
+    def summed(at, height):
+        value = blocks[0][at : at + height].astype(jnp.float32)
         for block in blocks[1:]:
-            value = value + block[rows, at : at + width].astype(jnp.float32)
+            value = value + block[at : at + height].astype(jnp.float32)
         return value
 
-    k_at = q_heads * HEAD_DIM
-    v_at = k_at + kv_heads * HEAD_DIM
-    s_at = v_at + kv_heads * HEAD_DIM
+    k_at, v_at = q_heads, q_heads + kv_heads
+    s_at = (q_heads + 2 * kv_heads) * out.shape[0]
     for s in range(samples):
         rows = slice(s * size, (s + 1) * size)
-        parts = summed(rows, s_at, LANES)
-        squares = parts[:, :1] + parts[:, LANES // 2 : LANES // 2 + 1]
+        tile = summed(s_at + s * size // LANES * STAT_ROWS, STAT_ROWS)
+        lying = jnp.broadcast_to(tile[:1] + tile[1:2], (size, LANES))
+        squares = jnp.sum(jnp.where(diagonal(size, s * size % LANES), lying, 0.0), axis=-1, keepdims=True)
         inverse = lax.rsqrt(squares * (1.0 / model_width) + NORM_EPSILON)
         cos, sin = cosine[s, first : first + size], sine[s, first : first + size]
         bias = mask[s, first : first + size, : first + size]
 
+        def head(at):
+            return summed(at * out.shape[0] + s * size, size) * inverse
+
         def rotated(at):
-            value = summed(rows, at, HEAD_DIM) * inverse
+            value = head(at)
             turned = pltpu.roll(value, HEAD_DIM // 2, 1)
             return (value * cos + turned * sin).astype(jnp.bfloat16)
 
         bias_all = jnp.concatenate([bias] * group, axis=0)
         for kv in range(kv_heads):
             lanes = slice(kv * HEAD_DIM, (kv + 1) * HEAD_DIM)
-            key = rotated(k_at + kv * HEAD_DIM)
-            value = (summed(rows, v_at + kv * HEAD_DIM, HEAD_DIM) * inverse).astype(jnp.bfloat16)
+            key = rotated(k_at + kv)
+            value = head(v_at + kv).astype(jnp.bfloat16)
             key_out[rows, lanes] = key
             value_out[rows, lanes] = value
             if n_before:
                 key = jnp.concatenate([k[rows, lanes] for k in before[0::2]] + [key], axis=0)
                 value = jnp.concatenate([v[rows, lanes] for v in before[1::2]] + [value], axis=0)
-            query = jnp.concatenate([rotated((kv * group + g) * HEAD_DIM) for g in range(group)], axis=0)
+            query = jnp.concatenate([rotated(kv * group + g) for g in range(group)], axis=0)
             scores = lax.dot_general(query, key, (((1,), (1,)), ((), ())), preferred_element_type=jnp.float32)
             scores = scores * HEAD_DIM ** (-0.5) + bias_all
             top = jnp.max(scores, axis=-1, keepdims=True)
@@ -140,8 +155,7 @@
                 out[rows, at : at + HEAD_DIM] = mixed[g * size : (g + 1) * size].astype(out.dtype)
 
 
-def attend(blocks, before, cosine, sine, mask, q_heads, kv_heads, model_width, after):
-    rows = blocks[0].shape[0]
+def attend(rows, blocks, before, cosine, sine, mask, q_heads, kv_heads, model_width, after):
     shapes = [(rows, heads * HEAD_DIM) for heads in (q_heads, kv_heads, kv_heads)]
     return pl.pallas_call(
         unread(
@@ -358,7 +372,7 @@
         gain, wq, wk, wv, _ = weights[number]
         head, arrays, part = (streams[h], shares[h], None) if number else (place, blocks, h)
         streams[h], ends = project_qkv(
-            head, arrays, part, total, gain[None], wq, wk, wv, replicas if paired else 1, latest
+            head, arrays, part, total, gain[None], wq, wk, wv, replicas, latest
         )
         latest = [streams[h]]
         if layout is None:
@@ -366,14 +380,14 @@
         if paired:
             sums[h] = trade_blocks(ends, "dp")
         else:
-            pieces = ends[0].reshape(replicas, part_rows, ends[0].shape[1])
+            pieces = jnp.stack([end.astype(jnp.bfloat16) for end in ends])
             pieces = lax.all_to_all(pieces, "dp", split_axis=0, concat_axis=0)
             sums[h] = [jnp.sum(pieces.astype(jnp.float32), axis=0)]
 
     def mix(h, number):
         nonlocal latest
         rows_out, keys, values = attend(
-            sums[h], before[number], *layout, q_heads, kv_heads, model_width, latest
+            part_rows, sums[h], before[number], *layout, q_heads, kv_heads, model_width, latest
         )
         latest = [keys]
         before[number].append((keys, values))

time: 189 us -> 186 us (0.984)
  waiting for transfers between devices: 41.1 us -> 38.8 us
    ppermute x81, waiting for transfers between devices: 33.7 us -> 31.3 us  [swapped(): lax.ppermute(value, axis, [(i, i ^ by) for i in range(lax.axis_size(axis))])]
where the time goes in v5:
time: 186 us
  starting transfers between devices  114 us (61%)
  waiting for transfers between devices  38.8 us (21%)
  Pallas kernels  20.6 us (11%)
  other arithmetic  9.31 us (5%)
  local copies, waits for them, and re-layouts  3.1 us (2%)
    ppermute x81, starting transfers between devices, swapped(): lax.ppermute(value, axis, [(i, i ^ by) for i in range(lax.axis_size(axis))])  99.7 us
    ppermute x81, waiting for transfers between devices, swapped(): lax.ppermute(value, axis, [(i, i ^ by) for i in range(lax.axis_size(axis))])  31.3 us
    ppermute x2, starting transfers between devices, per_device(): stream = lax.ppermute(stream, ('dp', 'tensor'), turn)  8.88 us
    pallas_call x8, Pallas kernels, attend(): pl.pallas_call(unread(len(after), len(blocks) + 2 * len(before) + 3, part...  8.17 us
    select_n x5, other arithmetic, layer_weights(): jnp.where(my_section == section, mine[index, 0], theirs[index, 0])  7.63 us
    pallas_call x8, Pallas kernels, project_qkv(): pl.pallas_call(unread(len(after), len(arrays) + 5, partial(qkv_kernel, le...  6.39 us
    ppermute x1, starting transfers between devices, per_device(): lax.ppermute(stream, ('dp', 'tensor'), turn)  5.14 us
    pallas_call x8, Pallas kernels, project_out(): pl.pallas_call(unread(len(after), placed + n_in + 1, partial(out_kernel,...  4.69 us
  transfers between devices with their start and end apart: 84, of which 23 were waited for; matrix products, arithmetic and copies ran while one was open for 5% of the time, Pallas kernels for 10%

profile of v5, /device:TPU:7, one launch (start us, length us, event | category | flops | bytes accessed | tf_op | source)
XLA Modules:
  0.0 186.1 jit_solution(10004402154821207297)
XLA Ops:
  5.4 5.1 %collective-permute-start = (bf16[64,1024]{1,0:T(8,128)(2,1)S(1)}, bf16[64,1024]{1,0:T(8,128)(2,1)S(1)}, u32[]{:S(2)}, u32[]{:S(2)}) collective-permute-start(bf16[64,1024]{1,0:T(8,128)(2,1)S(1)} %bitcast.51), channel_id=1, source_target_pairs={{0,0},{1,8},{2,16},{3,24},{8,1},{9,9},{10,17},{11,25},{16,2},{17,1... | collective-permute-start | bytes 393224 | tf_op jit(solution)/shard_map/ppermute | solution.py:356
  12.6 3.3 %collective-permute-done.refs_1_ = bf16[64,1024]{1,0:T(8,128)(2,1)S(1)} collective-permute-done((bf16[64,1024]{1,0:T(8,128)(2,1)S(1)}, bf16[64,1024]{1,0:T(8,128)(2,1)S(1)}, u32[]{:S(2)}, u32[]{:S(2)}) %collective-permute-start) | collective-permute-done | bytes 131104 | tf_op jit(solution)/shard_map/ppermute | solution.py:356
  15.9 1.3 collective-permute-start.3
  17.1 1.6 collective-permute-done.6
  19.0 1.7 select_bitcast_fusion.9
  20.7 1.2 collective-permute-start.1
  22.8 2.5 %select_bitcast_fusion.1 = (bf16[1024,1024]{1,0:T(8,128)(2,1)S(1)}, bf16[1024,1024]{1,0:T(8,128)(2,1)S(1)}, bf16[1024,1024]{1,0:T(8,128)(2,1)S(1)}, bf16[1024,1024]{1,0:T(8,128)(2,1)S(1)}) fusion(pred[]{:T(512)S(6)} %eq.4, bf16[2,1,1024,1024]{3,2,1,0:T(8,128)(2,1)} %collective-permute-done.5, bf16[2,1,1024,1024]{3,2,1,0:T(8,128)(2,1)S(1)} %copy-done.6, pred[]{:T(512)S(6)} %eq.5), kind=kLoop, calls=%fused_computation.1 | loop fusion | flops 4194304 | bytes 16777218 | tf_op jit(solution)/shard_map/jit(_where)/select_n | solution.py:342
  26.6 1.9 %collective-permute-start.8 = (bf16[400,128]{1,0:T(8,128)(2,1)S(1)}, bf16[400,128]{1,0:T(8,128)(2,1)S(1)}, u32[]{:S(2)}, u32[]{:S(2)}) collective-permute-start(bf16[400,128]{1,0:T(8,128)(2,1)S(1)} %get-tuple-element.86), channel_id=1, source_target_pairs={{0,8},{8,0},{16,24},{24,16},{1,9},{9,1},{17,25},{25,17},{2,10},{10... | collective-permute-start | bytes 307208 | tf_op jit(solution)/shard_map/ppermute | solution.py:271
  28.5 1.9 %collective-permute-start.9 = (bf16[400,128]{1,0:T(8,128)(2,1)S(1)}, bf16[400,128]{1,0:T(8,128)(2,1)S(1)}, u32[]{:S(2)}, u32[]{:S(2)}) collective-permute-start(bf16[400,128]{1,0:T(8,128)(2,1)S(1)} %get-tuple-element.87), channel_id=1, source_target_pairs={{0,16},{8,24},{16,0},{24,8},{1,17},{9,25},{17,1},{25,9},{2,18},{10... | collective-permute-start | bytes 307208 | tf_op jit(solution)/shard_map/ppermute | solution.py:271
  31.4 2.7 %select_bitcast_fusion = (bf16[1024,1024]{1,0:T(8,128)(2,1)S(1)}, bf16[1024,1024]{1,0:T(8,128)(2,1)S(1)}, bf16[1024,1024]{1,0:T(8,128)(2,1)S(1)}, bf16[1024,1024]{1,0:T(8,128)(2,1)S(1)}) fusion(pred[]{:T(512)S(6)} %eq.4, bf16[2,1,1024,1024]{3,2,1,0:T(8,128)(2,1)} %collective-permute-done.14, bf16[2,1,1024,1024]{3,2,1,0:T(8,128)(2,1)S(1)} %copy-done.7, pred[]{:T(512)S(6)} %eq.5), kind=kLoop, calls=%fused_computation | loop fusion | flops 4194304 | bytes 16777218 | tf_op jit(solution)/shard_map/jit(_where)/select_n | solution.py:342
  34.2 2.6 %collective-permute-done.10.refs_3_ = bf16[400,128]{1,0:T(8,128)(2,1)S(1)} collective-permute-done((bf16[400,128]{1,0:T(8,128)(2,1)S(1)}, bf16[400,128]{1,0:T(8,128)(2,1)S(1)}, u32[]{:S(2)}, u32[]{:S(2)}) %collective-permute-start.10) | collective-permute-done | bytes 102432 | tf_op jit(solution)/shard_map/ppermute | solution.py:271
  37.7 1.2 collective-permute-start.13
  38.9 2.5 %collective-permute-start.12 = (bf16[32,1024]{1,0:T(8,128)(2,1)S(1)}, bf16[32,1024]{1,0:T(8,128)(2,1)S(1)}, u32[]{:S(2)}, u32[]{:S(2)}) collective-permute-start(bf16[32,1024]{1,0:T(8,128)(2,1)S(1)} %get-tuple-element.91.refs_0_), channel_id=1, source_target_pairs={{0,16},{8,24},{16,0},{24,8},{1,17},{9,25},{17,1},{25,9},{2,18},{10... | collective-permute-start | bytes 196616 | tf_op jit(solution)/shard_map/ppermute | solution.py:271
  42.8 1.3 collective-permute-start.18
  44.1 1.2 collective-permute-start.19
  46.9 1.8 collective-permute-start.16
  48.7 1.2 collective-permute-start.15
  50.5 2.6 %collective-permute-done.20.refs_3_ = bf16[400,128]{1,0:T(8,128)(2,1)S(1)} collective-permute-done((bf16[400,128]{1,0:T(8,128)(2,1)S(1)}, bf16[400,128]{1,0:T(8,128)(2,1)S(1)}, u32[]{:S(2)}, u32[]{:S(2)}) %collective-permute-start.20) | collective-permute-done | bytes 102432 | tf_op jit(solution)/shard_map/ppermute | solution.py:271
  54.2 1.8 collective-permute-start.26
  56.0 3.2 %collective-permute-start.25 = (bf16[32,1024]{1,0:T(8,128)(2,1)S(1)}, bf16[32,1024]{1,0:T(8,128)(2,1)S(1)}, u32[]{:S(2)}, u32[]{:S(2)}) collective-permute-start(bf16[32,1024]{1,0:T(8,128)(2,1)S(1)} %get-tuple-element.106.refs_0_), channel_id=1, source_target_pairs={{0,16},{8,24},{16,0},{24,8},{1,17},{9,25},{17,1},{25,9},{2,18},{10... | collective-permute-start | bytes 196616 | tf_op jit(solution)/shard_map/ppermute | solution.py:271
  59.9 1.5 collective-permute-start.21
  61.4 2.2 %collective-permute-start.23 = (bf16[400,128]{1,0:T(8,128)(2,1)S(1)}, bf16[400,128]{1,0:T(8,128)(2,1)S(1)}, u32[]{:S(2)}, u32[]{:S(2)}) collective-permute-start(bf16[400,128]{1,0:T(8,128)(2,1)S(1)} %get-tuple-element.105), channel_id=1, source_target_pairs={{0,24},{8,16},{16,8},{24,0},{1,25},{9,17},{17,9},{25,1},{2,26},{10... | collective-permute-start | bytes 307208 | tf_op jit(solution)/shard_map/ppermute | solution.py:271
  67.5 2.3 %collective-permute-done.23.refs_3_ = bf16[400,128]{1,0:T(8,128)(2,1)S(1)} collective-permute-done((bf16[400,128]{1,0:T(8,128)(2,1)S(1)}, bf16[400,128]{1,0:T(8,128)(2,1)S(1)}, u32[]{:S(2)}, u32[]{:S(2)}) %collective-permute-start.23) | collective-permute-done | bytes 102432 | tf_op jit(solution)/shard_map/ppermute | solution.py:271
  70.8 2.3 %collective-permute-start.29 = (bf16[32,1024]{1,0:T(8,128)(2,1)S(1)}, bf16[32,1024]{1,0:T(8,128)(2,1)S(1)}, u32[]{:S(2)}, u32[]{:S(2)}) collective-permute-start(bf16[32,1024]{1,0:T(8,128)(2,1)S(1)} %get-tuple-element.107.refs_0_), channel_id=1, source_target_pairs={{0,24},{8,16},{16,8},{24,0},{1,25},{9,17},{17,9},{25,1},{2,26},{10... | collective-permute-start | bytes 196616 | tf_op jit(solution)/shard_map/ppermute | solution.py:271
  73.0 2.5 %collective-permute-start.28 = (bf16[32,1024]{1,0:T(8,128)(2,1)S(1)}, bf16[32,1024]{1,0:T(8,128)(2,1)S(1)}, u32[]{:S(2)}, u32[]{:S(2)}) collective-permute-start(bf16[32,1024]{1,0:T(8,128)(2,1)S(1)} %get-tuple-element.107.refs_0_), channel_id=1, source_target_pairs={{0,16},{8,24},{16,0},{24,8},{1,17},{9,25},{17,1},{25,9},{2,18},{10... | collective-permute-start | bytes 196616 | tf_op jit(solution)/shard_map/ppermute | solution.py:271
  76.2 1.5 collective-permute-start.36
  78.1 1.8 collective-permute-start.38
  80.6 1.3 collective-permute-start.34
  81.9 1.8 collective-permute-start.33
  84.2 1.9 %collective-permute-done.38.refs_3_ = bf16[400,128]{1,0:T(8,128)(2,1)S(1)} collective-permute-done((bf16[400,128]{1,0:T(8,128)(2,1)S(1)}, bf16[400,128]{1,0:T(8,128)(2,1)S(1)}, u32[]{:S(2)}, u32[]{:S(2)}) %collective-permute-start.38) | collective-permute-done | bytes 102432 | tf_op jit(solution)/shard_map/ppermute | solution.py:271
  87.3 2.0 %collective-permute-start.44 = (bf16[32,1024]{1,0:T(8,128)(2,1)S(1)}, bf16[32,1024]{1,0:T(8,128)(2,1)S(1)}, u32[]{:S(2)}, u32[]{:S(2)}) collective-permute-start(bf16[32,1024]{1,0:T(8,128)(2,1)S(1)} %get-tuple-element.121.refs_0_), channel_id=1, source_target_pairs={{0,24},{8,16},{16,8},{24,0},{1,25},{9,17},{17,9},{25,1},{2,26},{10... | collective-permute-start | bytes 196616 | tf_op jit(solution)/shard_map/ppermute | solution.py:271
  89.3 2.9 %collective-permute-start.43 = (bf16[32,1024]{1,0:T(8,128)(2,1)S(1)}, bf16[32,1024]{1,0:T(8,128)(2,1)S(1)}, u32[]{:S(2)}, u32[]{:S(2)}) collective-permute-start(bf16[32,1024]{1,0:T(8,128)(2,1)S(1)} %get-tuple-element.121.refs_0_), channel_id=1, source_target_pairs={{0,16},{8,24},{16,0},{24,8},{1,17},{9,25},{17,1},{25,9},{2,18},{10... | collective-permute-start | bytes 196616 | tf_op jit(solution)/shard_map/ppermute | solution.py:271
  92.9 1.5 collective-permute-start.39
  94.7 1.9 collective-permute-start.41
  98.3 1.5 collective-permute-start.48
  100.6 2.3 %collective-permute-done.41.refs_3_ = bf16[400,128]{1,0:T(8,128)(2,1)S(1)} collective-permute-done((bf16[400,128]{1,0:T(8,128)(2,1)S(1)}, bf16[400,128]{1,0:T(8,128)(2,1)S(1)}, u32[]{:S(2)}, u32[]{:S(2)}) %collective-permute-start.41) | collective-permute-done | bytes 102432 | tf_op jit(solution)/shard_map/ppermute | solution.py:271
  103.8 2.0 %collective-permute-start.47 = (bf16[32,1024]{1,0:T(8,128)(2,1)S(1)}, bf16[32,1024]{1,0:T(8,128)(2,1)S(1)}, u32[]{:S(2)}, u32[]{:S(2)}) collective-permute-start(bf16[32,1024]{1,0:T(8,128)(2,1)S(1)} %get-tuple-element.122.refs_0_), channel_id=1, source_target_pairs={{0,24},{8,16},{16,8},{24,0},{1,25},{9,17},{17,9},{25,1},{2,26},{10... | collective-permute-start | bytes 196616 | tf_op jit(solution)/shard_map/ppermute | solution.py:271
  105.8 2.7 %collective-permute-start.46 = (bf16[32,1024]{1,0:T(8,128)(2,1)S(1)}, bf16[32,1024]{1,0:T(8,128)(2,1)S(1)}, u32[]{:S(2)}, u32[]{:S(2)}) collective-permute-start(bf16[32,1024]{1,0:T(8,128)(2,1)S(1)} %get-tuple-element.122.refs_0_), channel_id=1, source_target_pairs={{0,16},{8,24},{16,0},{24,8},{1,17},{9,25},{17,1},{25,9},{2,18},{10... | collective-permute-start | bytes 196616 | tf_op jit(solution)/shard_map/ppermute | solution.py:271
  109.2 1.5 collective-permute-start.54
  111.2 1.7 collective-permute-start.56
  113.5 1.4 collective-permute-start.52
  114.9 1.2 collective-permute-start.51
  117.1 2.2 %collective-permute-done.56.refs_3_ = bf16[400,128]{1,0:T(8,128)(2,1)S(1)} collective-permute-done((bf16[400,128]{1,0:T(8,128)(2,1)S(1)}, bf16[400,128]{1,0:T(8,128)(2,1)S(1)}, u32[]{:S(2)}, u32[]{:S(2)}) %collective-permute-start.56) | collective-permute-done | bytes 102432 | tf_op jit(solution)/shard_map/ppermute | solution.py:271
  120.4 1.7 collective-permute-start.62
  122.1 3.0 %collective-permute-start.61 = (bf16[32,1024]{1,0:T(8,128)(2,1)S(1)}, bf16[32,1024]{1,0:T(8,128)(2,1)S(1)}, u32[]{:S(2)}, u32[]{:S(2)}) collective-permute-start(bf16[32,1024]{1,0:T(8,128)(2,1)S(1)} %get-tuple-element.136.refs_0_), channel_id=1, source_target_pairs={{0,16},{8,24},{16,0},{24,8},{1,17},{9,25},{17,1},{25,9},{2,18},{10... | collective-permute-start | bytes 196616 | tf_op jit(solution)/shard_map/ppermute | solution.py:271
  125.9 1.5 collective-permute-start.57
  127.9 1.7 collective-permute-start.59
  130.1 1.3 collective-permute-start.67
  131.4 1.4 collective-permute-start.66
  133.4 2.7 %collective-permute-done.59.refs_3_ = bf16[400,128]{1,0:T(8,128)(2,1)S(1)} collective-permute-done((bf16[400,128]{1,0:T(8,128)(2,1)S(1)}, bf16[400,128]{1,0:T(8,128)(2,1)S(1)}, u32[]{:S(2)}, u32[]{:S(2)}) %collective-permute-start.59) | collective-permute-done | bytes 102432 | tf_op jit(solution)/shard_map/ppermute | solution.py:271
  137.0 1.9 %collective-permute-start.65 = (bf16[32,1024]{1,0:T(8,128)(2,1)S(1)}, bf16[32,1024]{1,0:T(8,128)(2,1)S(1)}, u32[]{:S(2)}, u32[]{:S(2)}) collective-permute-start(bf16[32,1024]{1,0:T(8,128)(2,1)S(1)} %get-tuple-element.137.refs_1_), channel_id=1, source_target_pairs={{0,24},{8,16},{16,8},{24,0},{1,25},{9,17},{17,9},{25,1},{2,26},{10... | collective-permute-start | bytes 196616 | tf_op jit(solution)/shard_map/ppermute | solution.py:271
  138.9 2.8 %collective-permute-start.64 = (bf16[32,1024]{1,0:T(8,128)(2,1)S(1)}, bf16[32,1024]{1,0:T(8,128)(2,1)S(1)}, u32[]{:S(2)}, u32[]{:S(2)}) collective-permute-start(bf16[32,1024]{1,0:T(8,128)(2,1)S(1)} %get-tuple-element.137.refs_1_), channel_id=1, source_target_pairs={{0,16},{8,24},{16,0},{24,8},{1,17},{9,25},{17,1},{25,9},{2,18},{10... | collective-permute-start | bytes 196616 | tf_op jit(solution)/shard_map/ppermute | solution.py:271
  142.4 1.5 collective-permute-start.73
  144.5 1.6 collective-permute-start.75
  147.1 3.0 %collective-permute-done.74.refs_2_ = bf16[400,128]{1,0:T(8,128)(2,1)S(1)} collective-permute-done((bf16[400,128]{1,0:T(8,128)(2,1)S(1)}, bf16[400,128]{1,0:T(8,128)(2,1)S(1)}, u32[]{:S(2)}, u32[]{:S(2)}) %collective-permute-start.74) | collective-permute-done | bytes 102432 | tf_op jit(solution)/shard_map/ppermute | solution.py:271
  150.2 2.6 %collective-permute-done.75.refs_3_ = bf16[400,128]{1,0:T(8,128)(2,1)S(1)} collective-permute-done((bf16[400,128]{1,0:T(8,128)(2,1)S(1)}, bf16[400,128]{1,0:T(8,128)(2,1)S(1)}, u32[]{:S(2)}, u32[]{:S(2)}) %collective-permute-start.75) | collective-permute-done | bytes 102432 | tf_op jit(solution)/shard_map/ppermute | solution.py:271
  153.9 1.5 collective-permute-start.78
  155.4 2.7 %collective-permute-start.77 = (bf16[32,1024]{1,0:T(8,128)(2,1)S(1)}, bf16[32,1024]{1,0:T(8,128)(2,1)S(1)}, u32[]{:S(2)}, u32[]{:S(2)}) collective-permute-start(bf16[32,1024]{1,0:T(8,128)(2,1)S(1)} %get-tuple-element.149.refs_1_), channel_id=1, source_target_pairs={{0,16},{8,24},{16,0},{24,8},{1,17},{9,25},{17,1},{25,9},{2,18},{10... | collective-permute-start | bytes 196616 | tf_op jit(solution)/shard_map/ppermute | solution.py:271
  159.5 1.3 collective-permute-start.71
  163.6 1.3 collective-permute-start.81
  165.0 4.4 %collective-permute-start.72 = (bf16[32,1024]{1,0:T(8,128)(2,1)S(1)}, bf16[32,1024]{1,0:T(8,128)(2,1)S(1)}, u32[]{:S(2)}, u32[]{:S(2)}) collective-permute-start(bf16[32,1024]{1,0:T(8,128)(2,1)S(1)} %add_convert_fusion.1), channel_id=1, source_target_pairs={{0,0},{1,8},{2,16},{3,24},{8,1},{9,9},{10,17},{11,25},{16,2},{17,1... | collective-permute-start | bytes 196616 | tf_op jit(solution)/shard_map/ppermute | solution.py:426
  169.4 4.5 %collective-permute-start.82 = (bf16[32,1024]{1,0:T(8,128)(2,1)S(1)}, bf16[32,1024]{1,0:T(8,128)(2,1)S(1)}, u32[]{:S(2)}, u32[]{:S(2)}) collective-permute-start(bf16[32,1024]{1,0:T(8,128)(2,1)S(1)} %add_convert_fusion), channel_id=1, source_target_pairs={{0,0},{1,8},{2,16},{3,24},{8,1},{9,9},{10,17},{11,25},{16,2},{17,1... | collective-permute-start | bytes 196616 | tf_op jit(solution)/shard_map/ppermute | solution.py:426
  173.9 4.2 %collective-permute-done.82 = bf16[32,1024]{1,0:T(8,128)(2,1)S(1)} collective-permute-done((bf16[32,1024]{1,0:T(8,128)(2,1)S(1)}, bf16[32,1024]{1,0:T(8,128)(2,1)S(1)}, u32[]{:S(2)}, u32[]{:S(2)}) %collective-permute-start.82) | collective-permute-done | bytes 65568 | tf_op jit(solution)/shard_map/ppermute | solution.py:426
  178.1 6.4 %collective-permute-start.83 = (bf16[1,32,1024]{2,1,0:T(8,128)(2,1)S(1)}, bf16[1,32,1024]{2,1,0:T(8,128)(2,1)S(1)}, u32[]{:S(2)}, u32[]{:S(2)}) collective-permute-start(bf16[1,32,1024]{2,1,0:T(8,128)(2,1)S(1)} %select_bitcast_fusion.16), channel_id=1, source_target_pairs={{0,4},{4,0},{1,5},{5,1},{2,6},{6,2},{3,7},{7,3},{8,12},{12,8},{9,1... | collective-permute-start | bytes 196616 | tf_op jit(solution)/shard_map/ppermute | solution.py:271
  (165 shorter events, 46.3 us)
Async XLA Ops:
  2.2 19.9 %collective-permute-start.5 = (bf16[2,1,1024,1024]{3,2,1,0:T(8,128)(2,1)}, bf16[2,1,1024,1024]{3,2,1,0:T(8,128)(2,1)}, u32[]{:S(2)}, u32[]{:S(2)}) collective-permute-start(bf16[2,1,1024,1024]{3,2,1,0:T(8,128)(2,1)} %param.12), channel_id=1, source_target_pairs={{0,4},{4,0},{1,5},{5,1},{2,6},{6,2},{3,7},{7,3},{8,12},{12,8},{9,1... | collective-permute-start | bytes 12582920 | tf_op jit(solution)/shard_map/ppermute | solution.py:271
  2.5 28.8 %collective-permute-start.14 = (bf16[2,1,1024,1024]{3,2,1,0:T(8,128)(2,1)}, bf16[2,1,1024,1024]{3,2,1,0:T(8,128)(2,1)}, u32[]{:S(2)}, u32[]{:S(2)}) collective-permute-start(bf16[2,1,1024,1024]{3,2,1,0:T(8,128)(2,1)} %param.15), channel_id=1, source_target_pairs={{0,4},{4,0},{1,5},{5,1},{2,6},{6,2},{3,7},{7,3},{8,12},{12,8},{9,1... | collective-permute-start | bytes 12582920 | tf_op jit(solution)/shard_map/ppermute | solution.py:271
  2.7 16.0 %collective-permute-start.6 = (bf16[2,1,1024,256]{3,2,1,0:T(8,128)(2,1)}, bf16[2,1,1024,256]{3,2,1,0:T(8,128)(2,1)}, u32[]{:S(2)}, u32[]{:S(2)}) collective-permute-start(bf16[2,1,1024,256]{3,2,1,0:T(8,128)(2,1)} %param.13), channel_id=1, source_target_pairs={{0,4},{4,0},{1,5},{5,1},{2,6},{6,2},{3,7},{7,3},{8,12},{12,8},{9,1... | collective-permute-start | bytes 3145736 | tf_op jit(solution)/shard_map/ppermute | solution.py:271
  5.4 10.5 %collective-permute-start = (bf16[64,1024]{1,0:T(8,128)(2,1)S(1)}, bf16[64,1024]{1,0:T(8,128)(2,1)S(1)}, u32[]{:S(2)}, u32[]{:S(2)}) collective-permute-start(bf16[64,1024]{1,0:T(8,128)(2,1)S(1)} %bitcast.51), channel_id=1, source_target_pairs={{0,0},{1,8},{2,16},{3,24},{8,1},{9,9},{10,17},{11,25},{16,2},{17,1... | collective-permute-start | bytes 393224 | tf_op jit(solution)/shard_map/ppermute | solution.py:356
  10.6 10.1 %collective-permute-start.7 = (bf16[2,1,1024,256]{3,2,1,0:T(8,128)(2,1)}, bf16[2,1,1024,256]{3,2,1,0:T(8,128)(2,1)S(1)}, u32[]{:S(2)}, u32[]{:S(2)}) collective-permute-start(bf16[2,1,1024,256]{3,2,1,0:T(8,128)(2,1)} %param.14), channel_id=1, source_target_pairs={{0,4},{4,0},{1,5},{5,1},{2,6},{6,2},{3,7},{7,3},{8,12},{12,8},{9,1... | collective-permute-start | bytes 3145736 | tf_op jit(solution)/shard_map/ppermute | solution.py:271
  15.9 9.4 %collective-permute-start.3 = (bf16[64,1024]{1,0:T(8,128)(2,1)S(1)}, bf16[64,1024]{1,0:T(8,128)(2,1)S(1)}, u32[]{:S(2)}, u32[]{:S(2)}) collective-permute-start(bf16[64,1024]{1,0:T(8,128)(2,1)S(1)} %collective-permute-done.refs_1_), channel_id=1, source_target_pairs={{0,1},{1,0},{2,3},{3,2},{4,5},{5,4},{6,7},{7,6},{8,9},{9,8},{10,11... | collective-permute-start | bytes 393224 | tf_op jit(solution)/shard_map/ppermute | solution.py:271
  18.7 6.6 %collective-permute-start.2 = (bf16[64,1024]{1,0:T(8,128)(2,1)S(1)}, bf16[64,1024]{1,0:T(8,128)(2,1)S(1)}, u32[]{:S(2)}, u32[]{:S(2)}) collective-permute-start(bf16[64,1024]{1,0:T(8,128)(2,1)S(1)} %collective-permute-done.refs_1_), channel_id=1, source_target_pairs={{0,2},{1,3},{2,0},{3,1},{4,6},{5,7},{6,4},{7,5},{8,10},{9,11},{10,... | collective-permute-start | bytes 393224 | tf_op jit(solution)/shard_map/ppermute | solution.py:271
  26.6 7.5 %collective-permute-start.8 = (bf16[400,128]{1,0:T(8,128)(2,1)S(1)}, bf16[400,128]{1,0:T(8,128)(2,1)S(1)}, u32[]{:S(2)}, u32[]{:S(2)}) collective-permute-start(bf16[400,128]{1,0:T(8,128)(2,1)S(1)} %get-tuple-element.86), channel_id=1, source_target_pairs={{0,8},{8,0},{16,24},{24,16},{1,9},{9,1},{17,25},{25,17},{2,10},{10... | collective-permute-start | bytes 307208 | tf_op jit(solution)/shard_map/ppermute | solution.py:271
  30.4 6.4 %collective-permute-start.10 = (bf16[400,128]{1,0:T(8,128)(2,1)S(1)}, bf16[400,128]{1,0:T(8,128)(2,1)S(1)}, u32[]{:S(2)}, u32[]{:S(2)}) collective-permute-start(bf16[400,128]{1,0:T(8,128)(2,1)S(1)} %get-tuple-element.88), channel_id=1, source_target_pairs={{0,24},{8,16},{16,8},{24,0},{1,25},{9,17},{17,9},{25,1},{2,26},{10... | collective-permute-start | bytes 307208 | tf_op jit(solution)/shard_map/ppermute | solution.py:271
  37.7 7.5 %collective-permute-start.13 = (bf16[32,1024]{1,0:T(8,128)(2,1)S(1)}, bf16[32,1024]{1,0:T(8,128)(2,1)S(1)}, u32[]{:S(2)}, u32[]{:S(2)}) collective-permute-start(bf16[32,1024]{1,0:T(8,128)(2,1)S(1)} %get-tuple-element.91.refs_0_), channel_id=1, source_target_pairs={{0,24},{8,16},{16,8},{24,0},{1,25},{9,17},{17,9},{25,1},{2,26},{10... | collective-permute-start | bytes 196616 | tf_op jit(solution)/shard_map/ppermute | solution.py:271
  38.9 7.5 %collective-permute-start.12 = (bf16[32,1024]{1,0:T(8,128)(2,1)S(1)}, bf16[32,1024]{1,0:T(8,128)(2,1)S(1)}, u32[]{:S(2)}, u32[]{:S(2)}) collective-permute-start(bf16[32,1024]{1,0:T(8,128)(2,1)S(1)} %get-tuple-element.91.refs_0_), channel_id=1, source_target_pairs={{0,16},{8,24},{16,0},{24,8},{1,17},{9,25},{17,1},{25,9},{2,18},{10... | collective-permute-start | bytes 196616 | tf_op jit(solution)/shard_map/ppermute | solution.py:271
  42.8 5.9 %collective-permute-start.18 = (bf16[400,128]{1,0:T(8,128)(2,1)S(1)}, bf16[400,128]{1,0:T(8,128)(2,1)S(1)}, u32[]{:S(2)}, u32[]{:S(2)}) collective-permute-start(bf16[400,128]{1,0:T(8,128)(2,1)S(1)} %get-tuple-element.96), channel_id=1, source_target_pairs={{0,8},{8,0},{16,24},{24,16},{1,9},{9,1},{17,25},{25,17},{2,10},{10... | collective-permute-start | bytes 307208 | tf_op jit(solution)/shard_map/ppermute | solution.py:271
  44.1 6.4 %collective-permute-start.19 = (bf16[400,128]{1,0:T(8,128)(2,1)S(1)}, bf16[400,128]{1,0:T(8,128)(2,1)S(1)}, u32[]{:S(2)}, u32[]{:S(2)}) collective-permute-start(bf16[400,128]{1,0:T(8,128)(2,1)S(1)} %get-tuple-element.97), channel_id=1, source_target_pairs={{0,16},{8,24},{16,0},{24,8},{1,17},{9,25},{17,1},{25,9},{2,18},{10... | collective-permute-start | bytes 307208 | tf_op jit(solution)/shard_map/ppermute | solution.py:271
  45.3 7.8 %collective-permute-start.20 = (bf16[400,128]{1,0:T(8,128)(2,1)S(1)}, bf16[400,128]{1,0:T(8,128)(2,1)S(1)}, u32[]{:S(2)}, u32[]{:S(2)}) collective-permute-start(bf16[400,128]{1,0:T(8,128)(2,1)S(1)} %get-tuple-element.98), channel_id=1, source_target_pairs={{0,24},{8,16},{16,8},{24,0},{1,25},{9,17},{17,9},{25,1},{2,26},{10... | collective-permute-start | bytes 307208 | tf_op jit(solution)/shard_map/ppermute | solution.py:271
  46.9 12.3 %collective-permute-start.17 = (bf16[128,1024]{1,0:T(8,128)(2,1)S(1)}, bf16[128,1024]{1,0:T(8,128)(2,1)S(1)}, u32[]{:S(2)}, u32[]{:S(2)}) collective-permute-start(bf16[128,1024]{1,0:T(8,128)(2,1)S(1)} %project_out.8.refs_9_.refs_1_), channel_id=1, source_target_pairs={{0,1},{1,0},{2,3},{3,2},{4,5},{5,4},{6,7},{7,6},{8,9},{9,8},{10,11... | collective-permute-start | bytes 786440 | tf_op jit(solution)/shard_map/ppermute | solution.py:271
  46.9 12.3 %collective-permute-start.16 = (bf16[128,1024]{1,0:T(8,128)(2,1)S(1)}, bf16[128,1024]{1,0:T(8,128)(2,1)S(1)}, u32[]{:S(2)}, u32[]{:S(2)}) collective-permute-start(bf16[128,1024]{1,0:T(8,128)(2,1)S(1)} %project_out.8.refs_9_.refs_1_), channel_id=1, source_target_pairs={{0,2},{1,3},{2,0},{3,1},{4,6},{5,7},{6,4},{7,5},{8,10},{9,11},{10,... | collective-permute-start | bytes 786440 | tf_op jit(solution)/shard_map/ppermute | solution.py:271
  48.7 10.5 %collective-permute-start.15 = (bf16[128,1024]{1,0:T(8,128)(2,1)S(1)}, bf16[128,1024]{1,0:T(8,128)(2,1)S(1)}, u32[]{:S(2)}, u32[]{:S(2)}) collective-permute-start(bf16[128,1024]{1,0:T(8,128)(2,1)S(1)} %project_out.8.refs_9_.refs_1_), channel_id=1, source_target_pairs={{0,3},{1,2},{2,1},{3,0},{4,7},{5,6},{6,5},{7,4},{8,11},{9,10},{10,... | collective-permute-start | bytes 786440 | tf_op jit(solution)/shard_map/ppermute | solution.py:271
  54.2 7.2 %collective-permute-start.26 = (bf16[32,1024]{1,0:T(8,128)(2,1)S(1)}, bf16[32,1024]{1,0:T(8,128)(2,1)S(1)}, u32[]{:S(2)}, u32[]{:S(2)}) collective-permute-start(bf16[32,1024]{1,0:T(8,128)(2,1)S(1)} %get-tuple-element.106.refs_0_), channel_id=1, source_target_pairs={{0,24},{8,16},{16,8},{24,0},{1,25},{9,17},{17,9},{25,1},{2,26},{10... | collective-permute-start | bytes 196616 | tf_op jit(solution)/shard_map/ppermute | solution.py:271
  56.0 7.6 %collective-permute-start.25 = (bf16[32,1024]{1,0:T(8,128)(2,1)S(1)}, bf16[32,1024]{1,0:T(8,128)(2,1)S(1)}, u32[]{:S(2)}, u32[]{:S(2)}) collective-permute-start(bf16[32,1024]{1,0:T(8,128)(2,1)S(1)} %get-tuple-element.106.refs_0_), channel_id=1, source_target_pairs={{0,16},{8,24},{16,0},{24,8},{1,17},{9,25},{17,1},{25,9},{2,18},{10... | collective-permute-start | bytes 196616 | tf_op jit(solution)/shard_map/ppermute | solution.py:271
  59.9 6.0 %collective-permute-start.21 = (bf16[400,128]{1,0:T(8,128)(2,1)S(1)}, bf16[400,128]{1,0:T(8,128)(2,1)S(1)}, u32[]{:S(2)}, u32[]{:S(2)}) collective-permute-start(bf16[400,128]{1,0:T(8,128)(2,1)S(1)} %get-tuple-element.103), channel_id=1, source_target_pairs={{0,8},{8,0},{16,24},{24,16},{1,9},{9,1},{17,25},{25,17},{2,10},{10... | collective-permute-start | bytes 307208 | tf_op jit(solution)/shard_map/ppermute | solution.py:271
  61.4 6.1 %collective-permute-start.22 = (bf16[400,128]{1,0:T(8,128)(2,1)S(1)}, bf16[400,128]{1,0:T(8,128)(2,1)S(1)}, u32[]{:S(2)}, u32[]{:S(2)}) collective-permute-start(bf16[400,128]{1,0:T(8,128)(2,1)S(1)} %get-tuple-element.104), channel_id=1, source_target_pairs={{0,16},{8,24},{16,0},{24,8},{1,17},{9,25},{17,1},{25,9},{2,18},{10... | collective-permute-start | bytes 307208 | tf_op jit(solution)/shard_map/ppermute | solution.py:271
  61.4 8.4 %collective-permute-start.23 = (bf16[400,128]{1,0:T(8,128)(2,1)S(1)}, bf16[400,128]{1,0:T(8,128)(2,1)S(1)}, u32[]{:S(2)}, u32[]{:S(2)}) collective-permute-start(bf16[400,128]{1,0:T(8,128)(2,1)S(1)} %get-tuple-element.105), channel_id=1, source_target_pairs={{0,24},{8,16},{16,8},{24,0},{1,25},{9,17},{17,9},{25,1},{2,26},{10... | collective-permute-start | bytes 307208 | tf_op jit(solution)/shard_map/ppermute | solution.py:271
  64.1 11.5 %collective-permute-start.32 = (bf16[128,1024]{1,0:T(8,128)(2,1)S(1)}, bf16[128,1024]{1,0:T(8,128)(2,1)S(1)}, u32[]{:S(2)}, u32[]{:S(2)}) collective-permute-start(bf16[128,1024]{1,0:T(8,128)(2,1)S(1)} %project_out.9.refs_7_.refs_1_), channel_id=1, source_target_pairs={{0,1},{1,0},{2,3},{3,2},{4,5},{5,4},{6,7},{7,6},{8,9},{9,8},{10,11... | collective-permute-start | bytes 786440 | tf_op jit(solution)/shard_map/ppermute | solution.py:271
  64.1 11.4 %collective-permute-start.31 = (bf16[128,1024]{1,0:T(8,128)(2,1)S(1)}, bf16[128,1024]{1,0:T(8,128)(2,1)S(1)}, u32[]{:S(2)}, u32[]{:S(2)}) collective-permute-start(bf16[128,1024]{1,0:T(8,128)(2,1)S(1)} %project_out.9.refs_7_.refs_1_), channel_id=1, source_target_pairs={{0,2},{1,3},{2,0},{3,1},{4,6},{5,7},{6,4},{7,5},{8,10},{9,11},{10,... | collective-permute-start | bytes 786440 | tf_op jit(solution)/shard_map/ppermute | solution.py:271
  66.0 9.6 %collective-permute-start.30 = (bf16[128,1024]{1,0:T(8,128)(2,1)S(1)}, bf16[128,1024]{1,0:T(8,128)(2,1)S(1)}, u32[]{:S(2)}, u32[]{:S(2)}) collective-permute-start(bf16[128,1024]{1,0:T(8,128)(2,1)S(1)} %project_out.9.refs_7_.refs_1_), channel_id=1, source_target_pairs={{0,3},{1,2},{2,1},{3,0},{4,7},{5,6},{6,5},{7,4},{8,11},{9,10},{10,... | collective-permute-start | bytes 786440 | tf_op jit(solution)/shard_map/ppermute | solution.py:271
  70.8 7.3 %collective-permute-start.29 = (bf16[32,1024]{1,0:T(8,128)(2,1)S(1)}, bf16[32,1024]{1,0:T(8,128)(2,1)S(1)}, u32[]{:S(2)}, u32[]{:S(2)}) collective-permute-start(bf16[32,1024]{1,0:T(8,128)(2,1)S(1)} %get-tuple-element.107.refs_0_), channel_id=1, source_target_pairs={{0,24},{8,16},{16,8},{24,0},{1,25},{9,17},{17,9},{25,1},{2,26},{10... | collective-permute-start | bytes 196616 | tf_op jit(solution)/shard_map/ppermute | solution.py:271
  73.0 6.9 %collective-permute-start.28 = (bf16[32,1024]{1,0:T(8,128)(2,1)S(1)}, bf16[32,1024]{1,0:T(8,128)(2,1)S(1)}, u32[]{:S(2)}, u32[]{:S(2)}) collective-permute-start(bf16[32,1024]{1,0:T(8,128)(2,1)S(1)} %get-tuple-element.107.refs_0_), channel_id=1, source_target_pairs={{0,16},{8,24},{16,0},{24,8},{1,17},{9,25},{17,1},{25,9},{2,18},{10... | collective-permute-start | bytes 196616 | tf_op jit(solution)/shard_map/ppermute | solution.py:271
  77.8 6.4 %collective-permute-start.37 = (bf16[400,128]{1,0:T(8,128)(2,1)S(1)}, bf16[400,128]{1,0:T(8,128)(2,1)S(1)}, u32[]{:S(2)}, u32[]{:S(2)}) collective-permute-start(bf16[400,128]{1,0:T(8,128)(2,1)S(1)} %get-tuple-element.112), channel_id=1, source_target_pairs={{0,16},{8,24},{16,0},{24,8},{1,17},{9,25},{17,1},{25,9},{2,18},{10... | collective-permute-start | bytes 307208 | tf_op jit(solution)/shard_map/ppermute | solution.py:271
  78.1 8.0 %collective-permute-start.38 = (bf16[400,128]{1,0:T(8,128)(2,1)S(1)}, bf16[400,128]{1,0:T(8,128)(2,1)S(1)}, u32[]{:S(2)}, u32[]{:S(2)}) collective-permute-start(bf16[400,128]{1,0:T(8,128)(2,1)S(1)} %get-tuple-element.113), channel_id=1, source_target_pairs={{0,24},{8,16},{16,8},{24,0},{1,25},{9,17},{17,9},{25,1},{2,26},{10... | collective-permute-start | bytes 307208 | tf_op jit(solution)/shard_map/ppermute | solution.py:271
  80.4 11.8 %collective-permute-start.35 = (bf16[128,1024]{1,0:T(8,128)(2,1)S(1)}, bf16[128,1024]{1,0:T(8,128)(2,1)S(1)}, u32[]{:S(2)}, u32[]{:S(2)}) collective-permute-start(bf16[128,1024]{1,0:T(8,128)(2,1)S(1)} %project_out.10.refs_9_.refs_1_), channel_id=1, source_target_pairs={{0,1},{1,0},{2,3},{3,2},{4,5},{5,4},{6,7},{7,6},{8,9},{9,8},{10,11... | collective-permute-start | bytes 786440 | tf_op jit(solution)/shard_map/ppermute | solution.py:271
  80.6 11.6 %collective-permute-start.34 = (bf16[128,1024]{1,0:T(8,128)(2,1)S(1)}, bf16[128,1024]{1,0:T(8,128)(2,1)S(1)}, u32[]{:S(2)}, u32[]{:S(2)}) collective-permute-start(bf16[128,1024]{1,0:T(8,128)(2,1)S(1)} %project_out.10.refs_9_.refs_1_), channel_id=1, source_target_pairs={{0,2},{1,3},{2,0},{3,1},{4,6},{5,7},{6,4},{7,5},{8,10},{9,11},{10,... | collective-permute-start | bytes 786440 | tf_op jit(solution)/shard_map/ppermute | solution.py:271
  81.9 10.3 %collective-permute-start.33 = (bf16[128,1024]{1,0:T(8,128)(2,1)S(1)}, bf16[128,1024]{1,0:T(8,128)(2,1)S(1)}, u32[]{:S(2)}, u32[]{:S(2)}) collective-permute-start(bf16[128,1024]{1,0:T(8,128)(2,1)S(1)} %project_out.10.refs_9_.refs_1_), channel_id=1, source_target_pairs={{0,3},{1,2},{2,1},{3,0},{4,7},{5,6},{6,5},{7,4},{8,11},{9,10},{10,... | collective-permute-start | bytes 786440 | tf_op jit(solution)/shard_map/ppermute | solution.py:271
  87.3 7.5 %collective-permute-start.44 = (bf16[32,1024]{1,0:T(8,128)(2,1)S(1)}, bf16[32,1024]{1,0:T(8,128)(2,1)S(1)}, u32[]{:S(2)}, u32[]{:S(2)}) collective-permute-start(bf16[32,1024]{1,0:T(8,128)(2,1)S(1)} %get-tuple-element.121.refs_0_), channel_id=1, source_target_pairs={{0,24},{8,16},{16,8},{24,0},{1,25},{9,17},{17,9},{25,1},{2,26},{10... | collective-permute-start | bytes 196616 | tf_op jit(solution)/shard_map/ppermute | solution.py:271
  89.3 7.3 %collective-permute-start.43 = (bf16[32,1024]{1,0:T(8,128)(2,1)S(1)}, bf16[32,1024]{1,0:T(8,128)(2,1)S(1)}, u32[]{:S(2)}, u32[]{:S(2)}) collective-permute-start(bf16[32,1024]{1,0:T(8,128)(2,1)S(1)} %get-tuple-element.121.refs_0_), channel_id=1, source_target_pairs={{0,16},{8,24},{16,0},{24,8},{1,17},{9,25},{17,1},{25,9},{2,18},{10... | collective-permute-start | bytes 196616 | tf_op jit(solution)/shard_map/ppermute | solution.py:271
  94.4 6.2 %collective-permute-start.40 = (bf16[400,128]{1,0:T(8,128)(2,1)S(1)}, bf16[400,128]{1,0:T(8,128)(2,1)S(1)}, u32[]{:S(2)}, u32[]{:S(2)}) collective-permute-start(bf16[400,128]{1,0:T(8,128)(2,1)S(1)} %get-tuple-element.119), channel_id=1, source_target_pairs={{0,16},{8,24},{16,0},{24,8},{1,17},{9,25},{17,1},{25,9},{2,18},{10... | collective-permute-start | bytes 307208 | tf_op jit(solution)/shard_map/ppermute | solution.py:271
  94.7 8.1 %collective-permute-start.41 = (bf16[400,128]{1,0:T(8,128)(2,1)S(1)}, bf16[400,128]{1,0:T(8,128)(2,1)S(1)}, u32[]{:S(2)}, u32[]{:S(2)}) collective-permute-start(bf16[400,128]{1,0:T(8,128)(2,1)S(1)} %get-tuple-element.120), channel_id=1, source_target_pairs={{0,24},{8,16},{16,8},{24,0},{1,25},{9,17},{17,9},{25,1},{2,26},{10... | collective-permute-start | bytes 307208 | tf_op jit(solution)/shard_map/ppermute | solution.py:271
  97.0 11.5 %collective-permute-start.50 = (bf16[128,1024]{1,0:T(8,128)(2,1)S(1)}, bf16[128,1024]{1,0:T(8,128)(2,1)S(1)}, u32[]{:S(2)}, u32[]{:S(2)}) collective-permute-start(bf16[128,1024]{1,0:T(8,128)(2,1)S(1)} %project_out.11.refs_7_.refs_1_), channel_id=1, source_target_pairs={{0,1},{1,0},{2,3},{3,2},{4,5},{5,4},{6,7},{7,6},{8,9},{9,8},{10,11... | collective-permute-start | bytes 786440 | tf_op jit(solution)/shard_map/ppermute | solution.py:271
  97.1 11.4 %collective-permute-start.49 = (bf16[128,1024]{1,0:T(8,128)(2,1)S(1)}, bf16[128,1024]{1,0:T(8,128)(2,1)S(1)}, u32[]{:S(2)}, u32[]{:S(2)}) collective-permute-start(bf16[128,1024]{1,0:T(8,128)(2,1)S(1)} %project_out.11.refs_7_.refs_1_), channel_id=1, source_target_pairs={{0,2},{1,3},{2,0},{3,1},{4,6},{5,7},{6,4},{7,5},{8,10},{9,11},{10,... | collective-permute-start | bytes 786440 | tf_op jit(solution)/shard_map/ppermute | solution.py:271
  98.3 10.2 %collective-permute-start.48 = (bf16[128,1024]{1,0:T(8,128)(2,1)S(1)}, bf16[128,1024]{1,0:T(8,128)(2,1)S(1)}, u32[]{:S(2)}, u32[]{:S(2)}) collective-permute-start(bf16[128,1024]{1,0:T(8,128)(2,1)S(1)} %project_out.11.refs_7_.refs_1_), channel_id=1, source_target_pairs={{0,3},{1,2},{2,1},{3,0},{4,7},{5,6},{6,5},{7,4},{8,11},{9,10},{10,... | collective-permute-start | bytes 786440 | tf_op jit(solution)/shard_map/ppermute | solution.py:271
  103.8 7.4 %collective-permute-start.47 = (bf16[32,1024]{1,0:T(8,128)(2,1)S(1)}, bf16[32,1024]{1,0:T(8,128)(2,1)S(1)}, u32[]{:S(2)}, u32[]{:S(2)}) collective-permute-start(bf16[32,1024]{1,0:T(8,128)(2,1)S(1)} %get-tuple-element.122.refs_0_), channel_id=1, source_target_pairs={{0,24},{8,16},{16,8},{24,0},{1,25},{9,17},{17,9},{25,1},{2,26},{10... | collective-permute-start | bytes 196616 | tf_op jit(solution)/shard_map/ppermute | solution.py:271
  105.8 7.1 %collective-permute-start.46 = (bf16[32,1024]{1,0:T(8,128)(2,1)S(1)}, bf16[32,1024]{1,0:T(8,128)(2,1)S(1)}, u32[]{:S(2)}, u32[]{:S(2)}) collective-permute-start(bf16[32,1024]{1,0:T(8,128)(2,1)S(1)} %get-tuple-element.122.refs_0_), channel_id=1, source_target_pairs={{0,16},{8,24},{16,0},{24,8},{1,17},{9,25},{17,1},{25,9},{2,18},{10... | collective-permute-start | bytes 196616 | tf_op jit(solution)/shard_map/ppermute | solution.py:271
  110.7 6.3 %collective-permute-start.55 = (bf16[400,128]{1,0:T(8,128)(2,1)S(1)}, bf16[400,128]{1,0:T(8,128)(2,1)S(1)}, u32[]{:S(2)}, u32[]{:S(2)}) collective-permute-start(bf16[400,128]{1,0:T(8,128)(2,1)S(1)} %get-tuple-element.127), channel_id=1, source_target_pairs={{0,16},{8,24},{16,0},{24,8},{1,17},{9,25},{17,1},{25,9},{2,18},{10... | collective-permute-start | bytes 307208 | tf_op jit(solution)/shard_map/ppermute | solution.py:271
  111.2 8.1 %collective-permute-start.56 = (bf16[400,128]{1,0:T(8,128)(2,1)S(1)}, bf16[400,128]{1,0:T(8,128)(2,1)S(1)}, u32[]{:S(2)}, u32[]{:S(2)}) collective-permute-start(bf16[400,128]{1,0:T(8,128)(2,1)S(1)} %get-tuple-element.128), channel_id=1, source_target_pairs={{0,24},{8,16},{16,8},{24,0},{1,25},{9,17},{17,9},{25,1},{2,26},{10... | collective-permute-start | bytes 307208 | tf_op jit(solution)/shard_map/ppermute | solution.py:271
  113.4 11.8 %collective-permute-start.53 = (bf16[128,1024]{1,0:T(8,128)(2,1)S(1)}, bf16[128,1024]{1,0:T(8,128)(2,1)S(1)}, u32[]{:S(2)}, u32[]{:S(2)}) collective-permute-start(bf16[128,1024]{1,0:T(8,128)(2,1)S(1)} %project_out.12.refs_9_.refs_1_), channel_id=1, source_target_pairs={{0,1},{1,0},{2,3},{3,2},{4,5},{5,4},{6,7},{7,6},{8,9},{9,8},{10,11... | collective-permute-start | bytes 786440 | tf_op jit(solution)/shard_map/ppermute | solution.py:271
  113.5 11.7 %collective-permute-start.52 = (bf16[128,1024]{1,0:T(8,128)(2,1)S(1)}, bf16[128,1024]{1,0:T(8,128)(2,1)S(1)}, u32[]{:S(2)}, u32[]{:S(2)}) collective-permute-start(bf16[128,1024]{1,0:T(8,128)(2,1)S(1)} %project_out.12.refs_9_.refs_1_), channel_id=1, source_target_pairs={{0,2},{1,3},{2,0},{3,1},{4,6},{5,7},{6,4},{7,5},{8,10},{9,11},{10,... | collective-permute-start | bytes 786440 | tf_op jit(solution)/shard_map/ppermute | solution.py:271
  114.9 10.3 %collective-permute-start.51 = (bf16[128,1024]{1,0:T(8,128)(2,1)S(1)}, bf16[128,1024]{1,0:T(8,128)(2,1)S(1)}, u32[]{:S(2)}, u32[]{:S(2)}) collective-permute-start(bf16[128,1024]{1,0:T(8,128)(2,1)S(1)} %project_out.12.refs_9_.refs_1_), channel_id=1, source_target_pairs={{0,3},{1,2},{2,1},{3,0},{4,7},{5,6},{6,5},{7,4},{8,11},{9,10},{10,... | collective-permute-start | bytes 786440 | tf_op jit(solution)/shard_map/ppermute | solution.py:271
  120.4 7.4 %collective-permute-start.62 = (bf16[32,1024]{1,0:T(8,128)(2,1)S(1)}, bf16[32,1024]{1,0:T(8,128)(2,1)S(1)}, u32[]{:S(2)}, u32[]{:S(2)}) collective-permute-start(bf16[32,1024]{1,0:T(8,128)(2,1)S(1)} %get-tuple-element.136.refs_0_), channel_id=1, source_target_pairs={{0,24},{8,16},{16,8},{24,0},{1,25},{9,17},{17,9},{25,1},{2,26},{10... | collective-permute-start | bytes 196616 | tf_op jit(solution)/shard_map/ppermute | solution.py:271
  122.1 7.4 %collective-permute-start.61 = (bf16[32,1024]{1,0:T(8,128)(2,1)S(1)}, bf16[32,1024]{1,0:T(8,128)(2,1)S(1)}, u32[]{:S(2)}, u32[]{:S(2)}) collective-permute-start(bf16[32,1024]{1,0:T(8,128)(2,1)S(1)} %get-tuple-element.136.refs_0_), channel_id=1, source_target_pairs={{0,16},{8,24},{16,0},{24,8},{1,17},{9,25},{17,1},{25,9},{2,18},{10... | collective-permute-start | bytes 196616 | tf_op jit(solution)/shard_map/ppermute | solution.py:271
  127.4 6.1 %collective-permute-start.58 = (bf16[400,128]{1,0:T(8,128)(2,1)S(1)}, bf16[400,128]{1,0:T(8,128)(2,1)S(1)}, u32[]{:S(2)}, u32[]{:S(2)}) collective-permute-start(bf16[400,128]{1,0:T(8,128)(2,1)S(1)} %get-tuple-element.134), channel_id=1, source_target_pairs={{0,16},{8,24},{16,0},{24,8},{1,17},{9,25},{17,1},{25,9},{2,18},{10... | collective-permute-start | bytes 307208 | tf_op jit(solution)/shard_map/ppermute | solution.py:271
  127.9 8.2 %collective-permute-start.59 = (bf16[400,128]{1,0:T(8,128)(2,1)S(1)}, bf16[400,128]{1,0:T(8,128)(2,1)S(1)}, u32[]{:S(2)}, u32[]{:S(2)}) collective-permute-start(bf16[400,128]{1,0:T(8,128)(2,1)S(1)} %get-tuple-element.135), channel_id=1, source_target_pairs={{0,24},{8,16},{16,8},{24,0},{1,25},{9,17},{17,9},{25,1},{2,26},{10... | collective-permute-start | bytes 307208 | tf_op jit(solution)/shard_map/ppermute | solution.py:271
  130.0 11.7 %collective-permute-start.68 = (bf16[128,1024]{1,0:T(8,128)(2,1)S(1)}, bf16[128,1024]{1,0:T(8,128)(2,1)S(1)}, u32[]{:S(2)}, u32[]{:S(2)}) collective-permute-start(bf16[128,1024]{1,0:T(8,128)(2,1)S(1)} %project_out.13.refs_7_.refs_1_), channel_id=1, source_target_pairs={{0,1},{1,0},{2,3},{3,2},{4,5},{5,4},{6,7},{7,6},{8,9},{9,8},{10,11... | collective-permute-start | bytes 786440 | tf_op jit(solution)/shard_map/ppermute | solution.py:271
  130.1 11.6 %collective-permute-start.67 = (bf16[128,1024]{1,0:T(8,128)(2,1)S(1)}, bf16[128,1024]{1,0:T(8,128)(2,1)S(1)}, u32[]{:S(2)}, u32[]{:S(2)}) collective-permute-start(bf16[128,1024]{1,0:T(8,128)(2,1)S(1)} %project_out.13.refs_7_.refs_1_), channel_id=1, source_target_pairs={{0,2},{1,3},{2,0},{3,1},{4,6},{5,7},{6,4},{7,5},{8,10},{9,11},{10,... | collective-permute-start | bytes 786440 | tf_op jit(solution)/shard_map/ppermute | solution.py:271
  131.4 10.4 %collective-permute-start.66 = (bf16[128,1024]{1,0:T(8,128)(2,1)S(1)}, bf16[128,1024]{1,0:T(8,128)(2,1)S(1)}, u32[]{:S(2)}, u32[]{:S(2)}) collective-permute-start(bf16[128,1024]{1,0:T(8,128)(2,1)S(1)} %project_out.13.refs_7_.refs_1_), channel_id=1, source_target_pairs={{0,3},{1,2},{2,1},{3,0},{4,7},{5,6},{6,5},{7,4},{8,11},{9,10},{10,... | collective-permute-start | bytes 786440 | tf_op jit(solution)/shard_map/ppermute | solution.py:271
  137.0 7.5 %collective-permute-start.65 = (bf16[32,1024]{1,0:T(8,128)(2,1)S(1)}, bf16[32,1024]{1,0:T(8,128)(2,1)S(1)}, u32[]{:S(2)}, u32[]{:S(2)}) collective-permute-start(bf16[32,1024]{1,0:T(8,128)(2,1)S(1)} %get-tuple-element.137.refs_1_), channel_id=1, source_target_pairs={{0,24},{8,16},{16,8},{24,0},{1,25},{9,17},{17,9},{25,1},{2,26},{10... | collective-permute-start | bytes 196616 | tf_op jit(solution)/shard_map/ppermute | solution.py:271
  138.9 7.2 %collective-permute-start.64 = (bf16[32,1024]{1,0:T(8,128)(2,1)S(1)}, bf16[32,1024]{1,0:T(8,128)(2,1)S(1)}, u32[]{:S(2)}, u32[]{:S(2)}) collective-permute-start(bf16[32,1024]{1,0:T(8,128)(2,1)S(1)} %get-tuple-element.137.refs_1_), channel_id=1, source_target_pairs={{0,16},{8,24},{16,0},{24,8},{1,17},{9,25},{17,1},{25,9},{2,18},{10... | collective-permute-start | bytes 196616 | tf_op jit(solution)/shard_map/ppermute | solution.py:271
  143.9 6.2 %collective-permute-start.74 = (bf16[400,128]{1,0:T(8,128)(2,1)S(1)}, bf16[400,128]{1,0:T(8,128)(2,1)S(1)}, u32[]{:S(2)}, u32[]{:S(2)}) collective-permute-start(bf16[400,128]{1,0:T(8,128)(2,1)S(1)} %get-tuple-element.146), channel_id=1, source_target_pairs={{0,16},{8,24},{16,0},{24,8},{1,17},{9,25},{17,1},{25,9},{2,18},{10... | collective-permute-start | bytes 307208 | tf_op jit(solution)/shard_map/ppermute | solution.py:271
  144.5 8.2 %collective-permute-start.75 = (bf16[400,128]{1,0:T(8,128)(2,1)S(1)}, bf16[400,128]{1,0:T(8,128)(2,1)S(1)}, u32[]{:S(2)}, u32[]{:S(2)}) collective-permute-start(bf16[400,128]{1,0:T(8,128)(2,1)S(1)} %get-tuple-element.147), channel_id=1, source_target_pairs={{0,24},{8,16},{16,8},{24,0},{1,25},{9,17},{17,9},{25,1},{2,26},{10... | collective-permute-start | bytes 307208 | tf_op jit(solution)/shard_map/ppermute | solution.py:271
  158.7 6.2 %collective-permute-start.70 = (bf16[32,1024]{1,0:T(8,128)(2,1)S(1)}, bf16[32,1024]{1,0:T(8,128)(2,1)S(1)}, u32[]{:S(2)}, u32[]{:S(2)}) collective-permute-start(bf16[32,1024]{1,0:T(8,128)(2,1)S(1)} %get-tuple-element.142), channel_id=1, source_target_pairs={{0,2},{1,3},{2,0},{3,1},{4,6},{5,7},{6,4},{7,5},{8,10},{9,11},{10,... | collective-permute-start | bytes 196616 | tf_op jit(solution)/shard_map/ppermute | solution.py:271
  162.2 7.2 %collective-permute-start.79 = (bf16[32,1024]{1,0:T(8,128)(2,1)S(1)}, bf16[32,1024]{1,0:T(8,128)(2,1)S(1)}, u32[]{:S(2)}, u32[]{:S(2)}) collective-permute-start(bf16[32,1024]{1,0:T(8,128)(2,1)S(1)} %get-tuple-element.152), channel_id=1, source_target_pairs={{0,3},{1,2},{2,1},{3,0},{4,7},{5,6},{6,5},{7,4},{8,11},{9,10},{10,... | collective-permute-start | bytes 196616 | tf_op jit(solution)/shard_map/ppermute | solution.py:271
  162.9 6.4 %collective-permute-start.80 = (bf16[32,1024]{1,0:T(8,128)(2,1)S(1)}, bf16[32,1024]{1,0:T(8,128)(2,1)S(1)}, u32[]{:S(2)}, u32[]{:S(2)}) collective-permute-start(bf16[32,1024]{1,0:T(8,128)(2,1)S(1)} %get-tuple-element.153), channel_id=1, source_target_pairs={{0,2},{1,3},{2,0},{3,1},{4,6},{5,7},{6,4},{7,5},{8,10},{9,11},{10,... | collective-permute-start | bytes 196616 | tf_op jit(solution)/shard_map/ppermute | solution.py:271
  163.6 5.7 %collective-permute-start.81 = (bf16[32,1024]{1,0:T(8,128)(2,1)S(1)}, bf16[32,1024]{1,0:T(8,128)(2,1)S(1)}, u32[]{:S(2)}, u32[]{:S(2)}) collective-permute-start(bf16[32,1024]{1,0:T(8,128)(2,1)S(1)} %get-tuple-element.154), channel_id=1, source_target_pairs={{0,1},{1,0},{2,3},{3,2},{4,5},{5,4},{6,7},{7,6},{8,9},{9,8},{10,11... | collective-permute-start | bytes 196616 | tf_op jit(solution)/shard_map/ppermute | solution.py:271
  165.0 9.0 %collective-permute-start.72 = (bf16[32,1024]{1,0:T(8,128)(2,1)S(1)}, bf16[32,1024]{1,0:T(8,128)(2,1)S(1)}, u32[]{:S(2)}, u32[]{:S(2)}) collective-permute-start(bf16[32,1024]{1,0:T(8,128)(2,1)S(1)} %add_convert_fusion.1), channel_id=1, source_target_pairs={{0,0},{1,8},{2,16},{3,24},{8,1},{9,9},{10,17},{11,25},{16,2},{17,1... | collective-permute-start | bytes 196616 | tf_op jit(solution)/shard_map/ppermute | solution.py:426
  169.4 8.7 %collective-permute-start.82 = (bf16[32,1024]{1,0:T(8,128)(2,1)S(1)}, bf16[32,1024]{1,0:T(8,128)(2,1)S(1)}, u32[]{:S(2)}, u32[]{:S(2)}) collective-permute-start(bf16[32,1024]{1,0:T(8,128)(2,1)S(1)} %add_convert_fusion), channel_id=1, source_target_pairs={{0,0},{1,8},{2,16},{3,24},{8,1},{9,9},{10,17},{11,25},{16,2},{17,1... | collective-permute-start | bytes 196616 | tf_op jit(solution)/shard_map/ppermute | solution.py:426
  178.1 7.3 %collective-permute-start.83 = (bf16[1,32,1024]{2,1,0:T(8,128)(2,1)S(1)}, bf16[1,32,1024]{2,1,0:T(8,128)(2,1)S(1)}, u32[]{:S(2)}, u32[]{:S(2)}) collective-permute-start(bf16[1,32,1024]{2,1,0:T(8,128)(2,1)S(1)} %select_bitcast_fusion.16), channel_id=1, source_target_pairs={{0,4},{4,0},{1,5},{5,1},{2,6},{6,2},{3,7},{7,3},{8,12},{12,8},{9,1... | collective-permute-start | bytes 196616 | tf_op jit(solution)/shard_map/ppermute | solution.py:271
  (29 other events, 135.5 us)

commit v6 on v5

--- a/solution.py
+++ b/solution.py
@@ -365,7 +365,7 @@
     weights = [layer_weights(*layer) for layer in layers]
     streams, sums, mixed, shares = ([None] * parts for _ in range(4))
     before = [[] for _ in layers]
-    layout, latest = None, []
+    layout, latest, done = None, [], []
 
     def share_out(h, number):
         nonlocal layout, latest
@@ -404,31 +404,28 @@
             place_out if paired and last else None,
             weights[number][4],
             groups if paired and last else 1,
-            latest,
+            latest + done,
         )
         latest = ends[:1]
         if not paired:
             shares[h] = [lax.psum(ends[0].astype(jnp.float32), "tensor")]
         elif last:
-            shares[h] = trade_blocks(ends, "tensor")
+            share = total_of(trade_blocks(ends, "tensor"))
+            stream = lax.dynamic_slice_in_dim(streams[h], place[0] * part_rows, part_rows, 0)
+            done.append((stream.astype(jnp.float32) + share).astype(jnp.bfloat16))
         else:
             shares[h] = gather_blocks(ends[0], "tensor", groups)
 
     for step, h, number in steps_of(parts, len(layers)):
         (share_out, mix, bring_in)[step](h, number)
 
-    final = []
-    for stream, share in zip(streams, shares):
-        share = total_of(share)
-        if paired:
-            stream = lax.dynamic_slice_in_dim(stream, place[0] * part_rows, part_rows, 0)
-            stream = (stream.astype(jnp.float32) + share).astype(jnp.bfloat16)
-            stream = lax.ppermute(stream, ("dp", "tensor"), turn)
-        else:
-            stream = (stream.astype(jnp.float32) + share).astype(jnp.bfloat16)
+    final = [lax.ppermute(stream, ("dp", "tensor"), turn) for stream in done]
+    if not paired:
+        for stream, share in zip(streams, shares):
+            stream = (stream.astype(jnp.float32) + total_of(share)).astype(jnp.bfloat16)
             stream = lax.all_to_all(stream, "dp", split_axis=0, concat_axis=1, tiled=True)
-            stream = lax.dynamic_slice_in_dim(stream, my_group * local_width, local_width, 1)
-        final.append(stream.reshape(slots, part_len, local_width))
+            final.append(lax.dynamic_slice_in_dim(stream, my_group * local_width, local_width, 1))
+    final = [stream.reshape(slots, part_len, local_width) for stream in final]
     if parts == sections == 2:
         first = my_section == 0
         came = swapped(jnp.where(first, final[1], final[0]), "pipe", 1)

time: 186 us -> 186 us (level)
  waiting for transfers between devices: 38.8 us -> 33.8 us
  starting transfers between devices: 114 us -> 118 us
    ppermute x81, starting transfers between devices: 99.7 us -> 104 us  [swapped(): lax.ppermute(value, axis, [(i, i ^ by) for i in range(lax.axis_size(axis))])]
    ppermute x81, waiting for transfers between devices: 31.3 us -> 26.8 us  [swapped(): lax.ppermute(value, axis, [(i, i ^ by) for i in range(lax.axis_size(axis))])]
  transfers between devices with their start and end apart: 84 -> 84, of which waited for: 23 -> 22; matrix products, arithmetic and copies ran while one was open for 5% -> 5% of each run, Pallas kernels for 10% -> 10%
where the time goes in v6:
time: 186 us
  starting transfers between devices  118 us (63%)
  waiting for transfers between devices  33.8 us (18%)
  Pallas kernels  20.6 us (11%)
  other arithmetic  9.1 us (5%)
  local copies, waits for them, and re-layouts  3.1 us (2%)
    ppermute x81, starting transfers between devices, swapped(): lax.ppermute(value, axis, [(i, i ^ by) for i in range(lax.axis_size(axis))])  104 us
    ppermute x81, waiting for transfers between devices, swapped(): lax.ppermute(value, axis, [(i, i ^ by) for i in range(lax.axis_size(axis))])  26.8 us
    ppermute x2, starting transfers between devices, per_device(): final = [lax.ppermute(stream, ('dp', 'tensor'), turn) for stream in done]  8.87 us
    pallas_call x8, Pallas kernels, attend(): pl.pallas_call(unread(len(after), len(blocks) + 2 * len(before) + 3, part...  8.17 us
    select_n x5, other arithmetic, layer_weights(): jnp.where(my_section == section, mine[index, 0], theirs[index, 0])  7.42 us
    pallas_call x8, Pallas kernels, project_qkv(): pl.pallas_call(unread(len(after), len(arrays) + 5, partial(qkv_kernel, le...  6.38 us
    ppermute x1, starting transfers between devices, per_device(): lax.ppermute(stream, ('dp', 'tensor'), turn)  5.14 us
    pallas_call x8, Pallas kernels, project_out(): pl.pallas_call(unread(len(after), placed + n_in + 1, partial(out_kernel,...  4.69 us
  transfers between devices with their start and end apart: 84, of which 22 were waited for; matrix products, arithmetic and copies ran while one was open for 5% of the time, Pallas kernels for 10%

profile of v6, /device:TPU:7, one launch (start us, length us, event | category | flops | bytes accessed | tf_op | source)
XLA Modules:
  0.0 185.7 jit_solution(7291457232350097394)
XLA Ops:
  5.4 5.1 %collective-permute-start = (bf16[64,1024]{1,0:T(8,128)(2,1)S(1)}, bf16[64,1024]{1,0:T(8,128)(2,1)S(1)}, u32[]{:S(2)}, u32[]{:S(2)}) collective-permute-start(bf16[64,1024]{1,0:T(8,128)(2,1)S(1)} %bitcast.51), channel_id=1, source_target_pairs={{0,0},{1,8},{2,16},{3,24},{8,1},{9,9},{10,17},{11,25},{16,2},{17,1... | collective-permute-start | bytes 393224 | tf_op jit(solution)/shard_map/ppermute | solution.py:356
  12.6 3.3 %collective-permute-done.refs_1_ = bf16[64,1024]{1,0:T(8,128)(2,1)S(1)} collective-permute-done((bf16[64,1024]{1,0:T(8,128)(2,1)S(1)}, bf16[64,1024]{1,0:T(8,128)(2,1)S(1)}, u32[]{:S(2)}, u32[]{:S(2)}) %collective-permute-start) | collective-permute-done | bytes 131104 | tf_op jit(solution)/shard_map/ppermute | solution.py:356
  15.9 1.3 collective-permute-start.3
  17.1 1.8 collective-permute-start.2
  19.0 1.4 select_bitcast_fusion.9
  20.4 1.2 collective-permute-start.1
  22.6 2.5 %select_bitcast_fusion.1 = (bf16[1024,1024]{1,0:T(8,128)(2,1)S(1)}, bf16[1024,1024]{1,0:T(8,128)(2,1)S(1)}, bf16[1024,1024]{1,0:T(8,128)(2,1)S(1)}, bf16[1024,1024]{1,0:T(8,128)(2,1)S(1)}) fusion(pred[]{:T(512)S(6)} %eq.4, bf16[2,1,1024,1024]{3,2,1,0:T(8,128)(2,1)} %collective-permute-done.5, bf16[2,1,1024,1024]{3,2,1,0:T(8,128)(2,1)S(1)} %copy-done.6, pred[]{:T(512)S(6)} %eq.5), kind=kLoop, calls=%fused_computation.1 | loop fusion | flops 4194304 | bytes 16777218 | tf_op jit(solution)/shard_map/jit(_where)/select_n | solution.py:342
  26.6 3.6 %collective-permute-start.9 = (bf16[400,128]{1,0:T(8,128)(2,1)S(1)}, bf16[400,128]{1,0:T(8,128)(2,1)S(1)}, u32[]{:S(2)}, u32[]{:S(2)}) collective-permute-start(bf16[400,128]{1,0:T(8,128)(2,1)S(1)} %get-tuple-element.87), channel_id=1, source_target_pairs={{0,16},{8,24},{16,0},{24,8},{1,17},{9,25},{17,1},{25,9},{2,18},{10... | collective-permute-start | bytes 307208 | tf_op jit(solution)/shard_map/ppermute | solution.py:271
  30.9 2.7 %select_bitcast_fusion = (bf16[1024,1024]{1,0:T(8,128)(2,1)S(1)}, bf16[1024,1024]{1,0:T(8,128)(2,1)S(1)}, bf16[1024,1024]{1,0:T(8,128)(2,1)S(1)}, bf16[1024,1024]{1,0:T(8,128)(2,1)S(1)}) fusion(pred[]{:T(512)S(6)} %eq.4, bf16[2,1,1024,1024]{3,2,1,0:T(8,128)(2,1)} %collective-permute-done.14, bf16[2,1,1024,1024]{3,2,1,0:T(8,128)(2,1)S(1)} %copy-done.7, pred[]{:T(512)S(6)} %eq.5), kind=kLoop, calls=%fused_computation | loop fusion | flops 4194304 | bytes 16777218 | tf_op jit(solution)/shard_map/jit(_where)/select_n | solution.py:342
  33.7 2.9 %collective-permute-done.10.refs_3_ = bf16[400,128]{1,0:T(8,128)(2,1)S(1)} collective-permute-done((bf16[400,128]{1,0:T(8,128)(2,1)S(1)}, bf16[400,128]{1,0:T(8,128)(2,1)S(1)}, u32[]{:S(2)}, u32[]{:S(2)}) %collective-permute-start.10) | collective-permute-done | bytes 102432 | tf_op jit(solution)/shard_map/ppermute | solution.py:271
  37.9 3.1 %collective-permute-start.12 = (bf16[32,1024]{1,0:T(8,128)(2,1)S(1)}, bf16[32,1024]{1,0:T(8,128)(2,1)S(1)}, u32[]{:S(2)}, u32[]{:S(2)}) collective-permute-start(bf16[32,1024]{1,0:T(8,128)(2,1)S(1)} %get-tuple-element.91.refs_0_), channel_id=1, source_target_pairs={{0,16},{8,24},{16,0},{24,8},{1,17},{9,25},{17,1},{25,9},{2,18},{10... | collective-permute-start | bytes 196616 | tf_op jit(solution)/shard_map/ppermute | solution.py:271
  42.4 1.3 collective-permute-start.18
  43.7 1.2 collective-permute-start.19
  46.6 1.4 collective-permute-start.16
  48.0 1.2 collective-permute-start.15
  49.4 3.6 %collective-permute-done.20.refs_3_ = bf16[400,128]{1,0:T(8,128)(2,1)S(1)} collective-permute-done((bf16[400,128]{1,0:T(8,128)(2,1)S(1)}, bf16[400,128]{1,0:T(8,128)(2,1)S(1)}, u32[]{:S(2)}, u32[]{:S(2)}) %collective-permute-start.20) | collective-permute-done | bytes 102432 | tf_op jit(solution)/shard_map/ppermute | solution.py:271
  55.3 3.0 %collective-permute-start.25 = (bf16[32,1024]{1,0:T(8,128)(2,1)S(1)}, bf16[32,1024]{1,0:T(8,128)(2,1)S(1)}, u32[]{:S(2)}, u32[]{:S(2)}) collective-permute-start(bf16[32,1024]{1,0:T(8,128)(2,1)S(1)} %get-tuple-element.106.refs_0_), channel_id=1, source_target_pairs={{0,16},{8,24},{16,0},{24,8},{1,17},{9,25},{17,1},{25,9},{2,18},{10... | collective-permute-start | bytes 196616 | tf_op jit(solution)/shard_map/ppermute | solution.py:271
  59.0 1.5 collective-permute-start.21
  60.8 1.9 %collective-permute-start.23 = (bf16[400,128]{1,0:T(8,128)(2,1)S(1)}, bf16[400,128]{1,0:T(8,128)(2,1)S(1)}, u32[]{:S(2)}, u32[]{:S(2)}) collective-permute-start(bf16[400,128]{1,0:T(8,128)(2,1)S(1)} %get-tuple-element.105), channel_id=1, source_target_pairs={{0,24},{8,16},{16,8},{24,0},{1,25},{9,17},{17,9},{25,1},{2,26},{10... | collective-permute-start | bytes 307208 | tf_op jit(solution)/shard_map/ppermute | solution.py:271
  63.7 1.2 collective-permute-start.31
  65.0 1.9 %collective-permute-start.30 = (bf16[128,1024]{1,0:T(8,128)(2,1)S(1)}, bf16[128,1024]{1,0:T(8,128)(2,1)S(1)}, u32[]{:S(2)}, u32[]{:S(2)}) collective-permute-start(bf16[128,1024]{1,0:T(8,128)(2,1)S(1)} %project_out.9.refs_7_.refs_1_), channel_id=1, source_target_pairs={{0,3},{1,2},{2,1},{3,0},{4,7},{5,6},{6,5},{7,4},{8,11},{9,10},{10,... | collective-permute-start | bytes 786440 | tf_op jit(solution)/shard_map/ppermute | solution.py:271
  67.4 1.3 collective-permute-done.23.refs_3_
  69.6 2.3 %collective-permute-start.29 = (bf16[32,1024]{1,0:T(8,128)(2,1)S(1)}, bf16[32,1024]{1,0:T(8,128)(2,1)S(1)}, u32[]{:S(2)}, u32[]{:S(2)}) collective-permute-start(bf16[32,1024]{1,0:T(8,128)(2,1)S(1)} %get-tuple-element.107.refs_0_), channel_id=1, source_target_pairs={{0,24},{8,16},{16,8},{24,0},{1,25},{9,17},{17,9},{25,1},{2,26},{10... | collective-permute-start | bytes 196616 | tf_op jit(solution)/shard_map/ppermute | solution.py:271
  71.9 3.2 %collective-permute-start.28 = (bf16[32,1024]{1,0:T(8,128)(2,1)S(1)}, bf16[32,1024]{1,0:T(8,128)(2,1)S(1)}, u32[]{:S(2)}, u32[]{:S(2)}) collective-permute-start(bf16[32,1024]{1,0:T(8,128)(2,1)S(1)} %get-tuple-element.107.refs_0_), channel_id=1, source_target_pairs={{0,16},{8,24},{16,0},{24,8},{1,17},{9,25},{17,1},{25,9},{2,18},{10... | collective-permute-start | bytes 196616 | tf_op jit(solution)/shard_map/ppermute | solution.py:271
  75.8 1.5 collective-permute-start.36
  77.5 2.0 %collective-permute-start.38 = (bf16[400,128]{1,0:T(8,128)(2,1)S(1)}, bf16[400,128]{1,0:T(8,128)(2,1)S(1)}, u32[]{:S(2)}, u32[]{:S(2)}) collective-permute-start(bf16[400,128]{1,0:T(8,128)(2,1)S(1)} %get-tuple-element.113), channel_id=1, source_target_pairs={{0,24},{8,16},{16,8},{24,0},{1,25},{9,17},{17,9},{25,1},{2,26},{10... | collective-permute-start | bytes 307208 | tf_op jit(solution)/shard_map/ppermute | solution.py:271
  81.6 1.8 collective-permute-start.33
  83.5 2.0 %collective-permute-done.38.refs_3_ = bf16[400,128]{1,0:T(8,128)(2,1)S(1)} collective-permute-done((bf16[400,128]{1,0:T(8,128)(2,1)S(1)}, bf16[400,128]{1,0:T(8,128)(2,1)S(1)}, u32[]{:S(2)}, u32[]{:S(2)}) %collective-permute-start.38) | collective-permute-done | bytes 102432 | tf_op jit(solution)/shard_map/ppermute | solution.py:271
  86.7 2.2 %collective-permute-start.44 = (bf16[32,1024]{1,0:T(8,128)(2,1)S(1)}, bf16[32,1024]{1,0:T(8,128)(2,1)S(1)}, u32[]{:S(2)}, u32[]{:S(2)}) collective-permute-start(bf16[32,1024]{1,0:T(8,128)(2,1)S(1)} %get-tuple-element.121.refs_0_), channel_id=1, source_target_pairs={{0,24},{8,16},{16,8},{24,0},{1,25},{9,17},{17,9},{25,1},{2,26},{10... | collective-permute-start | bytes 196616 | tf_op jit(solution)/shard_map/ppermute | solution.py:271
  88.9 2.7 %collective-permute-start.43 = (bf16[32,1024]{1,0:T(8,128)(2,1)S(1)}, bf16[32,1024]{1,0:T(8,128)(2,1)S(1)}, u32[]{:S(2)}, u32[]{:S(2)}) collective-permute-start(bf16[32,1024]{1,0:T(8,128)(2,1)S(1)} %get-tuple-element.121.refs_0_), channel_id=1, source_target_pairs={{0,16},{8,24},{16,0},{24,8},{1,17},{9,25},{17,1},{25,9},{2,18},{10... | collective-permute-start | bytes 196616 | tf_op jit(solution)/shard_map/ppermute | solution.py:271
  92.2 1.5 collective-permute-start.39
  93.9 2.0 %collective-permute-start.41 = (bf16[400,128]{1,0:T(8,128)(2,1)S(1)}, bf16[400,128]{1,0:T(8,128)(2,1)S(1)}, u32[]{:S(2)}, u32[]{:S(2)}) collective-permute-start(bf16[400,128]{1,0:T(8,128)(2,1)S(1)} %get-tuple-element.120), channel_id=1, source_target_pairs={{0,24},{8,16},{16,8},{24,0},{1,25},{9,17},{17,9},{25,1},{2,26},{10... | collective-permute-start | bytes 307208 | tf_op jit(solution)/shard_map/ppermute | solution.py:271
  96.5 1.5 collective-permute-start.49
  97.9 1.2 collective-permute-start.48
  100.2 1.7 collective-permute-done.41.refs_3_
  102.9 2.3 %collective-permute-start.47 = (bf16[32,1024]{1,0:T(8,128)(2,1)S(1)}, bf16[32,1024]{1,0:T(8,128)(2,1)S(1)}, u32[]{:S(2)}, u32[]{:S(2)}) collective-permute-start(bf16[32,1024]{1,0:T(8,128)(2,1)S(1)} %get-tuple-element.122.refs_0_), channel_id=1, source_target_pairs={{0,24},{8,16},{16,8},{24,0},{1,25},{9,17},{17,9},{25,1},{2,26},{10... | collective-permute-start | bytes 196616 | tf_op jit(solution)/shard_map/ppermute | solution.py:271
  105.2 2.8 %collective-permute-start.46 = (bf16[32,1024]{1,0:T(8,128)(2,1)S(1)}, bf16[32,1024]{1,0:T(8,128)(2,1)S(1)}, u32[]{:S(2)}, u32[]{:S(2)}) collective-permute-start(bf16[32,1024]{1,0:T(8,128)(2,1)S(1)} %get-tuple-element.122.refs_0_), channel_id=1, source_target_pairs={{0,16},{8,24},{16,0},{24,8},{1,17},{9,25},{17,1},{25,9},{2,18},{10... | collective-permute-start | bytes 196616 | tf_op jit(solution)/shard_map/ppermute | solution.py:271
  108.7 1.5 collective-permute-start.54
  110.5 1.9 %collective-permute-start.56 = (bf16[400,128]{1,0:T(8,128)(2,1)S(1)}, bf16[400,128]{1,0:T(8,128)(2,1)S(1)}, u32[]{:S(2)}, u32[]{:S(2)}) collective-permute-start(bf16[400,128]{1,0:T(8,128)(2,1)S(1)} %get-tuple-element.128), channel_id=1, source_target_pairs={{0,24},{8,16},{16,8},{24,0},{1,25},{9,17},{17,9},{25,1},{2,26},{10... | collective-permute-start | bytes 307208 | tf_op jit(solution)/shard_map/ppermute | solution.py:271
  113.3 1.2 collective-permute-start.52
  115.6 1.2 collective-permute-done.55.refs_2_
  116.7 1.7 collective-permute-done.56.refs_3_
  119.6 2.1 %collective-permute-start.62 = (bf16[32,1024]{1,0:T(8,128)(2,1)S(1)}, bf16[32,1024]{1,0:T(8,128)(2,1)S(1)}, u32[]{:S(2)}, u32[]{:S(2)}) collective-permute-start(bf16[32,1024]{1,0:T(8,128)(2,1)S(1)} %get-tuple-element.136.refs_0_), channel_id=1, source_target_pairs={{0,24},{8,16},{16,8},{24,0},{1,25},{9,17},{17,9},{25,1},{2,26},{10... | collective-permute-start | bytes 196616 | tf_op jit(solution)/shard_map/ppermute | solution.py:271
  121.7 2.9 %collective-permute-start.61 = (bf16[32,1024]{1,0:T(8,128)(2,1)S(1)}, bf16[32,1024]{1,0:T(8,128)(2,1)S(1)}, u32[]{:S(2)}, u32[]{:S(2)}) collective-permute-start(bf16[32,1024]{1,0:T(8,128)(2,1)S(1)} %get-tuple-element.136.refs_0_), channel_id=1, source_target_pairs={{0,16},{8,24},{16,0},{24,8},{1,17},{9,25},{17,1},{25,9},{2,18},{10... | collective-permute-start | bytes 196616 | tf_op jit(solution)/shard_map/ppermute | solution.py:271
  125.4 1.5 collective-permute-start.57
  127.0 2.0 %collective-permute-start.59 = (bf16[400,128]{1,0:T(8,128)(2,1)S(1)}, bf16[400,128]{1,0:T(8,128)(2,1)S(1)}, u32[]{:S(2)}, u32[]{:S(2)}) collective-permute-start(bf16[400,128]{1,0:T(8,128)(2,1)S(1)} %get-tuple-element.135), channel_id=1, source_target_pairs={{0,24},{8,16},{16,8},{24,0},{1,25},{9,17},{17,9},{25,1},{2,26},{10... | collective-permute-start | bytes 307208 | tf_op jit(solution)/shard_map/ppermute | solution.py:271
  129.6 1.4 collective-permute-start.67
  130.9 1.3 collective-permute-start.66
  133.2 1.7 collective-permute-done.59.refs_3_
  135.9 2.7 %collective-permute-start.65 = (bf16[32,1024]{1,0:T(8,128)(2,1)S(1)}, bf16[32,1024]{1,0:T(8,128)(2,1)S(1)}, u32[]{:S(2)}, u32[]{:S(2)}) collective-permute-start(bf16[32,1024]{1,0:T(8,128)(2,1)S(1)} %get-tuple-element.137.refs_1_), channel_id=1, source_target_pairs={{0,24},{8,16},{16,8},{24,0},{1,25},{9,17},{17,9},{25,1},{2,26},{10... | collective-permute-start | bytes 196616 | tf_op jit(solution)/shard_map/ppermute | solution.py:271
  138.6 2.6 %collective-permute-start.64 = (bf16[32,1024]{1,0:T(8,128)(2,1)S(1)}, bf16[32,1024]{1,0:T(8,128)(2,1)S(1)}, u32[]{:S(2)}, u32[]{:S(2)}) collective-permute-start(bf16[32,1024]{1,0:T(8,128)(2,1)S(1)} %get-tuple-element.137.refs_1_), channel_id=1, source_target_pairs={{0,16},{8,24},{16,0},{24,8},{1,17},{9,25},{17,1},{25,9},{2,18},{10... | collective-permute-start | bytes 196616 | tf_op jit(solution)/shard_map/ppermute | solution.py:271
  141.9 1.5 collective-permute-start.73
  143.6 2.0 %collective-permute-start.75 = (bf16[400,128]{1,0:T(8,128)(2,1)S(1)}, bf16[400,128]{1,0:T(8,128)(2,1)S(1)}, u32[]{:S(2)}, u32[]{:S(2)}) collective-permute-start(bf16[400,128]{1,0:T(8,128)(2,1)S(1)} %get-tuple-element.147), channel_id=1, source_target_pairs={{0,24},{8,16},{16,8},{24,0},{1,25},{9,17},{17,9},{25,1},{2,26},{10... | collective-permute-start | bytes 307208 | tf_op jit(solution)/shard_map/ppermute | solution.py:271
  146.6 1.5 collective-permute-start.69
  148.1 1.2 collective-permute-start.71
  150.0 1.7 collective-permute-done.75.refs_3_
  152.8 2.4 %collective-permute-start.78 = (bf16[32,1024]{1,0:T(8,128)(2,1)S(1)}, bf16[32,1024]{1,0:T(8,128)(2,1)S(1)}, u32[]{:S(2)}, u32[]{:S(2)}) collective-permute-start(bf16[32,1024]{1,0:T(8,128)(2,1)S(1)} %get-tuple-element.149.refs_1_), channel_id=1, source_target_pairs={{0,24},{8,16},{16,8},{24,0},{1,25},{9,17},{17,9},{25,1},{2,26},{10... | collective-permute-start | bytes 196616 | tf_op jit(solution)/shard_map/ppermute | solution.py:271
  155.2 2.7 %collective-permute-start.77 = (bf16[32,1024]{1,0:T(8,128)(2,1)S(1)}, bf16[32,1024]{1,0:T(8,128)(2,1)S(1)}, u32[]{:S(2)}, u32[]{:S(2)}) collective-permute-start(bf16[32,1024]{1,0:T(8,128)(2,1)S(1)} %get-tuple-element.149.refs_1_), channel_id=1, source_target_pairs={{0,16},{8,24},{16,0},{24,8},{1,17},{9,25},{17,1},{25,9},{2,18},{10... | collective-permute-start | bytes 196616 | tf_op jit(solution)/shard_map/ppermute | solution.py:271
  158.1 3.1 %collective-permute-done.77.refs_3_ = bf16[32,1024]{1,0:T(8,128)(2,1)S(1)} collective-permute-done((bf16[32,1024]{1,0:T(8,128)(2,1)S(1)}, bf16[32,1024]{1,0:T(8,128)(2,1)S(1)}, u32[]{:S(2)}, u32[]{:S(2)}) %collective-permute-start.77) | collective-permute-done | bytes 65568 | tf_op jit(solution)/shard_map/ppermute | solution.py:271
  163.4 1.6 collective-permute-start.81
  165.0 4.0 %collective-permute-start.72 = (bf16[32,1024]{1,0:T(8,128)(2,1)S(1)}, bf16[32,1024]{1,0:T(8,128)(2,1)S(1)}, u32[]{:S(2)}, u32[]{:S(2)}) collective-permute-start(bf16[32,1024]{1,0:T(8,128)(2,1)S(1)} %add_convert_fusion.1.refs_7_), channel_id=1, source_target_pairs={{0,0},{1,8},{2,16},{3,24},{8,1},{9,9},{10,17},{11,25},{16,2},{17,1... | collective-permute-start | bytes 196616 | tf_op jit(solution)/shard_map/ppermute | solution.py:422
  169.1 4.9 %collective-permute-start.82 = (bf16[32,1024]{1,0:T(8,128)(2,1)S(1)}, bf16[32,1024]{1,0:T(8,128)(2,1)S(1)}, u32[]{:S(2)}, u32[]{:S(2)}) collective-permute-start(bf16[32,1024]{1,0:T(8,128)(2,1)S(1)} %add_convert_fusion), channel_id=1, source_target_pairs={{0,0},{1,8},{2,16},{3,24},{8,1},{9,9},{10,17},{11,25},{16,2},{17,1... | collective-permute-start | bytes 196616 | tf_op jit(solution)/shard_map/ppermute | solution.py:422
  174.0 3.7 %collective-permute-done.82 = bf16[32,1024]{1,0:T(8,128)(2,1)S(1)} collective-permute-done((bf16[32,1024]{1,0:T(8,128)(2,1)S(1)}, bf16[32,1024]{1,0:T(8,128)(2,1)S(1)}, u32[]{:S(2)}, u32[]{:S(2)}) %collective-permute-start.82) | collective-permute-done | bytes 65568 | tf_op jit(solution)/shard_map/ppermute | solution.py:422
  177.7 6.4 %collective-permute-start.83 = (bf16[1,32,1024]{2,1,0:T(8,128)(2,1)S(1)}, bf16[1,32,1024]{2,1,0:T(8,128)(2,1)S(1)}, u32[]{:S(2)}, u32[]{:S(2)}) collective-permute-start(bf16[1,32,1024]{2,1,0:T(8,128)(2,1)S(1)} %select_bitcast_fusion.16), channel_id=1, source_target_pairs={{0,4},{4,0},{1,5},{5,1},{2,6},{6,2},{3,7},{7,3},{8,12},{12,8},{9,1... | collective-permute-start | bytes 196616 | tf_op jit(solution)/shard_map/ppermute | solution.py:271
  (165 shorter events, 43.4 us)
Async XLA Ops:
  2.2 19.6 %collective-permute-start.5 = (bf16[2,1,1024,1024]{3,2,1,0:T(8,128)(2,1)}, bf16[2,1,1024,1024]{3,2,1,0:T(8,128)(2,1)}, u32[]{:S(2)}, u32[]{:S(2)}) collective-permute-start(bf16[2,1,1024,1024]{3,2,1,0:T(8,128)(2,1)} %param.12), channel_id=1, source_target_pairs={{0,4},{4,0},{1,5},{5,1},{2,6},{6,2},{3,7},{7,3},{8,12},{12,8},{9,1... | collective-permute-start | bytes 12582920 | tf_op jit(solution)/shard_map/ppermute | solution.py:271
  2.5 28.3 %collective-permute-start.14 = (bf16[2,1,1024,1024]{3,2,1,0:T(8,128)(2,1)}, bf16[2,1,1024,1024]{3,2,1,0:T(8,128)(2,1)}, u32[]{:S(2)}, u32[]{:S(2)}) collective-permute-start(bf16[2,1,1024,1024]{3,2,1,0:T(8,128)(2,1)} %param.15), channel_id=1, source_target_pairs={{0,4},{4,0},{1,5},{5,1},{2,6},{6,2},{3,7},{7,3},{8,12},{12,8},{9,1... | collective-permute-start | bytes 12582920 | tf_op jit(solution)/shard_map/ppermute | solution.py:271
  2.7 14.4 %collective-permute-start.6 = (bf16[2,1,1024,256]{3,2,1,0:T(8,128)(2,1)}, bf16[2,1,1024,256]{3,2,1,0:T(8,128)(2,1)S(1)}, u32[]{:S(2)}, u32[]{:S(2)}) collective-permute-start(bf16[2,1,1024,256]{3,2,1,0:T(8,128)(2,1)} %param.13), channel_id=1, source_target_pairs={{0,4},{4,0},{1,5},{5,1},{2,6},{6,2},{3,7},{7,3},{8,12},{12,8},{9,1... | collective-permute-start | bytes 3145736 | tf_op jit(solution)/shard_map/ppermute | solution.py:271
  5.4 10.5 %collective-permute-start = (bf16[64,1024]{1,0:T(8,128)(2,1)S(1)}, bf16[64,1024]{1,0:T(8,128)(2,1)S(1)}, u32[]{:S(2)}, u32[]{:S(2)}) collective-permute-start(bf16[64,1024]{1,0:T(8,128)(2,1)S(1)} %bitcast.51), channel_id=1, source_target_pairs={{0,0},{1,8},{2,16},{3,24},{8,1},{9,9},{10,17},{11,25},{16,2},{17,1... | collective-permute-start | bytes 393224 | tf_op jit(solution)/shard_map/ppermute | solution.py:356
  10.6 9.9 %collective-permute-start.7 = (bf16[2,1,1024,256]{3,2,1,0:T(8,128)(2,1)}, bf16[2,1,1024,256]{3,2,1,0:T(8,128)(2,1)S(1)}, u32[]{:S(2)}, u32[]{:S(2)}) collective-permute-start(bf16[2,1,1024,256]{3,2,1,0:T(8,128)(2,1)} %param.14), channel_id=1, source_target_pairs={{0,4},{4,0},{1,5},{5,1},{2,6},{6,2},{3,7},{7,3},{8,12},{12,8},{9,1... | collective-permute-start | bytes 3145736 | tf_op jit(solution)/shard_map/ppermute | solution.py:271
  15.9 9.2 %collective-permute-start.3 = (bf16[64,1024]{1,0:T(8,128)(2,1)S(1)}, bf16[64,1024]{1,0:T(8,128)(2,1)S(1)}, u32[]{:S(2)}, u32[]{:S(2)}) collective-permute-start(bf16[64,1024]{1,0:T(8,128)(2,1)S(1)} %collective-permute-done.refs_1_), channel_id=1, source_target_pairs={{0,1},{1,0},{2,3},{3,2},{4,5},{5,4},{6,7},{7,6},{8,9},{9,8},{10,11... | collective-permute-start | bytes 393224 | tf_op jit(solution)/shard_map/ppermute | solution.py:271
  17.1 8.0 %collective-permute-start.2 = (bf16[64,1024]{1,0:T(8,128)(2,1)S(1)}, bf16[64,1024]{1,0:T(8,128)(2,1)S(1)}, u32[]{:S(2)}, u32[]{:S(2)}) collective-permute-start(bf16[64,1024]{1,0:T(8,128)(2,1)S(1)} %collective-permute-done.refs_1_), channel_id=1, source_target_pairs={{0,2},{1,3},{2,0},{3,1},{4,6},{5,7},{6,4},{7,5},{8,10},{9,11},{10,... | collective-permute-start | bytes 393224 | tf_op jit(solution)/shard_map/ppermute | solution.py:271
  26.5 7.2 %collective-permute-start.8 = (bf16[400,128]{1,0:T(8,128)(2,1)S(1)}, bf16[400,128]{1,0:T(8,128)(2,1)S(1)}, u32[]{:S(2)}, u32[]{:S(2)}) collective-permute-start(bf16[400,128]{1,0:T(8,128)(2,1)S(1)} %get-tuple-element.86), channel_id=1, source_target_pairs={{0,8},{8,0},{16,24},{24,16},{1,9},{9,1},{17,25},{25,17},{2,10},{10... | collective-permute-start | bytes 307208 | tf_op jit(solution)/shard_map/ppermute | solution.py:271
  26.6 7.1 %collective-permute-start.9 = (bf16[400,128]{1,0:T(8,128)(2,1)S(1)}, bf16[400,128]{1,0:T(8,128)(2,1)S(1)}, u32[]{:S(2)}, u32[]{:S(2)}) collective-permute-start(bf16[400,128]{1,0:T(8,128)(2,1)S(1)} %get-tuple-element.87), channel_id=1, source_target_pairs={{0,16},{8,24},{16,0},{24,8},{1,17},{9,25},{17,1},{25,9},{2,18},{10... | collective-permute-start | bytes 307208 | tf_op jit(solution)/shard_map/ppermute | solution.py:271
  30.2 6.4 %collective-permute-start.10 = (bf16[400,128]{1,0:T(8,128)(2,1)S(1)}, bf16[400,128]{1,0:T(8,128)(2,1)S(1)}, u32[]{:S(2)}, u32[]{:S(2)}) collective-permute-start(bf16[400,128]{1,0:T(8,128)(2,1)S(1)} %get-tuple-element.88), channel_id=1, source_target_pairs={{0,24},{8,16},{16,8},{24,0},{1,25},{9,17},{17,9},{25,1},{2,26},{10... | collective-permute-start | bytes 307208 | tf_op jit(solution)/shard_map/ppermute | solution.py:271
  37.5 7.4 %collective-permute-start.13 = (bf16[32,1024]{1,0:T(8,128)(2,1)S(1)}, bf16[32,1024]{1,0:T(8,128)(2,1)S(1)}, u32[]{:S(2)}, u32[]{:S(2)}) collective-permute-start(bf16[32,1024]{1,0:T(8,128)(2,1)S(1)} %get-tuple-element.91.refs_0_), channel_id=1, source_target_pairs={{0,24},{8,16},{16,8},{24,0},{1,25},{9,17},{17,9},{25,1},{2,26},{10... | collective-permute-start | bytes 196616 | tf_op jit(solution)/shard_map/ppermute | solution.py:271
  37.9 8.1 %collective-permute-start.12 = (bf16[32,1024]{1,0:T(8,128)(2,1)S(1)}, bf16[32,1024]{1,0:T(8,128)(2,1)S(1)}, u32[]{:S(2)}, u32[]{:S(2)}) collective-permute-start(bf16[32,1024]{1,0:T(8,128)(2,1)S(1)} %get-tuple-element.91.refs_0_), channel_id=1, source_target_pairs={{0,16},{8,24},{16,0},{24,8},{1,17},{9,25},{17,1},{25,9},{2,18},{10... | collective-permute-start | bytes 196616 | tf_op jit(solution)/shard_map/ppermute | solution.py:271
  44.9 8.1 %collective-permute-start.20 = (bf16[400,128]{1,0:T(8,128)(2,1)S(1)}, bf16[400,128]{1,0:T(8,128)(2,1)S(1)}, u32[]{:S(2)}, u32[]{:S(2)}) collective-permute-start(bf16[400,128]{1,0:T(8,128)(2,1)S(1)} %get-tuple-element.98), channel_id=1, source_target_pairs={{0,24},{8,16},{16,8},{24,0},{1,25},{9,17},{17,9},{25,1},{2,26},{10... | collective-permute-start | bytes 307208 | tf_op jit(solution)/shard_map/ppermute | solution.py:271
  46.5 11.8 %collective-permute-start.17 = (bf16[128,1024]{1,0:T(8,128)(2,1)S(1)}, bf16[128,1024]{1,0:T(8,128)(2,1)S(1)}, u32[]{:S(2)}, u32[]{:S(2)}) collective-permute-start(bf16[128,1024]{1,0:T(8,128)(2,1)S(1)} %project_out.8.refs_9_.refs_1_), channel_id=1, source_target_pairs={{0,1},{1,0},{2,3},{3,2},{4,5},{5,4},{6,7},{7,6},{8,9},{9,8},{10,11... | collective-permute-start | bytes 786440 | tf_op jit(solution)/shard_map/ppermute | solution.py:271
  46.6 11.8 %collective-permute-start.16 = (bf16[128,1024]{1,0:T(8,128)(2,1)S(1)}, bf16[128,1024]{1,0:T(8,128)(2,1)S(1)}, u32[]{:S(2)}, u32[]{:S(2)}) collective-permute-start(bf16[128,1024]{1,0:T(8,128)(2,1)S(1)} %project_out.8.refs_9_.refs_1_), channel_id=1, source_target_pairs={{0,2},{1,3},{2,0},{3,1},{4,6},{5,7},{6,4},{7,5},{8,10},{9,11},{10,... | collective-permute-start | bytes 786440 | tf_op jit(solution)/shard_map/ppermute | solution.py:271
  48.0 10.4 %collective-permute-start.15 = (bf16[128,1024]{1,0:T(8,128)(2,1)S(1)}, bf16[128,1024]{1,0:T(8,128)(2,1)S(1)}, u32[]{:S(2)}, u32[]{:S(2)}) collective-permute-start(bf16[128,1024]{1,0:T(8,128)(2,1)S(1)} %project_out.8.refs_9_.refs_1_), channel_id=1, source_target_pairs={{0,3},{1,2},{2,1},{3,0},{4,7},{5,6},{6,5},{7,4},{8,11},{9,10},{10,... | collective-permute-start | bytes 786440 | tf_op jit(solution)/shard_map/ppermute | solution.py:271
  54.1 6.7 %collective-permute-start.26 = (bf16[32,1024]{1,0:T(8,128)(2,1)S(1)}, bf16[32,1024]{1,0:T(8,128)(2,1)S(1)}, u32[]{:S(2)}, u32[]{:S(2)}) collective-permute-start(bf16[32,1024]{1,0:T(8,128)(2,1)S(1)} %get-tuple-element.106.refs_0_), channel_id=1, source_target_pairs={{0,24},{8,16},{16,8},{24,0},{1,25},{9,17},{17,9},{25,1},{2,26},{10... | collective-permute-start | bytes 196616 | tf_op jit(solution)/shard_map/ppermute | solution.py:271
  55.3 7.4 %collective-permute-start.25 = (bf16[32,1024]{1,0:T(8,128)(2,1)S(1)}, bf16[32,1024]{1,0:T(8,128)(2,1)S(1)}, u32[]{:S(2)}, u32[]{:S(2)}) collective-permute-start(bf16[32,1024]{1,0:T(8,128)(2,1)S(1)} %get-tuple-element.106.refs_0_), channel_id=1, source_target_pairs={{0,16},{8,24},{16,0},{24,8},{1,17},{9,25},{17,1},{25,9},{2,18},{10... | collective-permute-start | bytes 196616 | tf_op jit(solution)/shard_map/ppermute | solution.py:271
  59.0 5.9 %collective-permute-start.21 = (bf16[400,128]{1,0:T(8,128)(2,1)S(1)}, bf16[400,128]{1,0:T(8,128)(2,1)S(1)}, u32[]{:S(2)}, u32[]{:S(2)}) collective-permute-start(bf16[400,128]{1,0:T(8,128)(2,1)S(1)} %get-tuple-element.103), channel_id=1, source_target_pairs={{0,8},{8,0},{16,24},{24,16},{1,9},{9,1},{17,25},{25,17},{2,10},{10... | collective-permute-start | bytes 307208 | tf_op jit(solution)/shard_map/ppermute | solution.py:271
  60.6 6.8 %collective-permute-start.22 = (bf16[400,128]{1,0:T(8,128)(2,1)S(1)}, bf16[400,128]{1,0:T(8,128)(2,1)S(1)}, u32[]{:S(2)}, u32[]{:S(2)}) collective-permute-start(bf16[400,128]{1,0:T(8,128)(2,1)S(1)} %get-tuple-element.104), channel_id=1, source_target_pairs={{0,16},{8,24},{16,0},{24,8},{1,17},{9,25},{17,1},{25,9},{2,18},{10... | collective-permute-start | bytes 307208 | tf_op jit(solution)/shard_map/ppermute | solution.py:271
  60.8 7.8 %collective-permute-start.23 = (bf16[400,128]{1,0:T(8,128)(2,1)S(1)}, bf16[400,128]{1,0:T(8,128)(2,1)S(1)}, u32[]{:S(2)}, u32[]{:S(2)}) collective-permute-start(bf16[400,128]{1,0:T(8,128)(2,1)S(1)} %get-tuple-element.105), channel_id=1, source_target_pairs={{0,24},{8,16},{16,8},{24,0},{1,25},{9,17},{17,9},{25,1},{2,26},{10... | collective-permute-start | bytes 307208 | tf_op jit(solution)/shard_map/ppermute | solution.py:271
  63.2 11.9 %collective-permute-start.32 = (bf16[128,1024]{1,0:T(8,128)(2,1)S(1)}, bf16[128,1024]{1,0:T(8,128)(2,1)S(1)}, u32[]{:S(2)}, u32[]{:S(2)}) collective-permute-start(bf16[128,1024]{1,0:T(8,128)(2,1)S(1)} %project_out.9.refs_7_.refs_1_), channel_id=1, source_target_pairs={{0,1},{1,0},{2,3},{3,2},{4,5},{5,4},{6,7},{7,6},{8,9},{9,8},{10,11... | collective-permute-start | bytes 786440 | tf_op jit(solution)/shard_map/ppermute | solution.py:271
  63.7 11.3 %collective-permute-start.31 = (bf16[128,1024]{1,0:T(8,128)(2,1)S(1)}, bf16[128,1024]{1,0:T(8,128)(2,1)S(1)}, u32[]{:S(2)}, u32[]{:S(2)}) collective-permute-start(bf16[128,1024]{1,0:T(8,128)(2,1)S(1)} %project_out.9.refs_7_.refs_1_), channel_id=1, source_target_pairs={{0,2},{1,3},{2,0},{3,1},{4,6},{5,7},{6,4},{7,5},{8,10},{9,11},{10,... | collective-permute-start | bytes 786440 | tf_op jit(solution)/shard_map/ppermute | solution.py:271
  65.0 10.1 %collective-permute-start.30 = (bf16[128,1024]{1,0:T(8,128)(2,1)S(1)}, bf16[128,1024]{1,0:T(8,128)(2,1)S(1)}, u32[]{:S(2)}, u32[]{:S(2)}) collective-permute-start(bf16[128,1024]{1,0:T(8,128)(2,1)S(1)} %project_out.9.refs_7_.refs_1_), channel_id=1, source_target_pairs={{0,3},{1,2},{2,1},{3,0},{4,7},{5,6},{6,5},{7,4},{8,11},{9,10},{10,... | collective-permute-start | bytes 786440 | tf_op jit(solution)/shard_map/ppermute | solution.py:271
  69.6 7.9 %collective-permute-start.29 = (bf16[32,1024]{1,0:T(8,128)(2,1)S(1)}, bf16[32,1024]{1,0:T(8,128)(2,1)S(1)}, u32[]{:S(2)}, u32[]{:S(2)}) collective-permute-start(bf16[32,1024]{1,0:T(8,128)(2,1)S(1)} %get-tuple-element.107.refs_0_), channel_id=1, source_target_pairs={{0,24},{8,16},{16,8},{24,0},{1,25},{9,17},{17,9},{25,1},{2,26},{10... | collective-permute-start | bytes 196616 | tf_op jit(solution)/shard_map/ppermute | solution.py:271
  71.9 7.6 %collective-permute-start.28 = (bf16[32,1024]{1,0:T(8,128)(2,1)S(1)}, bf16[32,1024]{1,0:T(8,128)(2,1)S(1)}, u32[]{:S(2)}, u32[]{:S(2)}) collective-permute-start(bf16[32,1024]{1,0:T(8,128)(2,1)S(1)} %get-tuple-element.107.refs_0_), channel_id=1, source_target_pairs={{0,16},{8,24},{16,0},{24,8},{1,17},{9,25},{17,1},{25,9},{2,18},{10... | collective-permute-start | bytes 196616 | tf_op jit(solution)/shard_map/ppermute | solution.py:271
  77.3 6.3 %collective-permute-start.37 = (bf16[400,128]{1,0:T(8,128)(2,1)S(1)}, bf16[400,128]{1,0:T(8,128)(2,1)S(1)}, u32[]{:S(2)}, u32[]{:S(2)}) collective-permute-start(bf16[400,128]{1,0:T(8,128)(2,1)S(1)} %get-tuple-element.112), channel_id=1, source_target_pairs={{0,16},{8,24},{16,0},{24,8},{1,17},{9,25},{17,1},{25,9},{2,18},{10... | collective-permute-start | bytes 307208 | tf_op jit(solution)/shard_map/ppermute | solution.py:271
  77.5 8.1 %collective-permute-start.38 = (bf16[400,128]{1,0:T(8,128)(2,1)S(1)}, bf16[400,128]{1,0:T(8,128)(2,1)S(1)}, u32[]{:S(2)}, u32[]{:S(2)}) collective-permute-start(bf16[400,128]{1,0:T(8,128)(2,1)S(1)} %get-tuple-element.113), channel_id=1, source_target_pairs={{0,24},{8,16},{16,8},{24,0},{1,25},{9,17},{17,9},{25,1},{2,26},{10... | collective-permute-start | bytes 307208 | tf_op jit(solution)/shard_map/ppermute | solution.py:271
  79.9 11.6 %collective-permute-start.35 = (bf16[128,1024]{1,0:T(8,128)(2,1)S(1)}, bf16[128,1024]{1,0:T(8,128)(2,1)S(1)}, u32[]{:S(2)}, u32[]{:S(2)}) collective-permute-start(bf16[128,1024]{1,0:T(8,128)(2,1)S(1)} %project_out.10.refs_9_.refs_1_), channel_id=1, source_target_pairs={{0,1},{1,0},{2,3},{3,2},{4,5},{5,4},{6,7},{7,6},{8,9},{9,8},{10,11... | collective-permute-start | bytes 786440 | tf_op jit(solution)/shard_map/ppermute | solution.py:271
  80.6 10.9 %collective-permute-start.34 = (bf16[128,1024]{1,0:T(8,128)(2,1)S(1)}, bf16[128,1024]{1,0:T(8,128)(2,1)S(1)}, u32[]{:S(2)}, u32[]{:S(2)}) collective-permute-start(bf16[128,1024]{1,0:T(8,128)(2,1)S(1)} %project_out.10.refs_9_.refs_1_), channel_id=1, source_target_pairs={{0,2},{1,3},{2,0},{3,1},{4,6},{5,7},{6,4},{7,5},{8,10},{9,11},{10,... | collective-permute-start | bytes 786440 | tf_op jit(solution)/shard_map/ppermute | solution.py:271
  81.6 9.9 %collective-permute-start.33 = (bf16[128,1024]{1,0:T(8,128)(2,1)S(1)}, bf16[128,1024]{1,0:T(8,128)(2,1)S(1)}, u32[]{:S(2)}, u32[]{:S(2)}) collective-permute-start(bf16[128,1024]{1,0:T(8,128)(2,1)S(1)} %project_out.10.refs_9_.refs_1_), channel_id=1, source_target_pairs={{0,3},{1,2},{2,1},{3,0},{4,7},{5,6},{6,5},{7,4},{8,11},{9,10},{10,... | collective-permute-start | bytes 786440 | tf_op jit(solution)/shard_map/ppermute | solution.py:271
  86.7 7.2 %collective-permute-start.44 = (bf16[32,1024]{1,0:T(8,128)(2,1)S(1)}, bf16[32,1024]{1,0:T(8,128)(2,1)S(1)}, u32[]{:S(2)}, u32[]{:S(2)}) collective-permute-start(bf16[32,1024]{1,0:T(8,128)(2,1)S(1)} %get-tuple-element.121.refs_0_), channel_id=1, source_target_pairs={{0,24},{8,16},{16,8},{24,0},{1,25},{9,17},{17,9},{25,1},{2,26},{10... | collective-permute-start | bytes 196616 | tf_op jit(solution)/shard_map/ppermute | solution.py:271
  88.9 7.1 %collective-permute-start.43 = (bf16[32,1024]{1,0:T(8,128)(2,1)S(1)}, bf16[32,1024]{1,0:T(8,128)(2,1)S(1)}, u32[]{:S(2)}, u32[]{:S(2)}) collective-permute-start(bf16[32,1024]{1,0:T(8,128)(2,1)S(1)} %get-tuple-element.121.refs_0_), channel_id=1, source_target_pairs={{0,16},{8,24},{16,0},{24,8},{1,17},{9,25},{17,1},{25,9},{2,18},{10... | collective-permute-start | bytes 196616 | tf_op jit(solution)/shard_map/ppermute | solution.py:271
  93.8 6.4 %collective-permute-start.40 = (bf16[400,128]{1,0:T(8,128)(2,1)S(1)}, bf16[400,128]{1,0:T(8,128)(2,1)S(1)}, u32[]{:S(2)}, u32[]{:S(2)}) collective-permute-start(bf16[400,128]{1,0:T(8,128)(2,1)S(1)} %get-tuple-element.119), channel_id=1, source_target_pairs={{0,16},{8,24},{16,0},{24,8},{1,17},{9,25},{17,1},{25,9},{2,18},{10... | collective-permute-start | bytes 307208 | tf_op jit(solution)/shard_map/ppermute | solution.py:271
  93.9 8.0 %collective-permute-start.41 = (bf16[400,128]{1,0:T(8,128)(2,1)S(1)}, bf16[400,128]{1,0:T(8,128)(2,1)S(1)}, u32[]{:S(2)}, u32[]{:S(2)}) collective-permute-start(bf16[400,128]{1,0:T(8,128)(2,1)S(1)} %get-tuple-element.120), channel_id=1, source_target_pairs={{0,24},{8,16},{16,8},{24,0},{1,25},{9,17},{17,9},{25,1},{2,26},{10... | collective-permute-start | bytes 307208 | tf_op jit(solution)/shard_map/ppermute | solution.py:271
  96.4 11.6 %collective-permute-start.50 = (bf16[128,1024]{1,0:T(8,128)(2,1)S(1)}, bf16[128,1024]{1,0:T(8,128)(2,1)S(1)}, u32[]{:S(2)}, u32[]{:S(2)}) collective-permute-start(bf16[128,1024]{1,0:T(8,128)(2,1)S(1)} %project_out.11.refs_7_.refs_1_), channel_id=1, source_target_pairs={{0,1},{1,0},{2,3},{3,2},{4,5},{5,4},{6,7},{7,6},{8,9},{9,8},{10,11... | collective-permute-start | bytes 786440 | tf_op jit(solution)/shard_map/ppermute | solution.py:271
  96.5 11.5 %collective-permute-start.49 = (bf16[128,1024]{1,0:T(8,128)(2,1)S(1)}, bf16[128,1024]{1,0:T(8,128)(2,1)S(1)}, u32[]{:S(2)}, u32[]{:S(2)}) collective-permute-start(bf16[128,1024]{1,0:T(8,128)(2,1)S(1)} %project_out.11.refs_7_.refs_1_), channel_id=1, source_target_pairs={{0,2},{1,3},{2,0},{3,1},{4,6},{5,7},{6,4},{7,5},{8,10},{9,11},{10,... | collective-permute-start | bytes 786440 | tf_op jit(solution)/shard_map/ppermute | solution.py:271
  97.9 10.0 %collective-permute-start.48 = (bf16[128,1024]{1,0:T(8,128)(2,1)S(1)}, bf16[128,1024]{1,0:T(8,128)(2,1)S(1)}, u32[]{:S(2)}, u32[]{:S(2)}) collective-permute-start(bf16[128,1024]{1,0:T(8,128)(2,1)S(1)} %project_out.11.refs_7_.refs_1_), channel_id=1, source_target_pairs={{0,3},{1,2},{2,1},{3,0},{4,7},{5,6},{6,5},{7,4},{8,11},{9,10},{10,... | collective-permute-start | bytes 786440 | tf_op jit(solution)/shard_map/ppermute | solution.py:271
  102.9 7.6 %collective-permute-start.47 = (bf16[32,1024]{1,0:T(8,128)(2,1)S(1)}, bf16[32,1024]{1,0:T(8,128)(2,1)S(1)}, u32[]{:S(2)}, u32[]{:S(2)}) collective-permute-start(bf16[32,1024]{1,0:T(8,128)(2,1)S(1)} %get-tuple-element.122.refs_0_), channel_id=1, source_target_pairs={{0,24},{8,16},{16,8},{24,0},{1,25},{9,17},{17,9},{25,1},{2,26},{10... | collective-permute-start | bytes 196616 | tf_op jit(solution)/shard_map/ppermute | solution.py:271
  105.2 7.2 %collective-permute-start.46 = (bf16[32,1024]{1,0:T(8,128)(2,1)S(1)}, bf16[32,1024]{1,0:T(8,128)(2,1)S(1)}, u32[]{:S(2)}, u32[]{:S(2)}) collective-permute-start(bf16[32,1024]{1,0:T(8,128)(2,1)S(1)} %get-tuple-element.122.refs_0_), channel_id=1, source_target_pairs={{0,16},{8,24},{16,0},{24,8},{1,17},{9,25},{17,1},{25,9},{2,18},{10... | collective-permute-start | bytes 196616 | tf_op jit(solution)/shard_map/ppermute | solution.py:271
  110.2 6.5 %collective-permute-start.55 = (bf16[400,128]{1,0:T(8,128)(2,1)S(1)}, bf16[400,128]{1,0:T(8,128)(2,1)S(1)}, u32[]{:S(2)}, u32[]{:S(2)}) collective-permute-start(bf16[400,128]{1,0:T(8,128)(2,1)S(1)} %get-tuple-element.127), channel_id=1, source_target_pairs={{0,16},{8,24},{16,0},{24,8},{1,17},{9,25},{17,1},{25,9},{2,18},{10... | collective-permute-start | bytes 307208 | tf_op jit(solution)/shard_map/ppermute | solution.py:271
  110.5 8.0 %collective-permute-start.56 = (bf16[400,128]{1,0:T(8,128)(2,1)S(1)}, bf16[400,128]{1,0:T(8,128)(2,1)S(1)}, u32[]{:S(2)}, u32[]{:S(2)}) collective-permute-start(bf16[400,128]{1,0:T(8,128)(2,1)S(1)} %get-tuple-element.128), channel_id=1, source_target_pairs={{0,24},{8,16},{16,8},{24,0},{1,25},{9,17},{17,9},{25,1},{2,26},{10... | collective-permute-start | bytes 307208 | tf_op jit(solution)/shard_map/ppermute | solution.py:271
  112.8 11.8 %collective-permute-start.53 = (bf16[128,1024]{1,0:T(8,128)(2,1)S(1)}, bf16[128,1024]{1,0:T(8,128)(2,1)S(1)}, u32[]{:S(2)}, u32[]{:S(2)}) collective-permute-start(bf16[128,1024]{1,0:T(8,128)(2,1)S(1)} %project_out.12.refs_9_.refs_1_), channel_id=1, source_target_pairs={{0,1},{1,0},{2,3},{3,2},{4,5},{5,4},{6,7},{7,6},{8,9},{9,8},{10,11... | collective-permute-start | bytes 786440 | tf_op jit(solution)/shard_map/ppermute | solution.py:271
  113.3 11.3 %collective-permute-start.52 = (bf16[128,1024]{1,0:T(8,128)(2,1)S(1)}, bf16[128,1024]{1,0:T(8,128)(2,1)S(1)}, u32[]{:S(2)}, u32[]{:S(2)}) collective-permute-start(bf16[128,1024]{1,0:T(8,128)(2,1)S(1)} %project_out.12.refs_9_.refs_1_), channel_id=1, source_target_pairs={{0,2},{1,3},{2,0},{3,1},{4,6},{5,7},{6,4},{7,5},{8,10},{9,11},{10,... | collective-permute-start | bytes 786440 | tf_op jit(solution)/shard_map/ppermute | solution.py:271
  114.6 10.1 %collective-permute-start.51 = (bf16[128,1024]{1,0:T(8,128)(2,1)S(1)}, bf16[128,1024]{1,0:T(8,128)(2,1)S(1)}, u32[]{:S(2)}, u32[]{:S(2)}) collective-permute-start(bf16[128,1024]{1,0:T(8,128)(2,1)S(1)} %project_out.12.refs_9_.refs_1_), channel_id=1, source_target_pairs={{0,3},{1,2},{2,1},{3,0},{4,7},{5,6},{6,5},{7,4},{8,11},{9,10},{10,... | collective-permute-start | bytes 786440 | tf_op jit(solution)/shard_map/ppermute | solution.py:271
  119.6 7.4 %collective-permute-start.62 = (bf16[32,1024]{1,0:T(8,128)(2,1)S(1)}, bf16[32,1024]{1,0:T(8,128)(2,1)S(1)}, u32[]{:S(2)}, u32[]{:S(2)}) collective-permute-start(bf16[32,1024]{1,0:T(8,128)(2,1)S(1)} %get-tuple-element.136.refs_0_), channel_id=1, source_target_pairs={{0,24},{8,16},{16,8},{24,0},{1,25},{9,17},{17,9},{25,1},{2,26},{10... | collective-permute-start | bytes 196616 | tf_op jit(solution)/shard_map/ppermute | solution.py:271
  121.7 7.3 %collective-permute-start.61 = (bf16[32,1024]{1,0:T(8,128)(2,1)S(1)}, bf16[32,1024]{1,0:T(8,128)(2,1)S(1)}, u32[]{:S(2)}, u32[]{:S(2)}) collective-permute-start(bf16[32,1024]{1,0:T(8,128)(2,1)S(1)} %get-tuple-element.136.refs_0_), channel_id=1, source_target_pairs={{0,16},{8,24},{16,0},{24,8},{1,17},{9,25},{17,1},{25,9},{2,18},{10... | collective-permute-start | bytes 196616 | tf_op jit(solution)/shard_map/ppermute | solution.py:271
  126.9 6.3 %collective-permute-start.58 = (bf16[400,128]{1,0:T(8,128)(2,1)S(1)}, bf16[400,128]{1,0:T(8,128)(2,1)S(1)}, u32[]{:S(2)}, u32[]{:S(2)}) collective-permute-start(bf16[400,128]{1,0:T(8,128)(2,1)S(1)} %get-tuple-element.134), channel_id=1, source_target_pairs={{0,16},{8,24},{16,0},{24,8},{1,17},{9,25},{17,1},{25,9},{2,18},{10... | collective-permute-start | bytes 307208 | tf_op jit(solution)/shard_map/ppermute | solution.py:271
  127.0 8.0 %collective-permute-start.59 = (bf16[400,128]{1,0:T(8,128)(2,1)S(1)}, bf16[400,128]{1,0:T(8,128)(2,1)S(1)}, u32[]{:S(2)}, u32[]{:S(2)}) collective-permute-start(bf16[400,128]{1,0:T(8,128)(2,1)S(1)} %get-tuple-element.135), channel_id=1, source_target_pairs={{0,24},{8,16},{16,8},{24,0},{1,25},{9,17},{17,9},{25,1},{2,26},{10... | collective-permute-start | bytes 307208 | tf_op jit(solution)/shard_map/ppermute | solution.py:271
  129.5 11.7 %collective-permute-start.68 = (bf16[128,1024]{1,0:T(8,128)(2,1)S(1)}, bf16[128,1024]{1,0:T(8,128)(2,1)S(1)}, u32[]{:S(2)}, u32[]{:S(2)}) collective-permute-start(bf16[128,1024]{1,0:T(8,128)(2,1)S(1)} %project_out.13.refs_7_.refs_1_), channel_id=1, source_target_pairs={{0,1},{1,0},{2,3},{3,2},{4,5},{5,4},{6,7},{7,6},{8,9},{9,8},{10,11... | collective-permute-start | bytes 786440 | tf_op jit(solution)/shard_map/ppermute | solution.py:271
  129.6 11.7 %collective-permute-start.67 = (bf16[128,1024]{1,0:T(8,128)(2,1)S(1)}, bf16[128,1024]{1,0:T(8,128)(2,1)S(1)}, u32[]{:S(2)}, u32[]{:S(2)}) collective-permute-start(bf16[128,1024]{1,0:T(8,128)(2,1)S(1)} %project_out.13.refs_7_.refs_1_), channel_id=1, source_target_pairs={{0,2},{1,3},{2,0},{3,1},{4,6},{5,7},{6,4},{7,5},{8,10},{9,11},{10,... | collective-permute-start | bytes 786440 | tf_op jit(solution)/shard_map/ppermute | solution.py:271
  130.9 10.3 %collective-permute-start.66 = (bf16[128,1024]{1,0:T(8,128)(2,1)S(1)}, bf16[128,1024]{1,0:T(8,128)(2,1)S(1)}, u32[]{:S(2)}, u32[]{:S(2)}) collective-permute-start(bf16[128,1024]{1,0:T(8,128)(2,1)S(1)} %project_out.13.refs_7_.refs_1_), channel_id=1, source_target_pairs={{0,3},{1,2},{2,1},{3,0},{4,7},{5,6},{6,5},{7,4},{8,11},{9,10},{10,... | collective-permute-start | bytes 786440 | tf_op jit(solution)/shard_map/ppermute | solution.py:271
  135.9 7.7 %collective-permute-start.65 = (bf16[32,1024]{1,0:T(8,128)(2,1)S(1)}, bf16[32,1024]{1,0:T(8,128)(2,1)S(1)}, u32[]{:S(2)}, u32[]{:S(2)}) collective-permute-start(bf16[32,1024]{1,0:T(8,128)(2,1)S(1)} %get-tuple-element.137.refs_1_), channel_id=1, source_target_pairs={{0,24},{8,16},{16,8},{24,0},{1,25},{9,17},{17,9},{25,1},{2,26},{10... | collective-permute-start | bytes 196616 | tf_op jit(solution)/shard_map/ppermute | solution.py:271
  138.6 7.0 %collective-permute-start.64 = (bf16[32,1024]{1,0:T(8,128)(2,1)S(1)}, bf16[32,1024]{1,0:T(8,128)(2,1)S(1)}, u32[]{:S(2)}, u32[]{:S(2)}) collective-permute-start(bf16[32,1024]{1,0:T(8,128)(2,1)S(1)} %get-tuple-element.137.refs_1_), channel_id=1, source_target_pairs={{0,16},{8,24},{16,0},{24,8},{1,17},{9,25},{17,1},{25,9},{2,18},{10... | collective-permute-start | bytes 196616 | tf_op jit(solution)/shard_map/ppermute | solution.py:271
  141.9 6.2 %collective-permute-start.73 = (bf16[400,128]{1,0:T(8,128)(2,1)S(1)}, bf16[400,128]{1,0:T(8,128)(2,1)S(1)}, u32[]{:S(2)}, u32[]{:S(2)}) collective-permute-start(bf16[400,128]{1,0:T(8,128)(2,1)S(1)} %get-tuple-element.145), channel_id=1, source_target_pairs={{0,8},{8,0},{16,24},{24,16},{1,9},{9,1},{17,25},{25,17},{2,10},{10... | collective-permute-start | bytes 307208 | tf_op jit(solution)/shard_map/ppermute | solution.py:271
  143.5 6.5 %collective-permute-start.74 = (bf16[400,128]{1,0:T(8,128)(2,1)S(1)}, bf16[400,128]{1,0:T(8,128)(2,1)S(1)}, u32[]{:S(2)}, u32[]{:S(2)}) collective-permute-start(bf16[400,128]{1,0:T(8,128)(2,1)S(1)} %get-tuple-element.146), channel_id=1, source_target_pairs={{0,16},{8,24},{16,0},{24,8},{1,17},{9,25},{17,1},{25,9},{2,18},{10... | collective-permute-start | bytes 307208 | tf_op jit(solution)/shard_map/ppermute | solution.py:271
  143.6 8.1 %collective-permute-start.75 = (bf16[400,128]{1,0:T(8,128)(2,1)S(1)}, bf16[400,128]{1,0:T(8,128)(2,1)S(1)}, u32[]{:S(2)}, u32[]{:S(2)}) collective-permute-start(bf16[400,128]{1,0:T(8,128)(2,1)S(1)} %get-tuple-element.147), channel_id=1, source_target_pairs={{0,24},{8,16},{16,8},{24,0},{1,25},{9,17},{17,9},{25,1},{2,26},{10... | collective-permute-start | bytes 307208 | tf_op jit(solution)/shard_map/ppermute | solution.py:271
  146.6 11.3 %collective-permute-start.69 = (bf16[32,1024]{1,0:T(8,128)(2,1)S(1)}, bf16[32,1024]{1,0:T(8,128)(2,1)S(1)}, u32[]{:S(2)}, u32[]{:S(2)}) collective-permute-start(bf16[32,1024]{1,0:T(8,128)(2,1)S(1)} %get-tuple-element.141), channel_id=1, source_target_pairs={{0,3},{1,2},{2,1},{3,0},{4,7},{5,6},{6,5},{7,4},{8,11},{9,10},{10,... | collective-permute-start | bytes 196616 | tf_op jit(solution)/shard_map/ppermute | solution.py:271
  148.1 9.8 %collective-permute-start.70 = (bf16[32,1024]{1,0:T(8,128)(2,1)S(1)}, bf16[32,1024]{1,0:T(8,128)(2,1)S(1)}, u32[]{:S(2)}, u32[]{:S(2)}) collective-permute-start(bf16[32,1024]{1,0:T(8,128)(2,1)S(1)} %get-tuple-element.142), channel_id=1, source_target_pairs={{0,2},{1,3},{2,0},{3,1},{4,6},{5,7},{6,4},{7,5},{8,10},{9,11},{10,... | collective-permute-start | bytes 196616 | tf_op jit(solution)/shard_map/ppermute | solution.py:271
  148.1 9.8 %collective-permute-start.71 = (bf16[32,1024]{1,0:T(8,128)(2,1)S(1)}, bf16[32,1024]{1,0:T(8,128)(2,1)S(1)}, u32[]{:S(2)}, u32[]{:S(2)}) collective-permute-start(bf16[32,1024]{1,0:T(8,128)(2,1)S(1)} %get-tuple-element.143), channel_id=1, source_target_pairs={{0,1},{1,0},{2,3},{3,2},{4,5},{5,4},{6,7},{7,6},{8,9},{9,8},{10,11... | collective-permute-start | bytes 196616 | tf_op jit(solution)/shard_map/ppermute | solution.py:271
  162.3 6.7 %collective-permute-start.79 = (bf16[32,1024]{1,0:T(8,128)(2,1)S(1)}, bf16[32,1024]{1,0:T(8,128)(2,1)S(1)}, u32[]{:S(2)}, u32[]{:S(2)}) collective-permute-start(bf16[32,1024]{1,0:T(8,128)(2,1)S(1)} %get-tuple-element.152), channel_id=1, source_target_pairs={{0,3},{1,2},{2,1},{3,0},{4,7},{5,6},{6,5},{7,4},{8,11},{9,10},{10,... | collective-permute-start | bytes 196616 | tf_op jit(solution)/shard_map/ppermute | solution.py:271
  165.0 9.0 %collective-permute-start.72 = (bf16[32,1024]{1,0:T(8,128)(2,1)S(1)}, bf16[32,1024]{1,0:T(8,128)(2,1)S(1)}, u32[]{:S(2)}, u32[]{:S(2)}) collective-permute-start(bf16[32,1024]{1,0:T(8,128)(2,1)S(1)} %add_convert_fusion.1.refs_7_), channel_id=1, source_target_pairs={{0,0},{1,8},{2,16},{3,24},{8,1},{9,9},{10,17},{11,25},{16,2},{17,1... | collective-permute-start | bytes 196616 | tf_op jit(solution)/shard_map/ppermute | solution.py:422
  169.1 8.6 %collective-permute-start.82 = (bf16[32,1024]{1,0:T(8,128)(2,1)S(1)}, bf16[32,1024]{1,0:T(8,128)(2,1)S(1)}, u32[]{:S(2)}, u32[]{:S(2)}) collective-permute-start(bf16[32,1024]{1,0:T(8,128)(2,1)S(1)} %add_convert_fusion), channel_id=1, source_target_pairs={{0,0},{1,8},{2,16},{3,24},{8,1},{9,9},{10,17},{11,25},{16,2},{17,1... | collective-permute-start | bytes 196616 | tf_op jit(solution)/shard_map/ppermute | solution.py:422
  177.7 7.3 %collective-permute-start.83 = (bf16[1,32,1024]{2,1,0:T(8,128)(2,1)S(1)}, bf16[1,32,1024]{2,1,0:T(8,128)(2,1)S(1)}, u32[]{:S(2)}, u32[]{:S(2)}) collective-permute-start(bf16[1,32,1024]{2,1,0:T(8,128)(2,1)S(1)} %select_bitcast_fusion.16), channel_id=1, source_target_pairs={{0,4},{4,0},{1,5},{5,1},{2,6},{6,2},{3,7},{7,3},{8,12},{12,8},{9,1... | collective-permute-start | bytes 196616 | tf_op jit(solution)/shard_map/ppermute | solution.py:271
  (29 other events, 135.7 us)
